TPU v7x, 512 devices: a whole 4x8x8 slice. The times are simulated.
512 devices in a mesh: skyy: 16 (over y, x_hi), skyx: 32 (over x_lo, z, core).
Axes of the slice: x: 4 (x_hi: 2, x_lo: 2; x = x_hi * 2 + x_lo), y: 8, z: 8, core: 2. Of those that a mesh axis runs over, the one named last changes fastest.
Arguments:
- cube: float32 [256, 512, 512], P('skyy', 'skyx'), may hold values from -8 to 8
- level_table: float32 [16], replicated, may hold values from 0.05 to 0.6
- level_index: int32 [4, 512], replicated, may hold values from 0 to 15
- amplitude: float32 [8, 256, 512], P(None, 'skyy', 'skyx'), may hold values from 0.3 to 2
- centre_index: int32 [8, 256, 512], P(None, 'skyy', 'skyx'), may hold values from 0 to 511
- spread: float32 [8, 256, 512], P(None, 'skyy', 'skyx'), may hold values from 3 to 30
Outputs:
- denoised: float32 [256, 512, 512], P('skyy', 'skyx')
- fitted: float32 [3, 8, 256, 512], P(None, None, 'skyy', 'skyx')
All inputs are finite; a program needn't handle non-finite values.
Results may differ from a plain program's by a relative error of at most 0.00002.
Values sent between devices are 32-bit elements; how exact they have to be, the bound alone decides.
No kernel may reach another device: no remote copies, remote signals or barrier semaphores. Data moves between devices by JAX's collectives and lax.ppermute only.
A program may use at most 64 MiB of HBM per device.

v0:
```python
import jax
import jax.numpy as jnp
from jax import lax
from jax.sharding import PartitionSpec as P


def with_halo(shard, sides, width):
    for axis, dim in sides:
        size, length = (lax.axis_size(axis), shard.shape[dim])
        up = [(i, (i + 1) % size) for i in range(size - 1)]
        down = [(j, i) for i, j in up]
        last = lax.slice_in_dim(shard, length - width, length, axis=dim)
        first = lax.slice_in_dim(shard, 0, width, axis=dim)
        before = lax.ppermute(last, axis, up)
        after = lax.ppermute(first, axis, down)
        shard = jnp.concatenate([before, shard, after], axis=dim)
    return shard


def smoothed_mirror_input(mirror_padded, target_axis, hole_spacing, axis_length):

    def gather_shifted(offset):
        return lax.slice_in_dim(mirror_padded, offset, offset + axis_length, axis=target_axis)

    return (
        gather_shifted(0)
        + gather_shifted(4 * hole_spacing)
        + 4.0 * (gather_shifted(hole_spacing) + gather_shifted(3 * hole_spacing))
        + 6.0 * gather_shifted(2 * hole_spacing)
    ) / 16.0


def smooth_each_channel(image_plane, hole_spacing):
    mirror_padded = jnp.pad(image_plane, ((0, 0), (0, 0), (2 * hole_spacing, 2 * hole_spacing)))
    return smoothed_mirror_input(mirror_padded, 2, hole_spacing, image_plane.shape[2])


def smooth_one_level(image_plane, hole_spacing):
    row_count = image_plane.shape[0]
    column_count = image_plane.shape[1]
    kernel_extent = 2 * hole_spacing
    spectral_cube = smooth_each_channel(image_plane, hole_spacing)
    mirror_padded = with_halo(spectral_cube, (("skyy", 0),), kernel_extent)
    smooth_over_rows = smoothed_mirror_input(mirror_padded, 0, hole_spacing, row_count)
    mirror_padded_columns = with_halo(smooth_over_rows, (("skyx", 1),), kernel_extent)
    return smoothed_mirror_input(mirror_padded_columns, 1, hole_spacing, column_count)


def stencil(mirror_padded):
    inner = mirror_padded[:, :, 1:-1, 1:-1]
    return 4.0 * inner - (
        mirror_padded[:, :, :-2, 1:-1]
        + mirror_padded[:, :, 2:, 1:-1]
        + mirror_padded[:, :, 1:-1, :-2]
        + mirror_padded[:, :, 1:-1, 2:]
    )


def rim_once(params):
    return with_halo(params, (("skyy", 2), ("skyx", 3)), 1)


def on_device(cube, level_table, level_index, amplitude, centre_index, spread):
    nch = cube.shape[2]
    entries = jnp.arange(level_table.shape[0], dtype=jnp.int32)
    picks = (level_index[:, :, None] == entries[None, None, :]).astype(jnp.float32)
    weight = jnp.sum(picks * level_table[None, None, :], axis=2)
    present_plane = cube
    total = jnp.zeros_like(cube)
    for scale_level in range(weight.shape[0]):
        next_plane = smooth_one_level(present_plane, 2**scale_level)
        total = total + weight[scale_level][None, None, :] * (present_plane - next_plane)
        present_plane = next_plane
    denoised = total + present_plane
    chans = jnp.arange(nch, dtype=jnp.float32)
    frac = (centre_index.astype(jnp.float32) + 0.5) / nch
    centre = frac * nch

    def add_model(acc, item):
        amp, mu, sig = item
        diff = chans[None, None, :] - mu[:, :, None]
        bump = jnp.exp(-diff * diff / (2.0 * sig[:, :, None] * sig[:, :, None]))
        return (acc + amp[:, :, None] * bump, None)

    model, _ = lax.scan(add_model, jnp.zeros_like(cube), (amplitude, centre, spread))
    resid = model - denoised

    def grads(item):
        amp, mu, sig = item
        sig3 = sig[:, :, None]
        diff = chans[None, None, :] - mu[:, :, None]
        bump = jnp.exp(-diff * diff / (2.0 * sig3 * sig3))
        g_amp = jnp.sum(resid * bump, axis=2) / nch
        term = resid * amp[:, :, None] * bump * diff / (sig3 * sig3)
        g_pos = jnp.sum(term, axis=2)
        g_sig = jnp.sum(term * diff / sig3, axis=2) / nch
        return jnp.stack([g_amp, g_pos, g_sig])

    per_comp = lax.map(grads, (amplitude, centre, spread))
    gradient = jnp.transpose(per_comp, (1, 0, 2, 3))
    params = jnp.stack([amplitude, frac, spread])
    first = stencil(rim_once(params))
    smoothing = stencil(rim_once(first))
    steps = jnp.array([0.5, 0.002, 2.0], jnp.float32)[:, None, None, None]
    lams = jnp.array([0.2, 0.5, 0.05], jnp.float32)[:, None, None, None]
    fitted = params - steps * (gradient + lams * smoothing)
    return (denoised, fitted)


def solution(mesh):
    placed = (
        P("skyy", "skyx", None),
        P(),
        P(),
        P(None, "skyy", "skyx"),
        P(None, "skyy", "skyx"),
        P(None, "skyy", "skyx"),
    )
    return jax.shard_map(
        on_device,
        mesh=mesh,
        in_specs=placed,
        out_specs=(P("skyy", "skyx", None), P(None, None, "skyy", "skyx")),
        check_vma=False,
    )
```

profile of v0, /device:TPU:34, one launch (start us, length us, event | category | flops | bytes accessed | tf_op | source)
XLA Modules:
  0.0 166.4 jit_solution(12302347424311080905)
XLA Ops:
  0.6 2.5 %broadcast_multiply_fusion.10 = (f32[16,16,512]{2,1,0:T(8,128)S(1)}, f32[16,16,512]{2,1,0:T(8,128)S(1)}) fusion(f32[16,16,512]{2,1,0:T(8,128)} %param.12), kind=kLoop, calls=%fused_computation.169 | loop fusion | flops 917504 | bytes 1572864 | tf_op jit(solution)/shard_map/div | solution.py:25
  3.2 4.0 %collective-permute-start = (f32[2,16,512]{2,1,0:T(8,128)S(1)}, f32[2,16,512]{2,1,0:T(8,128)S(1)}, u32[]{:S(2)}, u32[]{:S(2)}) collective-permute-start(f32[2,16,512]{2,1,0:T(8,128)S(1)} %get-tuple-element.172), channel_id=1, source_target_pairs={{0,32},{32,64},{64,96},{96,128},{128,160},{160,192},{192,224},{224... | collective-permute-start | bytes 196616 | tf_op jit(solution)/shard_map/ppermute | solution.py:14
  7.2 5.4 %collective-permute-start.1 = (f32[2,16,512]{2,1,0:T(8,128)S(1)}, f32[2,16,512]{2,1,0:T(8,128)S(1)}, u32[]{:S(2)}, u32[]{:S(2)}) collective-permute-start(f32[2,16,512]{2,1,0:T(8,128)S(1)} %get-tuple-element.173), channel_id=1, source_target_pairs={{32,0},{64,32},{96,64},{128,96},{160,128},{192,160},{224,192},{256... | collective-permute-start | bytes 196616 | tf_op jit(solution)/shard_map/ppermute | solution.py:15
  15.1 1.9 %collective-permute-start.2 = (f32[16,2,512]{2,1,0:T(2,128)S(1)}, f32[16,2,512]{2,1,0:T(2,128)S(1)}, u32[]{:S(2)}, u32[]{:S(2)}) collective-permute-start(f32[16,2,512]{2,1,0:T(2,128)S(1)} %get-tuple-element.170), channel_id=1, source_target_pairs={{0,1},{1,2},{2,3},{3,4},{4,5},{5,6},{6,7},{7,8},{8,9},{9,10},{10,1... | collective-permute-start | bytes 196616 | tf_op jit(solution)/shard_map/ppermute | solution.py:14
  17.0 9.8 %collective-permute-start.3 = (f32[16,2,512]{2,1,0:T(2,128)S(1)}, f32[16,2,512]{2,1,0:T(2,128)S(1)}, u32[]{:S(2)}, u32[]{:S(2)}) collective-permute-start(f32[16,2,512]{2,1,0:T(2,128)S(1)} %get-tuple-element.171), channel_id=1, source_target_pairs={{1,0},{2,1},{3,2},{4,3},{5,4},{6,5},{7,6},{8,7},{9,8},{10,9},{11,1... | collective-permute-start | bytes 196616 | tf_op jit(solution)/shard_map/ppermute | solution.py:15
  29.8 2.8 %collective-permute-start.4 = (f32[4,16,512]{2,1,0:T(8,128)S(1)}, f32[4,16,512]{2,1,0:T(8,128)S(1)}, u32[]{:S(2)}, u32[]{:S(2)}) collective-permute-start(f32[4,16,512]{2,1,0:T(8,128)S(1)} %get-tuple-element.168), channel_id=1, source_target_pairs={{0,32},{32,64},{64,96},{96,128},{128,160},{160,192},{192,224},{224... | collective-permute-start | bytes 393224 | tf_op jit(solution)/shard_map/ppermute | solution.py:14
  32.6 6.6 %collective-permute-start.5 = (f32[4,16,512]{2,1,0:T(8,128)S(1)}, f32[4,16,512]{2,1,0:T(8,128)S(1)}, u32[]{:S(2)}, u32[]{:S(2)}) collective-permute-start(f32[4,16,512]{2,1,0:T(8,128)S(1)} %get-tuple-element.169), channel_id=1, source_target_pairs={{32,0},{64,32},{96,64},{128,96},{160,128},{192,160},{224,192},{256... | collective-permute-start | bytes 393224 | tf_op jit(solution)/shard_map/ppermute | solution.py:15
  43.9 7.6 %collective-permute-start.7 = (f32[16,4,512]{2,1,0:T(4,128)S(1)}, f32[16,4,512]{2,1,0:T(4,128)S(1)}, u32[]{:S(2)}, u32[]{:S(2)}) collective-permute-start(f32[16,4,512]{2,1,0:T(4,128)S(1)} %get-tuple-element.167), channel_id=1, source_target_pairs={{1,0},{2,1},{3,2},{4,3},{5,4},{6,5},{7,6},{8,7},{9,8},{10,9},{11,1... | collective-permute-start | bytes 393224 | tf_op jit(solution)/shard_map/ppermute | solution.py:15
  55.9 2.9 %collective-permute-start.8 = (f32[8,16,512]{2,1,0:T(8,128)S(1)}, f32[8,16,512]{2,1,0:T(8,128)S(1)}, u32[]{:S(2)}, u32[]{:S(2)}) collective-permute-start(f32[8,16,512]{2,1,0:T(8,128)S(1)} %get-tuple-element.164), channel_id=1, source_target_pairs={{0,32},{32,64},{64,96},{96,128},{128,160},{160,192},{192,224},{224... | collective-permute-start | bytes 786440 | tf_op jit(solution)/shard_map/ppermute | solution.py:14
  58.8 6.5 %collective-permute-start.9 = (f32[8,16,512]{2,1,0:T(8,128)S(1)}, f32[8,16,512]{2,1,0:T(8,128)S(1)}, u32[]{:S(2)}, u32[]{:S(2)}) collective-permute-start(f32[8,16,512]{2,1,0:T(8,128)S(1)} %get-tuple-element.165), channel_id=1, source_target_pairs={{32,0},{64,32},{96,64},{128,96},{160,128},{192,160},{224,192},{256... | collective-permute-start | bytes 786440 | tf_op jit(solution)/shard_map/ppermute | solution.py:15
  67.9 7.5 %collective-permute-start.17 = (f32[3,8,1,16]{3,2,1,0:T(1,128)}, f32[3,8,1,16]{3,2,1,0:T(1,128)}, u32[]{:S(2)}, u32[]{:S(2)}) collective-permute-start(f32[3,8,1,16]{3,2,1,0:T(1,128)} %get-tuple-element.181), channel_id=1, source_target_pairs={{32,0},{64,32},{96,64},{128,96},{160,128},{192,160},{224,192},{256... | collective-permute-start | bytes 4616 | tf_op jit(solution)/shard_map/ppermute | solution.py:15
  81.1 5.8 %collective-permute-start.11 = (f32[16,8,512]{2,1,0:T(8,128)}, f32[16,8,512]{2,1,0:T(8,128)S(1)}, u32[]{:S(2)}, u32[]{:S(2)}) collective-permute-start(f32[16,8,512]{2,1,0:T(8,128)} %get-tuple-element.163), channel_id=1, source_target_pairs={{1,0},{2,1},{3,2},{4,3},{5,4},{6,5},{7,6},{8,7},{9,8},{10,9},{11,1... | collective-permute-start | bytes 786440 | tf_op jit(solution)/shard_map/ppermute | solution.py:15
  86.9 2.5 %while.23 = (s32[]{:T(128)}, f32[16,16,512]{2,1,0:T(8,128)S(1)}, f32[8,16,16]{2,1,0:T(8,128)S(1)}, f32[8,16,16]{2,1,0:T(8,128)S(1)}, f32[8,16,16]{2,1,0:T(8,128)S(1)}, /*index=5*/s32[]{:T(128)}, s32[]{:T(128)}) while((s32[]{:T(128)}, f32[16,16,512]{2,1,0:T(8,128)S(1)}, f32[8,16,16]{2,1,0:T(8,128)S(1)}, f32[8,16,16]{2,1,0:T(8,128)S(1)}, ...), condition=%wide.region_2.3_spmd.clone, body=%wide.region_1.2_spmd.clone.sunk | while | flops 918019 | bytes 1057887 | solution.py:85
  95.8 7.5 %collective-permute-start.13 = (f32[16,16,512]{2,1,0:T(8,128)S(1)}, f32[16,16,512]{2,1,0:T(8,128)S(1)}, u32[]{:S(2)}, u32[]{:S(2)}) collective-permute-start(f32[16,16,512]{2,1,0:T(8,128)S(1)} %get-tuple-element.138), channel_id=1, source_target_pairs={{32,0},{64,32},{96,64},{128,96},{160,128},{192,160},{224,192},{256... | collective-permute-start | bytes 1572872 | tf_op jit(solution)/shard_map/ppermute | solution.py:15
  103.5 1.9 %collective-permute-start.18 = (f32[3,8,18,1]{3,2,1,0:T(8,128)S(1)}, f32[3,8,18,1]{3,2,1,0:T(8,128)S(1)}, u32[]{:S(2)}, u32[]{:S(2)}) collective-permute-start(f32[3,8,18,1]{3,2,1,0:T(8,128)S(1)} %get-tuple-element.176), channel_id=1, source_target_pairs={{0,1},{1,2},{2,3},{3,4},{4,5},{5,6},{6,7},{7,8},{8,9},{9,10},{10,1... | collective-permute-start | bytes 5192 | tf_op jit(solution)/shard_map/ppermute | solution.py:14
  105.4 5.8 %collective-permute-start.19 = (f32[3,8,18,1]{3,2,1,0:T(8,128)S(1)}, f32[3,8,18,1]{3,2,1,0:T(8,128)S(1)}, u32[]{:S(2)}, u32[]{:S(2)}) collective-permute-start(f32[3,8,18,1]{3,2,1,0:T(8,128)S(1)} %get-tuple-element.177), channel_id=1, source_target_pairs={{1,0},{2,1},{3,2},{4,3},{5,4},{6,5},{7,6},{8,7},{9,8},{10,9},{11,1... | collective-permute-start | bytes 5192 | tf_op jit(solution)/shard_map/ppermute | solution.py:15
  111.3 2.3 %collective-permute-done.18 = f32[3,8,18,1]{3,2,1,0:T(8,128)S(1)} collective-permute-done((f32[3,8,18,1]{3,2,1,0:T(8,128)S(1)}, f32[3,8,18,1]{3,2,1,0:T(8,128)S(1)}, u32[]{:S(2)}, u32[]{:S(2)}) %collective-permute-start.18) | collective-permute-done | bytes 1760 | tf_op jit(solution)/shard_map/ppermute | solution.py:14
  119.0 7.5 %collective-permute-start.21 = (f32[3,8,1,16]{3,2,1,0:T(1,128)}, f32[3,8,1,16]{3,2,1,0:T(1,128)}, u32[]{:S(2)}, u32[]{:S(2)}) collective-permute-start(f32[3,8,1,16]{3,2,1,0:T(1,128)} %get-tuple-element.179), channel_id=1, source_target_pairs={{32,0},{64,32},{96,64},{128,96},{160,128},{192,160},{224,192},{256... | collective-permute-start | bytes 4616 | tf_op jit(solution)/shard_map/ppermute | solution.py:15
  129.5 5.8 %collective-permute-start.15 = (f32[16,16,512]{2,1,0:T(8,128)S(1)}, f32[16,16,512]{2,1,0:T(8,128)}, u32[]{:S(2)}, u32[]{:S(2)}) collective-permute-start(f32[16,16,512]{2,1,0:T(8,128)S(1)} %get-tuple-element.136), channel_id=1, source_target_pairs={{1,0},{2,1},{3,2},{4,3},{5,4},{6,5},{7,6},{8,7},{9,8},{10,9},{11,1... | collective-permute-start | bytes 1572872 | tf_op jit(solution)/shard_map/ppermute | solution.py:15
  137.6 2.0 %collective-permute-start.22 = (f32[3,8,18,1]{3,2,1,0:T(8,128)}, f32[3,8,18,1]{3,2,1,0:T(8,128)}, u32[]{:S(2)}, u32[]{:S(2)}) collective-permute-start(f32[3,8,18,1]{3,2,1,0:T(8,128)} %get-tuple-element.174), channel_id=1, source_target_pairs={{0,1},{1,2},{2,3},{3,4},{4,5},{5,6},{6,7},{7,8},{8,9},{9,10},{10,1... | collective-permute-start | bytes 5192 | tf_op jit(solution)/shard_map/ppermute | solution.py:14
  139.6 5.8 %collective-permute-start.23 = (f32[3,8,18,1]{3,2,1,0:T(8,128)}, f32[3,8,18,1]{3,2,1,0:T(8,128)}, u32[]{:S(2)}, u32[]{:S(2)}) collective-permute-start(f32[3,8,18,1]{3,2,1,0:T(8,128)} %get-tuple-element.175), channel_id=1, source_target_pairs={{1,0},{2,1},{3,2},{4,3},{5,4},{6,5},{7,6},{8,7},{9,8},{10,9},{11,1... | collective-permute-start | bytes 5192 | tf_op jit(solution)/shard_map/ppermute | solution.py:15
  146.1 2.8 %fusion.100 = (f32[16,16,512]{2,1,0:T(8,128)S(1)}, f32[16,16,512]{2,1,0:T(8,128)}) fusion(f32[16,16,512]{2,1,0:T(8,128)S(1)} %get-tuple-element.71, f32[16,16,512]{2,1,0:T(8,128)S(1)} %copy-done.1, f32[16,16,512]{2,1,0:T(8,128)} %collective-permute-done.15, f32[16,16,512]{2,1,0:T(8,128)S(1)} %get-tuple-element.136, ...), kind=kLoop, calls=%fused_computation.212 | loop fusion | flops 3276800 | bytes 5775360 | tf_op jit(solution)/shard_map/sub | solution.py:86
  148.9 14.8 %while.22 = (s32[]{:T(128)}, f32[8,3,16,16]{3,2,0,1:T(8,128)}, f32[8,16,16]{2,1,0:T(8,128)}, f32[8,16,16]{2,1,0:T(8,128)S(1)}, f32[16,16,512]{2,1,0:T(8,128)S(1)}, /*index=5*/f32[8,16,16]{2,1,0:T(8,128)S(1)}, s32[]{:T(128)}) while((s32[]{:T(128)}, f32[8,3,16,16]{3,2,0,1:T(8,128)}, f32[8,16,16]{2,1,0:T(8,128)}, ...), condition=%wide.region_7.8_spmd.clone, body=%wide.region_3.7_spmd.clone.sunk | while | flops 1837058 | bytes 575061 | solution.py:99
  164.3 2.1 %fusion.92 = f32[3,8,16,16]{3,2,1,0:T(8,128)} fusion(f32[3,8,18,1]{3,2,1,0:T(8,128)} %collective-permute-done.23, f32[3,8,1,16]{3,2,1,0:T(1,128)} %collective-permute-done.21, f32[3,8,16,16]{3,2,1,0:T(8,128)S(1)} %fusion.96, f32[3,8,1,16]{3,2,1,0:T(1,128)S(1)} %collective-permute-done.20, f32[3,8,18,1]{3,2,1,0:T(8,128)} %collective-permute-done.22, ...), kind=kLoop, calls=%fused_computation.176 | loop fusion | flops 116736 | bytes 104856 | tf_op jit(solution)/shard_map/sub | solution.py:106
  (172 shorter events, 57.6 us)
Async XLA Ops:
  3.2 9.8 %collective-permute-start = (f32[2,16,512]{2,1,0:T(8,128)S(1)}, f32[2,16,512]{2,1,0:T(8,128)S(1)}, u32[]{:S(2)}, u32[]{:S(2)}) collective-permute-start(f32[2,16,512]{2,1,0:T(8,128)S(1)} %get-tuple-element.172), channel_id=1, source_target_pairs={{0,32},{32,64},{64,96},{96,128},{128,160},{160,192},{192,224},{224... | collective-permute-start | bytes 196616 | tf_op jit(solution)/shard_map/ppermute | solution.py:14
  7.2 7.7 %collective-permute-start.1 = (f32[2,16,512]{2,1,0:T(8,128)S(1)}, f32[2,16,512]{2,1,0:T(8,128)S(1)}, u32[]{:S(2)}, u32[]{:S(2)}) collective-permute-start(f32[2,16,512]{2,1,0:T(8,128)S(1)} %get-tuple-element.173), channel_id=1, source_target_pairs={{32,0},{64,32},{96,64},{128,96},{160,128},{192,160},{224,192},{256... | collective-permute-start | bytes 196616 | tf_op jit(solution)/shard_map/ppermute | solution.py:15
  15.1 11.8 %collective-permute-start.2 = (f32[16,2,512]{2,1,0:T(2,128)S(1)}, f32[16,2,512]{2,1,0:T(2,128)S(1)}, u32[]{:S(2)}, u32[]{:S(2)}) collective-permute-start(f32[16,2,512]{2,1,0:T(2,128)S(1)} %get-tuple-element.170), channel_id=1, source_target_pairs={{0,1},{1,2},{2,3},{3,4},{4,5},{5,6},{6,7},{7,8},{8,9},{9,10},{10,1... | collective-permute-start | bytes 196616 | tf_op jit(solution)/shard_map/ppermute | solution.py:14
  17.0 11.7 %collective-permute-start.3 = (f32[16,2,512]{2,1,0:T(2,128)S(1)}, f32[16,2,512]{2,1,0:T(2,128)S(1)}, u32[]{:S(2)}, u32[]{:S(2)}) collective-permute-start(f32[16,2,512]{2,1,0:T(2,128)S(1)} %get-tuple-element.171), channel_id=1, source_target_pairs={{1,0},{2,1},{3,2},{4,3},{5,4},{6,5},{7,6},{8,7},{9,8},{10,9},{11,1... | collective-permute-start | bytes 196616 | tf_op jit(solution)/shard_map/ppermute | solution.py:15
  29.8 10.5 %collective-permute-start.4 = (f32[4,16,512]{2,1,0:T(8,128)S(1)}, f32[4,16,512]{2,1,0:T(8,128)S(1)}, u32[]{:S(2)}, u32[]{:S(2)}) collective-permute-start(f32[4,16,512]{2,1,0:T(8,128)S(1)} %get-tuple-element.168), channel_id=1, source_target_pairs={{0,32},{32,64},{64,96},{96,128},{128,160},{160,192},{192,224},{224... | collective-permute-start | bytes 393224 | tf_op jit(solution)/shard_map/ppermute | solution.py:14
  32.6 9.1 %collective-permute-start.5 = (f32[4,16,512]{2,1,0:T(8,128)S(1)}, f32[4,16,512]{2,1,0:T(8,128)S(1)}, u32[]{:S(2)}, u32[]{:S(2)}) collective-permute-start(f32[4,16,512]{2,1,0:T(8,128)S(1)} %get-tuple-element.169), channel_id=1, source_target_pairs={{32,0},{64,32},{96,64},{128,96},{160,128},{192,160},{224,192},{256... | collective-permute-start | bytes 393224 | tf_op jit(solution)/shard_map/ppermute | solution.py:15
  42.0 10.2 %collective-permute-start.6 = (f32[16,4,512]{2,1,0:T(4,128)S(1)}, f32[16,4,512]{2,1,0:T(4,128)S(1)}, u32[]{:S(2)}, u32[]{:S(2)}) collective-permute-start(f32[16,4,512]{2,1,0:T(4,128)S(1)} %get-tuple-element.166), channel_id=1, source_target_pairs={{0,1},{1,2},{2,3},{3,4},{4,5},{5,6},{6,7},{7,8},{8,9},{9,10},{10,1... | collective-permute-start | bytes 393224 | tf_op jit(solution)/shard_map/ppermute | solution.py:14
  43.9 10.1 %collective-permute-start.7 = (f32[16,4,512]{2,1,0:T(4,128)S(1)}, f32[16,4,512]{2,1,0:T(4,128)S(1)}, u32[]{:S(2)}, u32[]{:S(2)}) collective-permute-start(f32[16,4,512]{2,1,0:T(4,128)S(1)} %get-tuple-element.167), channel_id=1, source_target_pairs={{1,0},{2,1},{3,2},{4,3},{5,4},{6,5},{7,6},{8,7},{9,8},{10,9},{11,1... | collective-permute-start | bytes 393224 | tf_op jit(solution)/shard_map/ppermute | solution.py:15
  55.9 19.6 %collective-permute-start.8 = (f32[8,16,512]{2,1,0:T(8,128)S(1)}, f32[8,16,512]{2,1,0:T(8,128)S(1)}, u32[]{:S(2)}, u32[]{:S(2)}) collective-permute-start(f32[8,16,512]{2,1,0:T(8,128)S(1)} %get-tuple-element.164), channel_id=1, source_target_pairs={{0,32},{32,64},{64,96},{96,128},{128,160},{160,192},{192,224},{224... | collective-permute-start | bytes 786440 | tf_op jit(solution)/shard_map/ppermute | solution.py:14
  58.8 16.7 %collective-permute-start.9 = (f32[8,16,512]{2,1,0:T(8,128)S(1)}, f32[8,16,512]{2,1,0:T(8,128)S(1)}, u32[]{:S(2)}, u32[]{:S(2)}) collective-permute-start(f32[8,16,512]{2,1,0:T(8,128)S(1)} %get-tuple-element.165), channel_id=1, source_target_pairs={{32,0},{64,32},{96,64},{128,96},{160,128},{192,160},{224,192},{256... | collective-permute-start | bytes 786440 | tf_op jit(solution)/shard_map/ppermute | solution.py:15
  66.0 23.3 %collective-permute-start.16 = (f32[3,8,1,16]{3,2,1,0:T(1,128)}, f32[3,8,1,16]{3,2,1,0:T(1,128)S(1)}, u32[]{:S(2)}, u32[]{:S(2)}) collective-permute-start(f32[3,8,1,16]{3,2,1,0:T(1,128)} %get-tuple-element.180), channel_id=1, source_target_pairs={{0,32},{32,64},{64,96},{96,128},{128,160},{160,192},{192,224},{224... | collective-permute-start | bytes 4616 | tf_op jit(solution)/shard_map/ppermute | solution.py:14
  67.9 21.4 %collective-permute-start.17 = (f32[3,8,1,16]{3,2,1,0:T(1,128)}, f32[3,8,1,16]{3,2,1,0:T(1,128)}, u32[]{:S(2)}, u32[]{:S(2)}) collective-permute-start(f32[3,8,1,16]{3,2,1,0:T(1,128)} %get-tuple-element.181), channel_id=1, source_target_pairs={{32,0},{64,32},{96,64},{128,96},{160,128},{192,160},{224,192},{256... | collective-permute-start | bytes 4616 | tf_op jit(solution)/shard_map/ppermute | solution.py:15
  79.2 11.0 %collective-permute-start.10 = (f32[16,8,512]{2,1,0:T(8,128)}, f32[16,8,512]{2,1,0:T(8,128)S(1)}, u32[]{:S(2)}, u32[]{:S(2)}) collective-permute-start(f32[16,8,512]{2,1,0:T(8,128)} %get-tuple-element.162), channel_id=1, source_target_pairs={{0,1},{1,2},{2,3},{3,4},{4,5},{5,6},{6,7},{7,8},{8,9},{9,10},{10,1... | collective-permute-start | bytes 786440 | tf_op jit(solution)/shard_map/ppermute | solution.py:14
  81.1 9.9 %collective-permute-start.11 = (f32[16,8,512]{2,1,0:T(8,128)}, f32[16,8,512]{2,1,0:T(8,128)S(1)}, u32[]{:S(2)}, u32[]{:S(2)}) collective-permute-start(f32[16,8,512]{2,1,0:T(8,128)} %get-tuple-element.163), channel_id=1, source_target_pairs={{1,0},{2,1},{3,2},{4,3},{5,4},{6,5},{7,6},{8,7},{9,8},{10,9},{11,1... | collective-permute-start | bytes 786440 | tf_op jit(solution)/shard_map/ppermute | solution.py:15
  93.9 32.7 %collective-permute-start.12 = (f32[16,16,512]{2,1,0:T(8,128)S(1)}, f32[16,16,512]{2,1,0:T(8,128)S(1)}, u32[]{:S(2)}, u32[]{:S(2)}) collective-permute-start(f32[16,16,512]{2,1,0:T(8,128)S(1)} %get-tuple-element.138), channel_id=1, source_target_pairs={{0,32},{32,64},{64,96},{96,128},{128,160},{160,192},{192,224},{224... | collective-permute-start | bytes 1572872 | tf_op jit(solution)/shard_map/ppermute | solution.py:14
  95.8 30.7 %collective-permute-start.13 = (f32[16,16,512]{2,1,0:T(8,128)S(1)}, f32[16,16,512]{2,1,0:T(8,128)S(1)}, u32[]{:S(2)}, u32[]{:S(2)}) collective-permute-start(f32[16,16,512]{2,1,0:T(8,128)S(1)} %get-tuple-element.138), channel_id=1, source_target_pairs={{32,0},{64,32},{96,64},{128,96},{160,128},{192,160},{224,192},{256... | collective-permute-start | bytes 1572872 | tf_op jit(solution)/shard_map/ppermute | solution.py:15
  103.5 10.2 %collective-permute-start.18 = (f32[3,8,18,1]{3,2,1,0:T(8,128)S(1)}, f32[3,8,18,1]{3,2,1,0:T(8,128)S(1)}, u32[]{:S(2)}, u32[]{:S(2)}) collective-permute-start(f32[3,8,18,1]{3,2,1,0:T(8,128)S(1)} %get-tuple-element.176), channel_id=1, source_target_pairs={{0,1},{1,2},{2,3},{3,4},{4,5},{5,6},{6,7},{7,8},{8,9},{9,10},{10,1... | collective-permute-start | bytes 5192 | tf_op jit(solution)/shard_map/ppermute | solution.py:14
  105.4 10.0 %collective-permute-start.19 = (f32[3,8,18,1]{3,2,1,0:T(8,128)S(1)}, f32[3,8,18,1]{3,2,1,0:T(8,128)S(1)}, u32[]{:S(2)}, u32[]{:S(2)}) collective-permute-start(f32[3,8,18,1]{3,2,1,0:T(8,128)S(1)} %get-tuple-element.177), channel_id=1, source_target_pairs={{1,0},{2,1},{3,2},{4,3},{5,4},{6,5},{7,6},{8,7},{9,8},{10,9},{11,1... | collective-permute-start | bytes 5192 | tf_op jit(solution)/shard_map/ppermute | solution.py:15
  117.1 18.8 %collective-permute-start.20 = (f32[3,8,1,16]{3,2,1,0:T(1,128)}, f32[3,8,1,16]{3,2,1,0:T(1,128)S(1)}, u32[]{:S(2)}, u32[]{:S(2)}) collective-permute-start(f32[3,8,1,16]{3,2,1,0:T(1,128)} %get-tuple-element.178), channel_id=1, source_target_pairs={{0,32},{32,64},{64,96},{96,128},{128,160},{160,192},{192,224},{224... | collective-permute-start | bytes 4616 | tf_op jit(solution)/shard_map/ppermute | solution.py:14
  119.0 16.9 %collective-permute-start.21 = (f32[3,8,1,16]{3,2,1,0:T(1,128)}, f32[3,8,1,16]{3,2,1,0:T(1,128)}, u32[]{:S(2)}, u32[]{:S(2)}) collective-permute-start(f32[3,8,1,16]{3,2,1,0:T(1,128)} %get-tuple-element.179), channel_id=1, source_target_pairs={{32,0},{64,32},{96,64},{128,96},{160,128},{192,160},{224,192},{256... | collective-permute-start | bytes 4616 | tf_op jit(solution)/shard_map/ppermute | solution.py:15
  127.6 17.8 %collective-permute-start.14 = (f32[16,16,512]{2,1,0:T(8,128)S(1)}, f32[16,16,512]{2,1,0:T(8,128)}, u32[]{:S(2)}, u32[]{:S(2)}) collective-permute-start(f32[16,16,512]{2,1,0:T(8,128)S(1)} %get-tuple-element.136), channel_id=1, source_target_pairs={{0,1},{1,2},{2,3},{3,4},{4,5},{5,6},{6,7},{7,8},{8,9},{9,10},{10,1... | collective-permute-start | bytes 1572872 | tf_op jit(solution)/shard_map/ppermute | solution.py:14
  129.5 15.9 %collective-permute-start.15 = (f32[16,16,512]{2,1,0:T(8,128)S(1)}, f32[16,16,512]{2,1,0:T(8,128)}, u32[]{:S(2)}, u32[]{:S(2)}) collective-permute-start(f32[16,16,512]{2,1,0:T(8,128)S(1)} %get-tuple-element.136), channel_id=1, source_target_pairs={{1,0},{2,1},{3,2},{4,3},{5,4},{6,5},{7,6},{8,7},{9,8},{10,9},{11,1... | collective-permute-start | bytes 1572872 | tf_op jit(solution)/shard_map/ppermute | solution.py:15
  137.6 26.1 %collective-permute-start.22 = (f32[3,8,18,1]{3,2,1,0:T(8,128)}, f32[3,8,18,1]{3,2,1,0:T(8,128)}, u32[]{:S(2)}, u32[]{:S(2)}) collective-permute-start(f32[3,8,18,1]{3,2,1,0:T(8,128)} %get-tuple-element.174), channel_id=1, source_target_pairs={{0,1},{1,2},{2,3},{3,4},{4,5},{5,6},{6,7},{7,8},{8,9},{9,10},{10,1... | collective-permute-start | bytes 5192 | tf_op jit(solution)/shard_map/ppermute | solution.py:14
  139.6 24.0 %collective-permute-start.23 = (f32[3,8,18,1]{3,2,1,0:T(8,128)}, f32[3,8,18,1]{3,2,1,0:T(8,128)}, u32[]{:S(2)}, u32[]{:S(2)}) collective-permute-start(f32[3,8,18,1]{3,2,1,0:T(8,128)} %get-tuple-element.175), channel_id=1, source_target_pairs={{1,0},{2,1},{3,2},{4,3},{5,4},{6,5},{7,6},{8,7},{9,8},{10,9},{11,1... | collective-permute-start | bytes 5192 | tf_op jit(solution)/shard_map/ppermute | solution.py:15
  (17 other events, 76.1 us)
where the time goes:
time: 168 us; the launch traced here: 166 us
  starting transfers between devices  109 us (65%)
  other arithmetic  28.8 us (17%)
  waiting for transfers between devices  14.1 us (8%)
  local copies, waits for them, and re-layouts  13 us (8%)
    ppermute x12, starting transfers between devices, with_halo(): after = lax.ppermute(first, axis, down)  81.6 us
    ppermute x12, starting transfers between devices, with_halo(): before = lax.ppermute(last, axis, up)  27.1 us
    div x11, other arithmetic, smoothed_mirror_input(): (gather_shifted(0) + gather_shifted(4 * hole_spacing) + 4.0 * (gather_shi...  10.2 us
    ppermute x12, waiting for transfers between devices, with_halo(): after = lax.ppermute(first, axis, down)  9.69 us
    mul x8, local copies, waits for them, and re-layouts, grads(): term = resid * amp[:, :, None] * bump * diff / (sig3 * sig3)  5.59 us
    dynamic_update_slice x8, other arithmetic, on_device(): per_comp = lax.map(grads, (amplitude, centre, spread))  4.95 us
    ppermute x12, waiting for transfers between devices, with_halo(): before = lax.ppermute(last, axis, up)  4.44 us
    reduce_sum x8, other arithmetic, grads(): g_pos = jnp.sum(term, axis=2)  3.92 us
  transfers between devices with their start and end apart: 24, of which 10 were waited for; matrix products, arithmetic and copies ran while one was open for 17% of the time, Pallas kernels for 0%

commit v1 on v0

v1 whole, which is shorter than its diff:
```python
import functools
import math

import jax
import jax.numpy as jnp
import numpy as np
from jax import lax
from jax.experimental import pallas as pl
from jax.experimental.pallas import tpu as pltpu
from jax.sharding import PartitionSpec as P

TILE = 16
LEVELS = 4
COMPS = 8
LANES = 128
TAPS = (1, 4, 6, 4, 1)
VMEM_LIMIT = 56 * 1024 * 1024
STEPS = (0.5, 0.002, 2.0)
LAMS = (0.2, 0.5, 0.05)


def blur_matrix(length, gap):
    out = np.zeros((length, length), np.float64)
    for tap, factor in enumerate(TAPS):
        offset = (tap - 2) * gap
        for i in range(max(0, -offset), min(length, length - offset)):
            out[i, i + offset] = factor
    return out


def composites(length):
    made, now = [], np.eye(length)
    for level in range(LEVELS):
        now = blur_matrix(length, 2**level) @ now
        made.append(now)
    return made


def halves(matrix):
    bf16 = jnp.bfloat16
    high = np.asarray(matrix, np.float32).astype(bf16)
    low = (np.asarray(matrix, np.float32) - high.astype(np.float32)).astype(bf16)
    return high, low


def channel_matrices(nch):
    return np.stack([np.stack(halves(m.T)) for m in composites(nch)])


def scatter_matrices(length):
    whole = composites(length)
    kinds = []
    for start in (0, TILE * (length // TILE // 2), length - TILE):
        parts = []
        for m in whole:
            block = np.zeros((5 * TILE, TILE))
            for k in range(5 * TILE):
                at = start - 2 * TILE + k
                if 0 <= at < length:
                    block[k] = m[at, start : start + TILE]
            parts.append(halves(block))
        high = np.concatenate([p[0] for p in parts], axis=1)
        low = np.concatenate([p[1] for p in parts[2:]], axis=1)
        kinds.append(np.concatenate([high, high, low], axis=1))
    return np.stack(kinds)


def sent(values, axis, by):
    size = lax.axis_size(axis)
    if by > 0:
        pairs = [(i, i + by) for i in range(size - by)]
    else:
        pairs = [(i, i + by) for i in range(-by, size)]
    return lax.ppermute(values, axis, pairs)


def five(v, flag=None):
    total = (v[0] + v[4]) + 4.0 * (v[1] + v[3]) + 6.0 * v[2]
    return total if flag is None else total * flag


def split(v):
    high = v.astype(jnp.bfloat16)
    return high, (v - high.astype(jnp.float32)).astype(jnp.bfloat16)


def wavelet_kernel(
    kind_ref, flag_ref, a_ref, m2, m1, x_ref, p1, p2, w_ref, k_ref,
    o_m2, o_m1, o_0, o_p1, o_p2, rows_ref, y_ref,
):
    nch = x_ref.shape[2]
    tiles = (m2, m1, x_ref, p1, p2)
    outs = (o_m2, o_m1, o_0, o_p1, o_p2)
    flags = [flag_ref[i] for i in range(5)]

    lane_tiles = nch // LANES

    def row_pass(step, carry):
        sub = pl.ds(pl.multiple_of((step // lane_tiles) * 8, 8), 8)
        lane = pl.ds(pl.multiple_of((step % lane_tiles) * LANES, LANES), LANES)

        @functools.cache
        def value(level, at):
            tile = (at + 2 * TILE) // TILE
            if level == 0:
                return tiles[tile][at % TILE, sub, lane]
            gap = 2 ** (level - 1)
            taps = [value(level - 1, at + (t - 2) * gap) for t in range(5)]
            return five(taps, None if tile == 2 else flags[tile])

        reach = {1: 28, 2: 24, 3: 16, 4: 0}
        lag = {1: 2, 2: 6, 3: 14, 4: 30}
        for at in range(-30, TILE + 30):
            value(0, at)
            for level in range(1, LEVELS + 1):
                row = at - lag[level]
                if -reach[level] <= row < TILE + reach[level]:
                    got = value(level, row)
                    if 0 <= row < TILE:
                        rows_ref[level - 1, row, sub, lane] = got
        return carry

    lax.fori_loop(0, 2 * lane_tiles, row_pass, 0)

    half = nch // 2
    pixels = TILE * TILE

    def channel_pass(step, carry):
        level = step // 2
        lane = pl.ds(pl.multiple_of((step % 2) * half, half), half)
        high, low = split(rows_ref[level].reshape(pixels, nch))
        w_high = w_ref[level, 0, :, lane]
        dot = functools.partial(jnp.dot, preferred_element_type=jnp.float32)
        got = dot(high, w_high) + dot(low, w_high) + dot(high, w_ref[level, 1, :, lane])
        got = got * a_ref[level + 1, :, lane]
        high, low = split(got)
        high = high.reshape(TILE, TILE, half)
        at = pl.ds(pl.multiple_of(level * TILE, TILE), TILE)
        y_ref[:, at, lane] = high
        at = pl.ds(pl.multiple_of((level + LEVELS) * TILE, TILE), TILE)
        y_ref[:, at, lane] = low.reshape(TILE, TILE, half)

        @pl.when(level >= 2)
        def _():
            at = pl.ds(pl.multiple_of((level + 6) * TILE, TILE), TILE)
            y_ref[:, at, lane] = high

        return carry

    lax.fori_loop(0, 2 * LEVELS, channel_pass, 0)

    columns = k_ref[kind_ref[0]]

    def column_pass(row, carry):
        got = jnp.dot(columns, y_ref[row], preferred_element_type=jnp.float32)
        for i, out in enumerate(outs):
            part = got[i * TILE : (i + 1) * TILE]
            if i == 2:
                part = part + a_ref[0] * x_ref[row]
            out[row] = part
        return carry

    lax.fori_loop(0, TILE, column_pass, 0)


def wavelet_parts(kind, flags, coeff, tiles, nch, length):
    w = jnp.asarray(channel_matrices(nch))
    k = jnp.asarray(scatter_matrices(length))
    smem = pl.BlockSpec(memory_space=pltpu.SMEM)
    vmem = pl.BlockSpec(memory_space=pltpu.VMEM)
    shape = jax.ShapeDtypeStruct(tiles[2].shape, jnp.float32)
    return pl.pallas_call(
        wavelet_kernel,
        out_shape=[shape] * 5,
        in_specs=[smem, smem] + [vmem] * 8,
        out_specs=[vmem] * 5,
        scratch_shapes=[
            pltpu.VMEM((LEVELS, TILE, TILE, nch), jnp.float32),
            pltpu.VMEM((TILE, 10 * TILE, nch), jnp.bfloat16),
        ],
        compiler_params=pltpu.CompilerParams(vmem_limit_bytes=VMEM_LIMIT),
        cost_estimate=pl.CostEstimate(flops=4_000_000_000, bytes_accessed=9_000_000, transcendentals=0),
        name="wavelet_parts",
    )(kind, flags, coeff, *tiles, w, k)


def model_kernel(amp_ref, mu_ref, s_ref, model_ref):
    nch, pixels = model_ref.shape

    def body(step, carry):
        base = pl.multiple_of(step * 8, 8)
        chan = (lax.broadcasted_iota(jnp.int32, (8, pixels), 0) + base).astype(jnp.float32)
        total = jnp.zeros((8, pixels), jnp.float32)
        for k in range(COMPS):
            diff = chan - mu_ref[k : k + 1, :]
            total += amp_ref[k : k + 1, :] * jnp.exp2(diff * diff * s_ref[k : k + 1, :])
        model_ref[pl.ds(base, 8), :] = total
        return carry

    lax.fori_loop(0, nch // 8, body, 0)


def model_of(amp, mu, s, nch):
    vmem = pl.BlockSpec(memory_space=pltpu.VMEM)
    return pl.pallas_call(
        model_kernel,
        out_shape=jax.ShapeDtypeStruct((nch, amp.shape[1]), jnp.float32),
        in_specs=[vmem] * 3,
        out_specs=vmem,
        compiler_params=pltpu.CompilerParams(vmem_limit_bytes=VMEM_LIMIT),
        cost_estimate=pl.CostEstimate(flops=10_000_000, bytes_accessed=600_000, transcendentals=1_100_000),
        name="gaussian_model",
    )(amp, mu, s)


def step_kernel(
    o_0, o_m2, o_m1, o_p1, o_p2, model_ref, amp_ref, mu_ref, s_ref, inv_ref, base_ref,
    den_ref, fit_ref, r_ref,
):
    nch, pixels = model_ref.shape
    for row in range(TILE):
        got = o_0[row] + ((o_m2[row] + o_m1[row]) + (o_p1[row] + o_p2[row]))
        den_ref[row] = got
    for part in range(pixels // LANES):
        rows = LANES // TILE
        block = den_ref[part * rows : (part + 1) * rows].reshape(LANES, nch)
        at = slice(part * LANES, (part + 1) * LANES)
        r_ref[:, at] = model_ref[:, at] - block.T

    for part in range(pixels // LANES):
        at = slice(part * LANES, (part + 1) * LANES)
        sums = [[] for _ in range(3)]
        for first in range(0, COMPS, 4):
            chosen = range(first, first + 4)
            mus = [jnp.broadcast_to(mu_ref[k : k + 1, at], (8, LANES)) for k in chosen]
            scales = [jnp.broadcast_to(s_ref[k : k + 1, at], (8, LANES)) for k in chosen]

            def body(step, carry):
                chan = (lax.broadcasted_iota(jnp.int32, (8, LANES), 0) + step * 8).astype(jnp.float32)
                r = r_ref[pl.ds(pl.multiple_of(step * 8, 8), 8), at]
                out = []
                for mu, scale, (a, b, c) in zip(mus, scales, carry):
                    diff = chan - mu
                    one = r * jnp.exp2(diff * diff * scale)
                    two = one * diff
                    out.append((a + one, b + two, c + two * diff))
                return tuple(out)

            zero = jnp.zeros((8, LANES), jnp.float32)
            done = lax.fori_loop(0, nch // 8, body, ((zero,) * 3,) * 4, unroll=4)
            for four in done:
                for t in range(3):
                    sums[t].append(jnp.sum(four[t], axis=0, keepdims=True))
        amp = amp_ref[:, at]
        inv = inv_ref[:, at]
        slope = amp * inv * inv
        grads = (
            jnp.concatenate(sums[0], axis=0) * (1.0 / nch),
            jnp.concatenate(sums[1], axis=0) * slope,
            jnp.concatenate(sums[2], axis=0) * (slope * inv * (1.0 / nch)),
        )
        for t in range(3):
            fit_ref[t, :, at] = base_ref[t, :, at] - STEPS[t] * grads[t]


def gradient_step(parts, model, amp, mu, s, inv, base):
    vmem = pl.BlockSpec(memory_space=pltpu.VMEM)
    return pl.pallas_call(
        step_kernel,
        out_shape=[
            jax.ShapeDtypeStruct(parts[0].shape, jnp.float32),
            jax.ShapeDtypeStruct(base.shape, jnp.float32),
        ],
        in_specs=[vmem] * 11,
        out_specs=[vmem] * 2,
        scratch_shapes=[pltpu.VMEM(model.shape, jnp.float32)],
        compiler_params=pltpu.CompilerParams(vmem_limit_bytes=VMEM_LIMIT),
        cost_estimate=pl.CostEstimate(flops=15_000_000, bytes_accessed=4_000_000, transcendentals=1_100_000),
        name="gradient_step",
    )(*parts, model, amp, mu, s, inv, base)


def stencil(p):
    return 4.0 * p[:, :, 1:-1, 1:-1] - (
        p[:, :, :-2, 1:-1] + p[:, :, 2:, 1:-1] + p[:, :, 1:-1, :-2] + p[:, :, 1:-1, 2:]
    )


def inside(axis, length, border):
    at = jnp.arange(-border, length + border) + lax.axis_index(axis) * length
    return ((at >= 0) & (at < length * lax.axis_size(axis))).astype(jnp.float32)


def on_device(cube, level_table, level_index, amplitude, centre_index, spread):
    nch = cube.shape[2]
    pixels = TILE * TILE

    up1, down1 = sent(cube, "skyy", 1), sent(cube, "skyy", -1)
    up2, down2 = sent(cube, "skyy", 2), sent(cube, "skyy", -2)
    frac = (centre_index.astype(jnp.float32) + 0.5) / nch
    params = jnp.stack([amplitude, frac, spread])
    above = sent(params[:, :, -2:, :], "skyy", 1)
    below = sent(params[:, :, :2, :], "skyy", -1)

    entries = jnp.arange(level_table.shape[0], dtype=jnp.int32)
    picks = (level_index[:, :, None] == entries).astype(jnp.float32)
    weight = jnp.sum(picks * level_table, axis=2)
    one = jnp.ones((1, nch), jnp.float32)
    coeff = jnp.concatenate([weight, one]) - jnp.concatenate([0.0 * one, weight])
    scale = jnp.array([16.0 ** (-3 * j) for j in range(LEVELS + 1)], jnp.float32)
    coeff = (coeff * scale[:, None])[:, None, :]

    amp = amplitude.reshape(COMPS, pixels)
    mu = (frac * nch).reshape(COMPS, pixels)
    inv = 1.0 / spread.reshape(COMPS, pixels)
    s = (-0.5 * math.log2(math.e)) * inv * inv
    model = model_of(amp, mu, s, nch)

    iy, ny = lax.axis_index("skyy"), lax.axis_size("skyy")
    ix, nx = lax.axis_index("skyx"), lax.axis_size("skyx")
    near = iy + jnp.arange(-2, 3)
    flags = ((near >= 0) & (near < ny)).astype(jnp.float32)
    kind = jnp.where(ix == 0, 0, jnp.where(ix == nx - 1, 2, 1)).astype(jnp.int32)[None]
    o_m2, o_m1, o_0, o_p1, o_p2 = wavelet_parts(
        kind, flags, coeff, (up2, up1, cube, down1, down2), nch, nx * TILE
    )

    from_left1, from_right1 = sent(o_p1, "skyx", 1), sent(o_m1, "skyx", -1)
    from_left2, from_right2 = sent(o_p2, "skyx", 2), sent(o_m2, "skyx", -2)
    tall = jnp.concatenate([above, params, below], axis=2)
    left = sent(tall[:, :, :, -2:], "skyx", 1)
    right = sent(tall[:, :, :, :2], "skyx", -1)
    wide = jnp.concatenate([left, tall, right], axis=3)
    first = stencil(wide) * (inside("skyy", TILE, 1)[:, None] * inside("skyx", TILE, 1))
    smoothing = stencil(first)
    rate = jnp.array([a * b for a, b in zip(STEPS, LAMS)], jnp.float32)[:, None, None, None]
    base = (params - rate * smoothing).reshape(3, COMPS, pixels)

    denoised, fitted = gradient_step(
        (o_0, from_left2, from_left1, from_right1, from_right2), model, amp, mu, s, inv, base
    )
    return denoised, fitted.reshape(3, COMPS, TILE, TILE)


def solution(mesh):
    placed = (
        P("skyy", "skyx", None),
        P(),
        P(),
        P(None, "skyy", "skyx"),
        P(None, "skyy", "skyx"),
        P(None, "skyy", "skyx"),
    )
    return jax.shard_map(
        on_device,
        mesh=mesh,
        in_specs=placed,
        out_specs=(P("skyy", "skyx", None), P(None, None, "skyy", "skyx")),
        check_vma=False,
    )
```

time: 168 us -> 111 us (0.66)
  the two profiles are of different devices: /device:TPU:34 before, /device:TPU:26 now
where the time goes in v1:
time: 111 us; the launch traced here: 110 us
  starting transfers between devices  46.4 us (42%)
  waiting for transfers between devices  27.6 us (25%)
  Pallas kernels  20.3 us (18%)
  other arithmetic  7.35 us (7%)
  local copies, waits for them, and re-layouts  7.24 us (7%)
    ppermute x12, starting transfers between devices, sent(): return lax.ppermute(values, axis, pairs)  46.4 us
    ppermute x12, waiting for transfers between devices, sent(): return lax.ppermute(values, axis, pairs)  27.6 us
    pallas_call x1, Pallas kernels, wavelet_parts(): pl.pallas_call(wavelet_kernel, out_shape=[shape] * 5, in_specs=[smem, sme...  12 us
    pallas_call x1, Pallas kernels, gradient_step(): pl.pallas_call(step_kernel, out_shape=[jax.ShapeDtypeStruct(parts[0].shap...  5.06 us
    pallas_call x1, Pallas kernels, model_of(): pl.pallas_call(model_kernel, out_shape=jax.ShapeDtypeStruct((nch, amp.sha...  3.25 us
  transfers between devices with their start and end apart: 12, of which 4 were waited for; matrix products, arithmetic and copies ran while one was open for 10% of the time, Pallas kernels for 14%

profile of v1, /device:TPU:26, one launch (start us, length us, event | category | flops | bytes accessed | tf_op | source)
XLA Modules:
  0.0 109.8 jit_solution(2924442664146346119)
XLA Ops:
  0.6 4.7 %collective-permute-start = (f32[16,16,512]{2,1,0:T(8,128)}, f32[16,16,512]{2,1,0:T(8,128)S(1)}, u32[]{:S(2)}, u32[]{:S(2)}) collective-permute-start(f32[16,16,512]{2,1,0:T(8,128)} %x_ref.1), channel_id=1, source_target_pairs={{0,64},{32,96},{64,128},{96,160},{128,192},{160,224},{192,256},{22... | collective-permute-start | bytes 1572872 | tf_op jit(solution)/shard_map/ppermute | solution.py:74
  5.3 4.0 %collective-permute-start.1 = (f32[16,16,512]{2,1,0:T(8,128)}, f32[16,16,512]{2,1,0:T(8,128)S(1)}, u32[]{:S(2)}, u32[]{:S(2)}) collective-permute-start(f32[16,16,512]{2,1,0:T(8,128)} %x_ref.1), channel_id=1, source_target_pairs={{0,32},{32,64},{64,96},{96,128},{128,160},{160,192},{192,224},{224... | collective-permute-start | bytes 1572872 | tf_op jit(solution)/shard_map/ppermute | solution.py:74
  9.4 4.2 %collective-permute-start.2 = (f32[16,16,512]{2,1,0:T(8,128)}, f32[16,16,512]{2,1,0:T(8,128)S(1)}, u32[]{:S(2)}, u32[]{:S(2)}) collective-permute-start(f32[16,16,512]{2,1,0:T(8,128)} %x_ref.1), channel_id=1, source_target_pairs={{32,0},{64,32},{96,64},{128,96},{160,128},{192,160},{224,192},{256... | collective-permute-start | bytes 1572872 | tf_op jit(solution)/shard_map/ppermute | solution.py:74
  13.6 1.9 %collective-permute-start.3 = (f32[16,16,512]{2,1,0:T(8,128)}, f32[16,16,512]{2,1,0:T(8,128)S(1)}, u32[]{:S(2)}, u32[]{:S(2)}) collective-permute-start(f32[16,16,512]{2,1,0:T(8,128)} %x_ref.1), channel_id=1, source_target_pairs={{64,0},{96,32},{128,64},{160,96},{192,128},{224,160},{256,192},{28... | collective-permute-start | bytes 1572872 | tf_op jit(solution)/shard_map/ppermute | solution.py:74
  16.4 0.9 pad_maximum_fusion.12
  17.3 2.2 %collective-permute-start.9 = (f32[3,8,2,16]{3,2,1,0:T(2,128)S(1)}, f32[3,8,2,16]{3,2,1,0:T(2,128)S(1)}, u32[]{:S(2)}, u32[]{:S(2)}) collective-permute-start(f32[3,8,2,16]{3,2,1,0:T(2,128)S(1)} %get-tuple-element.19), channel_id=1, source_target_pairs={{32,0},{64,32},{96,64},{128,96},{160,128},{192,160},{224,192},{256... | collective-permute-start | bytes 9224 | tf_op jit(solution)/shard_map/ppermute | solution.py:74
  19.6 0.9 broadcast_divide_fusion
  22.8 15.1 %collective-permute-done.9 = f32[3,8,2,16]{3,2,1,0:T(2,128)S(1)} collective-permute-done((f32[3,8,2,16]{3,2,1,0:T(2,128)S(1)}, f32[3,8,2,16]{3,2,1,0:T(2,128)S(1)}, u32[]{:S(2)}, u32[]{:S(2)}) %collective-permute-start.9) | collective-permute-done | bytes 3104 | tf_op jit(solution)/shard_map/ppermute | solution.py:74
  37.9 5.6 %collective-permute-start.8 = (f32[3,8,2,16]{3,2,1,0:T(2,128)S(1)}, f32[3,8,2,16]{3,2,1,0:T(2,128)S(1)}, u32[]{:S(2)}, u32[]{:S(2)}) collective-permute-start(f32[3,8,2,16]{3,2,1,0:T(2,128)S(1)} %get-tuple-element.18), channel_id=1, source_target_pairs={{0,32},{32,64},{64,96},{96,128},{128,160},{160,192},{192,224},{224... | collective-permute-start | bytes 9224 | tf_op jit(solution)/shard_map/ppermute | solution.py:74
  44.0 1.5 %reshape.68.amp_ref = f32[8,256]{1,0:T(8,128)} reshape(f32[8,16,16]{2,1,0:T(8,128)} %param.13) | data formatting | bytes 16384 | tf_op jit(solution)/shard_map/reshape | solution.py:313
  46.8 3.2 %gaussian_model.1.model_ref = f32[512,256]{1,0:T(8,128)} custom-call(f32[8,256]{1,0:T(8,128)} %reshape.68.amp_ref, f32[8,256]{1,0:T(8,128)} %reshape.69.mu_ref, f32[8,256]{1,0:T(8,128)} %multiply_multiply_fusion.s_ref), custom_call_target="tpu_custom_call" | custom-call | flops 10000000 | bytes 600000 | tf_op jit(solution)/shard_map/gaussian_model/pallas_call | solution.py:205
  50.0 0.9 pad_maximum_fusion.10
  51.1 8.3 %collective-permute-start.11 = (f32[3,8,20,2]{3,2,1,0:T(8,128)S(1)}, f32[3,8,20,2]{3,2,1,0:T(8,128)S(1)}, u32[]{:S(2)}, u32[]{:S(2)}) collective-permute-start(f32[3,8,20,2]{3,2,1,0:T(8,128)S(1)} %get-tuple-element.17), channel_id=1, source_target_pairs={{1,0},{2,1},{3,2},{4,3},{5,4},{6,5},{7,6},{8,7},{9,8},{10,9},{11,1... | collective-permute-start | bytes 11528 | tf_op jit(solution)/shard_map/ppermute | solution.py:74
  59.4 1.9 %collective-permute-start.10 = (f32[3,8,20,2]{3,2,1,0:T(8,128)S(1)}, f32[3,8,20,2]{3,2,1,0:T(8,128)S(1)}, u32[]{:S(2)}, u32[]{:S(2)}) collective-permute-start(f32[3,8,20,2]{3,2,1,0:T(8,128)S(1)} %get-tuple-element.16), channel_id=1, source_target_pairs={{0,1},{1,2},{2,3},{3,4},{4,5},{5,6},{6,7},{7,8},{8,9},{9,10},{10,1... | collective-permute-start | bytes 11528 | tf_op jit(solution)/shard_map/ppermute | solution.py:74
  62.5 12.0 %wavelet_parts.1 = (f32[16,16,512]{2,1,0:T(8,128)}, f32[16,16,512]{2,1,0:T(8,128)}, f32[16,16,512]{2,1,0:T(8,128)}, f32[16,16,512]{2,1,0:T(8,128)}, f32[16,16,512]{2,1,0:T(8,128)}) custom-call(s32[1]{0:T(128)} %bitcast.kind_ref, f32[5]{0:T(128)} %and_convert_fusion.2.flag_ref, f32[5,1,512]{2,1,0:T(1,128)} %broadcast_in_dim.5.a_ref, ...), custom_call_target="tpu_custom_call" | custom-call | flops 4000000000 | bytes 9000000 | tf_op jit(solution)/shard_map/wavelet_parts/pallas_call | solution.py:172
  74.6 1.9 %collective-permute-start.4 = (f32[16,16,512]{2,1,0:T(8,128)}, f32[16,16,512]{2,1,0:T(8,128)S(1)}, u32[]{:S(2)}, u32[]{:S(2)}) collective-permute-start(f32[16,16,512]{2,1,0:T(8,128)} %get-tuple-element.10), channel_id=1, source_target_pairs={{0,2},{1,3},{2,4},{3,5},{4,6},{5,7},{6,8},{7,9},{8,10},{9,11},{10,... | collective-permute-start | bytes 1572872 | tf_op jit(solution)/shard_map/ppermute | solution.py:74
  76.5 1.9 %collective-permute-start.5 = (f32[16,16,512]{2,1,0:T(8,128)}, f32[16,16,512]{2,1,0:T(8,128)S(1)}, u32[]{:S(2)}, u32[]{:S(2)}) collective-permute-start(f32[16,16,512]{2,1,0:T(8,128)} %get-tuple-element.11), channel_id=1, source_target_pairs={{0,1},{1,2},{2,3},{3,4},{4,5},{5,6},{6,7},{7,8},{8,9},{9,10},{10,1... | collective-permute-start | bytes 1572872 | tf_op jit(solution)/shard_map/ppermute | solution.py:74
  78.4 5.8 %collective-permute-start.6 = (f32[16,16,512]{2,1,0:T(8,128)}, f32[16,16,512]{2,1,0:T(8,128)S(1)}, u32[]{:S(2)}, u32[]{:S(2)}) collective-permute-start(f32[16,16,512]{2,1,0:T(8,128)} %get-tuple-element.12), channel_id=1, source_target_pairs={{1,0},{2,1},{3,2},{4,3},{5,4},{6,5},{7,6},{8,7},{9,8},{10,9},{11,1... | collective-permute-start | bytes 1572872 | tf_op jit(solution)/shard_map/ppermute | solution.py:74
  84.2 3.9 %collective-permute-start.7 = (f32[16,16,512]{2,1,0:T(8,128)}, f32[16,16,512]{2,1,0:T(8,128)S(1)}, u32[]{:S(2)}, u32[]{:S(2)}) collective-permute-start(f32[16,16,512]{2,1,0:T(8,128)} %get-tuple-element.13), channel_id=1, source_target_pairs={{2,0},{3,1},{4,2},{5,3},{6,4},{7,5},{8,6},{9,7},{10,8},{11,9},{12,... | collective-permute-start | bytes 1572872 | tf_op jit(solution)/shard_map/ppermute | solution.py:74
  89.9 3.6 %collective-permute-done.4.o_m2 = f32[16,16,512]{2,1,0:T(8,128)S(1)} collective-permute-done((f32[16,16,512]{2,1,0:T(8,128)}, f32[16,16,512]{2,1,0:T(8,128)S(1)}, u32[]{:S(2)}, u32[]{:S(2)}) %collective-permute-start.4) | collective-permute-done | bytes 524320 | tf_op jit(solution)/shard_map/ppermute | solution.py:74
  93.5 5.1 %collective-permute-done.5.o_m1 = f32[16,16,512]{2,1,0:T(8,128)S(1)} collective-permute-done((f32[16,16,512]{2,1,0:T(8,128)}, f32[16,16,512]{2,1,0:T(8,128)S(1)}, u32[]{:S(2)}, u32[]{:S(2)}) %collective-permute-start.5) | collective-permute-done | bytes 524320 | tf_op jit(solution)/shard_map/ppermute | solution.py:74
  98.6 3.8 %collective-permute-done.7.o_p2 = f32[16,16,512]{2,1,0:T(8,128)S(1)} collective-permute-done((f32[16,16,512]{2,1,0:T(8,128)}, f32[16,16,512]{2,1,0:T(8,128)S(1)}, u32[]{:S(2)}, u32[]{:S(2)}) %collective-permute-start.7) | collective-permute-done | bytes 524320 | tf_op jit(solution)/shard_map/ppermute | solution.py:74
  103.2 5.1 %gradient_step.1 = (f32[16,16,512]{2,1,0:T(8,128)}, f32[3,8,256]{2,1,0:T(8,128)}) custom-call(f32[16,16,512]{2,1,0:T(8,128)} %get-tuple-element.9.o_0, f32[16,16,512]{2,1,0:T(8,128)} %copy-done.2, f32[16,16,512]{2,1,0:T(8,128)} %copy-done.3, f32[16,16,512]{2,1,0:T(8,128)} %copy-done.4, f32[16,16,512]{2,1,0:T(8,128)} %copy-done.5, ...), custom_call_target="tpu_custom_call" | custom-call | flops 15000000 | bytes 4000000 | tf_op jit(solution)/shard_map/gradient_step/pallas_call | solution.py:268
  108.2 1.5 %reshape.71 = f32[3,8,16,16]{3,2,1,0:T(8,128)} reshape(f32[3,8,256]{2,1,0:T(8,128)} %get-tuple-element.15) | data formatting | bytes 49152 | tf_op jit(solution)/shard_map/reshape | solution.py:342
  (49 shorter events, 8.9 us)
Async XLA Ops:
  0.6 58.8 %collective-permute-start = (f32[16,16,512]{2,1,0:T(8,128)}, f32[16,16,512]{2,1,0:T(8,128)S(1)}, u32[]{:S(2)}, u32[]{:S(2)}) collective-permute-start(f32[16,16,512]{2,1,0:T(8,128)} %x_ref.1), channel_id=1, source_target_pairs={{0,64},{32,96},{64,128},{96,160},{128,192},{160,224},{192,256},{22... | collective-permute-start | bytes 1572872 | tf_op jit(solution)/shard_map/ppermute | solution.py:74
  5.3 56.0 %collective-permute-start.1 = (f32[16,16,512]{2,1,0:T(8,128)}, f32[16,16,512]{2,1,0:T(8,128)S(1)}, u32[]{:S(2)}, u32[]{:S(2)}) collective-permute-start(f32[16,16,512]{2,1,0:T(8,128)} %x_ref.1), channel_id=1, source_target_pairs={{0,32},{32,64},{64,96},{96,128},{128,160},{160,192},{192,224},{224... | collective-permute-start | bytes 1572872 | tf_op jit(solution)/shard_map/ppermute | solution.py:74
  9.4 52.0 %collective-permute-start.2 = (f32[16,16,512]{2,1,0:T(8,128)}, f32[16,16,512]{2,1,0:T(8,128)S(1)}, u32[]{:S(2)}, u32[]{:S(2)}) collective-permute-start(f32[16,16,512]{2,1,0:T(8,128)} %x_ref.1), channel_id=1, source_target_pairs={{32,0},{64,32},{96,64},{128,96},{160,128},{192,160},{224,192},{256... | collective-permute-start | bytes 1572872 | tf_op jit(solution)/shard_map/ppermute | solution.py:74
  13.6 47.8 %collective-permute-start.3 = (f32[16,16,512]{2,1,0:T(8,128)}, f32[16,16,512]{2,1,0:T(8,128)S(1)}, u32[]{:S(2)}, u32[]{:S(2)}) collective-permute-start(f32[16,16,512]{2,1,0:T(8,128)} %x_ref.1), channel_id=1, source_target_pairs={{64,0},{96,32},{128,64},{160,96},{192,128},{224,160},{256,192},{28... | collective-permute-start | bytes 1572872 | tf_op jit(solution)/shard_map/ppermute | solution.py:74
  17.3 20.5 %collective-permute-start.9 = (f32[3,8,2,16]{3,2,1,0:T(2,128)S(1)}, f32[3,8,2,16]{3,2,1,0:T(2,128)S(1)}, u32[]{:S(2)}, u32[]{:S(2)}) collective-permute-start(f32[3,8,2,16]{3,2,1,0:T(2,128)S(1)} %get-tuple-element.19), channel_id=1, source_target_pairs={{32,0},{64,32},{96,64},{128,96},{160,128},{192,160},{224,192},{256... | collective-permute-start | bytes 9224 | tf_op jit(solution)/shard_map/ppermute | solution.py:74
  20.5 54.0 %copy-start.6 = (f32[8,256]{1,0:T(8,128)}, f32[8,256]{1,0:T(8,128)S(1)}, u32[]{:S(2)}) copy-start(f32[8,256]{1,0:T(8,128)S(1)} %div.13.inv_ref) | copy-start | bytes 24580
  37.9 12.2 %collective-permute-start.8 = (f32[3,8,2,16]{3,2,1,0:T(2,128)S(1)}, f32[3,8,2,16]{3,2,1,0:T(2,128)S(1)}, u32[]{:S(2)}, u32[]{:S(2)}) collective-permute-start(f32[3,8,2,16]{3,2,1,0:T(2,128)S(1)} %get-tuple-element.18), channel_id=1, source_target_pairs={{0,32},{32,64},{64,96},{96,128},{128,160},{160,192},{192,224},{224... | collective-permute-start | bytes 9224 | tf_op jit(solution)/shard_map/ppermute | solution.py:74
  51.1 33.0 %collective-permute-start.11 = (f32[3,8,20,2]{3,2,1,0:T(8,128)S(1)}, f32[3,8,20,2]{3,2,1,0:T(8,128)S(1)}, u32[]{:S(2)}, u32[]{:S(2)}) collective-permute-start(f32[3,8,20,2]{3,2,1,0:T(8,128)S(1)} %get-tuple-element.17), channel_id=1, source_target_pairs={{1,0},{2,1},{3,2},{4,3},{5,4},{6,5},{7,6},{8,7},{9,8},{10,9},{11,1... | collective-permute-start | bytes 11528 | tf_op jit(solution)/shard_map/ppermute | solution.py:74
  59.4 2.0 %copy-start.8 = (f32[16,16,512]{2,1,0:T(8,128)}, f32[16,16,512]{2,1,0:T(8,128)S(1)}, u32[]{:S(2)}) copy-start(f32[16,16,512]{2,1,0:T(8,128)S(1)} %collective-permute-done.m2) | copy-start | bytes 1572868
  59.4 28.7 %collective-permute-start.10 = (f32[3,8,20,2]{3,2,1,0:T(8,128)S(1)}, f32[3,8,20,2]{3,2,1,0:T(8,128)S(1)}, u32[]{:S(2)}, u32[]{:S(2)}) collective-permute-start(f32[3,8,20,2]{3,2,1,0:T(8,128)S(1)} %get-tuple-element.16), channel_id=1, source_target_pairs={{0,1},{1,2},{2,3},{3,4},{4,5},{5,6},{6,7},{7,8},{8,9},{9,10},{10,1... | collective-permute-start | bytes 11528 | tf_op jit(solution)/shard_map/ppermute | solution.py:74
  61.4 0.8 copy-start.9
  61.4 1.0 copy-start.10
  61.4 1.1 %copy-start.11 = (f32[16,16,512]{2,1,0:T(8,128)}, f32[16,16,512]{2,1,0:T(8,128)S(1)}, u32[]{:S(2)}) copy-start(f32[16,16,512]{2,1,0:T(8,128)S(1)} %collective-permute-done.3.p2) | copy-start | bytes 1572868
  62.5 25.6 %copy-start = (f32[8,16,16]{2,1,0:T(8,128)S(1)}, f32[8,16,16]{2,1,0:T(8,128)}, u32[]{:S(2)}) copy-start(f32[8,16,16]{2,1,0:T(8,128)} %param.13) | copy-start | bytes 24580
  62.5 25.6 %copy-start.1 = (f32[8,16,16]{2,1,0:T(8,128)S(1)}, f32[8,16,16]{2,1,0:T(8,128)}, u32[]{:S(2)}) copy-start(f32[8,16,16]{2,1,0:T(8,128)} %param.15) | copy-start | bytes 24580
  62.5 26.4 %copy-start.7 = (f32[3]{0:T(128)S(1)}, f32[3]{0:T(128)}, u32[]{:S(2)}) copy-start(f32[3]{0:T(128)} %constant.59.clone) | copy-start | bytes 40
  74.6 18.9 %collective-permute-start.4 = (f32[16,16,512]{2,1,0:T(8,128)}, f32[16,16,512]{2,1,0:T(8,128)S(1)}, u32[]{:S(2)}, u32[]{:S(2)}) collective-permute-start(f32[16,16,512]{2,1,0:T(8,128)} %get-tuple-element.10), channel_id=1, source_target_pairs={{0,2},{1,3},{2,4},{3,5},{4,6},{5,7},{6,8},{7,9},{8,10},{9,11},{10,... | collective-permute-start | bytes 1572872 | tf_op jit(solution)/shard_map/ppermute | solution.py:74
  76.5 22.1 %collective-permute-start.5 = (f32[16,16,512]{2,1,0:T(8,128)}, f32[16,16,512]{2,1,0:T(8,128)S(1)}, u32[]{:S(2)}, u32[]{:S(2)}) collective-permute-start(f32[16,16,512]{2,1,0:T(8,128)} %get-tuple-element.11), channel_id=1, source_target_pairs={{0,1},{1,2},{2,3},{3,4},{4,5},{5,6},{6,7},{7,8},{8,9},{9,10},{10,1... | collective-permute-start | bytes 1572872 | tf_op jit(solution)/shard_map/ppermute | solution.py:74
  78.4 20.2 %collective-permute-start.6 = (f32[16,16,512]{2,1,0:T(8,128)}, f32[16,16,512]{2,1,0:T(8,128)S(1)}, u32[]{:S(2)}, u32[]{:S(2)}) collective-permute-start(f32[16,16,512]{2,1,0:T(8,128)} %get-tuple-element.12), channel_id=1, source_target_pairs={{1,0},{2,1},{3,2},{4,3},{5,4},{6,5},{7,6},{8,7},{9,8},{10,9},{11,1... | collective-permute-start | bytes 1572872 | tf_op jit(solution)/shard_map/ppermute | solution.py:74
  84.2 18.2 %collective-permute-start.7 = (f32[16,16,512]{2,1,0:T(8,128)}, f32[16,16,512]{2,1,0:T(8,128)S(1)}, u32[]{:S(2)}, u32[]{:S(2)}) collective-permute-start(f32[16,16,512]{2,1,0:T(8,128)} %get-tuple-element.13), channel_id=1, source_target_pairs={{2,0},{3,1},{4,2},{5,3},{6,4},{7,5},{8,6},{9,7},{10,8},{11,9},{12,... | collective-permute-start | bytes 1572872 | tf_op jit(solution)/shard_map/ppermute | solution.py:74
  93.5 8.9 %copy-start.2 = (f32[16,16,512]{2,1,0:T(8,128)}, f32[16,16,512]{2,1,0:T(8,128)S(1)}, u32[]{:S(2)}) copy-start(f32[16,16,512]{2,1,0:T(8,128)S(1)} %collective-permute-done.4.o_m2) | copy-start | bytes 1572868
  98.6 3.8 %copy-start.3 = (f32[16,16,512]{2,1,0:T(8,128)}, f32[16,16,512]{2,1,0:T(8,128)S(1)}, u32[]{:S(2)}) copy-start(f32[16,16,512]{2,1,0:T(8,128)S(1)} %collective-permute-done.5.o_m1) | copy-start | bytes 1572868
  98.6 3.8 %copy-start.4 = (f32[16,16,512]{2,1,0:T(8,128)}, f32[16,16,512]{2,1,0:T(8,128)S(1)}, u32[]{:S(2)}) copy-start(f32[16,16,512]{2,1,0:T(8,128)S(1)} %collective-permute-done.6.o_p1) | copy-start | bytes 1572868
  102.4 0.8 copy-start.5

commit v2 on v1

v2 whole, which is shorter than its diff:
```python
import functools
import math

import jax
import jax.numpy as jnp
import numpy as np
from jax import lax
from jax.experimental import pallas as pl
from jax.experimental.pallas import tpu as pltpu
from jax.sharding import PartitionSpec as P

TILE = 16
LEVELS = 4
COMPS = 8
LANES = 128
TAPS = (1, 4, 6, 4, 1)
BEYOND = 2
W_ORDER = (0, 1, 2, 4, 3, 5)
VMEM_LIMIT = 20 * 1024 * 1024
PITCH = 32
EXT = 20 * PITCH
STEPS = (0.5, 0.002, 2.0)
LAMS = (0.2, 0.5, 0.05)


def blur_matrix(length, gap):
    out = np.zeros((length, length), np.float64)
    for tap, factor in enumerate(TAPS):
        offset = (tap - 2) * gap
        for i in range(max(0, -offset), min(length, length - offset)):
            out[i, i + offset] = factor
    return out


def composites(length):
    made, now = [], np.eye(length)
    for level in range(LEVELS):
        now = blur_matrix(length, 2**level) @ now
        made.append(now)
    return made


def halves(matrix):
    bf16 = jnp.bfloat16
    high = np.asarray(matrix, np.float32).astype(bf16)
    low = (np.asarray(matrix, np.float32) - high.astype(np.float32)).astype(bf16)
    return high, low


def channel_matrices(nch):
    parts = [halves(m.T) for m in composites(nch)]
    return np.stack([p[0] for p in parts] + [p[1] for p in parts[2:]])


def scatter_matrices(length):
    whole = composites(length)
    kinds = []
    for start in (0, TILE * (length // TILE // 2), length - TILE):
        parts = []
        for m in whole:
            block = np.zeros((5 * TILE, TILE))
            for k in range(5 * TILE):
                at = start - 2 * TILE + k
                if 0 <= at < length:
                    block[k] = m[at, start : start + TILE]
            parts.append(halves(block))
        high = np.concatenate([p[0] for p in parts], axis=1)
        low = np.concatenate([p[1] for p in parts[2:]], axis=1)
        kinds.append(np.concatenate([high, high, low], axis=1))
    return np.stack(kinds)


def sent(values, axis, by):
    size = lax.axis_size(axis)
    if by > 0:
        pairs = [(i, i + by) for i in range(size - by)]
    else:
        pairs = [(i, i + by) for i in range(-by, size)]
    return lax.ppermute(values, axis, pairs)


def own_row(t, row, amp_ref, index_ref, spread_ref, nch):
    if t == 0:
        return amp_ref[:, row, :]
    if t == 1:
        return (index_ref[:, row, :].astype(jnp.float32) + 0.5) * (1.0 / nch)
    return spread_ref[:, row, :]


def pack_kernel(x_ref, amp_ref, index_ref, spread_ref, up_ref, down_ref):
    nch = x_ref.shape[2]
    for out, first in ((up_ref, TILE - 2), (down_ref, 0)):
        for row in range(TILE):
            out[row] = x_ref[row]
        out[TILE] = jnp.zeros((TILE, nch), jnp.float32)
        for t in range(3):
            for r in range(2):
                lane = (2 * t + r) * TILE
                got = own_row(t, first + r, amp_ref, index_ref, spread_ref, nch)
                out[TILE, 0:COMPS, lane : lane + TILE] = got


def packed(cube, amplitude, centre_index, spread):
    vmem = pl.BlockSpec(memory_space=pltpu.VMEM)
    shape = (TILE + 1,) + cube.shape[1:]
    return pl.pallas_call(
        pack_kernel,
        out_shape=[pltpu.VMEM(shape, jnp.float32)] * 2,
        in_specs=[vmem] * 4,
        out_specs=[vmem] * 2,
        compiler_params=pltpu.CompilerParams(vmem_limit_bytes=VMEM_LIMIT),
        cost_estimate=pl.CostEstimate(flops=1000, bytes_accessed=1_000_000, transcendentals=0),
        name="pack",
    )(*[pltpu.with_memory_space_constraint(v, pltpu.HBM) for v in (cube, amplitude, centre_index, spread)])


def put_columns(out, ext_ref, shift):
    lane = lax.broadcasted_iota(jnp.int32, (COMPS, EXT), 1) % PITCH
    total = jnp.zeros((COMPS, EXT), jnp.float32)
    for t in range(3):
        moved = pltpu.roll(ext_ref[t], (2 * t - shift) % EXT, 1)
        total = jnp.where((lane >= 2 * t) & (lane < 2 * t + 2), moved, total)
    nch = out.shape[2]
    out[TILE] = jnp.zeros((TILE, nch), jnp.float32)
    out[TILE, 0:COMPS, :] = total[:, :nch]
    out[TILE, COMPS:, 0 : EXT - nch] = total[:, nch:]


def stencil(p):
    near = pltpu.roll(p, 1, 1) + pltpu.roll(p, EXT - 1, 1)
    return 4.0 * p - (near + (pltpu.roll(p, PITCH, 1) + pltpu.roll(p, EXT - PITCH, 1)))


def smoothed(ext_ref, left, right, place_ref):
    nch = left.shape[2]
    lane = lax.broadcasted_iota(jnp.int32, (COMPS, EXT), 1)
    row, column = lane // PITCH, lane % PITCH
    y = row + (place_ref[0] * TILE - 2)
    x = column + (place_ref[2] * TILE - 2)
    on_sky = (y >= 0) & (y < place_ref[1] * TILE) & (x >= 0) & (x < place_ref[3] * TILE)
    sides = [
        jnp.concatenate([ref[TILE, 0:COMPS, :], ref[TILE, COMPS:, 0 : EXT - nch]], axis=1)
        for ref in (left, right)
    ]
    out = []
    for t in range(3):
        p = ext_ref[t]
        p = jnp.where(column < 2, pltpu.roll(sides[0], (EXT - 2 * t) % EXT, 1), p)
        p = jnp.where(column >= TILE + 2, pltpu.roll(sides[1], (TILE + 2 - 2 * t) % EXT, 1), p)
        first = jnp.where(on_sky, stencil(p), 0.0)
        out.append(p - (STEPS[t] * LAMS[t]) * stencil(first))
    return out


def five(v, flag=None):
    total = (v[0] + v[4]) + 4.0 * (v[1] + v[3]) + 6.0 * v[2]
    return total if flag is None else total * flag


def split(v):
    high = v.astype(jnp.bfloat16)
    return high, (v - high.astype(jnp.float32)).astype(jnp.bfloat16)


def wavelet_kernel(
    place_ref, a_ref, m1, p1, m2, p2, x_ref, k_ref, own_ref, w_hbm,
    o_m2, o_m1, o_0, o_p1, o_p2, ext_ref, rows_ref, y_ref, w_ref, sems,
):
    nch = x_ref.shape[2]
    tiles = (m2, m1, x_ref, p1, p2)
    outs = (o_m2, o_m1, o_0, o_p1, o_p2)
    near = [place_ref[0] + i for i in (-2, -1, 0, 1, 2)]
    flags = [jnp.where((i >= 0) & (i < place_ref[1]), 1.0, 0.0) for i in near]
    loads = [pltpu.make_async_copy(w_hbm.at[i], w_ref.at[i], sems.at[i]) for i in range(LEVELS + 2)]
    for i in W_ORDER:
        loads[i].start()

    lane_tiles = nch // LANES

    def row_pass(step, carry):
        sub = pl.ds(pl.multiple_of((step // lane_tiles) * 8, 8), 8)
        lane = pl.ds(pl.multiple_of((step % lane_tiles) * LANES, LANES), LANES)

        @functools.cache
        def value(level, at):
            tile = (at + 2 * TILE) // TILE
            if level == 0:
                return tiles[tile][at % TILE - (BEYOND if tile == 0 else 0), sub, lane]
            gap = 2 ** (level - 1)
            taps = [value(level - 1, at + (t - 2) * gap) for t in range(5)]
            return five(taps, None if tile == 2 else flags[tile])

        reach = {1: 28, 2: 24, 3: 16, 4: 0}
        lag = {1: 2, 2: 6, 3: 14, 4: 30}
        for at in range(-30, TILE + 30):
            value(0, at)
            for level in range(1, LEVELS + 1):
                row = at - lag[level]
                if -reach[level] <= row < TILE + reach[level]:
                    got = value(level, row)
                    if 0 <= row < TILE:
                        rows_ref[level - 1, row, sub, lane] = got
        return carry

    lax.fori_loop(0, 2 * lane_tiles, row_pass, 0)

    pixels = TILE * TILE
    dot = functools.partial(jnp.dot, preferred_element_type=jnp.float32)
    for level in range(LEVELS):
        high, low = split(rows_ref[level].reshape(pixels, nch))
        loads[level].wait()
        got = dot(high, w_ref[level]) + dot(low, w_ref[level])
        if level >= 2:
            loads[level + 2].wait()
            got = got + dot(high, w_ref[level + 2])
        high, low = split(got * a_ref[level + 1])
        high = high.reshape(TILE, TILE, nch)
        y_ref[:, level * TILE : (level + 1) * TILE] = high
        at = (level + LEVELS) * TILE
        y_ref[:, at : at + TILE] = low.reshape(TILE, TILE, nch)
        if level >= 2:
            at = (level + 6) * TILE
            y_ref[:, at : at + TILE] = high

    kind = jnp.where(place_ref[2] == 0, 0, jnp.where(place_ref[2] == place_ref[3] - 1, 2, 1))
    columns = k_ref[kind]

    def column_pass(row, carry):
        got = dot(columns, y_ref[row])
        for i, out in enumerate(outs):
            part = got[i * TILE : (i + 1) * TILE]
            if i == 2:
                part = part + a_ref[0] * x_ref[row]
            out[row] = part
        return carry

    lax.fori_loop(0, TILE, column_pass, 0, unroll=4)

    ext_ref[...] = own_ref[...]
    for t in range(3):
        for r in range(2):
            lane = (2 * t + r) * TILE
            at = r * PITCH + 2
            ext_ref[t, :, at : at + TILE] = m1[TILE, 0:COMPS, lane : lane + TILE]
            at = (TILE + 2 + r) * PITCH + 2
            ext_ref[t, :, at : at + TILE] = p1[TILE, 0:COMPS, lane : lane + TILE]
    put_columns(o_p1, ext_ref, TILE)
    put_columns(o_m1, ext_ref, 2)


def kept(x):
    return pltpu.with_memory_space_constraint(x, pltpu.VMEM)


def wavelet_parts(place, coeff, tiles, own, nch, length):
    w = jnp.asarray(channel_matrices(nch))
    k = jnp.asarray(scatter_matrices(length))
    smem = pl.BlockSpec(memory_space=pltpu.SMEM)
    vmem = pl.BlockSpec(memory_space=pltpu.VMEM)
    plain = pltpu.VMEM(tiles[-1].shape, jnp.float32)
    taller = pltpu.VMEM(tiles[0].shape, jnp.float32)
    return pl.pallas_call(
        wavelet_kernel,
        out_shape=[plain, taller, plain, taller, plain, pltpu.VMEM(own.shape, jnp.float32)],
        in_specs=[smem] + [vmem] * 8 + [pl.BlockSpec(memory_space=pl.ANY)],
        out_specs=[vmem] * 6,
        scratch_shapes=[
            pltpu.VMEM((LEVELS, TILE, TILE, nch), jnp.float32),
            pltpu.VMEM((TILE, 10 * TILE, nch), jnp.bfloat16),
            pltpu.VMEM(w.shape, jnp.bfloat16),
            pltpu.SemaphoreType.DMA((LEVELS + 2,)),
        ],
        compiler_params=pltpu.CompilerParams(vmem_limit_bytes=VMEM_LIMIT),
        cost_estimate=pl.CostEstimate(flops=4_000_000_000, bytes_accessed=9_000_000, transcendentals=0),
        name="wavelet_parts",
    )(place, *[kept(x) for x in (coeff, *tiles, k, own)], pltpu.with_memory_space_constraint(w, pltpu.HBM))


def model_kernel(amp_ref, index_ref, spread_ref, model_ref, flat_ref, own_ref, scale_ref):
    nch, pixels = model_ref.shape
    own_ref[...] = jnp.zeros_like(own_ref)
    for t in range(3):
        for row in range(TILE):
            got = own_row(t, row, amp_ref, index_ref, spread_ref, nch)
            at = (row + 2) * PITCH + 2
            own_ref[t, :, at : at + TILE] = got
            flat_ref[t, :, row * TILE : (row + 1) * TILE] = got
    mu = flat_ref[1] * float(nch)
    inv = 1.0 / flat_ref[2]
    flat_ref[1] = mu
    flat_ref[2] = inv
    scale_ref[...] = (-0.5 * math.log2(math.e)) * inv * inv

    def body(step, carry):
        base = pl.multiple_of(step * 8, 8)
        chan = (lax.broadcasted_iota(jnp.int32, (8, pixels), 0) + base).astype(jnp.float32)
        total = jnp.zeros((8, pixels), jnp.float32)
        for k in range(COMPS):
            diff = chan - flat_ref[1, k : k + 1, :]
            bump = jnp.exp2(diff * diff * scale_ref[k : k + 1, :])
            total += flat_ref[0, k : k + 1, :] * bump
        model_ref[pl.ds(base, 8), :] = total
        return carry

    lax.fori_loop(0, nch // 8, body, 0, unroll=2)


def model_of(amplitude, centre_index, spread, nch):
    vmem = pl.BlockSpec(memory_space=pltpu.VMEM)
    pixels = TILE * TILE
    return pl.pallas_call(
        model_kernel,
        out_shape=[
            pltpu.VMEM((nch, pixels), jnp.float32),
            pltpu.VMEM((3, COMPS, pixels), jnp.float32),
            pltpu.VMEM((3, COMPS, EXT), jnp.float32),
        ],
        in_specs=[vmem] * 3,
        out_specs=[vmem] * 3,
        scratch_shapes=[pltpu.VMEM((COMPS, pixels), jnp.float32)],
        compiler_params=pltpu.CompilerParams(vmem_limit_bytes=VMEM_LIMIT),
        cost_estimate=pl.CostEstimate(flops=10_000_000, bytes_accessed=1_000_000, transcendentals=1_100_000),
        name="gaussian_model",
    )(amplitude, centre_index, spread)


def step_kernel(
    place_ref, o_0, o_m2, o_m1, o_p1, o_p2, model_ref, flat_ref, ext_ref,
    den_hbm, fit_ref, den_ref, r_ref, sem,
):
    nch, pixels = model_ref.shape
    rows = LANES // TILE
    parts = pixels // LANES
    copies = []
    bases = smoothed(ext_ref, o_m1, o_p1, place_ref)
    for part in range(parts):
        at = slice(part * rows, (part + 1) * rows)
        for row in range(part * rows, (part + 1) * rows):
            den_ref[row] = o_0[row] + ((o_m2[row] + o_m1[row]) + (o_p1[row] + o_p2[row]))
        copies.append(pltpu.make_async_copy(den_ref.at[at], den_hbm.at[at], sem.at[part]))
        copies[-1].start()

    for part in range(parts):
        block = den_ref[part * rows : (part + 1) * rows].reshape(LANES, nch)
        at = slice(part * LANES, (part + 1) * LANES)
        r_ref[:, at] = model_ref[:, at] - block.T

    for part in range(parts):
        at = slice(part * LANES, (part + 1) * LANES)
        sums = [[] for _ in range(3)]
        for first in range(0, COMPS, 4):
            chosen = range(first, first + 4)
            mus = [jnp.broadcast_to(flat_ref[1, k : k + 1, at], (8, LANES)) for k in chosen]
            inv = [jnp.broadcast_to(flat_ref[2, k : k + 1, at], (8, LANES)) for k in chosen]
            scales = [(-0.5 * math.log2(math.e)) * v * v for v in inv]

            def body(step, carry):
                base = pl.multiple_of(step * 8, 8)
                chan = (lax.broadcasted_iota(jnp.int32, (8, LANES), 0) + base).astype(jnp.float32)
                r = r_ref[pl.ds(base, 8), at]
                out = []
                for mu, scale, (a, b, c) in zip(mus, scales, carry):
                    diff = chan - mu
                    one = r * jnp.exp2(diff * diff * scale)
                    two = one * diff
                    out.append((a + one, b + two, c + two * diff))
                return tuple(out)

            zero = jnp.zeros((8, LANES), jnp.float32)
            done = lax.fori_loop(0, nch // 8, body, ((zero,) * 3,) * 4, unroll=8)
            for four in done:
                for t in range(3):
                    sums[t].append(jnp.sum(four[t], axis=0, keepdims=True))
        amp = flat_ref[0, :, at]
        inv = flat_ref[2, :, at]
        slope = amp * inv * inv
        grads = (
            jnp.concatenate(sums[0], axis=0) * (1.0 / nch),
            jnp.concatenate(sums[1], axis=0) * slope,
            jnp.concatenate(sums[2], axis=0) * (slope * inv * (1.0 / nch)),
        )
        for t in range(3):
            step = STEPS[t] * grads[t]
            for i in range(rows):
                row = part * rows + i
                lane = (row + 2) * PITCH + 2
                base = bases[t][:, lane : lane + TILE]
                fit_ref[t, :, row, :] = base - step[:, i * TILE : (i + 1) * TILE]

    for copy in copies:
        copy.wait()


def gradient_step(place, parts, model, flat, ext):
    vmem = pl.BlockSpec(memory_space=pltpu.VMEM)
    shape = parts[0].shape
    return pl.pallas_call(
        step_kernel,
        out_shape=[
            jax.ShapeDtypeStruct(shape, jnp.float32),
            jax.ShapeDtypeStruct((3, COMPS, TILE, TILE), jnp.float32),
        ],
        in_specs=[pl.BlockSpec(memory_space=pltpu.SMEM)] + [vmem] * 8,
        out_specs=[pl.BlockSpec(memory_space=pl.ANY), vmem],
        scratch_shapes=[
            pltpu.VMEM(shape, jnp.float32),
            pltpu.VMEM(model.shape, jnp.float32),
            pltpu.SemaphoreType.DMA((2,)),
        ],
        compiler_params=pltpu.CompilerParams(vmem_limit_bytes=VMEM_LIMIT),
        cost_estimate=pl.CostEstimate(flops=15_000_000, bytes_accessed=4_000_000, transcendentals=1_100_000),
        name="gradient_step",
    )(place, *[kept(x) for x in (*parts, model, flat, ext)])


def on_device(cube, level_table, level_index, amplitude, centre_index, spread):
    nch = cube.shape[2]
    places = [f(axis) for axis in ("skyy", "skyx") for f in (lax.axis_index, lax.axis_size)]
    place = jnp.stack([jnp.asarray(p, jnp.int32) for p in places])

    for_down, for_up = packed(cube, amplitude, centre_index, spread)
    up1, down1 = sent(for_down, "skyy", 1), sent(for_up, "skyy", -1)
    up2, down2 = sent(cube[BEYOND:], "skyy", 2), sent(cube[:-BEYOND], "skyy", -2)

    entries = jnp.arange(level_table.shape[0], dtype=jnp.int32)
    picks = (level_index[:, :, None] == entries).astype(jnp.float32)
    weight = jnp.sum(picks * level_table, axis=2)
    one = jnp.ones((1, nch), jnp.float32)
    coeff = jnp.concatenate([weight, one]) - jnp.concatenate([0.0 * one, weight])
    scale = jnp.array([16.0 ** (-3 * j) for j in range(LEVELS + 1)], jnp.float32)
    coeff = (coeff * scale[:, None])[:, None, :]
    model, flat, own = model_of(amplitude, centre_index, spread, nch)

    m2, m1, o_0, p1, p2, ext = wavelet_parts(
        place, coeff, (up1, down1, up2, down2, cube), own, nch, places[3] * TILE
    )

    left2, right2 = sent(p2, "skyx", 2), sent(m2, "skyx", -2)
    left1, right1 = sent(p1, "skyx", 1), sent(m1, "skyx", -1)
    return gradient_step(place, (o_0, left2, left1, right1, right2), model, flat, ext)


def solution(mesh):
    placed = (
        P("skyy", "skyx", None),
        P(),
        P(),
        P(None, "skyy", "skyx"),
        P(None, "skyy", "skyx"),
        P(None, "skyy", "skyx"),
    )
    return jax.shard_map(
        on_device,
        mesh=mesh,
        in_specs=placed,
        out_specs=(P("skyy", "skyx", None), P(None, None, "skyy", "skyx")),
        check_vma=False,
    )
```

time: 111 us -> 77.6 us (0.70)
  starting transfers between devices: 46.4 us -> 35.1 us
  waiting for transfers between devices: 27.6 us -> 20.5 us
  Pallas kernels: 20.3 us -> 14.3 us
  other arithmetic: 7.35 us -> 1.63 us
  local copies, waits for them, and re-layouts: 7.24 us -> 4.83 us
    ppermute x12 -> x8, starting transfers between devices: 46.4 us -> 35.1 us  [sent(): return lax.ppermute(values, axis, pairs)]
    ppermute x12 -> x8, waiting for transfers between devices: 27.6 us -> 20.5 us  [sent(): return lax.ppermute(values, axis, pairs)]
    pallas_call x3 -> x4, Pallas kernels: 20.3 us -> 14.3 us  [the longest x1 6.27 us: wavelet_parts(): pl.pallas_call(wavelet_kernel, out_shape=[plain, taller, plain, taller, p...]
    reshape x4 -> x0, local copies, waits for them, and re-layouts: 4.46 us -> none  [the longest x1 1.53 us: on_device(): return (denoised, fitted.reshape(3, COMPS, TILE, TILE))]
    slice x2 -> x1, local copies, waits for them, and re-layouts: 0.16 us -> 2.29 us  [on_device(): cube[:-BEYOND]]
    another operation x2 -> x1, other arithmetic: 1.74 us -> 0.08 us  [on_device(): place = jnp.stack([jnp.asarray(p, jnp.int32) for p in places])]
    concatenate x2 -> x0, other arithmetic: 1.2 us -> none  [the longest x1 0.93 us: on_device(): tall = jnp.concatenate([above, params, below], axis=2)]
    mul x3 -> x0, other arithmetic: 1.17 us -> none  [the longest x1 0.6 us: on_device(): s = -0.5 * math.log2(math.e) * inv * inv]
  transfers between devices with their start and end apart: 12 -> 8, of which waited for: 4 -> 3; matrix products, arithmetic and copies ran while one was open for 10% -> 5% of each run, Pallas kernels for 14% -> 2%
where the time goes in v2:
time: 77.6 us; the launch traced here: 77 us
  starting transfers between devices  35.1 us (45%)
  waiting for transfers between devices  20.5 us (26%)
  Pallas kernels  14.3 us (18%)
  local copies, waits for them, and re-layouts  4.83 us (6%)
  other arithmetic  1.63 us (2%)
    ppermute x8, starting transfers between devices, sent(): return lax.ppermute(values, axis, pairs)  35.1 us
    ppermute x8, waiting for transfers between devices, sent(): return lax.ppermute(values, axis, pairs)  20.5 us
    pallas_call x1, Pallas kernels, wavelet_parts(): pl.pallas_call(wavelet_kernel, out_shape=[plain, taller, plain, taller, p...  6.27 us
    pallas_call x1, Pallas kernels, gradient_step(): pl.pallas_call(step_kernel, out_shape=[jax.ShapeDtypeStruct(shape, jnp.fl...  5.23 us
    unnamed x10, local copies, waits for them, and re-layouts  2.53 us
    slice x1, local copies, waits for them, and re-layouts, on_device(): cube[:-BEYOND]  2.29 us
  transfers between devices with their start and end apart: 8, of which 3 were waited for; matrix products, arithmetic and copies ran while one was open for 5% of the time, Pallas kernels for 2%

profile of v2, /device:TPU:26, one launch (start us, length us, event | category | flops | bytes accessed | tf_op | source)
XLA Modules:
  0.0 77.0 jit_solution(13181035045315024849)
XLA Ops:
  0.6 0.0 copy-start.4
  0.6 0.0 copy-start
  0.7 1.3 %pack.1 = (f32[17,16,512]{2,1,0:T(8,128)S(1)}, f32[17,16,512]{2,1,0:T(8,128)S(1)}) custom-call(f32[16,16,512]{2,1,0:T(8,128)} %x_ref.3, f32[8,16,16]{2,1,0:T(8,128)} %amp_ref.3, s32[8,16,16]{2,1,0:T(8,128)} %index_ref.3, f32[8,16,16]{2,1,0:T(8,128)} %spread_ref.3), custom_call_target="tpu_custom_call" | custom-call | flops 1000 | bytes 1000000 | tf_op jit(solution)/shard_map/pack/pallas_call | solution.py:106
  2.0 4.0 %collective-permute-start = (f32[17,16,512]{2,1,0:T(8,128)S(1)}, f32[17,16,512]{2,1,0:T(8,128)S(1)}, u32[]{:S(2)}, u32[]{:S(2)}) collective-permute-start(f32[17,16,512]{2,1,0:T(8,128)S(1)} %get-tuple-element.13), channel_id=1, source_target_pairs={{0,32},{32,64},{64,96},{96,128},{128,160},{160,192},{192,224},{224... | collective-permute-start | bytes 1671176 | tf_op jit(solution)/shard_map/ppermute | solution.py:79
  6.0 4.2 %collective-permute-start.1 = (f32[17,16,512]{2,1,0:T(8,128)S(1)}, f32[17,16,512]{2,1,0:T(8,128)S(1)}, u32[]{:S(2)}, u32[]{:S(2)}) collective-permute-start(f32[17,16,512]{2,1,0:T(8,128)S(1)} %get-tuple-element.14), channel_id=1, source_target_pairs={{32,0},{64,32},{96,64},{128,96},{160,128},{192,160},{224,192},{256... | collective-permute-start | bytes 1671176 | tf_op jit(solution)/shard_map/ppermute | solution.py:79
  10.2 2.3 %fusion = (f32[14,16,512]{2,1,0:T(8,128)}, f32[14,16,512]{2,1,0:T(8,128)}) fusion(f32[16,16,512]{2,1,0:T(8,128)} %x_ref.3), kind=kLoop, calls=%fused_computation.4 | loop fusion | bytes 1835008 | tf_op jit(solution)/shard_map/slice | solution.py:423
  12.5 2.3 %collective-permute-start.3 = (f32[14,16,512]{2,1,0:T(8,128)}, f32[14,16,512]{2,1,0:T(8,128)S(1)}, u32[]{:S(2)}, u32[]{:S(2)}) collective-permute-start(f32[14,16,512]{2,1,0:T(8,128)} %get-tuple-element.24), channel_id=1, source_target_pairs={{64,0},{96,32},{128,64},{160,96},{192,128},{224,160},{256,192},{28... | collective-permute-start | bytes 1376264 | tf_op jit(solution)/shard_map/ppermute | solution.py:79
  14.9 5.5 %collective-permute-start.2 = (f32[14,16,512]{2,1,0:T(8,128)}, f32[14,16,512]{2,1,0:T(8,128)}, u32[]{:S(2)}, u32[]{:S(2)}) collective-permute-start(f32[14,16,512]{2,1,0:T(8,128)} %get-tuple-element.25), channel_id=1, source_target_pairs={{0,64},{32,96},{64,128},{96,160},{128,192},{160,224},{192,256},{22... | collective-permute-start | bytes 1376264 | tf_op jit(solution)/shard_map/ppermute | solution.py:79
  20.3 0.8 %select_reduce_fusion = f32[4,512]{1,0:T(4,128)S(1)} fusion(f32[16]{0:T(128)} %param.10, s32[4,512]{1,0:T(4,128)} %param.11), kind=kLoop, calls=%fused_computation | loop fusion | flops 96256 | bytes 16448 | tf_op jit(solution)/shard_map/reduce_sum | solution.py:427
  21.2 0.7 subtract_multiply_fusion
  21.9 0.8 %copy-done.1 = f32[8,16,16]{2,1,0:T(8,128)S(1)} copy-done((f32[8,16,16]{2,1,0:T(8,128)S(1)}, f32[8,16,16]{2,1,0:T(8,128)}, u32[]{:S(2)}) %copy-start.1) | copy-done | bytes 8216
  22.7 0.8 %copy-done.2 = s32[8,16,16]{2,1,0:T(8,128)S(1)} copy-done((s32[8,16,16]{2,1,0:T(8,128)S(1)}, s32[8,16,16]{2,1,0:T(8,128)}, u32[]{:S(2)}) %copy-start.2) | copy-done | bytes 8216
  23.6 0.8 %copy-done.3 = f32[8,16,16]{2,1,0:T(8,128)S(1)} copy-done((f32[8,16,16]{2,1,0:T(8,128)S(1)}, f32[8,16,16]{2,1,0:T(8,128)}, u32[]{:S(2)}) %copy-start.3) | copy-done | bytes 8216
  24.4 1.5 %gaussian_model.1 = (f32[512,256]{1,0:T(8,128)S(1)}, f32[3,8,256]{2,1,0:T(8,128)S(1)}, f32[3,8,640]{2,1,0:T(8,128)S(1)}) custom-call(f32[8,16,16]{2,1,0:T(8,128)S(1)} %copy-done.1, s32[8,16,16]{2,1,0:T(8,128)S(1)} %copy-done.2, f32[8,16,16]{2,1,0:T(8,128)S(1)} %copy-done.3), custom_call_target="tpu_custom_call" | custom-call | flops 10000000 | bytes 1000000 | tf_op jit(solution)/shard_map/gaussian_model/pallas_call | solution.py:311
  25.9 0.1 pad_add_fusion.place_ref
  26.0 10.1 %collective-permute-done.3.p2 = f32[14,16,512]{2,1,0:T(8,128)S(1)} collective-permute-done((f32[14,16,512]{2,1,0:T(8,128)}, f32[14,16,512]{2,1,0:T(8,128)S(1)}, u32[]{:S(2)}, u32[]{:S(2)}) %collective-permute-start.3) | collective-permute-done | bytes 458784 | tf_op jit(solution)/shard_map/ppermute | solution.py:79
  36.2 6.3 %wavelet_parts.1 = (f32[16,16,512]{2,1,0:T(8,128)S(1)}, f32[17,16,512]{2,1,0:T(8,128)S(1)}, f32[16,16,512]{2,1,0:T(8,128)S(1)}, f32[17,16,512]{2,1,0:T(8,128)S(1...) custom-call(s32[4]{0:T(128)S(1)} %pad_add_fusion.place_ref, f32[5,1,512]{2,1,0:T(1,128)S(1)} %broadcast_in_dim.2.a_ref, ...), custom_call_target="tpu_custom_call" | custom-call | flops 4000000000 | bytes 9000000 | tf_op jit(solution)/shard_map/wavelet_parts/pallas_call | solution.py:262
  42.4 1.9 %collective-permute-start.5 = (f32[17,16,512]{2,1,0:T(8,128)S(1)}, f32[17,16,512]{2,1,0:T(8,128)S(1)}, u32[]{:S(2)}, u32[]{:S(2)}) collective-permute-start(f32[17,16,512]{2,1,0:T(8,128)S(1)} %get-tuple-element.18), channel_id=1, source_target_pairs={{0,1},{1,2},{2,3},{3,4},{4,5},{5,6},{6,7},{7,8},{8,9},{9,10},{10,1... | collective-permute-start | bytes 1671176 | tf_op jit(solution)/shard_map/ppermute | solution.py:79
  44.4 9.2 %collective-permute-start.6 = (f32[17,16,512]{2,1,0:T(8,128)S(1)}, f32[17,16,512]{2,1,0:T(8,128)S(1)}, u32[]{:S(2)}, u32[]{:S(2)}) collective-permute-start(f32[17,16,512]{2,1,0:T(8,128)S(1)} %get-tuple-element.19), channel_id=1, source_target_pairs={{1,0},{2,1},{3,2},{4,3},{5,4},{6,5},{7,6},{8,7},{9,8},{10,9},{11,1... | collective-permute-start | bytes 1671176 | tf_op jit(solution)/shard_map/ppermute | solution.py:79
  53.5 1.9 %collective-permute-start.4 = (f32[16,16,512]{2,1,0:T(8,128)S(1)}, f32[16,16,512]{2,1,0:T(8,128)S(1)}, u32[]{:S(2)}, u32[]{:S(2)}) collective-permute-start(f32[16,16,512]{2,1,0:T(8,128)S(1)} %get-tuple-element.17), channel_id=1, source_target_pairs={{0,2},{1,3},{2,4},{3,5},{4,6},{5,7},{6,8},{7,9},{8,10},{9,11},{10,... | collective-permute-start | bytes 1572872 | tf_op jit(solution)/shard_map/ppermute | solution.py:79
  55.5 6.0 %collective-permute-start.7 = (f32[16,16,512]{2,1,0:T(8,128)S(1)}, f32[16,16,512]{2,1,0:T(8,128)S(1)}, u32[]{:S(2)}, u32[]{:S(2)}) collective-permute-start(f32[16,16,512]{2,1,0:T(8,128)S(1)} %get-tuple-element.20), channel_id=1, source_target_pairs={{2,0},{3,1},{4,2},{5,3},{6,4},{7,5},{8,6},{9,7},{10,8},{11,9},{12,... | collective-permute-start | bytes 1572872 | tf_op jit(solution)/shard_map/ppermute | solution.py:79
  61.5 8.5 %collective-permute-done.4.o_m2 = f32[16,16,512]{2,1,0:T(8,128)S(1)} collective-permute-done((f32[16,16,512]{2,1,0:T(8,128)S(1)}, f32[16,16,512]{2,1,0:T(8,128)S(1)}, u32[]{:S(2)}, u32[]{:S(2)}) %collective-permute-start.4) | collective-permute-done | bytes 524320 | tf_op jit(solution)/shard_map/ppermute | solution.py:79
  70.1 1.8 %collective-permute-done.7.o_p2 = f32[16,16,512]{2,1,0:T(8,128)S(1)} collective-permute-done((f32[16,16,512]{2,1,0:T(8,128)S(1)}, f32[16,16,512]{2,1,0:T(8,128)S(1)}, u32[]{:S(2)}, u32[]{:S(2)}) %collective-permute-start.7) | collective-permute-done | bytes 524320 | tf_op jit(solution)/shard_map/ppermute | solution.py:79
  71.8 5.2 %gradient_step.1 = (f32[16,16,512]{2,1,0:T(8,128)}, f32[3,8,16,16]{3,2,1,0:T(8,128)}) custom-call(s32[4]{0:T(128)S(1)} %pad_add_fusion.place_ref, f32[16,16,512]{2,1,0:T(8,128)S(1)} %get-tuple-element.16.o_0, f32[16,16,512]{2,1,0:T(8,128)S(1)} %collective-permute-done.4.o_m2, f32[17,16,512]{2,1,0:T(8,128)S(1)} %collective-permute-done.5.o_m1, ...), custom_call_target="tpu_custom_call" | custom-call | flops 15000000 | bytes 4000000 | tf_op jit(solution)/shard_map/gradient_step/pallas_call | solution.py:397
  (11 shorter events, 0.0 us)
Async XLA Ops:
  0.6 35.5 %copy-start.4 = (bf16[3,80,160]{2,1,0:T(8,128)(2,1)S(1)}, bf16[3,80,160]{2,1,0:T(8,128)(2,1)}, u32[]{:S(2)}) copy-start(bf16[3,80,160]{2,1,0:T(8,128)(2,1)} %constant.27.clone.k_ref) | copy-start | bytes 230404
  0.6 35.5 %copy-start = (f32[16,16,512]{2,1,0:T(8,128)S(1)}, f32[16,16,512]{2,1,0:T(8,128)}, u32[]{:S(2)}) copy-start(f32[16,16,512]{2,1,0:T(8,128)} %x_ref.3) | copy-start | bytes 1572868
  2.0 34.2 %collective-permute-start = (f32[17,16,512]{2,1,0:T(8,128)S(1)}, f32[17,16,512]{2,1,0:T(8,128)S(1)}, u32[]{:S(2)}, u32[]{:S(2)}) collective-permute-start(f32[17,16,512]{2,1,0:T(8,128)S(1)} %get-tuple-element.13), channel_id=1, source_target_pairs={{0,32},{32,64},{64,96},{96,128},{128,160},{160,192},{192,224},{224... | collective-permute-start | bytes 1671176 | tf_op jit(solution)/shard_map/ppermute | solution.py:79
  6.0 30.1 %collective-permute-start.1 = (f32[17,16,512]{2,1,0:T(8,128)S(1)}, f32[17,16,512]{2,1,0:T(8,128)S(1)}, u32[]{:S(2)}, u32[]{:S(2)}) collective-permute-start(f32[17,16,512]{2,1,0:T(8,128)S(1)} %get-tuple-element.14), channel_id=1, source_target_pairs={{32,0},{64,32},{96,64},{128,96},{160,128},{192,160},{224,192},{256... | collective-permute-start | bytes 1671176 | tf_op jit(solution)/shard_map/ppermute | solution.py:79
  12.5 23.6 %collective-permute-start.3 = (f32[14,16,512]{2,1,0:T(8,128)}, f32[14,16,512]{2,1,0:T(8,128)S(1)}, u32[]{:S(2)}, u32[]{:S(2)}) collective-permute-start(f32[14,16,512]{2,1,0:T(8,128)} %get-tuple-element.24), channel_id=1, source_target_pairs={{64,0},{96,32},{128,64},{160,96},{192,128},{224,160},{256,192},{28... | collective-permute-start | bytes 1376264 | tf_op jit(solution)/shard_map/ppermute | solution.py:79
  14.9 21.3 %collective-permute-start.2 = (f32[14,16,512]{2,1,0:T(8,128)}, f32[14,16,512]{2,1,0:T(8,128)}, u32[]{:S(2)}, u32[]{:S(2)}) collective-permute-start(f32[14,16,512]{2,1,0:T(8,128)} %get-tuple-element.25), channel_id=1, source_target_pairs={{0,64},{32,96},{64,128},{96,160},{128,192},{160,224},{192,256},{22... | collective-permute-start | bytes 1376264 | tf_op jit(solution)/shard_map/ppermute | solution.py:79
  21.9 0.8 %copy-start.1 = (f32[8,16,16]{2,1,0:T(8,128)S(1)}, f32[8,16,16]{2,1,0:T(8,128)}, u32[]{:S(2)}) copy-start(f32[8,16,16]{2,1,0:T(8,128)} %amp_ref.3) | copy-start | bytes 24580
  22.7 0.8 %copy-start.2 = (s32[8,16,16]{2,1,0:T(8,128)S(1)}, s32[8,16,16]{2,1,0:T(8,128)}, u32[]{:S(2)}) copy-start(s32[8,16,16]{2,1,0:T(8,128)} %index_ref.3) | copy-start | bytes 24580
  23.6 0.8 %copy-start.3 = (f32[8,16,16]{2,1,0:T(8,128)S(1)}, f32[8,16,16]{2,1,0:T(8,128)}, u32[]{:S(2)}) copy-start(f32[8,16,16]{2,1,0:T(8,128)} %spread_ref.3) | copy-start | bytes 24580
  42.4 29.4 %collective-permute-start.5 = (f32[17,16,512]{2,1,0:T(8,128)S(1)}, f32[17,16,512]{2,1,0:T(8,128)S(1)}, u32[]{:S(2)}, u32[]{:S(2)}) collective-permute-start(f32[17,16,512]{2,1,0:T(8,128)S(1)} %get-tuple-element.18), channel_id=1, source_target_pairs={{0,1},{1,2},{2,3},{3,4},{4,5},{5,6},{6,7},{7,8},{8,9},{9,10},{10,1... | collective-permute-start | bytes 1671176 | tf_op jit(solution)/shard_map/ppermute | solution.py:79
  44.4 27.5 %collective-permute-start.6 = (f32[17,16,512]{2,1,0:T(8,128)S(1)}, f32[17,16,512]{2,1,0:T(8,128)S(1)}, u32[]{:S(2)}, u32[]{:S(2)}) collective-permute-start(f32[17,16,512]{2,1,0:T(8,128)S(1)} %get-tuple-element.19), channel_id=1, source_target_pairs={{1,0},{2,1},{3,2},{4,3},{5,4},{6,5},{7,6},{8,7},{9,8},{10,9},{11,1... | collective-permute-start | bytes 1671176 | tf_op jit(solution)/shard_map/ppermute | solution.py:79
  53.5 16.5 %collective-permute-start.4 = (f32[16,16,512]{2,1,0:T(8,128)S(1)}, f32[16,16,512]{2,1,0:T(8,128)S(1)}, u32[]{:S(2)}, u32[]{:S(2)}) collective-permute-start(f32[16,16,512]{2,1,0:T(8,128)S(1)} %get-tuple-element.17), channel_id=1, source_target_pairs={{0,2},{1,3},{2,4},{3,5},{4,6},{5,7},{6,8},{7,9},{8,10},{9,11},{10,... | collective-permute-start | bytes 1572872 | tf_op jit(solution)/shard_map/ppermute | solution.py:79
  55.5 16.3 %collective-permute-start.7 = (f32[16,16,512]{2,1,0:T(8,128)S(1)}, f32[16,16,512]{2,1,0:T(8,128)S(1)}, u32[]{:S(2)}, u32[]{:S(2)}) collective-permute-start(f32[16,16,512]{2,1,0:T(8,128)S(1)} %get-tuple-element.20), channel_id=1, source_target_pairs={{2,0},{3,1},{4,2},{5,3},{6,4},{7,5},{8,6},{9,7},{10,8},{11,9},{12,... | collective-permute-start | bytes 1572872 | tf_op jit(solution)/shard_map/ppermute | solution.py:79

commit v3 on v2

--- a/solution.py
+++ b/solution.py
@@ -17,6 +17,7 @@
 BEYOND = 2
 W_ORDER = (0, 1, 2, 4, 3, 5)
 VMEM_LIMIT = 20 * 1024 * 1024
+ROLES = ((2, 3, 4, 1, 0), (2, 1, 0, 3, 4))
 PITCH = 32
 EXT = 20 * PITCH
 STEPS = (0.5, 0.002, 2.0)
@@ -66,7 +67,9 @@
             parts.append(halves(block))
         high = np.concatenate([p[0] for p in parts], axis=1)
         low = np.concatenate([p[1] for p in parts[2:]], axis=1)
-        kinds.append(np.concatenate([high, high, low], axis=1))
+        columns = np.concatenate([high, high, low], axis=1).reshape(5, TILE, -1)
+        for order in ROLES:
+            kinds.append(np.concatenate([columns[i] for i in order]))
     return np.stack(kinds)
 
 
@@ -77,6 +80,12 @@
     else:
         pairs = [(i, i + by) for i in range(-by, size)]
     return lax.ppermute(values, axis, pairs)
+
+
+def away(values, axis, by):
+    size = lax.axis_size(axis)
+    pairs = [(i, i + by if i % 2 else i - by) for i in range(size)]
+    return lax.ppermute(values, axis, [(i, j) for i, j in pairs if 0 <= j < size])
 
 
 def own_row(t, row, amp_ref, index_ref, spread_ref, nch):
@@ -114,16 +123,25 @@
     )(*[pltpu.with_memory_space_constraint(v, pltpu.HBM) for v in (cube, amplitude, centre_index, spread)])
 
 
-def put_columns(out, ext_ref, shift):
+def border_columns(ext_ref, shift):
     lane = lax.broadcasted_iota(jnp.int32, (COMPS, EXT), 1) % PITCH
     total = jnp.zeros((COMPS, EXT), jnp.float32)
     for t in range(3):
         moved = pltpu.roll(ext_ref[t], (2 * t - shift) % EXT, 1)
         total = jnp.where((lane >= 2 * t) & (lane < 2 * t + 2), moved, total)
+    return total
+
+
+def put_plane(out, index, lanes):
     nch = out.shape[2]
-    out[TILE] = jnp.zeros((TILE, nch), jnp.float32)
-    out[TILE, 0:COMPS, :] = total[:, :nch]
-    out[TILE, COMPS:, 0 : EXT - nch] = total[:, nch:]
+    out[index] = jnp.zeros((TILE, nch), jnp.float32)
+    out[index, 0:COMPS, :] = lanes[:, :nch]
+    out[index, COMPS:, 0 : EXT - nch] = lanes[:, nch:]
+
+
+def from_plane(ref, index):
+    nch = ref.shape[2]
+    return jnp.concatenate([ref[index, 0:COMPS, :], ref[index, COMPS:, 0 : EXT - nch]], axis=1)
 
 
 def stencil(p):
@@ -132,21 +150,16 @@
 
 
 def smoothed(ext_ref, left, right, place_ref):
-    nch = left.shape[2]
     lane = lax.broadcasted_iota(jnp.int32, (COMPS, EXT), 1)
     row, column = lane // PITCH, lane % PITCH
     y = row + (place_ref[0] * TILE - 2)
     x = column + (place_ref[2] * TILE - 2)
     on_sky = (y >= 0) & (y < place_ref[1] * TILE) & (x >= 0) & (x < place_ref[3] * TILE)
-    sides = [
-        jnp.concatenate([ref[TILE, 0:COMPS, :], ref[TILE, COMPS:, 0 : EXT - nch]], axis=1)
-        for ref in (left, right)
-    ]
     out = []
     for t in range(3):
         p = ext_ref[t]
-        p = jnp.where(column < 2, pltpu.roll(sides[0], (EXT - 2 * t) % EXT, 1), p)
-        p = jnp.where(column >= TILE + 2, pltpu.roll(sides[1], (TILE + 2 - 2 * t) % EXT, 1), p)
+        p = jnp.where(column < 2, pltpu.roll(left, (EXT - 2 * t) % EXT, 1), p)
+        p = jnp.where(column >= TILE + 2, pltpu.roll(right, (TILE + 2 - 2 * t) % EXT, 1), p)
         first = jnp.where(on_sky, stencil(p), 0.0)
         out.append(p - (STEPS[t] * LAMS[t]) * stencil(first))
     return out
@@ -164,11 +177,10 @@
 
 def wavelet_kernel(
     place_ref, a_ref, m1, p1, m2, p2, x_ref, k_ref, own_ref, w_hbm,
-    o_m2, o_m1, o_0, o_p1, o_p2, ext_ref, rows_ref, y_ref, w_ref, sems,
+    o_0, swap_ref, near_ref, far_ref, ext_ref, rows_ref, y_ref, w_ref, sems,
 ):
     nch = x_ref.shape[2]
     tiles = (m2, m1, x_ref, p1, p2)
-    outs = (o_m2, o_m1, o_0, o_p1, o_p2)
     near = [place_ref[0] + i for i in (-2, -1, 0, 1, 2)]
     flags = [jnp.where((i >= 0) & (i < place_ref[1]), 1.0, 0.0) for i in near]
     loads = [pltpu.make_async_copy(w_hbm.at[i], w_ref.at[i], sems.at[i]) for i in range(LEVELS + 2)]
@@ -223,15 +235,16 @@
             y_ref[:, at : at + TILE] = high
 
     kind = jnp.where(place_ref[2] == 0, 0, jnp.where(place_ref[2] == place_ref[3] - 1, 2, 1))
-    columns = k_ref[kind]
+    odd = place_ref[2] % 2
+    columns = k_ref[2 * kind + odd]
 
     def column_pass(row, carry):
         got = dot(columns, y_ref[row])
-        for i, out in enumerate(outs):
-            part = got[i * TILE : (i + 1) * TILE]
-            if i == 2:
-                part = part + a_ref[0] * x_ref[row]
-            out[row] = part
+        o_0[row] = got[:TILE] + a_ref[0] * x_ref[row]
+        swap_ref[row] = got[TILE : 2 * TILE]
+        swap_ref[row + TILE] = got[2 * TILE : 3 * TILE]
+        near_ref[row] = got[3 * TILE : 4 * TILE]
+        far_ref[row] = got[4 * TILE :]
         return carry
 
     lax.fori_loop(0, TILE, column_pass, 0, unroll=4)
@@ -244,8 +257,10 @@
             ext_ref[t, :, at : at + TILE] = m1[TILE, 0:COMPS, lane : lane + TILE]
             at = (TILE + 2 + r) * PITCH + 2
             ext_ref[t, :, at : at + TILE] = p1[TILE, 0:COMPS, lane : lane + TILE]
-    put_columns(o_p1, ext_ref, TILE)
-    put_columns(o_m1, ext_ref, 2)
+    to_right = border_columns(ext_ref, TILE)
+    to_left = border_columns(ext_ref, 2)
+    put_plane(swap_ref, 2 * TILE, jnp.where(odd == 0, to_right, to_left))
+    put_plane(near_ref, TILE, jnp.where(odd == 0, to_left, to_right))
 
 
 def kept(x):
@@ -259,11 +274,12 @@
     vmem = pl.BlockSpec(memory_space=pltpu.VMEM)
     plain = pltpu.VMEM(tiles[-1].shape, jnp.float32)
     taller = pltpu.VMEM(tiles[0].shape, jnp.float32)
+    pair = pltpu.VMEM((2 * TILE + 1,) + tiles[0].shape[1:], jnp.float32)
     return pl.pallas_call(
         wavelet_kernel,
-        out_shape=[plain, taller, plain, taller, plain, pltpu.VMEM(own.shape, jnp.float32)],
+        out_shape=[plain, pair, taller, plain, pltpu.VMEM(own.shape, jnp.float32)],
         in_specs=[smem] + [vmem] * 8 + [pl.BlockSpec(memory_space=pl.ANY)],
-        out_specs=[vmem] * 6,
+        out_specs=[vmem] * 5,
         scratch_shapes=[
             pltpu.VMEM((LEVELS, TILE, TILE, nch), jnp.float32),
             pltpu.VMEM((TILE, 10 * TILE, nch), jnp.bfloat16),
@@ -274,6 +290,28 @@
         cost_estimate=pl.CostEstimate(flops=4_000_000_000, bytes_accessed=9_000_000, transcendentals=0),
         name="wavelet_parts",
     )(place, *[kept(x) for x in (coeff, *tiles, k, own)], pltpu.with_memory_space_constraint(w, pltpu.HBM))
+
+
+def add_kernel(near_ref, swapped_ref, _, out_ref):
+    def body(row, carry):
+        out_ref[row] = near_ref[row] + swapped_ref[row + TILE]
+        return carry
+
+    lax.fori_loop(0, TILE, body, 0, unroll=4)
+    out_ref[TILE] = near_ref[TILE]
+
+
+def outward(near, swapped, far):
+    vmem = pl.BlockSpec(memory_space=pltpu.VMEM)
+    return pl.pallas_call(
+        add_kernel,
+        out_shape=pltpu.VMEM(near.shape, jnp.float32),
+        in_specs=[vmem] * 2 + [pl.BlockSpec(memory_space=pl.ANY)],
+        out_specs=vmem,
+        compiler_params=pltpu.CompilerParams(vmem_limit_bytes=VMEM_LIMIT),
+        cost_estimate=pl.CostEstimate(flops=100_000, bytes_accessed=1_500_000, transcendentals=0),
+        name="outward",
+    )(kept(near), kept(swapped), kept(far))
 
 
 def model_kernel(amp_ref, index_ref, spread_ref, model_ref, flat_ref, own_ref, scale_ref):
@@ -325,18 +363,21 @@
 
 
 def step_kernel(
-    place_ref, o_0, o_m2, o_m1, o_p1, o_p2, model_ref, flat_ref, ext_ref,
+    place_ref, o_0, swapped_ref, far_ref, near_ref, model_ref, flat_ref, ext_ref,
     den_hbm, fit_ref, den_ref, r_ref, sem,
 ):
     nch, pixels = model_ref.shape
     rows = LANES // TILE
     parts = pixels // LANES
     copies = []
-    bases = smoothed(ext_ref, o_m1, o_p1, place_ref)
+    even = place_ref[2] % 2 == 0
+    inner, outer = from_plane(swapped_ref, 2 * TILE), from_plane(near_ref, TILE)
+    left, right = jnp.where(even, outer, inner), jnp.where(even, inner, outer)
+    bases = smoothed(ext_ref, left, right, place_ref)
     for part in range(parts):
         at = slice(part * rows, (part + 1) * rows)
         for row in range(part * rows, (part + 1) * rows):
-            den_ref[row] = o_0[row] + ((o_m2[row] + o_m1[row]) + (o_p1[row] + o_p2[row]))
+            den_ref[row] = (o_0[row] + swapped_ref[row]) + (far_ref[row] + near_ref[row])
         copies.append(pltpu.make_async_copy(den_ref.at[at], den_hbm.at[at], sem.at[part]))
         copies[-1].start()
 
@@ -400,7 +441,7 @@
             jax.ShapeDtypeStruct(shape, jnp.float32),
             jax.ShapeDtypeStruct((3, COMPS, TILE, TILE), jnp.float32),
         ],
-        in_specs=[pl.BlockSpec(memory_space=pltpu.SMEM)] + [vmem] * 8,
+        in_specs=[pl.BlockSpec(memory_space=pltpu.SMEM)] + [vmem] * 7,
         out_specs=[pl.BlockSpec(memory_space=pl.ANY), vmem],
         scratch_shapes=[
             pltpu.VMEM(shape, jnp.float32),
@@ -431,13 +472,14 @@
     coeff = (coeff * scale[:, None])[:, None, :]
     model, flat, own = model_of(amplitude, centre_index, spread, nch)
 
-    m2, m1, o_0, p1, p2, ext = wavelet_parts(
+    o_0, swap, near, far, ext = wavelet_parts(
         place, coeff, (up1, down1, up2, down2, cube), own, nch, places[3] * TILE
     )
 
-    left2, right2 = sent(p2, "skyx", 2), sent(m2, "skyx", -2)
-    left1, right1 = sent(p1, "skyx", 1), sent(m1, "skyx", -1)
-    return gradient_step(place, (o_0, left2, left1, right1, right2), model, flat, ext)
+    swapped = lax.ppermute(swap, "skyx", [(i, i ^ 1) for i in range(places[3])])
+    far = away(far, "skyx", 2)
+    near = away(outward(near, swapped, far), "skyx", 1)
+    return gradient_step(place, (o_0, swapped, far, near), model, flat, ext)
 
 
 def solution(mesh):

time: 77.6 us -> 80.7 us (1.040)
  waiting for transfers between devices: 20.5 us -> 31.3 us
  local copies, waits for them, and re-layouts: 4.83 us -> 1.1 us
  starting transfers between devices: 35.1 us -> 32.7 us
  other arithmetic: 1.63 us -> 0.26 us
    ppermute x8 -> x4, starting transfers between devices: 35.1 us -> 16.2 us  [sent(): return lax.ppermute(values, axis, pairs)]
    ppermute x0 -> x3, starting transfers between devices: none -> 16.5 us  [the longest x2 14.6 us: away(): lax.ppermute(values, axis, [(i, j) for i, j in pairs if 0 <= j < size])]
    ppermute x0 -> x3, waiting for transfers between devices: none -> 16 us  [the longest x2 16 us: away(): lax.ppermute(values, axis, [(i, j) for i, j in pairs if 0 <= j < size])]
    ppermute x8 -> x4, waiting for transfers between devices: 20.5 us -> 15.3 us  [sent(): return lax.ppermute(values, axis, pairs)]
    unnamed x10 -> x16, local copies, waits for them, and re-layouts: 2.53 us -> 0.05 us
    slice x1, local copies, waits for them, and re-layouts: 2.29 us -> 1.04 us  [on_device(): cube[:-BEYOND]]
    pallas_call x1 -> x2, Pallas kernels: 6.27 us -> 6.34 us  [the longest x1 6.27 us: wavelet_parts(): pl.pallas_call(wavelet_kernel, out_shape=[plain, pair, taller, plain, plt...]
  transfers between devices with their start and end apart: 8 -> 7, of which waited for: 3 -> 3; matrix products, arithmetic and copies ran while one was open for 5% -> 2% of each run, Pallas kernels for 2% -> 2%
where the time goes in v3:
time: 80.7 us; the launch traced here: 80.4 us
  starting transfers between devices  32.7 us (41%)
  waiting for transfers between devices  31.3 us (39%)
  Pallas kernels  14.2 us (18%)
  local copies, waits for them, and re-layouts  1.1 us (1%)
  between operations  0.85 us (1%)
    ppermute x4, starting transfers between devices, sent(): return lax.ppermute(values, axis, pairs)  16.2 us
    ppermute x2, waiting for transfers between devices, away(): lax.ppermute(values, axis, [(i, j) for i, j in pairs if 0 <= j < size])  16 us
    ppermute x4, waiting for transfers between devices, sent(): return lax.ppermute(values, axis, pairs)  15.3 us
    ppermute x2, starting transfers between devices, away(): lax.ppermute(values, axis, [(i, j) for i, j in pairs if 0 <= j < size])  14.6 us
    pallas_call x1, Pallas kernels, wavelet_parts(): pl.pallas_call(wavelet_kernel, out_shape=[plain, pair, taller, plain, plt...  6.27 us
    pallas_call x1, Pallas kernels, gradient_step(): pl.pallas_call(step_kernel, out_shape=[jax.ShapeDtypeStruct(shape, jnp.fl...  5.18 us
    ppermute x1, starting transfers between devices, on_device(): swapped = lax.ppermute(swap, 'skyx', [(i, i ^ 1) for i in range(places[3])])  1.92 us
  transfers between devices with their start and end apart: 7, of which 3 were waited for; matrix products, arithmetic and copies ran while one was open for 2% of the time, Pallas kernels for 2%

profile of v3, /device:TPU:26, one launch (start us, length us, event | category | flops | bytes accessed | tf_op | source)
XLA Modules:
  0.0 80.4 jit_solution(435979846921868367)
XLA Ops:
  0.6 1.3 %pack.1 = (f32[17,16,512]{2,1,0:T(8,128)S(1)}, f32[17,16,512]{2,1,0:T(8,128)S(1)}) custom-call(f32[16,16,512]{2,1,0:T(8,128)} %x_ref.3, f32[8,16,16]{2,1,0:T(8,128)} %amp_ref.3, s32[8,16,16]{2,1,0:T(8,128)} %index_ref.3, f32[8,16,16]{2,1,0:T(8,128)} %spread_ref.3), custom_call_target="tpu_custom_call" | custom-call | flops 1000 | bytes 1000000 | tf_op jit(solution)/shard_map/pack/pallas_call | solution.py:115
  1.9 0.0 copy-start.6
  2.0 0.0 copy-start.7
  2.0 0.0 copy-start.1
  2.0 0.0 copy-start.2
  2.0 4.2 %collective-permute-start = (f32[17,16,512]{2,1,0:T(8,128)S(1)}, f32[17,16,512]{2,1,0:T(8,128)S(1)}, u32[]{:S(2)}, u32[]{:S(2)}) collective-permute-start(f32[17,16,512]{2,1,0:T(8,128)S(1)} %get-tuple-element.12), channel_id=1, source_target_pairs={{0,32},{32,64},{64,96},{96,128},{128,160},{160,192},{192,224},{224... | collective-permute-start | bytes 1671176 | tf_op jit(solution)/shard_map/ppermute | solution.py:82
  6.2 4.2 %collective-permute-start.1 = (f32[17,16,512]{2,1,0:T(8,128)S(1)}, f32[17,16,512]{2,1,0:T(8,128)S(1)}, u32[]{:S(2)}, u32[]{:S(2)}) collective-permute-start(f32[17,16,512]{2,1,0:T(8,128)S(1)} %get-tuple-element.13), channel_id=1, source_target_pairs={{32,0},{64,32},{96,64},{128,96},{160,128},{192,160},{224,192},{256... | collective-permute-start | bytes 1671176 | tf_op jit(solution)/shard_map/ppermute | solution.py:82
  10.4 1.0 %fusion = (f32[14,16,512]{2,1,0:T(8,128)}, f32[14,16,512]{2,1,0:T(8,128)}) fusion(f32[16,16,512]{2,1,0:T(8,128)S(1)} %copy-done), kind=kLoop, calls=%fused_computation.4 | loop fusion | bytes 1835008 | tf_op jit(solution)/shard_map/slice | solution.py:464
  11.4 2.3 %collective-permute-start.3 = (f32[14,16,512]{2,1,0:T(8,128)}, f32[14,16,512]{2,1,0:T(8,128)S(1)}, u32[]{:S(2)}, u32[]{:S(2)}) collective-permute-start(f32[14,16,512]{2,1,0:T(8,128)} %get-tuple-element.22), channel_id=1, source_target_pairs={{64,0},{96,32},{128,64},{160,96},{192,128},{224,160},{256,192},{28... | collective-permute-start | bytes 1376264 | tf_op jit(solution)/shard_map/ppermute | solution.py:82
  13.8 5.5 %collective-permute-start.2 = (f32[14,16,512]{2,1,0:T(8,128)}, f32[14,16,512]{2,1,0:T(8,128)}, u32[]{:S(2)}, u32[]{:S(2)}) collective-permute-start(f32[14,16,512]{2,1,0:T(8,128)} %get-tuple-element.23), channel_id=1, source_target_pairs={{0,64},{32,96},{64,128},{96,160},{128,192},{160,224},{192,256},{22... | collective-permute-start | bytes 1376264 | tf_op jit(solution)/shard_map/ppermute | solution.py:82
  19.3 0.0 copy-start.4
  19.3 0.1 select_reduce_fusion
  19.4 0.1 subtract_multiply_fusion
  19.5 1.4 %gaussian_model.1 = (f32[512,256]{1,0:T(8,128)S(1)}, f32[3,8,256]{2,1,0:T(8,128)S(1)}, f32[3,8,640]{2,1,0:T(8,128)S(1)}) custom-call(f32[8,16,16]{2,1,0:T(8,128)S(1)} %copy-done.1, s32[8,16,16]{2,1,0:T(8,128)S(1)} %copy-done.2, f32[8,16,16]{2,1,0:T(8,128)S(1)} %copy-done.3), custom_call_target="tpu_custom_call" | custom-call | flops 10000000 | bytes 1000000 | tf_op jit(solution)/shard_map/gaussian_model/pallas_call | solution.py:349
  21.0 0.1 pad_add_fusion.place_ref
  21.1 15.3 %collective-permute-done.3.p2 = f32[14,16,512]{2,1,0:T(8,128)S(1)} collective-permute-done((f32[14,16,512]{2,1,0:T(8,128)}, f32[14,16,512]{2,1,0:T(8,128)S(1)}, u32[]{:S(2)}, u32[]{:S(2)}) %collective-permute-start.3) | collective-permute-done | bytes 458784 | tf_op jit(solution)/shard_map/ppermute | solution.py:82
  36.3 6.3 %wavelet_parts.1 = (f32[16,16,512]{2,1,0:T(8,128)S(1)}, f32[33,16,512]{2,1,0:T(8,128)S(1)}, f32[17,16,512]{2,1,0:T(8,128)S(1)}, f32[16,16,512]{2,1,0:T(8,128)S(1)}, f32[3,8,640]{2,1,0:T(8,128)S(1)}) custom-call(s32[4]{0:T(128)S(1)} %pad_add_fusion.place_ref, f32[5,1,512]{2,1,0:T(1,128)S(1)} %broadcast_in_dim.2.a_ref, ...), custom_call_target="tpu_custom_call" | custom-call | flops 4000000000 | bytes 9000000 | tf_op jit(solution)/shard_map/wavelet_parts/pallas_call | solution.py:278
  42.6 1.9 %collective-permute-start.4 = (f32[33,16,512]{2,1,0:T(8,128)S(1)}, f32[33,16,512]{2,1,0:T(8,128)S(1)}, u32[]{:S(2)}, u32[]{:S(2)}) collective-permute-start(f32[33,16,512]{2,1,0:T(8,128)S(1)} %get-tuple-element.16), channel_id=1, source_target_pairs={{0,1},{1,0},{2,3},{3,2},{4,5},{5,4},{6,7},{7,6},{8,9},{9,8},{10,11... | collective-permute-start | bytes 3244040 | tf_op jit(solution)/shard_map/ppermute | solution.py:479
  44.5 10.9 %collective-permute-start.5 = (f32[16,16,512]{2,1,0:T(8,128)S(1)}, f32[16,16,512]{2,1,0:T(8,128)S(1)}, u32[]{:S(2)}, u32[]{:S(2)}) collective-permute-start(f32[16,16,512]{2,1,0:T(8,128)S(1)} %get-tuple-element.17), channel_id=1, source_target_pairs={{1,3},{2,0},{3,5},{4,2},{5,7},{6,4},{7,9},{8,6},{9,11},{10,8},{11,... | collective-permute-start | bytes 1572872 | tf_op jit(solution)/shard_map/ppermute | solution.py:88
  55.5 6.7 %collective-permute-done.5._.far_ref = f32[16,16,512]{2,1,0:T(8,128)S(1)} collective-permute-done((f32[16,16,512]{2,1,0:T(8,128)S(1)}, f32[16,16,512]{2,1,0:T(8,128)S(1)}, u32[]{:S(2)}, u32[]{:S(2)}) %collective-permute-start.5) | collective-permute-done | bytes 524320 | tf_op jit(solution)/shard_map/ppermute | solution.py:88
  62.1 0.1 outward.1
  62.2 3.6 %collective-permute-start.6 = (f32[17,16,512]{2,1,0:T(8,128)S(1)}, f32[17,16,512]{2,1,0:T(8,128)S(1)}, u32[]{:S(2)}, u32[]{:S(2)}) collective-permute-start(f32[17,16,512]{2,1,0:T(8,128)S(1)} %outward.1), channel_id=1, source_target_pairs={{1,2},{2,1},{3,4},{4,3},{5,6},{6,5},{7,8},{8,7},{9,10},{10,9},{11,... | collective-permute-start | bytes 1671176 | tf_op jit(solution)/shard_map/ppermute | solution.py:88
  65.9 9.3 %collective-permute-done.6.near_ref = f32[17,16,512]{2,1,0:T(8,128)S(1)} collective-permute-done((f32[17,16,512]{2,1,0:T(8,128)S(1)}, f32[17,16,512]{2,1,0:T(8,128)S(1)}, u32[]{:S(2)}, u32[]{:S(2)}) %collective-permute-start.6) | collective-permute-done | bytes 557088 | tf_op jit(solution)/shard_map/ppermute | solution.py:88
  75.2 5.2 %gradient_step.1 = (f32[16,16,512]{2,1,0:T(8,128)}, f32[3,8,16,16]{3,2,1,0:T(8,128)}) custom-call(s32[4]{0:T(128)S(1)} %pad_add_fusion.place_ref, f32[16,16,512]{2,1,0:T(8,128)S(1)} %get-tuple-element.15.o_0, f32[33,16,512]{2,1,0:T(8,128)S(1)} %collective-permute-done.4.swapped_ref, f32[16,16,512]{2,1,0:T(8,128)S(1)} %collective-permute-done.5._.far_ref, ...), custom_call_target="tpu_custom_call" | custom-call | flops 15000000 | bytes 4000000 | tf_op jit(solution)/shard_map/gradient_step/pallas_call | solution.py:438
  (16 shorter events, 0.0 us)
Async XLA Ops:
  0.6 9.8 %copy-start = (f32[16,16,512]{2,1,0:T(8,128)S(1)}, f32[16,16,512]{2,1,0:T(8,128)}, u32[]{:S(2)}) copy-start(f32[16,16,512]{2,1,0:T(8,128)} %x_ref.3) | copy-start | bytes 1572868
  1.9 17.4 %copy-start.5 = (s32[4,512]{1,0:T(4,128)S(1)}, s32[4,512]{1,0:T(4,128)}, u32[]{:S(2)}) copy-start(s32[4,512]{1,0:T(4,128)} %param.11) | copy-start | bytes 24580
  1.9 17.4 %copy-start.6 = (f32[16]{0:T(128)S(1)}, f32[16]{0:T(128)}, u32[]{:S(2)}) copy-start(f32[16]{0:T(128)} %param.10) | copy-start | bytes 196
  2.0 17.5 %copy-start.7 = (f32[5]{0:T(128)S(1)}, f32[5]{0:T(128)}, u32[]{:S(2)}) copy-start(f32[5]{0:T(128)} %constant.25.clone) | copy-start | bytes 64
  2.0 17.5 %copy-start.1 = (f32[8,16,16]{2,1,0:T(8,128)S(1)}, f32[8,16,16]{2,1,0:T(8,128)}, u32[]{:S(2)}) copy-start(f32[8,16,16]{2,1,0:T(8,128)} %amp_ref.3) | copy-start | bytes 24580
  2.0 17.5 %copy-start.2 = (s32[8,16,16]{2,1,0:T(8,128)S(1)}, s32[8,16,16]{2,1,0:T(8,128)}, u32[]{:S(2)}) copy-start(s32[8,16,16]{2,1,0:T(8,128)} %index_ref.3) | copy-start | bytes 24580
  2.0 17.5 %copy-start.3 = (f32[8,16,16]{2,1,0:T(8,128)S(1)}, f32[8,16,16]{2,1,0:T(8,128)}, u32[]{:S(2)}) copy-start(f32[8,16,16]{2,1,0:T(8,128)} %spread_ref.3) | copy-start | bytes 24580
  2.0 34.3 %collective-permute-start = (f32[17,16,512]{2,1,0:T(8,128)S(1)}, f32[17,16,512]{2,1,0:T(8,128)S(1)}, u32[]{:S(2)}, u32[]{:S(2)}) collective-permute-start(f32[17,16,512]{2,1,0:T(8,128)S(1)} %get-tuple-element.12), channel_id=1, source_target_pairs={{0,32},{32,64},{64,96},{96,128},{128,160},{160,192},{192,224},{224... | collective-permute-start | bytes 1671176 | tf_op jit(solution)/shard_map/ppermute | solution.py:82
  6.2 30.1 %collective-permute-start.1 = (f32[17,16,512]{2,1,0:T(8,128)S(1)}, f32[17,16,512]{2,1,0:T(8,128)S(1)}, u32[]{:S(2)}, u32[]{:S(2)}) collective-permute-start(f32[17,16,512]{2,1,0:T(8,128)S(1)} %get-tuple-element.13), channel_id=1, source_target_pairs={{32,0},{64,32},{96,64},{128,96},{160,128},{192,160},{224,192},{256... | collective-permute-start | bytes 1671176 | tf_op jit(solution)/shard_map/ppermute | solution.py:82
  11.4 24.9 %collective-permute-start.3 = (f32[14,16,512]{2,1,0:T(8,128)}, f32[14,16,512]{2,1,0:T(8,128)S(1)}, u32[]{:S(2)}, u32[]{:S(2)}) collective-permute-start(f32[14,16,512]{2,1,0:T(8,128)} %get-tuple-element.22), channel_id=1, source_target_pairs={{64,0},{96,32},{128,64},{160,96},{192,128},{224,160},{256,192},{28... | collective-permute-start | bytes 1376264 | tf_op jit(solution)/shard_map/ppermute | solution.py:82
  13.8 22.5 %collective-permute-start.2 = (f32[14,16,512]{2,1,0:T(8,128)}, f32[14,16,512]{2,1,0:T(8,128)}, u32[]{:S(2)}, u32[]{:S(2)}) collective-permute-start(f32[14,16,512]{2,1,0:T(8,128)} %get-tuple-element.23), channel_id=1, source_target_pairs={{0,64},{32,96},{64,128},{96,160},{128,192},{160,224},{192,256},{22... | collective-permute-start | bytes 1376264 | tf_op jit(solution)/shard_map/ppermute | solution.py:82
  19.3 17.0 %copy-start.4 = (bf16[6,80,160]{2,1,0:T(8,128)(2,1)S(1)}, bf16[6,80,160]{2,1,0:T(8,128)(2,1)}, u32[]{:S(2)}) copy-start(bf16[6,80,160]{2,1,0:T(8,128)(2,1)} %constant.27.clone.k_ref) | copy-start | bytes 460804
  42.6 19.5 %collective-permute-start.4 = (f32[33,16,512]{2,1,0:T(8,128)S(1)}, f32[33,16,512]{2,1,0:T(8,128)S(1)}, u32[]{:S(2)}, u32[]{:S(2)}) collective-permute-start(f32[33,16,512]{2,1,0:T(8,128)S(1)} %get-tuple-element.16), channel_id=1, source_target_pairs={{0,1},{1,0},{2,3},{3,2},{4,5},{5,4},{6,7},{7,6},{8,9},{9,8},{10,11... | collective-permute-start | bytes 3244040 | tf_op jit(solution)/shard_map/ppermute | solution.py:479
  44.5 17.6 %collective-permute-start.5 = (f32[16,16,512]{2,1,0:T(8,128)S(1)}, f32[16,16,512]{2,1,0:T(8,128)S(1)}, u32[]{:S(2)}, u32[]{:S(2)}) collective-permute-start(f32[16,16,512]{2,1,0:T(8,128)S(1)} %get-tuple-element.17), channel_id=1, source_target_pairs={{1,3},{2,0},{3,5},{4,2},{5,7},{6,4},{7,9},{8,6},{9,11},{10,8},{11,... | collective-permute-start | bytes 1572872 | tf_op jit(solution)/shard_map/ppermute | solution.py:88
  62.2 13.0 %collective-permute-start.6 = (f32[17,16,512]{2,1,0:T(8,128)S(1)}, f32[17,16,512]{2,1,0:T(8,128)S(1)}, u32[]{:S(2)}, u32[]{:S(2)}) collective-permute-start(f32[17,16,512]{2,1,0:T(8,128)S(1)} %outward.1), channel_id=1, source_target_pairs={{1,2},{2,1},{3,4},{4,3},{5,6},{6,5},{7,8},{8,7},{9,10},{10,9},{11,... | collective-permute-start | bytes 1671176 | tf_op jit(solution)/shard_map/ppermute | solution.py:88

commit v4 on v3

--- a/solution.py
+++ b/solution.py
@@ -15,7 +15,6 @@
 LANES = 128
 TAPS = (1, 4, 6, 4, 1)
 BEYOND = 2
-W_ORDER = (0, 1, 2, 4, 3, 5)
 VMEM_LIMIT = 20 * 1024 * 1024
 ROLES = ((2, 3, 4, 1, 0), (2, 1, 0, 3, 4))
 PITCH = 32
@@ -176,16 +175,13 @@
 
 
 def wavelet_kernel(
-    place_ref, a_ref, m1, p1, m2, p2, x_ref, k_ref, own_ref, w_hbm,
-    o_0, swap_ref, near_ref, far_ref, ext_ref, rows_ref, y_ref, w_ref, sems,
+    place_ref, a_ref, m1, p1, m2, p2, x_ref, k_ref, own_ref, w_ref,
+    o_0, swap_ref, near_ref, far_ref, ext_ref, rows_ref, y_ref,
 ):
     nch = x_ref.shape[2]
     tiles = (m2, m1, x_ref, p1, p2)
     near = [place_ref[0] + i for i in (-2, -1, 0, 1, 2)]
     flags = [jnp.where((i >= 0) & (i < place_ref[1]), 1.0, 0.0) for i in near]
-    loads = [pltpu.make_async_copy(w_hbm.at[i], w_ref.at[i], sems.at[i]) for i in range(LEVELS + 2)]
-    for i in W_ORDER:
-        loads[i].start()
 
     lane_tiles = nch // LANES
 
@@ -220,10 +216,8 @@
     dot = functools.partial(jnp.dot, preferred_element_type=jnp.float32)
     for level in range(LEVELS):
         high, low = split(rows_ref[level].reshape(pixels, nch))
-        loads[level].wait()
         got = dot(high, w_ref[level]) + dot(low, w_ref[level])
         if level >= 2:
-            loads[level + 2].wait()
             got = got + dot(high, w_ref[level + 2])
         high, low = split(got * a_ref[level + 1])
         high = high.reshape(TILE, TILE, nch)
@@ -267,32 +261,30 @@
     return pltpu.with_memory_space_constraint(x, pltpu.VMEM)
 
 
-def wavelet_parts(place, coeff, tiles, own, nch, length):
-    w = jnp.asarray(channel_matrices(nch))
+def wavelet_parts(place, coeff, tiles, own, w, nch, length):
     k = jnp.asarray(scatter_matrices(length))
     smem = pl.BlockSpec(memory_space=pltpu.SMEM)
     vmem = pl.BlockSpec(memory_space=pltpu.VMEM)
     plain = pltpu.VMEM(tiles[-1].shape, jnp.float32)
     taller = pltpu.VMEM(tiles[0].shape, jnp.float32)
+    padded = pltpu.VMEM((TILE + 1,) + tiles[0].shape[1:], jnp.float32)
     pair = pltpu.VMEM((2 * TILE + 1,) + tiles[0].shape[1:], jnp.float32)
     return pl.pallas_call(
         wavelet_kernel,
-        out_shape=[plain, pair, taller, plain, pltpu.VMEM(own.shape, jnp.float32)],
-        in_specs=[smem] + [vmem] * 8 + [pl.BlockSpec(memory_space=pl.ANY)],
+        out_shape=[plain, pair, taller, padded, pltpu.VMEM(own.shape, jnp.float32)],
+        in_specs=[smem] + [vmem] * 9,
         out_specs=[vmem] * 5,
         scratch_shapes=[
             pltpu.VMEM((LEVELS, TILE, TILE, nch), jnp.float32),
             pltpu.VMEM((TILE, 10 * TILE, nch), jnp.bfloat16),
-            pltpu.VMEM(w.shape, jnp.bfloat16),
-            pltpu.SemaphoreType.DMA((LEVELS + 2,)),
         ],
         compiler_params=pltpu.CompilerParams(vmem_limit_bytes=VMEM_LIMIT),
         cost_estimate=pl.CostEstimate(flops=4_000_000_000, bytes_accessed=9_000_000, transcendentals=0),
         name="wavelet_parts",
-    )(place, *[kept(x) for x in (coeff, *tiles, k, own)], pltpu.with_memory_space_constraint(w, pltpu.HBM))
-
-
-def add_kernel(near_ref, swapped_ref, _, out_ref):
+    )(place, *[kept(x) for x in (coeff, *tiles, k, own, w)])
+
+
+def add_kernel(near_ref, swapped_ref, out_ref):
     def body(row, carry):
         out_ref[row] = near_ref[row] + swapped_ref[row + TILE]
         return carry
@@ -301,20 +293,22 @@
     out_ref[TILE] = near_ref[TILE]
 
 
-def outward(near, swapped, far):
+def outward(near, swapped):
     vmem = pl.BlockSpec(memory_space=pltpu.VMEM)
     return pl.pallas_call(
         add_kernel,
         out_shape=pltpu.VMEM(near.shape, jnp.float32),
-        in_specs=[vmem] * 2 + [pl.BlockSpec(memory_space=pl.ANY)],
+        in_specs=[vmem] * 2,
         out_specs=vmem,
         compiler_params=pltpu.CompilerParams(vmem_limit_bytes=VMEM_LIMIT),
         cost_estimate=pl.CostEstimate(flops=100_000, bytes_accessed=1_500_000, transcendentals=0),
         name="outward",
-    )(kept(near), kept(swapped), kept(far))
-
-
-def model_kernel(amp_ref, index_ref, spread_ref, model_ref, flat_ref, own_ref, scale_ref):
+    )(kept(near), kept(swapped))
+
+
+def model_kernel(amp_ref, index_ref, spread_ref, w_hbm, model_ref, flat_ref, own_ref, w_ref, scale_ref, sem):
+    load = pltpu.make_async_copy(w_hbm, w_ref, sem)
+    load.start()
     nch, pixels = model_ref.shape
     own_ref[...] = jnp.zeros_like(own_ref)
     for t in range(3):
@@ -341,9 +335,11 @@
         return carry
 
     lax.fori_loop(0, nch // 8, body, 0, unroll=2)
+    load.wait()
 
 
 def model_of(amplitude, centre_index, spread, nch):
+    w = jnp.asarray(channel_matrices(nch))
     vmem = pl.BlockSpec(memory_space=pltpu.VMEM)
     pixels = TILE * TILE
     return pl.pallas_call(
@@ -352,14 +348,15 @@
             pltpu.VMEM((nch, pixels), jnp.float32),
             pltpu.VMEM((3, COMPS, pixels), jnp.float32),
             pltpu.VMEM((3, COMPS, EXT), jnp.float32),
+            pltpu.VMEM(w.shape, w.dtype),
         ],
-        in_specs=[vmem] * 3,
-        out_specs=[vmem] * 3,
-        scratch_shapes=[pltpu.VMEM((COMPS, pixels), jnp.float32)],
+        in_specs=[vmem] * 3 + [pl.BlockSpec(memory_space=pl.ANY)],
+        out_specs=[vmem] * 4,
+        scratch_shapes=[pltpu.VMEM((COMPS, pixels), jnp.float32), pltpu.SemaphoreType.DMA],
         compiler_params=pltpu.CompilerParams(vmem_limit_bytes=VMEM_LIMIT),
         cost_estimate=pl.CostEstimate(flops=10_000_000, bytes_accessed=1_000_000, transcendentals=1_100_000),
         name="gaussian_model",
-    )(amplitude, centre_index, spread)
+    )(amplitude, centre_index, spread, pltpu.with_memory_space_constraint(w, pltpu.HBM))
 
 
 def step_kernel(
@@ -381,6 +378,8 @@
         copies.append(pltpu.make_async_copy(den_ref.at[at], den_hbm.at[at], sem.at[part]))
         copies[-1].start()
 
+    shape = (COMPS, rows, LANES)
+    own_lanes = lax.broadcasted_iota(jnp.int32, shape, 2) // TILE == lax.broadcasted_iota(jnp.int32, shape, 1)
     for part in range(parts):
         block = den_ref[part * rows : (part + 1) * rows].reshape(LANES, nch)
         at = slice(part * LANES, (part + 1) * LANES)
@@ -421,12 +420,13 @@
             jnp.concatenate(sums[2], axis=0) * (slope * inv * (1.0 / nch)),
         )
         for t in range(3):
-            step = STEPS[t] * grads[t]
-            for i in range(rows):
-                row = part * rows + i
-                lane = (row + 2) * PITCH + 2
-                base = bases[t][:, lane : lane + TILE]
-                fit_ref[t, :, row, :] = base - step[:, i * TILE : (i + 1) * TILE]
+            lanes = [(part * rows + i + 2) * PITCH + 2 for i in range(rows)]
+            base = jnp.concatenate([bases[t][:, lane : lane + TILE] for lane in lanes], axis=1)
+            new = base - STEPS[t] * grads[t]
+            spread_out = jnp.where(own_lanes, jnp.broadcast_to(new[:, None, :], own_lanes.shape), 0.0)
+            for shift in (LANES // 2, LANES // 4, LANES // 8):
+                spread_out = spread_out + pltpu.roll(spread_out, shift, 2)
+            fit_ref[t, :, part * rows : (part + 1) * rows, :] = spread_out[:, :, :TILE]
 
     for copy in copies:
         copy.wait()
@@ -470,15 +470,15 @@
     coeff = jnp.concatenate([weight, one]) - jnp.concatenate([0.0 * one, weight])
     scale = jnp.array([16.0 ** (-3 * j) for j in range(LEVELS + 1)], jnp.float32)
     coeff = (coeff * scale[:, None])[:, None, :]
-    model, flat, own = model_of(amplitude, centre_index, spread, nch)
+    model, flat, own, w = model_of(amplitude, centre_index, spread, nch)
 
     o_0, swap, near, far, ext = wavelet_parts(
-        place, coeff, (up1, down1, up2, down2, cube), own, nch, places[3] * TILE
+        place, coeff, (up1, down1, up2, down2, cube), own, w, nch, places[3] * TILE
     )
 
     swapped = lax.ppermute(swap, "skyx", [(i, i ^ 1) for i in range(places[3])])
     far = away(far, "skyx", 2)
-    near = away(outward(near, swapped, far), "skyx", 1)
+    near = away(outward(near, swapped), "skyx", 1)
     return gradient_step(place, (o_0, swapped, far, near), model, flat, ext)
 
 

time: 80.7 us -> 72.5 us (0.90)
  waiting for transfers between devices: 31.3 us -> 20.5 us
  local copies, waits for them, and re-layouts: 1.1 us -> 4.84 us
  starting transfers between devices: 32.7 us -> 31.3 us
  other arithmetic: 0.26 us -> 1.63 us
  Pallas kernels: 14.2 us -> 12.9 us
    ppermute x4, waiting for transfers between devices: 15.3 us -> 9.68 us  [sent(): return lax.ppermute(values, axis, pairs)]
    ppermute x2, waiting for transfers between devices: 16 us -> 10.8 us  [away(): lax.ppermute(values, axis, [(i, j) for i, j in pairs if 0 <= j < size])]
    unnamed x16 -> x10, local copies, waits for them, and re-layouts: 0.05 us -> 2.53 us
    slice x1, local copies, waits for them, and re-layouts: 1.04 us -> 2.3 us  [on_device(): cube[:-BEYOND]]
    ppermute x2, starting transfers between devices: 14.6 us -> 13.3 us  [away(): lax.ppermute(values, axis, [(i, j) for i, j in pairs if 0 <= j < size])]
    pallas_call x1, Pallas kernels: 5.18 us -> 4.16 us  [gradient_step(): pl.pallas_call(step_kernel, out_shape=[jax.ShapeDtypeStruct(shape, jnp.fl...]
    pallas_call x1, Pallas kernels: 6.27 us -> 5.45 us  [wavelet_parts(): pl.pallas_call(wavelet_kernel, out_shape=[plain, pair, taller, padded, pl...]
  transfers between devices with their start and end apart: 7 -> 7, of which waited for: 3 -> 3; matrix products, arithmetic and copies ran while one was open for 2% -> 5% of each run, Pallas kernels for 2% -> 3%
where the time goes in v4:
time: 72.5 us; the launch traced here: 71.9 us
  starting transfers between devices  31.3 us (43%)
  waiting for transfers between devices  20.5 us (28%)
  Pallas kernels  12.9 us (18%)
  local copies, waits for them, and re-layouts  4.84 us (7%)
  other arithmetic  1.63 us (2%)
  between operations  0.77 us (1%)
    ppermute x4, starting transfers between devices, sent(): return lax.ppermute(values, axis, pairs)  16.1 us
    ppermute x2, starting transfers between devices, away(): lax.ppermute(values, axis, [(i, j) for i, j in pairs if 0 <= j < size])  13.3 us
    ppermute x2, waiting for transfers between devices, away(): lax.ppermute(values, axis, [(i, j) for i, j in pairs if 0 <= j < size])  10.8 us
    ppermute x4, waiting for transfers between devices, sent(): return lax.ppermute(values, axis, pairs)  9.68 us
    pallas_call x1, Pallas kernels, wavelet_parts(): pl.pallas_call(wavelet_kernel, out_shape=[plain, pair, taller, padded, pl...  5.45 us
    pallas_call x1, Pallas kernels, gradient_step(): pl.pallas_call(step_kernel, out_shape=[jax.ShapeDtypeStruct(shape, jnp.fl...  4.16 us
    unnamed x10, local copies, waits for them, and re-layouts  2.53 us
    slice x1, local copies, waits for them, and re-layouts, on_device(): cube[:-BEYOND]  2.3 us
  transfers between devices with their start and end apart: 7, of which 3 were waited for; matrix products, arithmetic and copies ran while one was open for 5% of the time, Pallas kernels for 3%

profile of v4, /device:TPU:26, one launch (start us, length us, event | category | flops | bytes accessed | tf_op | source)
XLA Modules:
  0.0 71.9 jit_solution(13820092684082164272)
XLA Ops:
  0.6 0.0 copy-start.4
  0.6 0.0 copy-start
  0.7 1.3 %pack.1 = (f32[17,16,512]{2,1,0:T(8,128)S(1)}, f32[17,16,512]{2,1,0:T(8,128)S(1)}) custom-call(f32[16,16,512]{2,1,0:T(8,128)} %x_ref.3, f32[8,16,16]{2,1,0:T(8,128)} %amp_ref.3, s32[8,16,16]{2,1,0:T(8,128)} %index_ref.3, f32[8,16,16]{2,1,0:T(8,128)} %spread_ref.3), custom_call_target="tpu_custom_call" | custom-call | flops 1000 | bytes 1000000 | tf_op jit(solution)/shard_map/pack/pallas_call | solution.py:114
  2.0 4.0 %collective-permute-start = (f32[17,16,512]{2,1,0:T(8,128)S(1)}, f32[17,16,512]{2,1,0:T(8,128)S(1)}, u32[]{:S(2)}, u32[]{:S(2)}) collective-permute-start(f32[17,16,512]{2,1,0:T(8,128)S(1)} %get-tuple-element.13), channel_id=1, source_target_pairs={{0,32},{32,64},{64,96},{96,128},{128,160},{160,192},{192,224},{224... | collective-permute-start | bytes 1671176 | tf_op jit(solution)/shard_map/ppermute | solution.py:81
  6.0 4.2 %collective-permute-start.1 = (f32[17,16,512]{2,1,0:T(8,128)S(1)}, f32[17,16,512]{2,1,0:T(8,128)S(1)}, u32[]{:S(2)}, u32[]{:S(2)}) collective-permute-start(f32[17,16,512]{2,1,0:T(8,128)S(1)} %get-tuple-element.14), channel_id=1, source_target_pairs={{32,0},{64,32},{96,64},{128,96},{160,128},{192,160},{224,192},{256... | collective-permute-start | bytes 1671176 | tf_op jit(solution)/shard_map/ppermute | solution.py:81
  10.2 2.3 %fusion = (f32[14,16,512]{2,1,0:T(8,128)}, f32[14,16,512]{2,1,0:T(8,128)}) fusion(f32[16,16,512]{2,1,0:T(8,128)} %x_ref.3), kind=kLoop, calls=%fused_computation.4 | loop fusion | bytes 1835008 | tf_op jit(solution)/shard_map/slice | solution.py:464
  12.5 2.3 %collective-permute-start.3 = (f32[14,16,512]{2,1,0:T(8,128)}, f32[14,16,512]{2,1,0:T(8,128)S(1)}, u32[]{:S(2)}, u32[]{:S(2)}) collective-permute-start(f32[14,16,512]{2,1,0:T(8,128)} %get-tuple-element.24), channel_id=1, source_target_pairs={{64,0},{96,32},{128,64},{160,96},{192,128},{224,160},{256,192},{28... | collective-permute-start | bytes 1376264 | tf_op jit(solution)/shard_map/ppermute | solution.py:81
  14.9 5.5 %collective-permute-start.2 = (f32[14,16,512]{2,1,0:T(8,128)}, f32[14,16,512]{2,1,0:T(8,128)}, u32[]{:S(2)}, u32[]{:S(2)}) collective-permute-start(f32[14,16,512]{2,1,0:T(8,128)} %get-tuple-element.25), channel_id=1, source_target_pairs={{0,64},{32,96},{64,128},{96,160},{128,192},{160,224},{192,256},{22... | collective-permute-start | bytes 1376264 | tf_op jit(solution)/shard_map/ppermute | solution.py:81
  20.4 0.8 %select_reduce_fusion = f32[4,512]{1,0:T(4,128)S(1)} fusion(f32[16]{0:T(128)} %param.10, s32[4,512]{1,0:T(4,128)} %param.11), kind=kLoop, calls=%fused_computation | loop fusion | flops 96256 | bytes 16448 | tf_op jit(solution)/shard_map/reduce_sum | solution.py:468
  21.2 0.7 %subtract_multiply_fusion = f32[5,512]{1,0:T(8,128)S(1)} fusion(f32[4,512]{1,0:T(4,128)S(1)} %select_reduce_fusion, f32[5]{0:T(128)} %constant.25.clone), kind=kLoop, calls=%fused_computation.2 | loop fusion | flops 5120 | bytes 18452 | tf_op jit(solution)/shard_map/mul | solution.py:472
  21.9 0.8 %copy-done.1 = f32[8,16,16]{2,1,0:T(8,128)S(1)} copy-done((f32[8,16,16]{2,1,0:T(8,128)S(1)}, f32[8,16,16]{2,1,0:T(8,128)}, u32[]{:S(2)}) %copy-start.1) | copy-done | bytes 8216
  22.8 0.8 %copy-done.2 = s32[8,16,16]{2,1,0:T(8,128)S(1)} copy-done((s32[8,16,16]{2,1,0:T(8,128)S(1)}, s32[8,16,16]{2,1,0:T(8,128)}, u32[]{:S(2)}) %copy-start.2) | copy-done | bytes 8216
  23.6 0.8 %copy-done.3 = f32[8,16,16]{2,1,0:T(8,128)S(1)} copy-done((f32[8,16,16]{2,1,0:T(8,128)S(1)}, f32[8,16,16]{2,1,0:T(8,128)}, u32[]{:S(2)}) %copy-start.3) | copy-done | bytes 8216
  24.4 1.9 %gaussian_model.1 = (f32[512,256]{1,0:T(8,128)S(1)}, f32[3,8,256]{2,1,0:T(8,128)S(1)}, f32[3,8,640]{2,1,0:T(8,128)S(1)}, bf16[6,512,512]{2,1,0:T(8,128)(2,1)S(1)}) custom-call(f32[8,16,16]{2,1,0:T(8,128)S(1)} %copy-done.1, s32[8,16,16]{2,1,0:T(8,128)S(1)} %copy-done.2, f32[8,16,16]{2,1,0:T(8,128)S(1)} %copy-done.3, bf16[6,512,512]{2,1,0:T(8,128)(2,1)} %constant.26.clone.w_hbm), custom_call_target="tpu_custom_call" | custom-call | flops 10000000 | bytes 1000000 | tf_op jit(solution)/shard_map/gaussian_model/pallas_call | solution.py:345
  26.4 0.1 pad_add_fusion.place_ref
  26.5 9.7 %collective-permute-done.3.p2 = f32[14,16,512]{2,1,0:T(8,128)S(1)} collective-permute-done((f32[14,16,512]{2,1,0:T(8,128)}, f32[14,16,512]{2,1,0:T(8,128)S(1)}, u32[]{:S(2)}, u32[]{:S(2)}) %collective-permute-start.3) | collective-permute-done | bytes 458784 | tf_op jit(solution)/shard_map/ppermute | solution.py:81
  36.2 5.4 %wavelet_parts.1 = (f32[16,16,512]{2,1,0:T(8,128)S(1)}, f32[33,16,512]{2,1,0:T(8,128)S(1)}, f32[17,16,512]{2,1,0:T(8,128)S(1)}, f32[17,16,512]{2,1,0:T(8,128)S(1)}, f32[3,8,640]{2,1,0:T(8,128)S(1)}) custom-call(s32[4]{0:T(128)S(1)} %pad_add_fusion.place_ref, f32[5,1,512]{2,1,0:T(1,128)S(1)} %broadcast_in_dim.2.a_ref, ...), custom_call_target="tpu_custom_call" | custom-call | flops 4000000000 | bytes 9000000 | tf_op jit(solution)/shard_map/wavelet_parts/pallas_call | solution.py:272
  41.6 1.9 %collective-permute-start.4 = (f32[33,16,512]{2,1,0:T(8,128)S(1)}, f32[33,16,512]{2,1,0:T(8,128)S(1)}, u32[]{:S(2)}, u32[]{:S(2)}) collective-permute-start(f32[33,16,512]{2,1,0:T(8,128)S(1)} %get-tuple-element.18), channel_id=1, source_target_pairs={{0,1},{1,0},{2,3},{3,2},{4,5},{5,4},{6,7},{7,6},{8,9},{9,8},{10,11... | collective-permute-start | bytes 3244040 | tf_op jit(solution)/shard_map/ppermute | solution.py:479
  43.5 10.9 %collective-permute-start.5 = (f32[17,16,512]{2,1,0:T(8,128)S(1)}, f32[17,16,512]{2,1,0:T(8,128)S(1)}, u32[]{:S(2)}, u32[]{:S(2)}) collective-permute-start(f32[17,16,512]{2,1,0:T(8,128)S(1)} %get-tuple-element.19), channel_id=1, source_target_pairs={{1,3},{2,0},{3,5},{4,2},{5,7},{6,4},{7,9},{8,6},{9,11},{10,8},{11,... | collective-permute-start | bytes 1671176 | tf_op jit(solution)/shard_map/ppermute | solution.py:87
  54.5 0.1 outward.1
  54.6 2.4 %collective-permute-start.6 = (f32[17,16,512]{2,1,0:T(8,128)S(1)}, f32[17,16,512]{2,1,0:T(8,128)S(1)}, u32[]{:S(2)}, u32[]{:S(2)}) collective-permute-start(f32[17,16,512]{2,1,0:T(8,128)S(1)} %outward.1), channel_id=1, source_target_pairs={{1,2},{2,1},{3,4},{4,3},{5,6},{6,5},{7,8},{8,7},{9,10},{10,9},{11,... | collective-permute-start | bytes 1671176 | tf_op jit(solution)/shard_map/ppermute | solution.py:87
  57.0 4.5 %collective-permute-done.5.far_ref = f32[17,16,512]{2,1,0:T(8,128)S(1)} collective-permute-done((f32[17,16,512]{2,1,0:T(8,128)S(1)}, f32[17,16,512]{2,1,0:T(8,128)S(1)}, u32[]{:S(2)}, u32[]{:S(2)}) %collective-permute-start.5) | collective-permute-done | bytes 557088 | tf_op jit(solution)/shard_map/ppermute | solution.py:87
  61.5 6.2 %collective-permute-done.6.near_ref = f32[17,16,512]{2,1,0:T(8,128)S(1)} collective-permute-done((f32[17,16,512]{2,1,0:T(8,128)S(1)}, f32[17,16,512]{2,1,0:T(8,128)S(1)}, u32[]{:S(2)}, u32[]{:S(2)}) %collective-permute-start.6) | collective-permute-done | bytes 557088 | tf_op jit(solution)/shard_map/ppermute | solution.py:87
  67.7 4.2 %gradient_step.1 = (f32[16,16,512]{2,1,0:T(8,128)}, f32[3,8,16,16]{3,2,1,0:T(8,128)}) custom-call(s32[4]{0:T(128)S(1)} %pad_add_fusion.place_ref, f32[16,16,512]{2,1,0:T(8,128)S(1)} %get-tuple-element.17.o_0, f32[33,16,512]{2,1,0:T(8,128)S(1)} %collective-permute-done.4.swapped_ref, f32[17,16,512]{2,1,0:T(8,128)S(1)} %collective-permute-done.5.far_ref, ...), custom_call_target="tpu_custom_call" | custom-call | flops 15000000 | bytes 4000000 | tf_op jit(solution)/shard_map/gradient_step/pallas_call | solution.py:438
  (10 shorter events, 0.0 us)
Async XLA Ops:
  0.6 35.5 %copy-start.4 = (bf16[6,80,160]{2,1,0:T(8,128)(2,1)S(1)}, bf16[6,80,160]{2,1,0:T(8,128)(2,1)}, u32[]{:S(2)}) copy-start(bf16[6,80,160]{2,1,0:T(8,128)(2,1)} %constant.27.clone.k_ref) | copy-start | bytes 460804
  0.6 35.5 %copy-start = (f32[16,16,512]{2,1,0:T(8,128)S(1)}, f32[16,16,512]{2,1,0:T(8,128)}, u32[]{:S(2)}) copy-start(f32[16,16,512]{2,1,0:T(8,128)} %x_ref.3) | copy-start | bytes 1572868
  2.0 34.2 %collective-permute-start = (f32[17,16,512]{2,1,0:T(8,128)S(1)}, f32[17,16,512]{2,1,0:T(8,128)S(1)}, u32[]{:S(2)}, u32[]{:S(2)}) collective-permute-start(f32[17,16,512]{2,1,0:T(8,128)S(1)} %get-tuple-element.13), channel_id=1, source_target_pairs={{0,32},{32,64},{64,96},{96,128},{128,160},{160,192},{192,224},{224... | collective-permute-start | bytes 1671176 | tf_op jit(solution)/shard_map/ppermute | solution.py:81
  6.0 30.1 %collective-permute-start.1 = (f32[17,16,512]{2,1,0:T(8,128)S(1)}, f32[17,16,512]{2,1,0:T(8,128)S(1)}, u32[]{:S(2)}, u32[]{:S(2)}) collective-permute-start(f32[17,16,512]{2,1,0:T(8,128)S(1)} %get-tuple-element.14), channel_id=1, source_target_pairs={{32,0},{64,32},{96,64},{128,96},{160,128},{192,160},{224,192},{256... | collective-permute-start | bytes 1671176 | tf_op jit(solution)/shard_map/ppermute | solution.py:81
  12.5 23.6 %collective-permute-start.3 = (f32[14,16,512]{2,1,0:T(8,128)}, f32[14,16,512]{2,1,0:T(8,128)S(1)}, u32[]{:S(2)}, u32[]{:S(2)}) collective-permute-start(f32[14,16,512]{2,1,0:T(8,128)} %get-tuple-element.24), channel_id=1, source_target_pairs={{64,0},{96,32},{128,64},{160,96},{192,128},{224,160},{256,192},{28... | collective-permute-start | bytes 1376264 | tf_op jit(solution)/shard_map/ppermute | solution.py:81
  14.9 21.3 %collective-permute-start.2 = (f32[14,16,512]{2,1,0:T(8,128)}, f32[14,16,512]{2,1,0:T(8,128)}, u32[]{:S(2)}, u32[]{:S(2)}) collective-permute-start(f32[14,16,512]{2,1,0:T(8,128)} %get-tuple-element.25), channel_id=1, source_target_pairs={{0,64},{32,96},{64,128},{96,160},{128,192},{160,224},{192,256},{22... | collective-permute-start | bytes 1376264 | tf_op jit(solution)/shard_map/ppermute | solution.py:81
  21.9 0.8 %copy-start.1 = (f32[8,16,16]{2,1,0:T(8,128)S(1)}, f32[8,16,16]{2,1,0:T(8,128)}, u32[]{:S(2)}) copy-start(f32[8,16,16]{2,1,0:T(8,128)} %amp_ref.3) | copy-start | bytes 24580
  22.8 0.8 %copy-start.2 = (s32[8,16,16]{2,1,0:T(8,128)S(1)}, s32[8,16,16]{2,1,0:T(8,128)}, u32[]{:S(2)}) copy-start(s32[8,16,16]{2,1,0:T(8,128)} %index_ref.3) | copy-start | bytes 24580
  23.6 0.8 %copy-start.3 = (f32[8,16,16]{2,1,0:T(8,128)S(1)}, f32[8,16,16]{2,1,0:T(8,128)}, u32[]{:S(2)}) copy-start(f32[8,16,16]{2,1,0:T(8,128)} %spread_ref.3) | copy-start | bytes 24580
  41.6 12.9 %collective-permute-start.4 = (f32[33,16,512]{2,1,0:T(8,128)S(1)}, f32[33,16,512]{2,1,0:T(8,128)S(1)}, u32[]{:S(2)}, u32[]{:S(2)}) collective-permute-start(f32[33,16,512]{2,1,0:T(8,128)S(1)} %get-tuple-element.18), channel_id=1, source_target_pairs={{0,1},{1,0},{2,3},{3,2},{4,5},{5,4},{6,7},{7,6},{8,9},{9,8},{10,11... | collective-permute-start | bytes 3244040 | tf_op jit(solution)/shard_map/ppermute | solution.py:479
  43.5 18.0 %collective-permute-start.5 = (f32[17,16,512]{2,1,0:T(8,128)S(1)}, f32[17,16,512]{2,1,0:T(8,128)S(1)}, u32[]{:S(2)}, u32[]{:S(2)}) collective-permute-start(f32[17,16,512]{2,1,0:T(8,128)S(1)} %get-tuple-element.19), channel_id=1, source_target_pairs={{1,3},{2,0},{3,5},{4,2},{5,7},{6,4},{7,9},{8,6},{9,11},{10,8},{11,... | collective-permute-start | bytes 1671176 | tf_op jit(solution)/shard_map/ppermute | solution.py:87
  54.6 13.2 %collective-permute-start.6 = (f32[17,16,512]{2,1,0:T(8,128)S(1)}, f32[17,16,512]{2,1,0:T(8,128)S(1)}, u32[]{:S(2)}, u32[]{:S(2)}) collective-permute-start(f32[17,16,512]{2,1,0:T(8,128)S(1)} %outward.1), channel_id=1, source_target_pairs={{1,2},{2,1},{3,4},{4,3},{5,6},{6,5},{7,8},{8,7},{9,10},{10,9},{11,... | collective-permute-start | bytes 1671176 | tf_op jit(solution)/shard_map/ppermute | solution.py:87

commit v5 on v4

--- a/solution.py
+++ b/solution.py
@@ -17,8 +17,8 @@
 BEYOND = 2
 VMEM_LIMIT = 20 * 1024 * 1024
 ROLES = ((2, 3, 4, 1, 0), (2, 1, 0, 3, 4))
-PITCH = 32
-EXT = 20 * PITCH
+PITCH = 24
+EXT = 512
 STEPS = (0.5, 0.002, 2.0)
 LAMS = (0.2, 0.5, 0.05)
 
@@ -95,33 +95,6 @@
     return spread_ref[:, row, :]
 
 
-def pack_kernel(x_ref, amp_ref, index_ref, spread_ref, up_ref, down_ref):
-    nch = x_ref.shape[2]
-    for out, first in ((up_ref, TILE - 2), (down_ref, 0)):
-        for row in range(TILE):
-            out[row] = x_ref[row]
-        out[TILE] = jnp.zeros((TILE, nch), jnp.float32)
-        for t in range(3):
-            for r in range(2):
-                lane = (2 * t + r) * TILE
-                got = own_row(t, first + r, amp_ref, index_ref, spread_ref, nch)
-                out[TILE, 0:COMPS, lane : lane + TILE] = got
-
-
-def packed(cube, amplitude, centre_index, spread):
-    vmem = pl.BlockSpec(memory_space=pltpu.VMEM)
-    shape = (TILE + 1,) + cube.shape[1:]
-    return pl.pallas_call(
-        pack_kernel,
-        out_shape=[pltpu.VMEM(shape, jnp.float32)] * 2,
-        in_specs=[vmem] * 4,
-        out_specs=[vmem] * 2,
-        compiler_params=pltpu.CompilerParams(vmem_limit_bytes=VMEM_LIMIT),
-        cost_estimate=pl.CostEstimate(flops=1000, bytes_accessed=1_000_000, transcendentals=0),
-        name="pack",
-    )(*[pltpu.with_memory_space_constraint(v, pltpu.HBM) for v in (cube, amplitude, centre_index, spread)])
-
-
 def border_columns(ext_ref, shift):
     lane = lax.broadcasted_iota(jnp.int32, (COMPS, EXT), 1) % PITCH
     total = jnp.zeros((COMPS, EXT), jnp.float32)
@@ -131,16 +104,31 @@
     return total
 
 
-def put_plane(out, index, lanes):
-    nch = out.shape[2]
-    out[index] = jnp.zeros((TILE, nch), jnp.float32)
-    out[index, 0:COMPS, :] = lanes[:, :nch]
-    out[index, COMPS:, 0 : EXT - nch] = lanes[:, nch:]
-
-
-def from_plane(ref, index):
-    nch = ref.shape[2]
-    return jnp.concatenate([ref[index, 0:COMPS, :], ref[index, COMPS:, 0 : EXT - nch]], axis=1)
+def border_rows(rows, first):
+    lane = lax.broadcasted_iota(jnp.int32, (COMPS, EXT), 1)
+    total = jnp.zeros((COMPS, EXT), jnp.float32)
+    for t in range(3):
+        moved = pltpu.roll(rows[t], ((2 * t - first) * PITCH) % EXT, 1)
+        total = jnp.where((lane >= 2 * t * PITCH) & (lane < (2 * t + 2) * PITCH), moved, total)
+    return total
+
+
+def with_columns(own, left, right):
+    column = lax.broadcasted_iota(jnp.int32, (COMPS, EXT), 1) % PITCH
+    out = []
+    for t in range(3):
+        p = jnp.where(column < 2, pltpu.roll(left, (EXT - 2 * t) % EXT, 1), own[t])
+        out.append(jnp.where(column >= TILE + 2, pltpu.roll(right, (TILE + 2 - 2 * t) % EXT, 1), p))
+    return out
+
+
+def with_rows(own, above, below):
+    row = lax.broadcasted_iota(jnp.int32, (COMPS, EXT), 1) // PITCH
+    out = []
+    for t in range(3):
+        p = jnp.where(row < 2, pltpu.roll(above, (EXT - 2 * t * PITCH) % EXT, 1), own[t])
+        out.append(jnp.where(row >= TILE + 2, pltpu.roll(below, ((TILE + 2 - 2 * t) * PITCH) % EXT, 1), p))
+    return out
 
 
 def stencil(p):
@@ -148,22 +136,40 @@
     return 4.0 * p - (near + (pltpu.roll(p, PITCH, 1) + pltpu.roll(p, EXT - PITCH, 1)))
 
 
-def smoothed(ext_ref, left, right, place_ref):
+def smoothed(params):
     lane = lax.broadcasted_iota(jnp.int32, (COMPS, EXT), 1)
-    row, column = lane // PITCH, lane % PITCH
-    y = row + (place_ref[0] * TILE - 2)
-    x = column + (place_ref[2] * TILE - 2)
-    on_sky = (y >= 0) & (y < place_ref[1] * TILE) & (x >= 0) & (x < place_ref[3] * TILE)
+    y = lane // PITCH + (lax.axis_index("skyy") * TILE - 2)
+    x = lane % PITCH + (lax.axis_index("skyx") * TILE - 2)
+    ny, nx = lax.axis_size("skyy") * TILE, lax.axis_size("skyx") * TILE
+    on_sky = (y >= 0) & (y < ny) & (x >= 0) & (x < nx)
     out = []
-    for t in range(3):
-        p = ext_ref[t]
-        p = jnp.where(column < 2, pltpu.roll(left, (EXT - 2 * t) % EXT, 1), p)
-        p = jnp.where(column >= TILE + 2, pltpu.roll(right, (TILE + 2 - 2 * t) % EXT, 1), p)
+    for t, p in enumerate(params):
         first = jnp.where(on_sky, stencil(p), 0.0)
         out.append(p - (STEPS[t] * LAMS[t]) * stencil(first))
     return out
 
 
+def base_kernel(ext_ref, above_ref, below_ref, base_ref):
+    params = smoothed(with_rows(ext_ref, above_ref[...], below_ref[...]))
+    for t in range(3):
+        for row in range(TILE):
+            lane = (row + 2) * PITCH + 2
+            base_ref[t, :, row * TILE : (row + 1) * TILE] = params[t][:, lane : lane + TILE]
+
+
+def base_of(ext, above, below):
+    vmem = pl.BlockSpec(memory_space=pltpu.VMEM)
+    return pl.pallas_call(
+        base_kernel,
+        out_shape=pltpu.VMEM((3, COMPS, TILE * TILE), jnp.float32),
+        in_specs=[vmem] * 3,
+        out_specs=vmem,
+        compiler_params=pltpu.CompilerParams(vmem_limit_bytes=VMEM_LIMIT),
+        cost_estimate=pl.CostEstimate(flops=200_000, bytes_accessed=100_000, transcendentals=0),
+        name="smoothed_base",
+    )(*[kept(x) for x in (ext, above, below)])
+
+
 def five(v, flag=None):
     total = (v[0] + v[4]) + 4.0 * (v[1] + v[3]) + 6.0 * v[2]
     return total if flag is None else total * flag
@@ -175,13 +181,14 @@
 
 
 def wavelet_kernel(
-    place_ref, a_ref, m1, p1, m2, p2, x_ref, k_ref, own_ref, w_ref,
-    o_0, swap_ref, near_ref, far_ref, ext_ref, rows_ref, y_ref,
+    a_ref, m1, p1, m2, p2, x_ref, k_ref, own_ref, inner_ref, outer_ref, w_ref,
+    o_0, swap_ref, near_ref, far_ref, ext_ref, up_ref, down_ref, rows_ref, y_ref,
 ):
     nch = x_ref.shape[2]
     tiles = (m2, m1, x_ref, p1, p2)
-    near = [place_ref[0] + i for i in (-2, -1, 0, 1, 2)]
-    flags = [jnp.where((i >= 0) & (i < place_ref[1]), 1.0, 0.0) for i in near]
+    iy, ix = lax.axis_index("skyy"), lax.axis_index("skyx")
+    near = [iy + i for i in (-2, -1, 0, 1, 2)]
+    flags = [jnp.where((i >= 0) & (i < lax.axis_size("skyy")), 1.0, 0.0) for i in near]
 
     lane_tiles = nch // LANES
 
@@ -228,8 +235,8 @@
             at = (level + 6) * TILE
             y_ref[:, at : at + TILE] = high
 
-    kind = jnp.where(place_ref[2] == 0, 0, jnp.where(place_ref[2] == place_ref[3] - 1, 2, 1))
-    odd = place_ref[2] % 2
+    kind = jnp.where(ix == 0, 0, jnp.where(ix == lax.axis_size("skyx") - 1, 2, 1))
+    odd = lax.rem(ix, 2)
     columns = k_ref[2 * kind + odd]
 
     def column_pass(row, carry):
@@ -243,37 +250,30 @@
 
     lax.fori_loop(0, TILE, column_pass, 0, unroll=4)
 
-    ext_ref[...] = own_ref[...]
-    for t in range(3):
-        for r in range(2):
-            lane = (2 * t + r) * TILE
-            at = r * PITCH + 2
-            ext_ref[t, :, at : at + TILE] = m1[TILE, 0:COMPS, lane : lane + TILE]
-            at = (TILE + 2 + r) * PITCH + 2
-            ext_ref[t, :, at : at + TILE] = p1[TILE, 0:COMPS, lane : lane + TILE]
-    to_right = border_columns(ext_ref, TILE)
-    to_left = border_columns(ext_ref, 2)
-    put_plane(swap_ref, 2 * TILE, jnp.where(odd == 0, to_right, to_left))
-    put_plane(near_ref, TILE, jnp.where(odd == 0, to_left, to_right))
+    inner, outer = inner_ref[...], outer_ref[...]
+    left, right = jnp.where(odd == 0, outer, inner), jnp.where(odd == 0, inner, outer)
+    params = with_columns(own_ref, left, right)
+    for t in range(3):
+        ext_ref[t] = params[t]
+    up_ref[...] = border_rows(params, 2)
+    down_ref[...] = border_rows(params, TILE)
 
 
 def kept(x):
     return pltpu.with_memory_space_constraint(x, pltpu.VMEM)
 
 
-def wavelet_parts(place, coeff, tiles, own, w, nch, length):
+def wavelet_parts(coeff, tiles, own, sides, w, nch, length):
     k = jnp.asarray(scatter_matrices(length))
-    smem = pl.BlockSpec(memory_space=pltpu.SMEM)
     vmem = pl.BlockSpec(memory_space=pltpu.VMEM)
     plain = pltpu.VMEM(tiles[-1].shape, jnp.float32)
-    taller = pltpu.VMEM(tiles[0].shape, jnp.float32)
-    padded = pltpu.VMEM((TILE + 1,) + tiles[0].shape[1:], jnp.float32)
-    pair = pltpu.VMEM((2 * TILE + 1,) + tiles[0].shape[1:], jnp.float32)
+    pair = pltpu.VMEM((2 * TILE,) + tiles[0].shape[1:], jnp.float32)
+    rows = pltpu.VMEM((COMPS, EXT), jnp.float32)
     return pl.pallas_call(
         wavelet_kernel,
-        out_shape=[plain, pair, taller, padded, pltpu.VMEM(own.shape, jnp.float32)],
-        in_specs=[smem] + [vmem] * 9,
-        out_specs=[vmem] * 5,
+        out_shape=[plain, pair, plain, plain, pltpu.VMEM(own.shape, jnp.float32), rows, rows],
+        in_specs=[vmem] * 11,
+        out_specs=[vmem] * 7,
         scratch_shapes=[
             pltpu.VMEM((LEVELS, TILE, TILE, nch), jnp.float32),
             pltpu.VMEM((TILE, 10 * TILE, nch), jnp.bfloat16),
@@ -281,7 +281,7 @@
         compiler_params=pltpu.CompilerParams(vmem_limit_bytes=VMEM_LIMIT),
         cost_estimate=pl.CostEstimate(flops=4_000_000_000, bytes_accessed=9_000_000, transcendentals=0),
         name="wavelet_parts",
-    )(place, *[kept(x) for x in (coeff, *tiles, k, own, w)])
+    )(*[kept(x) for x in (coeff, *tiles, k, own, *sides, w)])
 
 
 def add_kernel(near_ref, swapped_ref, out_ref):
@@ -290,7 +290,6 @@
         return carry
 
     lax.fori_loop(0, TILE, body, 0, unroll=4)
-    out_ref[TILE] = near_ref[TILE]
 
 
 def outward(near, swapped):
@@ -306,7 +305,7 @@
     )(kept(near), kept(swapped))
 
 
-def model_kernel(amp_ref, index_ref, spread_ref, w_hbm, model_ref, flat_ref, own_ref, w_ref, scale_ref, sem):
+def model_kernel(amp_ref, index_ref, spread_ref, w_hbm, model_ref, flat_ref, own_ref, inner_ref, outer_ref, w_ref, scale_ref, sem):
     load = pltpu.make_async_copy(w_hbm, w_ref, sem)
     load.start()
     nch, pixels = model_ref.shape
@@ -317,6 +316,10 @@
             at = (row + 2) * PITCH + 2
             own_ref[t, :, at : at + TILE] = got
             flat_ref[t, :, row * TILE : (row + 1) * TILE] = got
+    even = lax.rem(lax.axis_index("skyx"), 2) == 0
+    to_right, to_left = border_columns(own_ref, TILE), border_columns(own_ref, 2)
+    inner_ref[...] = jnp.where(even, to_right, to_left)
+    outer_ref[...] = jnp.where(even, to_left, to_right)
     mu = flat_ref[1] * float(nch)
     inv = 1.0 / flat_ref[2]
     flat_ref[1] = mu
@@ -348,10 +351,12 @@
             pltpu.VMEM((nch, pixels), jnp.float32),
             pltpu.VMEM((3, COMPS, pixels), jnp.float32),
             pltpu.VMEM((3, COMPS, EXT), jnp.float32),
+            pltpu.VMEM((COMPS, EXT), jnp.float32),
+            pltpu.VMEM((COMPS, EXT), jnp.float32),
             pltpu.VMEM(w.shape, w.dtype),
         ],
         in_specs=[vmem] * 3 + [pl.BlockSpec(memory_space=pl.ANY)],
-        out_specs=[vmem] * 4,
+        out_specs=[vmem] * 6,
         scratch_shapes=[pltpu.VMEM((COMPS, pixels), jnp.float32), pltpu.SemaphoreType.DMA],
         compiler_params=pltpu.CompilerParams(vmem_limit_bytes=VMEM_LIMIT),
         cost_estimate=pl.CostEstimate(flops=10_000_000, bytes_accessed=1_000_000, transcendentals=1_100_000),
@@ -360,17 +365,13 @@
 
 
 def step_kernel(
-    place_ref, o_0, swapped_ref, far_ref, near_ref, model_ref, flat_ref, ext_ref,
+    o_0, swapped_ref, far_ref, near_ref, model_ref, flat_ref, base_ref,
     den_hbm, fit_ref, den_ref, r_ref, sem,
 ):
     nch, pixels = model_ref.shape
     rows = LANES // TILE
     parts = pixels // LANES
     copies = []
-    even = place_ref[2] % 2 == 0
-    inner, outer = from_plane(swapped_ref, 2 * TILE), from_plane(near_ref, TILE)
-    left, right = jnp.where(even, outer, inner), jnp.where(even, inner, outer)
-    bases = smoothed(ext_ref, left, right, place_ref)
     for part in range(parts):
         at = slice(part * rows, (part + 1) * rows)
         for row in range(part * rows, (part + 1) * rows):
@@ -420,9 +421,7 @@
             jnp.concatenate(sums[2], axis=0) * (slope * inv * (1.0 / nch)),
         )
         for t in range(3):
-            lanes = [(part * rows + i + 2) * PITCH + 2 for i in range(rows)]
-            base = jnp.concatenate([bases[t][:, lane : lane + TILE] for lane in lanes], axis=1)
-            new = base - STEPS[t] * grads[t]
+            new = base_ref[t, :, at] - STEPS[t] * grads[t]
             spread_out = jnp.where(own_lanes, jnp.broadcast_to(new[:, None, :], own_lanes.shape), 0.0)
             for shift in (LANES // 2, LANES // 4, LANES // 8):
                 spread_out = spread_out + pltpu.roll(spread_out, shift, 2)
@@ -432,7 +431,7 @@
         copy.wait()
 
 
-def gradient_step(place, parts, model, flat, ext):
+def gradient_step(parts, model, flat, base):
     vmem = pl.BlockSpec(memory_space=pltpu.VMEM)
     shape = parts[0].shape
     return pl.pallas_call(
@@ -441,7 +440,7 @@
             jax.ShapeDtypeStruct(shape, jnp.float32),
             jax.ShapeDtypeStruct((3, COMPS, TILE, TILE), jnp.float32),
         ],
-        in_specs=[pl.BlockSpec(memory_space=pltpu.SMEM)] + [vmem] * 7,
+        in_specs=[vmem] * 7,
         out_specs=[pl.BlockSpec(memory_space=pl.ANY), vmem],
         scratch_shapes=[
             pltpu.VMEM(shape, jnp.float32),
@@ -451,16 +450,15 @@
         compiler_params=pltpu.CompilerParams(vmem_limit_bytes=VMEM_LIMIT),
         cost_estimate=pl.CostEstimate(flops=15_000_000, bytes_accessed=4_000_000, transcendentals=1_100_000),
         name="gradient_step",
-    )(place, *[kept(x) for x in (*parts, model, flat, ext)])
+    )(*[kept(x) for x in (*parts, model, flat, base)])
 
 
 def on_device(cube, level_table, level_index, amplitude, centre_index, spread):
     nch = cube.shape[2]
-    places = [f(axis) for axis in ("skyy", "skyx") for f in (lax.axis_index, lax.axis_size)]
-    place = jnp.stack([jnp.asarray(p, jnp.int32) for p in places])
-
-    for_down, for_up = packed(cube, amplitude, centre_index, spread)
-    up1, down1 = sent(for_down, "skyy", 1), sent(for_up, "skyy", -1)
+    size = lax.axis_size("skyx")
+    partner = [(i, i ^ 1) for i in range(size)]
+
+    up1, down1 = sent(cube, "skyy", 1), sent(cube, "skyy", -1)
     up2, down2 = sent(cube[BEYOND:], "skyy", 2), sent(cube[:-BEYOND], "skyy", -2)
 
     entries = jnp.arange(level_table.shape[0], dtype=jnp.int32)
@@ -470,16 +468,17 @@
     coeff = jnp.concatenate([weight, one]) - jnp.concatenate([0.0 * one, weight])
     scale = jnp.array([16.0 ** (-3 * j) for j in range(LEVELS + 1)], jnp.float32)
     coeff = (coeff * scale[:, None])[:, None, :]
-    model, flat, own, w = model_of(amplitude, centre_index, spread, nch)
-
-    o_0, swap, near, far, ext = wavelet_parts(
-        place, coeff, (up1, down1, up2, down2, cube), own, w, nch, places[3] * TILE
+    model, flat, own, inner, outer, w = model_of(amplitude, centre_index, spread, nch)
+    sides = lax.ppermute(inner, "skyx", partner), away(outer, "skyx", 1)
+    o_0, swap, near, far, ext, for_up, for_down = wavelet_parts(
+        coeff, (up1, down1, up2, down2, cube), own, sides, w, nch, size * TILE
     )
 
-    swapped = lax.ppermute(swap, "skyx", [(i, i ^ 1) for i in range(places[3])])
+    swapped = lax.ppermute(swap, "skyx", partner)
     far = away(far, "skyx", 2)
     near = away(outward(near, swapped), "skyx", 1)
-    return gradient_step(place, (o_0, swapped, far, near), model, flat, ext)
+    above, below = sent(for_down, "skyy", 1), sent(for_up, "skyy", -1)
+    return gradient_step((o_0, swapped, far, near), model, flat, base_of(ext, above, below))
 
 
 def solution(mesh):

time: 72.5 us -> 69.3 us (0.956)
  the two profiles are of different devices: /device:TPU:26 before, /device:TPU:33 now
where the time goes in v5:
time: 69.3 us; the launch traced here: 68.7 us
  starting transfers between devices  38.4 us (55%)
  waiting for transfers between devices  15.3 us (22%)
  Pallas kernels  10.2 us (15%)
  local copies, waits for them, and re-layouts  3.79 us (5%)
  between operations  0.85 us (1%)
    ppermute x6, starting transfers between devices, sent(): return lax.ppermute(values, axis, pairs)  21.6 us
    ppermute x6, waiting for transfers between devices, sent(): return lax.ppermute(values, axis, pairs)  13 us
    ppermute x3, starting transfers between devices, away(): lax.ppermute(values, axis, [(i, j) for i, j in pairs if 0 <= j < size])  10.7 us
    pallas_call x1, Pallas kernels, wavelet_parts(): pl.pallas_call(wavelet_kernel, out_shape=[plain, pair, plain, plain, pltp...  4.4 us
    ppermute x1, starting transfers between devices, on_device(): sides = (lax.ppermute(inner, 'skyx', partner), away(outer, 'skyx', 1))  3.7 us
    pallas_call x1, Pallas kernels, gradient_step(): pl.pallas_call(step_kernel, out_shape=[jax.ShapeDtypeStruct(shape, jnp.fl...  3.24 us
    unnamed x16, local copies, waits for them, and re-layouts  2.54 us
    ppermute x1, starting transfers between devices, on_device(): swapped = lax.ppermute(swap, 'skyx', partner)  2.4 us
  transfers between devices with their start and end apart: 11, of which 5 were waited for; matrix products, arithmetic and copies ran while one was open for 2% of the time, Pallas kernels for 4%

profile of v5, /device:TPU:33, one launch (start us, length us, event | category | flops | bytes accessed | tf_op | source)
XLA Modules:
  0.0 68.7 jit_solution(16980375272119715398)
XLA Ops:
  0.7 4.7 %collective-permute-start.1 = (f32[16,16,512]{2,1,0:T(8,128)}, f32[16,16,512]{2,1,0:T(8,128)S(1)}, u32[]{:S(2)}, u32[]{:S(2)}) collective-permute-start(f32[16,16,512]{2,1,0:T(8,128)} %x_ref.1), channel_id=1, source_target_pairs={{32,0},{64,32},{96,64},{128,96},{160,128},{192,160},{224,192},{256... | collective-permute-start | bytes 1572872 | tf_op jit(solution)/shard_map/ppermute | solution.py:81
  5.4 2.2 %collective-permute-start = (f32[16,16,512]{2,1,0:T(8,128)}, f32[16,16,512]{2,1,0:T(8,128)S(1)}, u32[]{:S(2)}, u32[]{:S(2)}) collective-permute-start(f32[16,16,512]{2,1,0:T(8,128)} %x_ref.1), channel_id=1, source_target_pairs={{0,32},{32,64},{64,96},{96,128},{128,160},{160,192},{192,224},{224... | collective-permute-start | bytes 1572872 | tf_op jit(solution)/shard_map/ppermute | solution.py:81
  7.6 1.2 %fusion = (f32[14,16,512]{2,1,0:T(8,128)S(1)}, f32[14,16,512]{2,1,0:T(8,128)S(1)}) fusion(f32[16,16,512]{2,1,0:T(8,128)} %x_ref.1), kind=kLoop, calls=%fused_computation.3 | loop fusion | bytes 1835008 | tf_op jit(solution)/shard_map/slice | solution.py:462
  8.9 2.1 %collective-permute-start.3 = (f32[14,16,512]{2,1,0:T(8,128)S(1)}, f32[14,16,512]{2,1,0:T(8,128)S(1)}, u32[]{:S(2)}, u32[]{:S(2)}) collective-permute-start(f32[14,16,512]{2,1,0:T(8,128)S(1)} %get-tuple-element.28), channel_id=1, source_target_pairs={{64,0},{96,32},{128,64},{160,96},{192,128},{224,160},{256,192},{28... | collective-permute-start | bytes 1376264 | tf_op jit(solution)/shard_map/ppermute | solution.py:81
  11.0 3.2 %collective-permute-start.2 = (f32[14,16,512]{2,1,0:T(8,128)S(1)}, f32[14,16,512]{2,1,0:T(8,128)S(1)}, u32[]{:S(2)}, u32[]{:S(2)}) collective-permute-start(f32[14,16,512]{2,1,0:T(8,128)S(1)} %get-tuple-element.29), channel_id=1, source_target_pairs={{0,64},{32,96},{64,128},{96,160},{128,192},{160,224},{192,256},{22... | collective-permute-start | bytes 1376264 | tf_op jit(solution)/shard_map/ppermute | solution.py:81
  14.2 0.8 %copy-done.1 = f32[8,16,16]{2,1,0:T(8,128)S(1)} copy-done((f32[8,16,16]{2,1,0:T(8,128)S(1)}, f32[8,16,16]{2,1,0:T(8,128)}, u32[]{:S(2)}) %copy-start.1) | copy-done | bytes 8216
  15.0 0.8 %copy-done.2 = s32[8,16,16]{2,1,0:T(8,128)S(1)} copy-done((s32[8,16,16]{2,1,0:T(8,128)S(1)}, s32[8,16,16]{2,1,0:T(8,128)}, u32[]{:S(2)}) %copy-start.2) | copy-done | bytes 8216
  15.9 0.8 %copy-done.3 = f32[8,16,16]{2,1,0:T(8,128)S(1)} copy-done((f32[8,16,16]{2,1,0:T(8,128)S(1)}, f32[8,16,16]{2,1,0:T(8,128)}, u32[]{:S(2)}) %copy-start.3) | copy-done | bytes 8216
  16.7 2.1 %gaussian_model.1 = (f32[512,256]{1,0:T(8,128)S(1)}, f32[3,8,256]{2,1,0:T(8,128)S(1)}, f32[3,8,512]{2,1,0:T(8,128)S(1)}, f32[8,512]{1,0:T(8,128)S(1)}, f32[8,512...) custom-call(f32[8,16,16]{2,1,0:T(8,128)S(1)} %copy-done.1, s32[8,16,16]{2,1,0:T(8,128)S(1)} %copy-done.2, ...), custom_call_target="tpu_custom_call" | custom-call | flops 10000000 | bytes 1000000 | tf_op jit(solution)/shard_map/gaussian_model/pallas_call | solution.py:348
  18.8 3.7 %collective-permute-start.4 = (f32[8,512]{1,0:T(8,128)S(1)}, f32[8,512]{1,0:T(8,128)S(1)}, u32[]{:S(2)}, u32[]{:S(2)}) collective-permute-start(f32[8,512]{1,0:T(8,128)S(1)} %get-tuple-element.16), channel_id=1, source_target_pairs={{0,1},{1,0},{2,3},{3,2},{4,5},{5,4},{6,7},{7,6},{8,9},{9,8},{10,11... | collective-permute-start | bytes 49160 | tf_op jit(solution)/shard_map/ppermute | solution.py:472
  22.6 0.7 %collective-permute-done.4.inner_ref = f32[8,512]{1,0:T(8,128)S(1)} collective-permute-done((f32[8,512]{1,0:T(8,128)S(1)}, f32[8,512]{1,0:T(8,128)S(1)}, u32[]{:S(2)}, u32[]{:S(2)}) %collective-permute-start.4) | collective-permute-done | bytes 16416 | tf_op jit(solution)/shard_map/ppermute | solution.py:472
  23.3 4.2 %collective-permute-start.5 = (f32[8,512]{1,0:T(8,128)S(1)}, f32[8,512]{1,0:T(8,128)S(1)}, u32[]{:S(2)}, u32[]{:S(2)}) collective-permute-start(f32[8,512]{1,0:T(8,128)S(1)} %get-tuple-element.17), channel_id=1, source_target_pairs={{1,2},{2,1},{3,4},{4,3},{5,6},{6,5},{7,8},{8,7},{9,10},{10,9},{11,... | collective-permute-start | bytes 49160 | tf_op jit(solution)/shard_map/ppermute | solution.py:87
  27.6 1.6 %collective-permute-done.5.outer_ref = f32[8,512]{1,0:T(8,128)S(1)} collective-permute-done((f32[8,512]{1,0:T(8,128)S(1)}, f32[8,512]{1,0:T(8,128)S(1)}, u32[]{:S(2)}, u32[]{:S(2)}) %collective-permute-start.5) | collective-permute-done | bytes 16416 | tf_op jit(solution)/shard_map/ppermute | solution.py:87
  29.2 0.3 collective-permute-done.m1
  29.6 4.4 %wavelet_parts.1 = (f32[16,16,512]{2,1,0:T(8,128)S(1)}, f32[32,16,512]{2,1,0:T(8,128)S(1)}, f32[16,16,512]{2,1,0:T(8,128)S(1)}, f32[16,16,512]{2,1,0:T(8,128)S(1...) custom-call(f32[5,1,512]{2,1,0:T(1,128)S(1)} %broadcast_in_dim.2.a_ref, ...), custom_call_target="tpu_custom_call" | custom-call | flops 4000000000 | bytes 9000000 | tf_op jit(solution)/shard_map/wavelet_parts/pallas_call | solution.py:272
  34.0 2.4 %collective-permute-start.6 = (f32[32,16,512]{2,1,0:T(8,128)S(1)}, f32[32,16,512]{2,1,0:T(8,128)S(1)}, u32[]{:S(2)}, u32[]{:S(2)}) collective-permute-start(f32[32,16,512]{2,1,0:T(8,128)S(1)} %get-tuple-element.20), channel_id=1, source_target_pairs={{0,1},{1,0},{2,3},{3,2},{4,5},{5,4},{6,7},{7,6},{8,9},{9,8},{10,11... | collective-permute-start | bytes 3145736 | tf_op jit(solution)/shard_map/ppermute | solution.py:477
  36.4 4.0 %collective-permute-start.7 = (f32[16,16,512]{2,1,0:T(8,128)S(1)}, f32[16,16,512]{2,1,0:T(8,128)S(1)}, u32[]{:S(2)}, u32[]{:S(2)}) collective-permute-start(f32[16,16,512]{2,1,0:T(8,128)S(1)} %get-tuple-element.21), channel_id=1, source_target_pairs={{1,3},{2,0},{3,5},{4,2},{5,7},{6,4},{7,9},{8,6},{9,11},{10,8},{11,... | collective-permute-start | bytes 1572872 | tf_op jit(solution)/shard_map/ppermute | solution.py:87
  40.5 2.5 %collective-permute-start.8 = (f32[16,16,512]{2,1,0:T(8,128)S(1)}, f32[16,16,512]{2,1,0:T(8,128)S(1)}, u32[]{:S(2)}, u32[]{:S(2)}) collective-permute-start(f32[16,16,512]{2,1,0:T(8,128)S(1)} %outward.1), channel_id=1, source_target_pairs={{1,2},{2,1},{3,4},{4,3},{5,6},{6,5},{7,8},{8,7},{9,10},{10,9},{11,... | collective-permute-start | bytes 1572872 | tf_op jit(solution)/shard_map/ppermute | solution.py:87
  43.0 7.5 %collective-permute-start.9 = (f32[8,512]{1,0:T(8,128)S(1)}, f32[8,512]{1,0:T(8,128)S(1)}, u32[]{:S(2)}, u32[]{:S(2)}) collective-permute-start(f32[8,512]{1,0:T(8,128)S(1)} %get-tuple-element.26), channel_id=1, source_target_pairs={{0,32},{32,64},{64,96},{96,128},{128,160},{160,192},{192,224},{224... | collective-permute-start | bytes 49160 | tf_op jit(solution)/shard_map/ppermute | solution.py:81
  50.5 1.9 %collective-permute-start.10 = (f32[8,512]{1,0:T(8,128)S(1)}, f32[8,512]{1,0:T(8,128)S(1)}, u32[]{:S(2)}, u32[]{:S(2)}) collective-permute-start(f32[8,512]{1,0:T(8,128)S(1)} %get-tuple-element.27), channel_id=1, source_target_pairs={{32,0},{64,32},{96,64},{128,96},{160,128},{192,160},{224,192},{256... | collective-permute-start | bytes 49160 | tf_op jit(solution)/shard_map/ppermute | solution.py:81
  52.4 7.4 %collective-permute-done.9.above_ref = f32[8,512]{1,0:T(8,128)S(1)} collective-permute-done((f32[8,512]{1,0:T(8,128)S(1)}, f32[8,512]{1,0:T(8,128)S(1)}, u32[]{:S(2)}, u32[]{:S(2)}) %collective-permute-start.9) | collective-permute-done | bytes 16416 | tf_op jit(solution)/shard_map/ppermute | solution.py:81
  59.8 5.2 %collective-permute-done.10.below_ref = f32[8,512]{1,0:T(8,128)S(1)} collective-permute-done((f32[8,512]{1,0:T(8,128)S(1)}, f32[8,512]{1,0:T(8,128)S(1)}, u32[]{:S(2)}, u32[]{:S(2)}) %collective-permute-start.10) | collective-permute-done | bytes 16416 | tf_op jit(solution)/shard_map/ppermute | solution.py:81
  65.1 0.4 smoothed_base.1.base_ref
  65.5 3.2 %gradient_step.1 = (f32[16,16,512]{2,1,0:T(8,128)}, f32[3,8,16,16]{3,2,1,0:T(8,128)}) custom-call(f32[16,16,512]{2,1,0:T(8,128)S(1)} %get-tuple-element.19.o_0, f32[32,16,512]{2,1,0:T(8,128)S(1)} %collective-permute-done.6.swapped_ref, f32[16,16,512]{2,1,0:T(8,128)S(1)} %collective-permute-done.7.far_ref, ...), custom_call_target="tpu_custom_call" | custom-call | flops 15000000 | bytes 4000000 | tf_op jit(solution)/shard_map/gradient_step/pallas_call | solution.py:437
  (23 shorter events, 0.3 us)
Async XLA Ops:
  0.6 26.9 %copy-start.7 = (f32[5]{0:T(128)S(1)}, f32[5]{0:T(128)}, u32[]{:S(2)}) copy-start(f32[5]{0:T(128)} %constant.12.clone) | copy-start | bytes 64
  0.6 28.9 %copy-start.4 = (bf16[6,80,160]{2,1,0:T(8,128)(2,1)S(1)}, bf16[6,80,160]{2,1,0:T(8,128)(2,1)}, u32[]{:S(2)}) copy-start(bf16[6,80,160]{2,1,0:T(8,128)(2,1)} %constant.14.clone.k_ref) | copy-start | bytes 460804
  0.7 28.9 %copy-start = (f32[16,16,512]{2,1,0:T(8,128)S(1)}, f32[16,16,512]{2,1,0:T(8,128)}, u32[]{:S(2)}) copy-start(f32[16,16,512]{2,1,0:T(8,128)} %x_ref.1) | copy-start | bytes 1572868
  0.7 21.8 %copy-start.5 = (s32[4,512]{1,0:T(4,128)S(1)}, s32[4,512]{1,0:T(4,128)}, u32[]{:S(2)}) copy-start(s32[4,512]{1,0:T(4,128)} %param.11) | copy-start | bytes 24580
  0.7 21.8 %copy-start.6 = (f32[16]{0:T(128)S(1)}, f32[16]{0:T(128)}, u32[]{:S(2)}) copy-start(f32[16]{0:T(128)} %param.10) | copy-start | bytes 196
  0.7 28.5 %collective-permute-start.1 = (f32[16,16,512]{2,1,0:T(8,128)}, f32[16,16,512]{2,1,0:T(8,128)S(1)}, u32[]{:S(2)}, u32[]{:S(2)}) collective-permute-start(f32[16,16,512]{2,1,0:T(8,128)} %x_ref.1), channel_id=1, source_target_pairs={{32,0},{64,32},{96,64},{128,96},{160,128},{192,160},{224,192},{256... | collective-permute-start | bytes 1572872 | tf_op jit(solution)/shard_map/ppermute | solution.py:81
  5.4 24.2 %collective-permute-start = (f32[16,16,512]{2,1,0:T(8,128)}, f32[16,16,512]{2,1,0:T(8,128)S(1)}, u32[]{:S(2)}, u32[]{:S(2)}) collective-permute-start(f32[16,16,512]{2,1,0:T(8,128)} %x_ref.1), channel_id=1, source_target_pairs={{0,32},{32,64},{64,96},{96,128},{128,160},{160,192},{192,224},{224... | collective-permute-start | bytes 1572872 | tf_op jit(solution)/shard_map/ppermute | solution.py:81
  8.9 20.4 %collective-permute-start.3 = (f32[14,16,512]{2,1,0:T(8,128)S(1)}, f32[14,16,512]{2,1,0:T(8,128)S(1)}, u32[]{:S(2)}, u32[]{:S(2)}) collective-permute-start(f32[14,16,512]{2,1,0:T(8,128)S(1)} %get-tuple-element.28), channel_id=1, source_target_pairs={{64,0},{96,32},{128,64},{160,96},{192,128},{224,160},{256,192},{28... | collective-permute-start | bytes 1376264 | tf_op jit(solution)/shard_map/ppermute | solution.py:81
  11.0 18.3 %collective-permute-start.2 = (f32[14,16,512]{2,1,0:T(8,128)S(1)}, f32[14,16,512]{2,1,0:T(8,128)S(1)}, u32[]{:S(2)}, u32[]{:S(2)}) collective-permute-start(f32[14,16,512]{2,1,0:T(8,128)S(1)} %get-tuple-element.29), channel_id=1, source_target_pairs={{0,64},{32,96},{64,128},{96,160},{128,192},{160,224},{192,256},{22... | collective-permute-start | bytes 1376264 | tf_op jit(solution)/shard_map/ppermute | solution.py:81
  14.2 0.8 %copy-start.1 = (f32[8,16,16]{2,1,0:T(8,128)S(1)}, f32[8,16,16]{2,1,0:T(8,128)}, u32[]{:S(2)}) copy-start(f32[8,16,16]{2,1,0:T(8,128)} %amp_ref.1) | copy-start | bytes 24580
  15.0 0.8 %copy-start.2 = (s32[8,16,16]{2,1,0:T(8,128)S(1)}, s32[8,16,16]{2,1,0:T(8,128)}, u32[]{:S(2)}) copy-start(s32[8,16,16]{2,1,0:T(8,128)} %index_ref.1) | copy-start | bytes 24580
  15.8 0.8 %copy-start.3 = (f32[8,16,16]{2,1,0:T(8,128)S(1)}, f32[8,16,16]{2,1,0:T(8,128)}, u32[]{:S(2)}) copy-start(f32[8,16,16]{2,1,0:T(8,128)} %spread_ref.1) | copy-start | bytes 24580
  18.8 4.5 %collective-permute-start.4 = (f32[8,512]{1,0:T(8,128)S(1)}, f32[8,512]{1,0:T(8,128)S(1)}, u32[]{:S(2)}, u32[]{:S(2)}) collective-permute-start(f32[8,512]{1,0:T(8,128)S(1)} %get-tuple-element.16), channel_id=1, source_target_pairs={{0,1},{1,0},{2,3},{3,2},{4,5},{5,4},{6,7},{7,6},{8,9},{9,8},{10,11... | collective-permute-start | bytes 49160 | tf_op jit(solution)/shard_map/ppermute | solution.py:472
  23.3 5.9 %collective-permute-start.5 = (f32[8,512]{1,0:T(8,128)S(1)}, f32[8,512]{1,0:T(8,128)S(1)}, u32[]{:S(2)}, u32[]{:S(2)}) collective-permute-start(f32[8,512]{1,0:T(8,128)S(1)} %get-tuple-element.17), channel_id=1, source_target_pairs={{1,2},{2,1},{3,4},{4,3},{5,6},{6,5},{7,8},{8,7},{9,10},{10,9},{11,... | collective-permute-start | bytes 49160 | tf_op jit(solution)/shard_map/ppermute | solution.py:87
  34.0 6.4 %collective-permute-start.6 = (f32[32,16,512]{2,1,0:T(8,128)S(1)}, f32[32,16,512]{2,1,0:T(8,128)S(1)}, u32[]{:S(2)}, u32[]{:S(2)}) collective-permute-start(f32[32,16,512]{2,1,0:T(8,128)S(1)} %get-tuple-element.20), channel_id=1, source_target_pairs={{0,1},{1,0},{2,3},{3,2},{4,5},{5,4},{6,7},{7,6},{8,9},{9,8},{10,11... | collective-permute-start | bytes 3145736 | tf_op jit(solution)/shard_map/ppermute | solution.py:477
  36.4 29.1 %collective-permute-start.7 = (f32[16,16,512]{2,1,0:T(8,128)S(1)}, f32[16,16,512]{2,1,0:T(8,128)S(1)}, u32[]{:S(2)}, u32[]{:S(2)}) collective-permute-start(f32[16,16,512]{2,1,0:T(8,128)S(1)} %get-tuple-element.21), channel_id=1, source_target_pairs={{1,3},{2,0},{3,5},{4,2},{5,7},{6,4},{7,9},{8,6},{9,11},{10,8},{11,... | collective-permute-start | bytes 1572872 | tf_op jit(solution)/shard_map/ppermute | solution.py:87
  40.5 25.0 %collective-permute-start.8 = (f32[16,16,512]{2,1,0:T(8,128)S(1)}, f32[16,16,512]{2,1,0:T(8,128)S(1)}, u32[]{:S(2)}, u32[]{:S(2)}) collective-permute-start(f32[16,16,512]{2,1,0:T(8,128)S(1)} %outward.1), channel_id=1, source_target_pairs={{1,2},{2,1},{3,4},{4,3},{5,6},{6,5},{7,8},{8,7},{9,10},{10,9},{11,... | collective-permute-start | bytes 1572872 | tf_op jit(solution)/shard_map/ppermute | solution.py:87
  43.0 16.9 %collective-permute-start.9 = (f32[8,512]{1,0:T(8,128)S(1)}, f32[8,512]{1,0:T(8,128)S(1)}, u32[]{:S(2)}, u32[]{:S(2)}) collective-permute-start(f32[8,512]{1,0:T(8,128)S(1)} %get-tuple-element.26), channel_id=1, source_target_pairs={{0,32},{32,64},{64,96},{96,128},{128,160},{160,192},{192,224},{224... | collective-permute-start | bytes 49160 | tf_op jit(solution)/shard_map/ppermute | solution.py:81
  50.5 14.6 %collective-permute-start.10 = (f32[8,512]{1,0:T(8,128)S(1)}, f32[8,512]{1,0:T(8,128)S(1)}, u32[]{:S(2)}, u32[]{:S(2)}) collective-permute-start(f32[8,512]{1,0:T(8,128)S(1)} %get-tuple-element.27), channel_id=1, source_target_pairs={{32,0},{64,32},{96,64},{128,96},{160,128},{192,160},{224,192},{256... | collective-permute-start | bytes 49160 | tf_op jit(solution)/shard_map/ppermute | solution.py:81

commit v6 on v5

--- a/solution.py
+++ b/solution.py
@@ -17,6 +17,7 @@
 BEYOND = 2
 VMEM_LIMIT = 20 * 1024 * 1024
 ROLES = ((2, 3, 4, 1, 0), (2, 1, 0, 3, 4))
+PIXELS = TILE * TILE
 PITCH = 24
 EXT = 512
 STEPS = (0.5, 0.002, 2.0)
@@ -49,7 +50,14 @@
 
 def channel_matrices(nch):
     parts = [halves(m.T) for m in composites(nch)]
-    return np.stack([p[0] for p in parts] + [p[1] for p in parts[2:]])
+    half, quarter = nch // 2, nch // 4
+    out = []
+    for whole in [p[0] for p in parts] + [p[1] for p in parts[2:]]:
+        across = whole[quarter : quarter + half, quarter : quarter + half].copy()
+        across[:quarter, :quarter] = 0
+        across[quarter:, quarter:] = 0
+        out.append(np.stack([whole[:half, :half], across, whole[half:, half:]]))
+    return np.stack(out)
 
 
 def scatter_matrices(length):
@@ -95,21 +103,44 @@
     return spread_ref[:, row, :]
 
 
+def pack_kernel(cube_hbm, amp_ref, index_ref, spread_ref, up_ref, down_ref, sem):
+    nch = cube_hbm.shape[1]
+    copies = []
+    for i, out in enumerate((up_ref, down_ref)):
+        copies.append(pltpu.make_async_copy(cube_hbm, out.at[0:PIXELS], sem.at[i]))
+        copies[-1].start()
+    for out, first in ((up_ref, TILE - 2), (down_ref, 0)):
+        out[PIXELS:, :] = jnp.zeros((COMPS, nch), jnp.float32)
+        for t in range(3):
+            for r in range(2):
+                lane = (2 * t + r) * PITCH + 2
+                got = own_row(t, first + r, amp_ref, index_ref, spread_ref, nch)
+                out[PIXELS:, lane : lane + TILE] = got
+    for copy in copies:
+        copy.wait()
+
+
+def packed(cube, amplitude, centre_index, spread):
+    vmem = pl.BlockSpec(memory_space=pltpu.VMEM)
+    hbm = [pltpu.with_memory_space_constraint(v, pltpu.HBM) for v in (cube, amplitude, centre_index, spread)]
+    return pl.pallas_call(
+        pack_kernel,
+        out_shape=[pltpu.VMEM((PIXELS + COMPS, cube.shape[1]), jnp.float32)] * 2,
+        in_specs=[pl.BlockSpec(memory_space=pl.ANY)] + [vmem] * 3,
+        out_specs=[vmem] * 2,
+        scratch_shapes=[pltpu.SemaphoreType.DMA((2,))],
+        compiler_params=pltpu.CompilerParams(vmem_limit_bytes=VMEM_LIMIT),
+        cost_estimate=pl.CostEstimate(flops=1000, bytes_accessed=1_000_000, transcendentals=0),
+        name="pack",
+    )(*hbm)
+
+
 def border_columns(ext_ref, shift):
     lane = lax.broadcasted_iota(jnp.int32, (COMPS, EXT), 1) % PITCH
     total = jnp.zeros((COMPS, EXT), jnp.float32)
     for t in range(3):
         moved = pltpu.roll(ext_ref[t], (2 * t - shift) % EXT, 1)
         total = jnp.where((lane >= 2 * t) & (lane < 2 * t + 2), moved, total)
-    return total
-
-
-def border_rows(rows, first):
-    lane = lax.broadcasted_iota(jnp.int32, (COMPS, EXT), 1)
-    total = jnp.zeros((COMPS, EXT), jnp.float32)
-    for t in range(3):
-        moved = pltpu.roll(rows[t], ((2 * t - first) * PITCH) % EXT, 1)
-        total = jnp.where((lane >= 2 * t * PITCH) & (lane < (2 * t + 2) * PITCH), moved, total)
     return total
 
 
@@ -149,27 +180,6 @@
     return out
 
 
-def base_kernel(ext_ref, above_ref, below_ref, base_ref):
-    params = smoothed(with_rows(ext_ref, above_ref[...], below_ref[...]))
-    for t in range(3):
-        for row in range(TILE):
-            lane = (row + 2) * PITCH + 2
-            base_ref[t, :, row * TILE : (row + 1) * TILE] = params[t][:, lane : lane + TILE]
-
-
-def base_of(ext, above, below):
-    vmem = pl.BlockSpec(memory_space=pltpu.VMEM)
-    return pl.pallas_call(
-        base_kernel,
-        out_shape=pltpu.VMEM((3, COMPS, TILE * TILE), jnp.float32),
-        in_specs=[vmem] * 3,
-        out_specs=vmem,
-        compiler_params=pltpu.CompilerParams(vmem_limit_bytes=VMEM_LIMIT),
-        cost_estimate=pl.CostEstimate(flops=200_000, bytes_accessed=100_000, transcendentals=0),
-        name="smoothed_base",
-    )(*[kept(x) for x in (ext, above, below)])
-
-
 def five(v, flag=None):
     total = (v[0] + v[4]) + 4.0 * (v[1] + v[3]) + 6.0 * v[2]
     return total if flag is None else total * flag
@@ -181,8 +191,8 @@
 
 
 def wavelet_kernel(
-    a_ref, m1, p1, m2, p2, x_ref, k_ref, own_ref, inner_ref, outer_ref, w_ref,
-    o_0, swap_ref, near_ref, far_ref, ext_ref, up_ref, down_ref, rows_ref, y_ref,
+    a_ref, m1, p1, m2, p2, x_ref, k_ref, own_ref, w_ref,
+    o_0, swap_ref, near_ref, far_ref, ext_ref, rows_ref, y_ref,
 ):
     nch = x_ref.shape[2]
     tiles = (m2, m1, x_ref, p1, p2)
@@ -200,6 +210,9 @@
         def value(level, at):
             tile = (at + 2 * TILE) // TILE
             if level == 0:
+                if tile in (1, 3):
+                    start = pl.multiple_of(at % TILE * TILE + step // lane_tiles * 8, 8)
+                    return tiles[tile][pl.ds(start, 8), lane]
                 return tiles[tile][at % TILE - (BEYOND if tile == 0 else 0), sub, lane]
             gap = 2 ** (level - 1)
             taps = [value(level - 1, at + (t - 2) * gap) for t in range(5)]
@@ -219,61 +232,76 @@
 
     lax.fori_loop(0, 2 * lane_tiles, row_pass, 0)
 
-    pixels = TILE * TILE
-    dot = functools.partial(jnp.dot, preferred_element_type=jnp.float32)
+    half, quarter = nch // 2, nch // 4
+
+    def product(v, index):
+        blocks = [
+            jnp.dot(v[:, at : at + half], w_ref[index, i], preferred_element_type=jnp.float32)
+            for i, at in enumerate((0, quarter, half))
+        ]
+        return blocks
+
     for level in range(LEVELS):
-        high, low = split(rows_ref[level].reshape(pixels, nch))
-        got = dot(high, w_ref[level]) + dot(low, w_ref[level])
+        high, low = split(rows_ref[level].reshape(PIXELS, nch))
+        terms = [product(high, level), product(low, level)]
         if level >= 2:
-            got = got + dot(high, w_ref[level + 2])
-        high, low = split(got * a_ref[level + 1])
-        high = high.reshape(TILE, TILE, nch)
-        y_ref[:, level * TILE : (level + 1) * TILE] = high
-        at = (level + LEVELS) * TILE
-        y_ref[:, at : at + TILE] = low.reshape(TILE, TILE, nch)
-        if level >= 2:
-            at = (level + 6) * TILE
-            y_ref[:, at : at + TILE] = high
+            terms.append(product(high, level + 2))
+        first, middle, last = [functools.reduce(lambda a, b: a + b, v) for v in zip(*terms)]
+        pieces = (
+            first[:, :quarter],
+            first[:, quarter:] + middle[:, :quarter],
+            middle[:, quarter:] + last[:, :quarter],
+            last[:, quarter:],
+        )
+        for i, piece in enumerate(pieces):
+            lane = slice(i * quarter, (i + 1) * quarter)
+            high, low = split(piece * a_ref[level + 1, :, lane])
+            high = high.reshape(TILE, TILE, quarter)
+            y_ref[:, level * TILE : (level + 1) * TILE, lane] = high
+            at = (level + LEVELS) * TILE
+            y_ref[:, at : at + TILE, lane] = low.reshape(TILE, TILE, quarter)
+            if level >= 2:
+                at = (level + 6) * TILE
+                y_ref[:, at : at + TILE, lane] = high
 
     kind = jnp.where(ix == 0, 0, jnp.where(ix == lax.axis_size("skyx") - 1, 2, 1))
     odd = lax.rem(ix, 2)
     columns = k_ref[2 * kind + odd]
 
     def column_pass(row, carry):
-        got = dot(columns, y_ref[row])
+        got = jnp.dot(columns, y_ref[row], preferred_element_type=jnp.float32)
+        at = pl.ds(pl.multiple_of(row * TILE, TILE), TILE)
+        at_more = pl.ds(pl.multiple_of(row * TILE + PIXELS, TILE), TILE)
         o_0[row] = got[:TILE] + a_ref[0] * x_ref[row]
-        swap_ref[row] = got[TILE : 2 * TILE]
-        swap_ref[row + TILE] = got[2 * TILE : 3 * TILE]
-        near_ref[row] = got[3 * TILE : 4 * TILE]
-        far_ref[row] = got[4 * TILE :]
+        swap_ref[at] = got[TILE : 2 * TILE]
+        swap_ref[at_more] = got[2 * TILE : 3 * TILE]
+        near_ref[at] = got[3 * TILE : 4 * TILE]
+        far_ref[at] = got[4 * TILE :]
         return carry
 
     lax.fori_loop(0, TILE, column_pass, 0, unroll=4)
 
-    inner, outer = inner_ref[...], outer_ref[...]
-    left, right = jnp.where(odd == 0, outer, inner), jnp.where(odd == 0, inner, outer)
-    params = with_columns(own_ref, left, right)
+    params = with_rows(own_ref, m1[PIXELS:, :], p1[PIXELS:, :])
     for t in range(3):
         ext_ref[t] = params[t]
-    up_ref[...] = border_rows(params, 2)
-    down_ref[...] = border_rows(params, TILE)
+    to_right, to_left = border_columns(ext_ref, TILE), border_columns(ext_ref, 2)
+    swap_ref[2 * PIXELS :, :] = jnp.where(odd == 0, to_right, to_left)
+    near_ref[PIXELS:, :] = jnp.where(odd == 0, to_left, to_right)
 
 
 def kept(x):
     return pltpu.with_memory_space_constraint(x, pltpu.VMEM)
 
 
-def wavelet_parts(coeff, tiles, own, sides, w, nch, length):
+def wavelet_parts(coeff, tiles, own, w, nch, length):
     k = jnp.asarray(scatter_matrices(length))
     vmem = pl.BlockSpec(memory_space=pltpu.VMEM)
-    plain = pltpu.VMEM(tiles[-1].shape, jnp.float32)
-    pair = pltpu.VMEM((2 * TILE,) + tiles[0].shape[1:], jnp.float32)
-    rows = pltpu.VMEM((COMPS, EXT), jnp.float32)
+    shapes = [tiles[-1].shape] + [(n, nch) for n in (2 * PIXELS + COMPS, PIXELS + COMPS, PIXELS + COMPS)] + [own.shape]
     return pl.pallas_call(
         wavelet_kernel,
-        out_shape=[plain, pair, plain, plain, pltpu.VMEM(own.shape, jnp.float32), rows, rows],
-        in_specs=[vmem] * 11,
-        out_specs=[vmem] * 7,
+        out_shape=[pltpu.VMEM(shape, jnp.float32) for shape in shapes],
+        in_specs=[vmem] * 9,
+        out_specs=[vmem] * 5,
         scratch_shapes=[
             pltpu.VMEM((LEVELS, TILE, TILE, nch), jnp.float32),
             pltpu.VMEM((TILE, 10 * TILE, nch), jnp.bfloat16),
@@ -281,15 +309,18 @@
         compiler_params=pltpu.CompilerParams(vmem_limit_bytes=VMEM_LIMIT),
         cost_estimate=pl.CostEstimate(flops=4_000_000_000, bytes_accessed=9_000_000, transcendentals=0),
         name="wavelet_parts",
-    )(*[kept(x) for x in (coeff, *tiles, k, own, *sides, w)])
+    )(*[kept(x) for x in (coeff, *tiles, k, own, w)])
 
 
 def add_kernel(near_ref, swapped_ref, out_ref):
     def body(row, carry):
-        out_ref[row] = near_ref[row] + swapped_ref[row + TILE]
+        at = pl.ds(pl.multiple_of(row * TILE, TILE), TILE)
+        more = pl.ds(pl.multiple_of(row * TILE + PIXELS, TILE), TILE)
+        out_ref[at] = near_ref[at] + swapped_ref[more]
         return carry
 
     lax.fori_loop(0, TILE, body, 0, unroll=4)
+    out_ref[PIXELS:, :] = near_ref[PIXELS:, :]
 
 
 def outward(near, swapped):
@@ -305,7 +336,7 @@
     )(kept(near), kept(swapped))
 
 
-def model_kernel(amp_ref, index_ref, spread_ref, w_hbm, model_ref, flat_ref, own_ref, inner_ref, outer_ref, w_ref, scale_ref, sem):
+def model_kernel(amp_ref, index_ref, spread_ref, w_hbm, model_ref, flat_ref, own_ref, w_ref, scale_ref, sem):
     load = pltpu.make_async_copy(w_hbm, w_ref, sem)
     load.start()
     nch, pixels = model_ref.shape
@@ -316,10 +347,6 @@
             at = (row + 2) * PITCH + 2
             own_ref[t, :, at : at + TILE] = got
             flat_ref[t, :, row * TILE : (row + 1) * TILE] = got
-    even = lax.rem(lax.axis_index("skyx"), 2) == 0
-    to_right, to_left = border_columns(own_ref, TILE), border_columns(own_ref, 2)
-    inner_ref[...] = jnp.where(even, to_right, to_left)
-    outer_ref[...] = jnp.where(even, to_left, to_right)
     mu = flat_ref[1] * float(nch)
     inv = 1.0 / flat_ref[2]
     flat_ref[1] = mu
@@ -351,12 +378,10 @@
             pltpu.VMEM((nch, pixels), jnp.float32),
             pltpu.VMEM((3, COMPS, pixels), jnp.float32),
             pltpu.VMEM((3, COMPS, EXT), jnp.float32),
-            pltpu.VMEM((COMPS, EXT), jnp.float32),
-            pltpu.VMEM((COMPS, EXT), jnp.float32),
             pltpu.VMEM(w.shape, w.dtype),
         ],
         in_specs=[vmem] * 3 + [pl.BlockSpec(memory_space=pl.ANY)],
-        out_specs=[vmem] * 6,
+        out_specs=[vmem] * 4,
         scratch_shapes=[pltpu.VMEM((COMPS, pixels), jnp.float32), pltpu.SemaphoreType.DMA],
         compiler_params=pltpu.CompilerParams(vmem_limit_bytes=VMEM_LIMIT),
         cost_estimate=pl.CostEstimate(flops=10_000_000, bytes_accessed=1_000_000, transcendentals=1_100_000),
@@ -365,17 +390,22 @@
 
 
 def step_kernel(
-    o_0, swapped_ref, far_ref, near_ref, model_ref, flat_ref, base_ref,
+    o_0, swapped_ref, far_ref, near_ref, model_ref, flat_ref, ext_ref,
     den_hbm, fit_ref, den_ref, r_ref, sem,
 ):
     nch, pixels = model_ref.shape
     rows = LANES // TILE
     parts = pixels // LANES
     copies = []
+    inner, outer = swapped_ref[2 * PIXELS :, :], near_ref[PIXELS:, :]
+    even = lax.rem(lax.axis_index("skyx"), 2) == 0
+    left, right = jnp.where(even, outer, inner), jnp.where(even, inner, outer)
+    bases = smoothed(with_columns(ext_ref, left, right))
     for part in range(parts):
         at = slice(part * rows, (part + 1) * rows)
         for row in range(part * rows, (part + 1) * rows):
-            den_ref[row] = (o_0[row] + swapped_ref[row]) + (far_ref[row] + near_ref[row])
+            flat = slice(row * TILE, (row + 1) * TILE)
+            den_ref[row] = (o_0[row] + swapped_ref[flat]) + (far_ref[flat] + near_ref[flat])
         copies.append(pltpu.make_async_copy(den_ref.at[at], den_hbm.at[at], sem.at[part]))
         copies[-1].start()
 
@@ -421,7 +451,9 @@
             jnp.concatenate(sums[2], axis=0) * (slope * inv * (1.0 / nch)),
         )
         for t in range(3):
-            new = base_ref[t, :, at] - STEPS[t] * grads[t]
+            lanes = [(part * rows + i + 2) * PITCH + 2 for i in range(rows)]
+            base = jnp.concatenate([bases[t][:, lane : lane + TILE] for lane in lanes], axis=1)
+            new = base - STEPS[t] * grads[t]
             spread_out = jnp.where(own_lanes, jnp.broadcast_to(new[:, None, :], own_lanes.shape), 0.0)
             for shift in (LANES // 2, LANES // 4, LANES // 8):
                 spread_out = spread_out + pltpu.roll(spread_out, shift, 2)
@@ -431,7 +463,7 @@
         copy.wait()
 
 
-def gradient_step(parts, model, flat, base):
+def gradient_step(parts, model, flat, ext):
     vmem = pl.BlockSpec(memory_space=pltpu.VMEM)
     shape = parts[0].shape
     return pl.pallas_call(
@@ -450,7 +482,7 @@
         compiler_params=pltpu.CompilerParams(vmem_limit_bytes=VMEM_LIMIT),
         cost_estimate=pl.CostEstimate(flops=15_000_000, bytes_accessed=4_000_000, transcendentals=1_100_000),
         name="gradient_step",
-    )(*[kept(x) for x in (*parts, model, flat, base)])
+    )(*[kept(x) for x in (*parts, model, flat, ext)])
 
 
 def on_device(cube, level_table, level_index, amplitude, centre_index, spread):
@@ -458,7 +490,8 @@
     size = lax.axis_size("skyx")
     partner = [(i, i ^ 1) for i in range(size)]
 
-    up1, down1 = sent(cube, "skyy", 1), sent(cube, "skyy", -1)
+    for_down, for_up = packed(cube.reshape(PIXELS, nch), amplitude, centre_index, spread)
+    up1, down1 = sent(for_down, "skyy", 1), sent(for_up, "skyy", -1)
     up2, down2 = sent(cube[BEYOND:], "skyy", 2), sent(cube[:-BEYOND], "skyy", -2)
 
     entries = jnp.arange(level_table.shape[0], dtype=jnp.int32)
@@ -468,17 +501,13 @@
     coeff = jnp.concatenate([weight, one]) - jnp.concatenate([0.0 * one, weight])
     scale = jnp.array([16.0 ** (-3 * j) for j in range(LEVELS + 1)], jnp.float32)
     coeff = (coeff * scale[:, None])[:, None, :]
-    model, flat, own, inner, outer, w = model_of(amplitude, centre_index, spread, nch)
-    sides = lax.ppermute(inner, "skyx", partner), away(outer, "skyx", 1)
-    o_0, swap, near, far, ext, for_up, for_down = wavelet_parts(
-        coeff, (up1, down1, up2, down2, cube), own, sides, w, nch, size * TILE
-    )
+    model, flat, own, w = model_of(amplitude, centre_index, spread, nch)
+    o_0, swap, near, far, ext = wavelet_parts(coeff, (up1, down1, up2, down2, cube), own, w, nch, size * TILE)
 
     swapped = lax.ppermute(swap, "skyx", partner)
     far = away(far, "skyx", 2)
     near = away(outward(near, swapped), "skyx", 1)
-    above, below = sent(for_down, "skyy", 1), sent(for_up, "skyy", -1)
-    return gradient_step((o_0, swapped, far, near), model, flat, base_of(ext, above, below))
+    return gradient_step((o_0, swapped, far, near), model, flat, ext)
 
 
 def solution(mesh):

time: 69.3 us -> 70.9 us (1.023)
  the two profiles are of different devices: /device:TPU:33 before, /device:TPU:26 now
where the time goes in v6:
time: 70.9 us; the launch traced here: 70.5 us
  starting transfers between devices  31.4 us (44%)
  waiting for transfers between devices  24.8 us (35%)
  Pallas kernels  11.9 us (17%)
  local copies, waits for them, and re-layouts  1.27 us (2%)
  between operations  0.86 us (1%)
    ppermute x4, starting transfers between devices, sent(): return lax.ppermute(values, axis, pairs)  16.2 us
    ppermute x4, waiting for transfers between devices, sent(): return lax.ppermute(values, axis, pairs)  14.4 us
    ppermute x2, starting transfers between devices, away(): lax.ppermute(values, axis, [(i, j) for i, j in pairs if 0 <= j < size])  13.3 us
    ppermute x2, waiting for transfers between devices, away(): lax.ppermute(values, axis, [(i, j) for i, j in pairs if 0 <= j < size])  10.4 us
    pallas_call x1, Pallas kernels, wavelet_parts(): pl.pallas_call(wavelet_kernel, out_shape=[pltpu.VMEM(shape, jnp.float32)...  4.14 us
    pallas_call x1, Pallas kernels, gradient_step(): pl.pallas_call(step_kernel, out_shape=[jax.ShapeDtypeStruct(shape, jnp.fl...  3.61 us
    pallas_call x1, Pallas kernels, packed(): pl.pallas_call(pack_kernel, out_shape=[pltpu.VMEM((PIXELS + COMPS, cube.s...  2.2 us
    ppermute x1, starting transfers between devices, on_device(): swapped = lax.ppermute(swap, 'skyx', partner)  1.92 us
  transfers between devices with their start and end apart: 7, of which 3 were waited for; matrix products, arithmetic and copies ran while one was open for 2% of the time, Pallas kernels for 3%

profile of v6, /device:TPU:26, one launch (start us, length us, event | category | flops | bytes accessed | tf_op | source)
XLA Modules:
  0.0 70.5 jit_solution(1669492963407522833)
XLA Ops:
  0.6 0.0 copy-start.7
  0.7 2.2 %pack.1 = (f32[264,512]{1,0:T(8,128)S(1)}, f32[264,512]{1,0:T(8,128)S(1)}) custom-call(f32[256,512]{1,0:T(8,128)} %bitcast.1, f32[8,16,16]{2,1,0:T(8,128)} %amp_ref.3, s32[8,16,16]{2,1,0:T(8,128)} %index_ref.3, f32[8,16,16]{2,1,0:T(8,128)} %spread_ref.3), custom_call_target="tpu_custom_call" | custom-call | flops 1000 | bytes 1000000 | tf_op jit(solution)/shard_map/pack/pallas_call | solution.py:126
  2.9 0.0 copy-start
  2.9 0.0 copy-start.4
  2.9 4.2 %collective-permute-start = (f32[264,512]{1,0:T(8,128)S(1)}, f32[264,512]{1,0:T(8,128)S(1)}, u32[]{:S(2)}, u32[]{:S(2)}) collective-permute-start(f32[264,512]{1,0:T(8,128)S(1)} %get-tuple-element.13), channel_id=1, source_target_pairs={{0,32},{32,64},{64,96},{96,128},{128,160},{160,192},{192,224},{224... | collective-permute-start | bytes 1622024 | tf_op jit(solution)/shard_map/ppermute | solution.py:89
  7.1 4.2 %collective-permute-start.1 = (f32[264,512]{1,0:T(8,128)S(1)}, f32[264,512]{1,0:T(8,128)S(1)}, u32[]{:S(2)}, u32[]{:S(2)}) collective-permute-start(f32[264,512]{1,0:T(8,128)S(1)} %get-tuple-element.14), channel_id=1, source_target_pairs={{32,0},{64,32},{96,64},{128,96},{160,128},{192,160},{224,192},{256... | collective-permute-start | bytes 1622024 | tf_op jit(solution)/shard_map/ppermute | solution.py:89
  11.3 1.2 %fusion = (f32[14,16,512]{2,1,0:T(8,128)S(1)}, f32[14,16,512]{2,1,0:T(8,128)S(1)}) fusion(f32[16,16,512]{2,1,0:T(8,128)} %x_ref.1), kind=kLoop, calls=%fused_computation.3 | loop fusion | bytes 1835008 | tf_op jit(solution)/shard_map/slice | solution.py:495
  12.5 2.4 %collective-permute-start.3 = (f32[14,16,512]{2,1,0:T(8,128)S(1)}, f32[14,16,512]{2,1,0:T(8,128)S(1)}, u32[]{:S(2)}, u32[]{:S(2)}) collective-permute-start(f32[14,16,512]{2,1,0:T(8,128)S(1)} %get-tuple-element.24), channel_id=1, source_target_pairs={{64,0},{96,32},{128,64},{160,96},{192,128},{224,160},{256,192},{28... | collective-permute-start | bytes 1376264 | tf_op jit(solution)/shard_map/ppermute | solution.py:89
  14.9 5.5 %collective-permute-start.2 = (f32[14,16,512]{2,1,0:T(8,128)S(1)}, f32[14,16,512]{2,1,0:T(8,128)S(1)}, u32[]{:S(2)}, u32[]{:S(2)}) collective-permute-start(f32[14,16,512]{2,1,0:T(8,128)S(1)} %get-tuple-element.25), channel_id=1, source_target_pairs={{0,64},{32,96},{64,128},{96,160},{128,192},{160,224},{192,256},{22... | collective-permute-start | bytes 1376264 | tf_op jit(solution)/shard_map/ppermute | solution.py:89
  20.4 0.1 select_reduce_fusion
  20.5 0.1 subtract_multiply_fusion
  20.6 1.9 %gaussian_model.1 = (f32[512,256]{1,0:T(8,128)S(1)}, f32[3,8,256]{2,1,0:T(8,128)S(1)}, f32[3,8,512]{2,1,0:T(8,128)S(1)}, bf16[6,3,256,256]{3,2,1,0:T(8,128)(2,1)S(1)}) custom-call(f32[8,16,16]{2,1,0:T(8,128)S(1)} %copy-done.1, s32[8,16,16]{2,1,0:T(8,128)S(1)} %copy-done.2, f32[8,16,16]{2,1,0:T(8,128)S(1)} %copy-done.3, ...), custom_call_target="tpu_custom_call" | custom-call | flops 10000000 | bytes 1000000 | tf_op jit(solution)/shard_map/gaussian_model/pallas_call | solution.py:375
  22.5 14.4 %collective-permute-done.3.p2 = f32[14,16,512]{2,1,0:T(8,128)S(1)} collective-permute-done((f32[14,16,512]{2,1,0:T(8,128)S(1)}, f32[14,16,512]{2,1,0:T(8,128)S(1)}, u32[]{:S(2)}, u32[]{:S(2)}) %collective-permute-start.3) | collective-permute-done | bytes 458784 | tf_op jit(solution)/shard_map/ppermute | solution.py:89
  36.9 0.0 collective-permute-done.2.m2
  36.9 0.0 collective-permute-done.m1
  36.9 0.0 collective-permute-done.1.p1
  36.9 4.1 %wavelet_parts.1 = (f32[16,16,512]{2,1,0:T(8,128)S(1)}, f32[520,512]{1,0:T(8,128)S(1)}, f32[264,512]{1,0:T(8,128)S(1)}, f32[264,512]{1,0:T(8,128)S(1)}, f32[3,8,512]{2,1,0:T(8,128)S(1)}) custom-call(f32[5,1,512]{2,1,0:T(1,128)S(1)} %broadcast_in_dim.2.a_ref, f32[264,512]{1,0:T(8,128)S(1)} %collective-permute-done.m1, ...), custom_call_target="tpu_custom_call" | custom-call | flops 4000000000 | bytes 9000000 | tf_op jit(solution)/shard_map/wavelet_parts/pallas_call | solution.py:300
  41.1 1.9 %collective-permute-start.4 = (f32[520,512]{1,0:T(8,128)S(1)}, f32[520,512]{1,0:T(8,128)S(1)}, u32[]{:S(2)}, u32[]{:S(2)}) collective-permute-start(f32[520,512]{1,0:T(8,128)S(1)} %get-tuple-element.18), channel_id=1, source_target_pairs={{0,1},{1,0},{2,3},{3,2},{4,5},{5,4},{6,7},{7,6},{8,9},{9,8},{10,11... | collective-permute-start | bytes 3194888 | tf_op jit(solution)/shard_map/ppermute | solution.py:507
  43.0 10.9 %collective-permute-start.5 = (f32[264,512]{1,0:T(8,128)S(1)}, f32[264,512]{1,0:T(8,128)S(1)}, u32[]{:S(2)}, u32[]{:S(2)}) collective-permute-start(f32[264,512]{1,0:T(8,128)S(1)} %get-tuple-element.19), channel_id=1, source_target_pairs={{1,3},{2,0},{3,5},{4,2},{5,7},{6,4},{7,9},{8,6},{9,11},{10,8},{11,... | collective-permute-start | bytes 1622024 | tf_op jit(solution)/shard_map/ppermute | solution.py:95
  53.9 0.1 outward.1
  54.0 2.4 %collective-permute-start.6 = (f32[264,512]{1,0:T(8,128)S(1)}, f32[264,512]{1,0:T(8,128)S(1)}, u32[]{:S(2)}, u32[]{:S(2)}) collective-permute-start(f32[264,512]{1,0:T(8,128)S(1)} %outward.1), channel_id=1, source_target_pairs={{1,2},{2,1},{3,4},{4,3},{5,6},{6,5},{7,8},{8,7},{9,10},{10,9},{11,... | collective-permute-start | bytes 1622024 | tf_op jit(solution)/shard_map/ppermute | solution.py:95
  56.4 4.4 %collective-permute-done.5.far_ref = f32[264,512]{1,0:T(8,128)S(1)} collective-permute-done((f32[264,512]{1,0:T(8,128)S(1)}, f32[264,512]{1,0:T(8,128)S(1)}, u32[]{:S(2)}, u32[]{:S(2)}) %collective-permute-start.5) | collective-permute-done | bytes 540704 | tf_op jit(solution)/shard_map/ppermute | solution.py:95
  60.8 6.1 %collective-permute-done.6.near_ref = f32[264,512]{1,0:T(8,128)S(1)} collective-permute-done((f32[264,512]{1,0:T(8,128)S(1)}, f32[264,512]{1,0:T(8,128)S(1)}, u32[]{:S(2)}, u32[]{:S(2)}) %collective-permute-start.6) | collective-permute-done | bytes 540704 | tf_op jit(solution)/shard_map/ppermute | solution.py:95
  66.8 3.6 %gradient_step.1 = (f32[16,16,512]{2,1,0:T(8,128)}, f32[3,8,16,16]{3,2,1,0:T(8,128)}) custom-call(f32[16,16,512]{2,1,0:T(8,128)S(1)} %get-tuple-element.17.o_0, f32[520,512]{1,0:T(8,128)S(1)} %collective-permute-done.4.swapped_ref, f32[264,512]{1,0:T(8,128)S(1)} %collective-permute-done.5.far_ref, f32[264,512]{1,0:T(8,128)S(1)} %collective-permute-done.6.near_ref, ...), custom_call_target="tpu_custom_call" | custom-call | flops 15000000 | bytes 4000000 | tf_op jit(solution)/shard_map/gradient_step/pallas_call | solution.py:469
  (15 shorter events, 0.0 us)
Async XLA Ops:
  0.6 19.9 %copy-start.7 = (f32[5]{0:T(128)S(1)}, f32[5]{0:T(128)}, u32[]{:S(2)}) copy-start(f32[5]{0:T(128)} %constant.12.clone) | copy-start | bytes 64
  0.6 20.0 %copy-start.3 = (f32[8,16,16]{2,1,0:T(8,128)S(1)}, f32[8,16,16]{2,1,0:T(8,128)}, u32[]{:S(2)}) copy-start(f32[8,16,16]{2,1,0:T(8,128)} %spread_ref.3) | copy-start | bytes 24580
  0.7 20.0 %copy-start.2 = (s32[8,16,16]{2,1,0:T(8,128)S(1)}, s32[8,16,16]{2,1,0:T(8,128)}, u32[]{:S(2)}) copy-start(s32[8,16,16]{2,1,0:T(8,128)} %index_ref.3) | copy-start | bytes 24580
  0.7 20.0 %copy-start.1 = (f32[8,16,16]{2,1,0:T(8,128)S(1)}, f32[8,16,16]{2,1,0:T(8,128)}, u32[]{:S(2)}) copy-start(f32[8,16,16]{2,1,0:T(8,128)} %amp_ref.3) | copy-start | bytes 24580
  0.7 19.7 %copy-start.5 = (s32[4,512]{1,0:T(4,128)S(1)}, s32[4,512]{1,0:T(4,128)}, u32[]{:S(2)}) copy-start(s32[4,512]{1,0:T(4,128)} %param.11) | copy-start | bytes 24580
  0.7 19.7 %copy-start.6 = (f32[16]{0:T(128)S(1)}, f32[16]{0:T(128)}, u32[]{:S(2)}) copy-start(f32[16]{0:T(128)} %param.10) | copy-start | bytes 196
  2.9 34.0 %copy-start = (f32[16,16,512]{2,1,0:T(8,128)S(1)}, f32[16,16,512]{2,1,0:T(8,128)}, u32[]{:S(2)}) copy-start(f32[16,16,512]{2,1,0:T(8,128)} %x_ref.1) | copy-start | bytes 1572868
  2.9 34.0 %copy-start.4 = (bf16[6,80,160]{2,1,0:T(8,128)(2,1)S(1)}, bf16[6,80,160]{2,1,0:T(8,128)(2,1)}, u32[]{:S(2)}) copy-start(bf16[6,80,160]{2,1,0:T(8,128)(2,1)} %constant.14.clone.k_ref) | copy-start | bytes 460804
  2.9 34.0 %collective-permute-start = (f32[264,512]{1,0:T(8,128)S(1)}, f32[264,512]{1,0:T(8,128)S(1)}, u32[]{:S(2)}, u32[]{:S(2)}) collective-permute-start(f32[264,512]{1,0:T(8,128)S(1)} %get-tuple-element.13), channel_id=1, source_target_pairs={{0,32},{32,64},{64,96},{96,128},{128,160},{160,192},{192,224},{224... | collective-permute-start | bytes 1622024 | tf_op jit(solution)/shard_map/ppermute | solution.py:89
  7.1 29.8 %collective-permute-start.1 = (f32[264,512]{1,0:T(8,128)S(1)}, f32[264,512]{1,0:T(8,128)S(1)}, u32[]{:S(2)}, u32[]{:S(2)}) collective-permute-start(f32[264,512]{1,0:T(8,128)S(1)} %get-tuple-element.14), channel_id=1, source_target_pairs={{32,0},{64,32},{96,64},{128,96},{160,128},{192,160},{224,192},{256... | collective-permute-start | bytes 1622024 | tf_op jit(solution)/shard_map/ppermute | solution.py:89
  12.5 24.3 %collective-permute-start.3 = (f32[14,16,512]{2,1,0:T(8,128)S(1)}, f32[14,16,512]{2,1,0:T(8,128)S(1)}, u32[]{:S(2)}, u32[]{:S(2)}) collective-permute-start(f32[14,16,512]{2,1,0:T(8,128)S(1)} %get-tuple-element.24), channel_id=1, source_target_pairs={{64,0},{96,32},{128,64},{160,96},{192,128},{224,160},{256,192},{28... | collective-permute-start | bytes 1376264 | tf_op jit(solution)/shard_map/ppermute | solution.py:89
  14.9 22.0 %collective-permute-start.2 = (f32[14,16,512]{2,1,0:T(8,128)S(1)}, f32[14,16,512]{2,1,0:T(8,128)S(1)}, u32[]{:S(2)}, u32[]{:S(2)}) collective-permute-start(f32[14,16,512]{2,1,0:T(8,128)S(1)} %get-tuple-element.25), channel_id=1, source_target_pairs={{0,64},{32,96},{64,128},{96,160},{128,192},{160,224},{192,256},{22... | collective-permute-start | bytes 1376264 | tf_op jit(solution)/shard_map/ppermute | solution.py:89
  41.1 12.9 %collective-permute-start.4 = (f32[520,512]{1,0:T(8,128)S(1)}, f32[520,512]{1,0:T(8,128)S(1)}, u32[]{:S(2)}, u32[]{:S(2)}) collective-permute-start(f32[520,512]{1,0:T(8,128)S(1)} %get-tuple-element.18), channel_id=1, source_target_pairs={{0,1},{1,0},{2,3},{3,2},{4,5},{5,4},{6,7},{7,6},{8,9},{9,8},{10,11... | collective-permute-start | bytes 3194888 | tf_op jit(solution)/shard_map/ppermute | solution.py:507
  43.0 17.8 %collective-permute-start.5 = (f32[264,512]{1,0:T(8,128)S(1)}, f32[264,512]{1,0:T(8,128)S(1)}, u32[]{:S(2)}, u32[]{:S(2)}) collective-permute-start(f32[264,512]{1,0:T(8,128)S(1)} %get-tuple-element.19), channel_id=1, source_target_pairs={{1,3},{2,0},{3,5},{4,2},{5,7},{6,4},{7,9},{8,6},{9,11},{10,8},{11,... | collective-permute-start | bytes 1622024 | tf_op jit(solution)/shard_map/ppermute | solution.py:95
  54.0 12.8 %collective-permute-start.6 = (f32[264,512]{1,0:T(8,128)S(1)}, f32[264,512]{1,0:T(8,128)S(1)}, u32[]{:S(2)}, u32[]{:S(2)}) collective-permute-start(f32[264,512]{1,0:T(8,128)S(1)} %outward.1), channel_id=1, source_target_pairs={{1,2},{2,1},{3,4},{4,3},{5,6},{6,5},{7,8},{8,7},{9,10},{10,9},{11,... | collective-permute-start | bytes 1622024 | tf_op jit(solution)/shard_map/ppermute | solution.py:95

commit v7 on v6

--- a/solution.py
+++ b/solution.py
@@ -16,9 +16,10 @@
 TAPS = (1, 4, 6, 4, 1)
 BEYOND = 2
 VMEM_LIMIT = 20 * 1024 * 1024
-ROLES = ((2, 3, 4, 1, 0), (2, 1, 0, 3, 4))
+ROLES = ((2, 3, 1, 4, 0), (2, 1, 3, 0, 4))
 PIXELS = TILE * TILE
 PITCH = 24
+FIRST_ROWS = 256
 EXT = 512
 STEPS = (0.5, 0.002, 2.0)
 LAMS = (0.2, 0.5, 0.05)
@@ -103,32 +104,32 @@
     return spread_ref[:, row, :]
 
 
-def pack_kernel(cube_hbm, amp_ref, index_ref, spread_ref, up_ref, down_ref, sem):
+def pack_kernel(cube_hbm, amp_hbm, index_hbm, spread_hbm, out_ref, amp_ref, index_ref, spread_ref, sem):
+    pairs = ((amp_hbm, amp_ref), (index_hbm, index_ref), (spread_hbm, spread_ref), (cube_hbm, out_ref.at[0:PIXELS]))
+    copies = [pltpu.make_async_copy(a, b, sem.at[i]) for i, (a, b) in enumerate(pairs)]
+    for copy in copies:
+        copy.start()
     nch = cube_hbm.shape[1]
-    copies = []
-    for i, out in enumerate((up_ref, down_ref)):
-        copies.append(pltpu.make_async_copy(cube_hbm, out.at[0:PIXELS], sem.at[i]))
-        copies[-1].start()
-    for out, first in ((up_ref, TILE - 2), (down_ref, 0)):
-        out[PIXELS:, :] = jnp.zeros((COMPS, nch), jnp.float32)
+    out_ref[PIXELS:, :] = jnp.zeros((COMPS, nch), jnp.float32)
+    for copy in copies[:3]:
+        copy.wait()
+    for start, first in ((0, TILE - 2), (FIRST_ROWS, 0)):
         for t in range(3):
             for r in range(2):
-                lane = (2 * t + r) * PITCH + 2
+                lane = start + (2 * t + r) * PITCH + 2
                 got = own_row(t, first + r, amp_ref, index_ref, spread_ref, nch)
-                out[PIXELS:, lane : lane + TILE] = got
-    for copy in copies:
-        copy.wait()
+                out_ref[PIXELS:, lane : lane + TILE] = got
+    copies[3].wait()
 
 
 def packed(cube, amplitude, centre_index, spread):
-    vmem = pl.BlockSpec(memory_space=pltpu.VMEM)
     hbm = [pltpu.with_memory_space_constraint(v, pltpu.HBM) for v in (cube, amplitude, centre_index, spread)]
     return pl.pallas_call(
         pack_kernel,
-        out_shape=[pltpu.VMEM((PIXELS + COMPS, cube.shape[1]), jnp.float32)] * 2,
-        in_specs=[pl.BlockSpec(memory_space=pl.ANY)] + [vmem] * 3,
-        out_specs=[vmem] * 2,
-        scratch_shapes=[pltpu.SemaphoreType.DMA((2,))],
+        out_shape=pltpu.VMEM((PIXELS + COMPS, cube.shape[1]), jnp.float32),
+        in_specs=[pl.BlockSpec(memory_space=pl.ANY)] * 4,
+        out_specs=pl.BlockSpec(memory_space=pltpu.VMEM),
+        scratch_shapes=[pltpu.VMEM(v.shape, v.dtype) for v in hbm[1:]] + [pltpu.SemaphoreType.DMA((4,))],
         compiler_params=pltpu.CompilerParams(vmem_limit_bytes=VMEM_LIMIT),
         cost_estimate=pl.CostEstimate(flops=1000, bytes_accessed=1_000_000, transcendentals=0),
         name="pack",
@@ -158,7 +159,7 @@
     out = []
     for t in range(3):
         p = jnp.where(row < 2, pltpu.roll(above, (EXT - 2 * t * PITCH) % EXT, 1), own[t])
-        out.append(jnp.where(row >= TILE + 2, pltpu.roll(below, ((TILE + 2 - 2 * t) * PITCH) % EXT, 1), p))
+        out.append(jnp.where(row >= TILE + 2, pltpu.roll(below, ((TILE + 2 - 2 * t) * PITCH - FIRST_ROWS) % EXT, 1), p))
     return out
 
 
@@ -194,7 +195,7 @@
     a_ref, m1, p1, m2, p2, x_ref, k_ref, own_ref, w_ref,
     o_0, swap_ref, near_ref, far_ref, ext_ref, rows_ref, y_ref,
 ):
-    nch = x_ref.shape[2]
+    nch = x_ref.shape[1]
     tiles = (m2, m1, x_ref, p1, p2)
     iy, ix = lax.axis_index("skyy"), lax.axis_index("skyx")
     near = [iy + i for i in (-2, -1, 0, 1, 2)]
@@ -210,7 +211,7 @@
         def value(level, at):
             tile = (at + 2 * TILE) // TILE
             if level == 0:
-                if tile in (1, 3):
+                if tile in (1, 2, 3):
                     start = pl.multiple_of(at % TILE * TILE + step // lane_tiles * 8, 8)
                     return tiles[tile][pl.ds(start, 8), lane]
                 return tiles[tile][at % TILE - (BEYOND if tile == 0 else 0), sub, lane]
@@ -272,7 +273,7 @@
         got = jnp.dot(columns, y_ref[row], preferred_element_type=jnp.float32)
         at = pl.ds(pl.multiple_of(row * TILE, TILE), TILE)
         at_more = pl.ds(pl.multiple_of(row * TILE + PIXELS, TILE), TILE)
-        o_0[row] = got[:TILE] + a_ref[0] * x_ref[row]
+        o_0[row] = got[:TILE] + a_ref[0] * x_ref[at]
         swap_ref[at] = got[TILE : 2 * TILE]
         swap_ref[at_more] = got[2 * TILE : 3 * TILE]
         near_ref[at] = got[3 * TILE : 4 * TILE]
@@ -285,8 +286,8 @@
     for t in range(3):
         ext_ref[t] = params[t]
     to_right, to_left = border_columns(ext_ref, TILE), border_columns(ext_ref, 2)
-    swap_ref[2 * PIXELS :, :] = jnp.where(odd == 0, to_right, to_left)
-    near_ref[PIXELS:, :] = jnp.where(odd == 0, to_left, to_right)
+    swap_ref[2 * PIXELS : 2 * PIXELS + COMPS] = jnp.where(odd == 0, to_right, to_left)
+    swap_ref[2 * PIXELS + COMPS :] = jnp.where(odd == 0, to_left, to_right)
 
 
 def kept(x):
@@ -296,7 +297,8 @@
 def wavelet_parts(coeff, tiles, own, w, nch, length):
     k = jnp.asarray(scatter_matrices(length))
     vmem = pl.BlockSpec(memory_space=pltpu.VMEM)
-    shapes = [tiles[-1].shape] + [(n, nch) for n in (2 * PIXELS + COMPS, PIXELS + COMPS, PIXELS + COMPS)] + [own.shape]
+    heights = (2 * (PIXELS + COMPS), PIXELS, PIXELS + COMPS)
+    shapes = [(TILE, TILE, nch)] + [(n, nch) for n in heights] + [own.shape]
     return pl.pallas_call(
         wavelet_kernel,
         out_shape=[pltpu.VMEM(shape, jnp.float32) for shape in shapes],
@@ -320,14 +322,14 @@
         return carry
 
     lax.fori_loop(0, TILE, body, 0, unroll=4)
-    out_ref[PIXELS:, :] = near_ref[PIXELS:, :]
+    out_ref[PIXELS:, :] = swapped_ref[2 * PIXELS + COMPS :]
 
 
 def outward(near, swapped):
     vmem = pl.BlockSpec(memory_space=pltpu.VMEM)
     return pl.pallas_call(
         add_kernel,
-        out_shape=pltpu.VMEM(near.shape, jnp.float32),
+        out_shape=pltpu.VMEM((PIXELS + COMPS, near.shape[1]), jnp.float32),
         in_specs=[vmem] * 2,
         out_specs=vmem,
         compiler_params=pltpu.CompilerParams(vmem_limit_bytes=VMEM_LIMIT),
@@ -397,7 +399,7 @@
     rows = LANES // TILE
     parts = pixels // LANES
     copies = []
-    inner, outer = swapped_ref[2 * PIXELS :, :], near_ref[PIXELS:, :]
+    inner, outer = swapped_ref[2 * PIXELS : 2 * PIXELS + COMPS], near_ref[PIXELS:, :]
     even = lax.rem(lax.axis_index("skyx"), 2) == 0
     left, right = jnp.where(even, outer, inner), jnp.where(even, inner, outer)
     bases = smoothed(with_columns(ext_ref, left, right))
@@ -490,8 +492,8 @@
     size = lax.axis_size("skyx")
     partner = [(i, i ^ 1) for i in range(size)]
 
-    for_down, for_up = packed(cube.reshape(PIXELS, nch), amplitude, centre_index, spread)
-    up1, down1 = sent(for_down, "skyy", 1), sent(for_up, "skyy", -1)
+    tile = packed(cube.reshape(PIXELS, nch), amplitude, centre_index, spread)
+    up1, down1 = sent(tile, "skyy", 1), sent(tile, "skyy", -1)
     up2, down2 = sent(cube[BEYOND:], "skyy", 2), sent(cube[:-BEYOND], "skyy", -2)
 
     entries = jnp.arange(level_table.shape[0], dtype=jnp.int32)
@@ -502,11 +504,11 @@
     scale = jnp.array([16.0 ** (-3 * j) for j in range(LEVELS + 1)], jnp.float32)
     coeff = (coeff * scale[:, None])[:, None, :]
     model, flat, own, w = model_of(amplitude, centre_index, spread, nch)
-    o_0, swap, near, far, ext = wavelet_parts(coeff, (up1, down1, up2, down2, cube), own, w, nch, size * TILE)
+    o_0, swap, near, far, ext = wavelet_parts(coeff, (up1, down1, up2, down2, tile), own, w, nch, size * TILE)
 
     swapped = lax.ppermute(swap, "skyx", partner)
     far = away(far, "skyx", 2)
-    near = away(outward(near, swapped), "skyx", 1)
+    near = away(outward(near, swapped), "skyx", -2)
     return gradient_step((o_0, swapped, far, near), model, flat, ext)
 
 

time: 70.9 us -> 68.4 us (0.965)
  the two profiles are of different devices: /device:TPU:26 before, /device:TPU:38 now
where the time goes in v7:
time: 68.4 us; the launch traced here: 68 us
  starting transfers between devices  29.3 us (43%)
  waiting for transfers between devices  25.5 us (37%)
  Pallas kernels  11 us (16%)
  local copies, waits for them, and re-layouts  1.27 us (2%)
  between operations  0.84 us (1%)
    ppermute x4, starting transfers between devices, sent(): return lax.ppermute(values, axis, pairs)  14.2 us
    ppermute x4, waiting for transfers between devices, sent(): return lax.ppermute(values, axis, pairs)  14 us
    ppermute x2, starting transfers between devices, away(): lax.ppermute(values, axis, [(i, j) for i, j in pairs if 0 <= j < size])  13.1 us
    ppermute x2, waiting for transfers between devices, away(): lax.ppermute(values, axis, [(i, j) for i, j in pairs if 0 <= j < size])  11.4 us
    pallas_call x1, Pallas kernels, wavelet_parts(): pl.pallas_call(wavelet_kernel, out_shape=[pltpu.VMEM(shape, jnp.float32)...  4.19 us
    pallas_call x1, Pallas kernels, gradient_step(): pl.pallas_call(step_kernel, out_shape=[jax.ShapeDtypeStruct(shape, jnp.fl...  3.61 us
    ppermute x1, starting transfers between devices, on_device(): swapped = lax.ppermute(swap, 'skyx', partner)  1.92 us
    pallas_call x1, Pallas kernels, model_of(): pl.pallas_call(model_kernel, out_shape=[pltpu.VMEM((nch, pixels), jnp.flo...  1.85 us
  transfers between devices with their start and end apart: 7, of which 4 were waited for; matrix products, arithmetic and copies ran while one was open for 2% of the time, Pallas kernels for 3%

profile of v7, /device:TPU:38, one launch (start us, length us, event | category | flops | bytes accessed | tf_op | source)
XLA Modules:
  0.0 68.0 jit_solution(12834399982180280555)
XLA Ops:
  0.6 0.0 copy-start.6
  0.7 1.3 %pack.1.x_ref = f32[264,512]{1,0:T(8,128)S(1)} custom-call(f32[256,512]{1,0:T(8,128)} %bitcast.1, f32[8,16,16]{2,1,0:T(8,128)} %amp_ref.1, s32[8,16,16]{2,1,0:T(8,128)} %index_ref.1, f32[8,16,16]{2,1,0:T(8,128)} %spread_ref.1), custom_call_target="tpu_custom_call" | custom-call | flops 1000 | bytes 1000000 | tf_op jit(solution)/shard_map/pack/pallas_call | solution.py:127
  2.0 0.0 copy-start.3
  2.0 3.4 %collective-permute-start.1 = (f32[264,512]{1,0:T(8,128)S(1)}, f32[264,512]{1,0:T(8,128)S(1)}, u32[]{:S(2)}, u32[]{:S(2)}) collective-permute-start(f32[264,512]{1,0:T(8,128)S(1)} %pack.1.x_ref), channel_id=1, source_target_pairs={{32,0},{64,32},{96,64},{128,96},{160,128},{192,160},{224,192},{256... | collective-permute-start | bytes 1622024 | tf_op jit(solution)/shard_map/ppermute | solution.py:90
  5.4 4.9 %collective-permute-start = (f32[264,512]{1,0:T(8,128)S(1)}, f32[264,512]{1,0:T(8,128)S(1)}, u32[]{:S(2)}, u32[]{:S(2)}) collective-permute-start(f32[264,512]{1,0:T(8,128)S(1)} %pack.1.x_ref), channel_id=1, source_target_pairs={{0,32},{32,64},{64,96},{96,128},{128,160},{160,192},{192,224},{224... | collective-permute-start | bytes 1622024 | tf_op jit(solution)/shard_map/ppermute | solution.py:90
  10.4 1.2 %fusion = (f32[14,16,512]{2,1,0:T(8,128)S(1)}, f32[14,16,512]{2,1,0:T(8,128)S(1)}) fusion(f32[16,16,512]{2,1,0:T(8,128)} %param.9), kind=kLoop, calls=%fused_computation.3 | loop fusion | bytes 1835008 | tf_op jit(solution)/shard_map/slice | solution.py:497
  11.6 3.6 %collective-permute-start.3 = (f32[14,16,512]{2,1,0:T(8,128)S(1)}, f32[14,16,512]{2,1,0:T(8,128)S(1)}, u32[]{:S(2)}, u32[]{:S(2)}) collective-permute-start(f32[14,16,512]{2,1,0:T(8,128)S(1)} %get-tuple-element.20), channel_id=1, source_target_pairs={{64,0},{96,32},{128,64},{160,96},{192,128},{224,160},{256,192},{28... | collective-permute-start | bytes 1376264 | tf_op jit(solution)/shard_map/ppermute | solution.py:90
  15.2 2.3 %collective-permute-start.2 = (f32[14,16,512]{2,1,0:T(8,128)S(1)}, f32[14,16,512]{2,1,0:T(8,128)S(1)}, u32[]{:S(2)}, u32[]{:S(2)}) collective-permute-start(f32[14,16,512]{2,1,0:T(8,128)S(1)} %get-tuple-element.21), channel_id=1, source_target_pairs={{0,64},{32,96},{64,128},{96,160},{128,192},{160,224},{192,256},{22... | collective-permute-start | bytes 1376264 | tf_op jit(solution)/shard_map/ppermute | solution.py:90
  17.5 0.1 select_reduce_fusion
  17.6 0.1 subtract_multiply_fusion
  17.7 1.9 %gaussian_model.1 = (f32[512,256]{1,0:T(8,128)S(1)}, f32[3,8,256]{2,1,0:T(8,128)S(1)}, f32[3,8,512]{2,1,0:T(8,128)S(1)}, bf16[6,3,256,256]{3,2,1,0:T(8,128)(2,1)S(1)}) custom-call(f32[8,16,16]{2,1,0:T(8,128)S(1)} %copy-done, s32[8,16,16]{2,1,0:T(8,128)S(1)} %copy-done.1, f32[8,16,16]{2,1,0:T(8,128)S(1)} %copy-done.2, ...), custom_call_target="tpu_custom_call" | custom-call | flops 10000000 | bytes 1000000 | tf_op jit(solution)/shard_map/gaussian_model/pallas_call | solution.py:377
  19.5 5.6 %collective-permute-done.3.p2 = f32[14,16,512]{2,1,0:T(8,128)S(1)} collective-permute-done((f32[14,16,512]{2,1,0:T(8,128)S(1)}, f32[14,16,512]{2,1,0:T(8,128)S(1)}, u32[]{:S(2)}, u32[]{:S(2)}) %collective-permute-start.3) | collective-permute-done | bytes 458784 | tf_op jit(solution)/shard_map/ppermute | solution.py:90
  25.2 8.4 %collective-permute-done.2.m2 = f32[14,16,512]{2,1,0:T(8,128)S(1)} collective-permute-done((f32[14,16,512]{2,1,0:T(8,128)S(1)}, f32[14,16,512]{2,1,0:T(8,128)S(1)}, u32[]{:S(2)}, u32[]{:S(2)}) %collective-permute-start.2) | collective-permute-done | bytes 458784 | tf_op jit(solution)/shard_map/ppermute | solution.py:90
  33.6 0.0 collective-permute-done.1.p1
  33.6 0.0 collective-permute-done.m1
  33.6 4.2 %wavelet_parts.1 = (f32[16,16,512]{2,1,0:T(8,128)S(1)}, f32[528,512]{1,0:T(8,128)S(1)}, f32[256,512]{1,0:T(8,128)S(1)}, f32[264,512]{1,0:T(8,128)S(1)}, f32[3,8,512]{2,1,0:T(8,128)S(1)}) custom-call(f32[5,1,512]{2,1,0:T(1,128)S(1)} %broadcast_in_dim.2.a_ref, f32[264,512]{1,0:T(8,128)S(1)} %collective-permute-done.m1, ...), custom_call_target="tpu_custom_call" | custom-call | flops 4000000000 | bytes 9000000 | tf_op jit(solution)/shard_map/wavelet_parts/pallas_call | solution.py:302
  37.8 1.9 %collective-permute-start.4 = (f32[528,512]{1,0:T(8,128)S(1)}, f32[528,512]{1,0:T(8,128)S(1)}, u32[]{:S(2)}, u32[]{:S(2)}) collective-permute-start(f32[528,512]{1,0:T(8,128)S(1)} %get-tuple-element.14), channel_id=1, source_target_pairs={{0,1},{1,0},{2,3},{3,2},{4,5},{5,4},{6,7},{7,6},{8,9},{9,8},{10,11... | collective-permute-start | bytes 3244040 | tf_op jit(solution)/shard_map/ppermute | solution.py:509
  39.7 11.2 %collective-permute-start.5 = (f32[264,512]{1,0:T(8,128)S(1)}, f32[264,512]{1,0:T(8,128)S(1)}, u32[]{:S(2)}, u32[]{:S(2)}) collective-permute-start(f32[264,512]{1,0:T(8,128)S(1)} %get-tuple-element.15), channel_id=1, source_target_pairs={{1,3},{2,0},{3,5},{4,2},{5,7},{6,4},{7,9},{8,6},{9,11},{10,8},{11,... | collective-permute-start | bytes 1622024 | tf_op jit(solution)/shard_map/ppermute | solution.py:96
  50.9 0.0 collective-permute-done.4.swapped_ref
  51.0 0.1 outward.1
  51.1 1.9 %collective-permute-start.6 = (f32[264,512]{1,0:T(8,128)S(1)}, f32[264,512]{1,0:T(8,128)S(1)}, u32[]{:S(2)}, u32[]{:S(2)}) collective-permute-start(f32[264,512]{1,0:T(8,128)S(1)} %outward.1), channel_id=1, source_target_pairs={{0,2},{2,4},{3,1},{4,6},{5,3},{6,8},{7,5},{8,10},{9,7},{10,12},{11... | collective-permute-start | bytes 1622024 | tf_op jit(solution)/shard_map/ppermute | solution.py:96
  53.0 8.6 %collective-permute-done.5.far_ref = f32[264,512]{1,0:T(8,128)S(1)} collective-permute-done((f32[264,512]{1,0:T(8,128)S(1)}, f32[264,512]{1,0:T(8,128)S(1)}, u32[]{:S(2)}, u32[]{:S(2)}) %collective-permute-start.5) | collective-permute-done | bytes 540704 | tf_op jit(solution)/shard_map/ppermute | solution.py:96
  61.6 2.8 %collective-permute-done.6.near_ref = f32[264,512]{1,0:T(8,128)S(1)} collective-permute-done((f32[264,512]{1,0:T(8,128)S(1)}, f32[264,512]{1,0:T(8,128)S(1)}, u32[]{:S(2)}, u32[]{:S(2)}) %collective-permute-start.6) | collective-permute-done | bytes 540704 | tf_op jit(solution)/shard_map/ppermute | solution.py:96
  64.4 3.6 %gradient_step.1 = (f32[16,16,512]{2,1,0:T(8,128)}, f32[3,8,16,16]{3,2,1,0:T(8,128)}) custom-call(f32[16,16,512]{2,1,0:T(8,128)S(1)} %get-tuple-element.13.o_0, f32[528,512]{1,0:T(8,128)S(1)} %collective-permute-done.4.swapped_ref, f32[264,512]{1,0:T(8,128)S(1)} %collective-permute-done.5.far_ref, f32[264,512]{1,0:T(8,128)S(1)} %collective-permute-done.6.near_ref, ...), custom_call_target="tpu_custom_call" | custom-call | flops 15000000 | bytes 4000000 | tf_op jit(solution)/shard_map/gradient_step/pallas_call | solution.py:471
  (13 shorter events, 0.0 us)
Async XLA Ops:
  0.6 16.9 %copy-start.6 = (f32[5]{0:T(128)S(1)}, f32[5]{0:T(128)}, u32[]{:S(2)}) copy-start(f32[5]{0:T(128)} %constant.12.clone) | copy-start | bytes 64
  0.6 17.0 %copy-start.2 = (f32[8,16,16]{2,1,0:T(8,128)S(1)}, f32[8,16,16]{2,1,0:T(8,128)}, u32[]{:S(2)}) copy-start(f32[8,16,16]{2,1,0:T(8,128)} %spread_ref.1) | copy-start | bytes 24580
  0.7 17.0 %copy-start.1 = (s32[8,16,16]{2,1,0:T(8,128)S(1)}, s32[8,16,16]{2,1,0:T(8,128)}, u32[]{:S(2)}) copy-start(s32[8,16,16]{2,1,0:T(8,128)} %index_ref.1) | copy-start | bytes 24580
  0.7 17.0 %copy-start = (f32[8,16,16]{2,1,0:T(8,128)S(1)}, f32[8,16,16]{2,1,0:T(8,128)}, u32[]{:S(2)}) copy-start(f32[8,16,16]{2,1,0:T(8,128)} %amp_ref.1) | copy-start | bytes 24580
  0.7 16.8 %copy-start.4 = (s32[4,512]{1,0:T(4,128)S(1)}, s32[4,512]{1,0:T(4,128)}, u32[]{:S(2)}) copy-start(s32[4,512]{1,0:T(4,128)} %param.11) | copy-start | bytes 24580
  0.7 16.8 %copy-start.5 = (f32[16]{0:T(128)S(1)}, f32[16]{0:T(128)}, u32[]{:S(2)}) copy-start(f32[16]{0:T(128)} %param.10) | copy-start | bytes 196
  2.0 31.6 %copy-start.3 = (bf16[6,80,160]{2,1,0:T(8,128)(2,1)S(1)}, bf16[6,80,160]{2,1,0:T(8,128)(2,1)}, u32[]{:S(2)}) copy-start(bf16[6,80,160]{2,1,0:T(8,128)(2,1)} %constant.14.clone.k_ref) | copy-start | bytes 460804
  2.0 31.6 %collective-permute-start.1 = (f32[264,512]{1,0:T(8,128)S(1)}, f32[264,512]{1,0:T(8,128)S(1)}, u32[]{:S(2)}, u32[]{:S(2)}) collective-permute-start(f32[264,512]{1,0:T(8,128)S(1)} %pack.1.x_ref), channel_id=1, source_target_pairs={{32,0},{64,32},{96,64},{128,96},{160,128},{192,160},{224,192},{256... | collective-permute-start | bytes 1622024 | tf_op jit(solution)/shard_map/ppermute | solution.py:90
  5.4 28.2 %collective-permute-start = (f32[264,512]{1,0:T(8,128)S(1)}, f32[264,512]{1,0:T(8,128)S(1)}, u32[]{:S(2)}, u32[]{:S(2)}) collective-permute-start(f32[264,512]{1,0:T(8,128)S(1)} %pack.1.x_ref), channel_id=1, source_target_pairs={{0,32},{32,64},{64,96},{96,128},{128,160},{160,192},{192,224},{224... | collective-permute-start | bytes 1622024 | tf_op jit(solution)/shard_map/ppermute | solution.py:90
  11.6 13.6 %collective-permute-start.3 = (f32[14,16,512]{2,1,0:T(8,128)S(1)}, f32[14,16,512]{2,1,0:T(8,128)S(1)}, u32[]{:S(2)}, u32[]{:S(2)}) collective-permute-start(f32[14,16,512]{2,1,0:T(8,128)S(1)} %get-tuple-element.20), channel_id=1, source_target_pairs={{64,0},{96,32},{128,64},{160,96},{192,128},{224,160},{256,192},{28... | collective-permute-start | bytes 1376264 | tf_op jit(solution)/shard_map/ppermute | solution.py:90
  15.2 18.4 %collective-permute-start.2 = (f32[14,16,512]{2,1,0:T(8,128)S(1)}, f32[14,16,512]{2,1,0:T(8,128)S(1)}, u32[]{:S(2)}, u32[]{:S(2)}) collective-permute-start(f32[14,16,512]{2,1,0:T(8,128)S(1)} %get-tuple-element.21), channel_id=1, source_target_pairs={{0,64},{32,96},{64,128},{96,160},{128,192},{160,224},{192,256},{22... | collective-permute-start | bytes 1376264 | tf_op jit(solution)/shard_map/ppermute | solution.py:90
  37.8 13.2 %collective-permute-start.4 = (f32[528,512]{1,0:T(8,128)S(1)}, f32[528,512]{1,0:T(8,128)S(1)}, u32[]{:S(2)}, u32[]{:S(2)}) collective-permute-start(f32[528,512]{1,0:T(8,128)S(1)} %get-tuple-element.14), channel_id=1, source_target_pairs={{0,1},{1,0},{2,3},{3,2},{4,5},{5,4},{6,7},{7,6},{8,9},{9,8},{10,11... | collective-permute-start | bytes 3244040 | tf_op jit(solution)/shard_map/ppermute | solution.py:509
  39.7 21.9 %collective-permute-start.5 = (f32[264,512]{1,0:T(8,128)S(1)}, f32[264,512]{1,0:T(8,128)S(1)}, u32[]{:S(2)}, u32[]{:S(2)}) collective-permute-start(f32[264,512]{1,0:T(8,128)S(1)} %get-tuple-element.15), channel_id=1, source_target_pairs={{1,3},{2,0},{3,5},{4,2},{5,7},{6,4},{7,9},{8,6},{9,11},{10,8},{11,... | collective-permute-start | bytes 1622024 | tf_op jit(solution)/shard_map/ppermute | solution.py:96
  51.1 13.4 %collective-permute-start.6 = (f32[264,512]{1,0:T(8,128)S(1)}, f32[264,512]{1,0:T(8,128)S(1)}, u32[]{:S(2)}, u32[]{:S(2)}) collective-permute-start(f32[264,512]{1,0:T(8,128)S(1)} %outward.1), channel_id=1, source_target_pairs={{0,2},{2,4},{3,1},{4,6},{5,3},{6,8},{7,5},{8,10},{9,7},{10,12},{11... | collective-permute-start | bytes 1622024 | tf_op jit(solution)/shard_map/ppermute | solution.py:96

commit v8 on v7

--- a/solution.py
+++ b/solution.py
@@ -16,11 +16,12 @@
 TAPS = (1, 4, 6, 4, 1)
 BEYOND = 2
 VMEM_LIMIT = 20 * 1024 * 1024
-ROLES = ((2, 3, 1, 4, 0), (2, 1, 3, 0, 4))
+ROLES = ((3, 1, 0, 2, 4), (1, 3, 4, 2, 0))
 PIXELS = TILE * TILE
-PITCH = 24
-FIRST_ROWS = 256
-EXT = 512
+PITCH = TILE
+EXT = 384
+OWN = 2 * PITCH
+FIRST_ROWS = 128
 STEPS = (0.5, 0.002, 2.0)
 LAMS = (0.2, 0.5, 0.05)
 
@@ -116,7 +117,7 @@
     for start, first in ((0, TILE - 2), (FIRST_ROWS, 0)):
         for t in range(3):
             for r in range(2):
-                lane = start + (2 * t + r) * PITCH + 2
+                lane = start + (2 * t + r) * PITCH
                 got = own_row(t, first + r, amp_ref, index_ref, spread_ref, nch)
                 out_ref[PIXELS:, lane : lane + TILE] = got
     copies[3].wait()
@@ -145,15 +146,6 @@
     return total
 
 
-def with_columns(own, left, right):
-    column = lax.broadcasted_iota(jnp.int32, (COMPS, EXT), 1) % PITCH
-    out = []
-    for t in range(3):
-        p = jnp.where(column < 2, pltpu.roll(left, (EXT - 2 * t) % EXT, 1), own[t])
-        out.append(jnp.where(column >= TILE + 2, pltpu.roll(right, (TILE + 2 - 2 * t) % EXT, 1), p))
-    return out
-
-
 def with_rows(own, above, below):
     row = lax.broadcasted_iota(jnp.int32, (COMPS, EXT), 1) // PITCH
     out = []
@@ -163,21 +155,33 @@
     return out
 
 
-def stencil(p):
-    near = pltpu.roll(p, 1, 1) + pltpu.roll(p, EXT - 1, 1)
-    return 4.0 * p - (near + (pltpu.roll(p, PITCH, 1) + pltpu.roll(p, EXT - PITCH, 1)))
-
-
-def smoothed(params):
+def up_and_down(p):
+    return pltpu.roll(p, PITCH, 1) + pltpu.roll(p, EXT - PITCH, 1)
+
+
+def smoothed(params, left, right):
     lane = lax.broadcasted_iota(jnp.int32, (COMPS, EXT), 1)
+    column = lane % PITCH
+    at_left, at_right = column == 0, column == TILE - 1
     y = lane // PITCH + (lax.axis_index("skyy") * TILE - 2)
-    x = lane % PITCH + (lax.axis_index("skyx") * TILE - 2)
-    ny, nx = lax.axis_size("skyy") * TILE, lax.axis_size("skyx") * TILE
-    on_sky = (y >= 0) & (y < ny) & (x >= 0) & (x < nx)
+    on_sky = (y >= 0) & (y < lax.axis_size("skyy") * TILE)
+    ix = lax.axis_index("skyx")
+    beside = on_sky & ((at_left & (ix > 0)) | (at_right & (ix < lax.axis_size("skyx") - 1)))
+
+    def laplacian(p, side):
+        before = jnp.where(at_left, side, pltpu.roll(p, 1, 1))
+        after = jnp.where(at_right, side, pltpu.roll(p, EXT - 1, 1))
+        return 4.0 * p - ((before + after) + up_and_down(p))
+
     out = []
     for t, p in enumerate(params):
-        first = jnp.where(on_sky, stencil(p), 0.0)
-        out.append(p - (STEPS[t] * LAMS[t]) * stencil(first))
+        lefts = [pltpu.roll(left, (EXT - 2 * t - 1 + i) % EXT, 1) for i in range(2)]
+        rights = [pltpu.roll(right, (TILE - 1 - 2 * t - i) % EXT, 1) for i in range(2)]
+        one, two = [jnp.where(at_left, a, b) for a, b in zip(lefts, rights)]
+        first = jnp.where(on_sky, laplacian(p, one), 0.0)
+        first_beside = jnp.where(beside, 4.0 * one - ((two + p) + up_and_down(one)), 0.0)
+        new = p - (STEPS[t] * LAMS[t]) * laplacian(first, first_beside)
+        out.append(pltpu.roll(new, EXT - OWN, 1)[:, :PIXELS])
     return out
 
 
@@ -191,9 +195,39 @@
     return high, (v - high.astype(jnp.float32)).astype(jnp.bfloat16)
 
 
+def column_kind():
+    ix = lax.axis_index("skyx")
+    kind = jnp.where(ix == 0, 0, jnp.where(ix == lax.axis_size("skyx") - 1, 2, 1))
+    return 2 * kind + lax.rem(ix, 2)
+
+
+def own_kernel(a_ref, x_ref, k_ref, y_ref, _, o_0):
+    columns = k_ref[column_kind(), 3 * TILE : 4 * TILE]
+
+    def column_pass(row, carry):
+        got = jnp.dot(columns, y_ref[row], preferred_element_type=jnp.float32)
+        o_0[row] = got + a_ref[0] * x_ref[pl.ds(pl.multiple_of(row * TILE, TILE), TILE)]
+        return carry
+
+    lax.fori_loop(0, TILE, column_pass, 0, unroll=4)
+
+
+def own_part(coeff, tile, k, y, after, nch):
+    vmem = pl.BlockSpec(memory_space=pltpu.VMEM)
+    return pl.pallas_call(
+        own_kernel,
+        out_shape=pltpu.VMEM((TILE, TILE, nch), jnp.float32),
+        in_specs=[vmem] * 4 + [pl.BlockSpec(memory_space=pl.ANY)],
+        out_specs=vmem,
+        compiler_params=pltpu.CompilerParams(vmem_limit_bytes=VMEM_LIMIT),
+        cost_estimate=pl.CostEstimate(flops=100_000_000, bytes_accessed=500_000, transcendentals=0),
+        name="own_part",
+    )(*[kept(x) for x in (coeff, tile, k, y, after)])
+
+
 def wavelet_kernel(
     a_ref, m1, p1, m2, p2, x_ref, k_ref, own_ref, w_ref,
-    o_0, swap_ref, near_ref, far_ref, ext_ref, rows_ref, y_ref,
+    swap_ref, far_ref, ext_ref, y_ref, rows_ref,
 ):
     nch = x_ref.shape[1]
     tiles = (m2, m1, x_ref, p1, p2)
@@ -265,80 +299,76 @@
                 at = (level + 6) * TILE
                 y_ref[:, at : at + TILE, lane] = high
 
-    kind = jnp.where(ix == 0, 0, jnp.where(ix == lax.axis_size("skyx") - 1, 2, 1))
     odd = lax.rem(ix, 2)
-    columns = k_ref[2 * kind + odd]
+    columns = k_ref[column_kind(), : 3 * TILE]
 
     def column_pass(row, carry):
         got = jnp.dot(columns, y_ref[row], preferred_element_type=jnp.float32)
         at = pl.ds(pl.multiple_of(row * TILE, TILE), TILE)
         at_more = pl.ds(pl.multiple_of(row * TILE + PIXELS, TILE), TILE)
-        o_0[row] = got[:TILE] + a_ref[0] * x_ref[at]
-        swap_ref[at] = got[TILE : 2 * TILE]
-        swap_ref[at_more] = got[2 * TILE : 3 * TILE]
-        near_ref[at] = got[3 * TILE : 4 * TILE]
-        far_ref[at] = got[4 * TILE :]
+        swap_ref[at] = got[:TILE]
+        swap_ref[at_more] = got[TILE : 2 * TILE]
+        far_ref[at] = got[2 * TILE :]
         return carry
 
     lax.fori_loop(0, TILE, column_pass, 0, unroll=4)
 
-    params = with_rows(own_ref, m1[PIXELS:, :], p1[PIXELS:, :])
+    params = with_rows(own_ref, m1[PIXELS:, :EXT], p1[PIXELS:, :EXT])
     for t in range(3):
         ext_ref[t] = params[t]
-    to_right, to_left = border_columns(ext_ref, TILE), border_columns(ext_ref, 2)
-    swap_ref[2 * PIXELS : 2 * PIXELS + COMPS] = jnp.where(odd == 0, to_right, to_left)
-    swap_ref[2 * PIXELS + COMPS :] = jnp.where(odd == 0, to_left, to_right)
+    to_right, to_left = border_columns(ext_ref, TILE - 2), border_columns(ext_ref, 0)
+    swap_ref[2 * PIXELS : 2 * PIXELS + COMPS, :EXT] = jnp.where(odd == 0, to_right, to_left)
+    swap_ref[2 * PIXELS + COMPS :, :EXT] = jnp.where(odd == 0, to_left, to_right)
 
 
 def kept(x):
     return pltpu.with_memory_space_constraint(x, pltpu.VMEM)
 
 
-def wavelet_parts(coeff, tiles, own, w, nch, length):
-    k = jnp.asarray(scatter_matrices(length))
+def wavelet_parts(coeff, tiles, k, own, w, nch):
     vmem = pl.BlockSpec(memory_space=pltpu.VMEM)
-    heights = (2 * (PIXELS + COMPS), PIXELS, PIXELS + COMPS)
-    shapes = [(TILE, TILE, nch)] + [(n, nch) for n in heights] + [own.shape]
+    shapes = [(2 * (PIXELS + COMPS), nch), (PIXELS + COMPS, nch), own.shape]
+    outs = [pltpu.VMEM(shape, jnp.float32) for shape in shapes]
     return pl.pallas_call(
         wavelet_kernel,
-        out_shape=[pltpu.VMEM(shape, jnp.float32) for shape in shapes],
+        out_shape=outs + [pltpu.VMEM((TILE, 10 * TILE, nch), jnp.bfloat16)],
         in_specs=[vmem] * 9,
-        out_specs=[vmem] * 5,
-        scratch_shapes=[
-            pltpu.VMEM((LEVELS, TILE, TILE, nch), jnp.float32),
-            pltpu.VMEM((TILE, 10 * TILE, nch), jnp.bfloat16),
-        ],
+        out_specs=[vmem] * 4,
+        scratch_shapes=[pltpu.VMEM((LEVELS, TILE, TILE, nch), jnp.float32)],
         compiler_params=pltpu.CompilerParams(vmem_limit_bytes=VMEM_LIMIT),
         cost_estimate=pl.CostEstimate(flops=4_000_000_000, bytes_accessed=9_000_000, transcendentals=0),
         name="wavelet_parts",
     )(*[kept(x) for x in (coeff, *tiles, k, own, w)])
 
 
-def add_kernel(near_ref, swapped_ref, out_ref):
-    def body(row, carry):
+def outward_kernel(k_ref, y_ref, swapped_ref, out_ref):
+    columns = k_ref[column_kind(), 4 * TILE :]
+
+    def column_pass(row, carry):
+        got = jnp.dot(columns, y_ref[row], preferred_element_type=jnp.float32)
         at = pl.ds(pl.multiple_of(row * TILE, TILE), TILE)
         more = pl.ds(pl.multiple_of(row * TILE + PIXELS, TILE), TILE)
-        out_ref[at] = near_ref[at] + swapped_ref[more]
+        out_ref[at] = got + swapped_ref[more]
         return carry
 
-    lax.fori_loop(0, TILE, body, 0, unroll=4)
+    lax.fori_loop(0, TILE, column_pass, 0, unroll=4)
     out_ref[PIXELS:, :] = swapped_ref[2 * PIXELS + COMPS :]
 
 
-def outward(near, swapped):
+def outward(k, y, swapped):
     vmem = pl.BlockSpec(memory_space=pltpu.VMEM)
     return pl.pallas_call(
-        add_kernel,
-        out_shape=pltpu.VMEM((PIXELS + COMPS, near.shape[1]), jnp.float32),
-        in_specs=[vmem] * 2,
+        outward_kernel,
+        out_shape=pltpu.VMEM((PIXELS + COMPS, swapped.shape[1]), jnp.float32),
+        in_specs=[vmem] * 3,
         out_specs=vmem,
         compiler_params=pltpu.CompilerParams(vmem_limit_bytes=VMEM_LIMIT),
         cost_estimate=pl.CostEstimate(flops=100_000, bytes_accessed=1_500_000, transcendentals=0),
         name="outward",
-    )(kept(near), kept(swapped))
-
-
-def model_kernel(amp_ref, index_ref, spread_ref, w_hbm, model_ref, flat_ref, own_ref, w_ref, scale_ref, sem):
+    )(*[kept(x) for x in (k, y, swapped)])
+
+
+def model_kernel(amp_ref, index_ref, spread_ref, w_hbm, model_ref, flat_ref, own_ref, w_ref, bump_ref, scale_ref, sem):
     load = pltpu.make_async_copy(w_hbm, w_ref, sem)
     load.start()
     nch, pixels = model_ref.shape
@@ -346,7 +376,7 @@
     for t in range(3):
         for row in range(TILE):
             got = own_row(t, row, amp_ref, index_ref, spread_ref, nch)
-            at = (row + 2) * PITCH + 2
+            at = (row + 2) * PITCH
             own_ref[t, :, at : at + TILE] = got
             flat_ref[t, :, row * TILE : (row + 1) * TILE] = got
     mu = flat_ref[1] * float(nch)
@@ -362,6 +392,7 @@
         for k in range(COMPS):
             diff = chan - flat_ref[1, k : k + 1, :]
             bump = jnp.exp2(diff * diff * scale_ref[k : k + 1, :])
+            bump_ref[k, pl.ds(base, 8), :] = bump
             total += flat_ref[0, k : k + 1, :] * bump
         model_ref[pl.ds(base, 8), :] = total
         return carry
@@ -381,9 +412,10 @@
             pltpu.VMEM((3, COMPS, pixels), jnp.float32),
             pltpu.VMEM((3, COMPS, EXT), jnp.float32),
             pltpu.VMEM(w.shape, w.dtype),
+            pltpu.VMEM((COMPS, nch, pixels), jnp.float32),
         ],
         in_specs=[vmem] * 3 + [pl.BlockSpec(memory_space=pl.ANY)],
-        out_specs=[vmem] * 4,
+        out_specs=[vmem] * 5,
         scratch_shapes=[pltpu.VMEM((COMPS, pixels), jnp.float32), pltpu.SemaphoreType.DMA],
         compiler_params=pltpu.CompilerParams(vmem_limit_bytes=VMEM_LIMIT),
         cost_estimate=pl.CostEstimate(flops=10_000_000, bytes_accessed=1_000_000, transcendentals=1_100_000),
@@ -392,17 +424,17 @@
 
 
 def step_kernel(
-    o_0, swapped_ref, far_ref, near_ref, model_ref, flat_ref, ext_ref,
+    o_0, swapped_ref, far_ref, near_ref, model_ref, bump_ref, flat_ref, ext_ref,
     den_hbm, fit_ref, den_ref, r_ref, sem,
 ):
     nch, pixels = model_ref.shape
     rows = LANES // TILE
     parts = pixels // LANES
     copies = []
-    inner, outer = swapped_ref[2 * PIXELS : 2 * PIXELS + COMPS], near_ref[PIXELS:, :]
+    inner, outer = swapped_ref[2 * PIXELS : 2 * PIXELS + COMPS, :EXT], near_ref[PIXELS:, :EXT]
     even = lax.rem(lax.axis_index("skyx"), 2) == 0
     left, right = jnp.where(even, outer, inner), jnp.where(even, inner, outer)
-    bases = smoothed(with_columns(ext_ref, left, right))
+    bases = smoothed([ext_ref[t] for t in range(3)], left, right)
     for part in range(parts):
         at = slice(part * rows, (part + 1) * rows)
         for row in range(part * rows, (part + 1) * rows):
@@ -424,17 +456,15 @@
         for first in range(0, COMPS, 4):
             chosen = range(first, first + 4)
             mus = [jnp.broadcast_to(flat_ref[1, k : k + 1, at], (8, LANES)) for k in chosen]
-            inv = [jnp.broadcast_to(flat_ref[2, k : k + 1, at], (8, LANES)) for k in chosen]
-            scales = [(-0.5 * math.log2(math.e)) * v * v for v in inv]
 
             def body(step, carry):
                 base = pl.multiple_of(step * 8, 8)
                 chan = (lax.broadcasted_iota(jnp.int32, (8, LANES), 0) + base).astype(jnp.float32)
                 r = r_ref[pl.ds(base, 8), at]
                 out = []
-                for mu, scale, (a, b, c) in zip(mus, scales, carry):
+                for k, mu, (a, b, c) in zip(chosen, mus, carry):
                     diff = chan - mu
-                    one = r * jnp.exp2(diff * diff * scale)
+                    one = r * bump_ref[k, pl.ds(base, 8), at]
                     two = one * diff
                     out.append((a + one, b + two, c + two * diff))
                 return tuple(out)
@@ -453,9 +483,7 @@
             jnp.concatenate(sums[2], axis=0) * (slope * inv * (1.0 / nch)),
         )
         for t in range(3):
-            lanes = [(part * rows + i + 2) * PITCH + 2 for i in range(rows)]
-            base = jnp.concatenate([bases[t][:, lane : lane + TILE] for lane in lanes], axis=1)
-            new = base - STEPS[t] * grads[t]
+            new = bases[t][:, at] - STEPS[t] * grads[t]
             spread_out = jnp.where(own_lanes, jnp.broadcast_to(new[:, None, :], own_lanes.shape), 0.0)
             for shift in (LANES // 2, LANES // 4, LANES // 8):
                 spread_out = spread_out + pltpu.roll(spread_out, shift, 2)
@@ -465,7 +493,7 @@
         copy.wait()
 
 
-def gradient_step(parts, model, flat, ext):
+def gradient_step(parts, model, bump, flat, ext):
     vmem = pl.BlockSpec(memory_space=pltpu.VMEM)
     shape = parts[0].shape
     return pl.pallas_call(
@@ -474,7 +502,7 @@
             jax.ShapeDtypeStruct(shape, jnp.float32),
             jax.ShapeDtypeStruct((3, COMPS, TILE, TILE), jnp.float32),
         ],
-        in_specs=[vmem] * 7,
+        in_specs=[vmem] * 8,
         out_specs=[pl.BlockSpec(memory_space=pl.ANY), vmem],
         scratch_shapes=[
             pltpu.VMEM(shape, jnp.float32),
@@ -484,7 +512,7 @@
         compiler_params=pltpu.CompilerParams(vmem_limit_bytes=VMEM_LIMIT),
         cost_estimate=pl.CostEstimate(flops=15_000_000, bytes_accessed=4_000_000, transcendentals=1_100_000),
         name="gradient_step",
-    )(*[kept(x) for x in (*parts, model, flat, ext)])
+    )(*[kept(x) for x in (*parts, model, bump, flat, ext)])
 
 
 def on_device(cube, level_table, level_index, amplitude, centre_index, spread):
@@ -503,13 +531,16 @@
     coeff = jnp.concatenate([weight, one]) - jnp.concatenate([0.0 * one, weight])
     scale = jnp.array([16.0 ** (-3 * j) for j in range(LEVELS + 1)], jnp.float32)
     coeff = (coeff * scale[:, None])[:, None, :]
-    model, flat, own, w = model_of(amplitude, centre_index, spread, nch)
-    o_0, swap, near, far, ext = wavelet_parts(coeff, (up1, down1, up2, down2, tile), own, w, nch, size * TILE)
+    model, flat, own, w, bump = model_of(amplitude, centre_index, spread, nch)
+    k = jnp.asarray(scatter_matrices(size * TILE))
+    swap, far, ext, y = wavelet_parts(coeff, (up1, down1, up2, down2, tile), k, own, w, nch)
 
     swapped = lax.ppermute(swap, "skyx", partner)
     far = away(far, "skyx", 2)
-    near = away(outward(near, swapped), "skyx", -2)
-    return gradient_step((o_0, swapped, far, near), model, flat, ext)
+    total = outward(k, y, swapped)
+    near = away(total, "skyx", -2)
+    o_0 = own_part(coeff, tile, k, y, total, nch)
+    return gradient_step((o_0, swapped, far, near), model, bump, flat, ext)
 
 
 def solution(mesh):

time: 68.4 us -> 68.4 us (level)
  Pallas kernels: 11 us -> 11.7 us
  waiting for transfers between devices: 25.5 us -> 24.8 us
    pallas_call x2 -> x3, Pallas kernels: 4.29 us -> 5.76 us  [the longest x1 4.14 us: wavelet_parts(): pl.pallas_call(wavelet_kernel, out_shape=outs + [pltpu.VMEM((TILE, 10 * T...]
    ppermute x2, waiting for transfers between devices: 11.4 us -> 10.6 us  [away(): lax.ppermute(values, axis, [(i, j) for i, j in pairs if 0 <= j < size])]
  transfers between devices with their start and end apart: 7 -> 7, of which waited for: 4 -> 4; matrix products, arithmetic and copies ran while one was open for 2% -> 2% of each run, Pallas kernels for 3% -> 5%
where the time goes in v8:
time: 68.4 us; the launch traced here: 68.1 us
  starting transfers between devices  29.3 us (43%)
  waiting for transfers between devices  24.8 us (36%)
  Pallas kernels  11.7 us (17%)
  local copies, waits for them, and re-layouts  1.29 us (2%)
  between operations  0.83 us (1%)
    ppermute x4, starting transfers between devices, sent(): return lax.ppermute(values, axis, pairs)  14.2 us
    ppermute x4, waiting for transfers between devices, sent(): return lax.ppermute(values, axis, pairs)  14.1 us
    ppermute x2, starting transfers between devices, away(): lax.ppermute(values, axis, [(i, j) for i, j in pairs if 0 <= j < size])  13.1 us
    ppermute x2, waiting for transfers between devices, away(): lax.ppermute(values, axis, [(i, j) for i, j in pairs if 0 <= j < size])  10.6 us
    pallas_call x1, Pallas kernels, wavelet_parts(): pl.pallas_call(wavelet_kernel, out_shape=outs + [pltpu.VMEM((TILE, 10 * T...  4.14 us
    pallas_call x1, Pallas kernels, gradient_step(): pl.pallas_call(step_kernel, out_shape=[jax.ShapeDtypeStruct(shape, jnp.fl...  2.99 us
    ppermute x1, starting transfers between devices, on_device(): swapped = lax.ppermute(swap, 'skyx', partner)  1.92 us
    pallas_call x1, Pallas kernels, model_of(): pl.pallas_call(model_kernel, out_shape=[pltpu.VMEM((nch, pixels), jnp.flo...  1.72 us
  transfers between devices with their start and end apart: 7, of which 4 were waited for; matrix products, arithmetic and copies ran while one was open for 2% of the time, Pallas kernels for 5%

profile of v8, /device:TPU:38, one launch (start us, length us, event | category | flops | bytes accessed | tf_op | source)
XLA Modules:
  0.0 68.1 jit_solution(15043024357733301915)
XLA Ops:
  0.6 0.0 copy-start.6
  0.7 1.3 %pack.1.x_ref = f32[264,512]{1,0:T(8,128)S(1)} custom-call(f32[256,512]{1,0:T(8,128)} %bitcast.1, f32[8,16,16]{2,1,0:T(8,128)} %amp_ref.1, s32[8,16,16]{2,1,0:T(8,128)} %index_ref.1, f32[8,16,16]{2,1,0:T(8,128)} %spread_ref.1), custom_call_target="tpu_custom_call" | custom-call | flops 1000 | bytes 1000000 | tf_op jit(solution)/shard_map/pack/pallas_call | solution.py:128
  2.0 0.0 copy-start
  2.0 3.4 %collective-permute-start.1 = (f32[264,512]{1,0:T(8,128)S(1)}, f32[264,512]{1,0:T(8,128)S(1)}, u32[]{:S(2)}, u32[]{:S(2)}) collective-permute-start(f32[264,512]{1,0:T(8,128)S(1)} %pack.1.x_ref), channel_id=1, source_target_pairs={{32,0},{64,32},{96,64},{128,96},{160,128},{192,160},{224,192},{256... | collective-permute-start | bytes 1622024 | tf_op jit(solution)/shard_map/ppermute | solution.py:91
  5.4 4.9 %collective-permute-start = (f32[264,512]{1,0:T(8,128)S(1)}, f32[264,512]{1,0:T(8,128)S(1)}, u32[]{:S(2)}, u32[]{:S(2)}) collective-permute-start(f32[264,512]{1,0:T(8,128)S(1)} %pack.1.x_ref), channel_id=1, source_target_pairs={{0,32},{32,64},{64,96},{96,128},{128,160},{160,192},{192,224},{224... | collective-permute-start | bytes 1622024 | tf_op jit(solution)/shard_map/ppermute | solution.py:91
  10.4 1.2 %fusion = (f32[14,16,512]{2,1,0:T(8,128)S(1)}, f32[14,16,512]{2,1,0:T(8,128)S(1)}) fusion(f32[16,16,512]{2,1,0:T(8,128)} %param.9), kind=kLoop, calls=%fused_computation.3 | loop fusion | bytes 1835008 | tf_op jit(solution)/shard_map/slice | solution.py:525
  11.6 3.6 %collective-permute-start.3 = (f32[14,16,512]{2,1,0:T(8,128)S(1)}, f32[14,16,512]{2,1,0:T(8,128)S(1)}, u32[]{:S(2)}, u32[]{:S(2)}) collective-permute-start(f32[14,16,512]{2,1,0:T(8,128)S(1)} %get-tuple-element.20), channel_id=1, source_target_pairs={{64,0},{96,32},{128,64},{160,96},{192,128},{224,160},{256,192},{28... | collective-permute-start | bytes 1376264 | tf_op jit(solution)/shard_map/ppermute | solution.py:91
  15.2 2.3 %collective-permute-start.2 = (f32[14,16,512]{2,1,0:T(8,128)S(1)}, f32[14,16,512]{2,1,0:T(8,128)S(1)}, u32[]{:S(2)}, u32[]{:S(2)}) collective-permute-start(f32[14,16,512]{2,1,0:T(8,128)S(1)} %get-tuple-element.21), channel_id=1, source_target_pairs={{0,64},{32,96},{64,128},{96,160},{128,192},{160,224},{192,256},{22... | collective-permute-start | bytes 1376264 | tf_op jit(solution)/shard_map/ppermute | solution.py:91
  17.5 0.1 select_reduce_fusion
  17.6 0.1 subtract_multiply_fusion
  17.7 1.7 %gaussian_model.1 = (f32[512,256]{1,0:T(8,128)S(1)}, f32[3,8,256]{2,1,0:T(8,128)S(1)}, f32[3,8,384]{2,1,0:T(8,128)S(1)}, bf16[6,3,256,256]{3,2,1,0:T(8,128)(2,1)S(1)}, f32[8,512,256]{2,1,0:T(8,128)S(1)}) custom-call(f32[8,16,16]{2,1,0:T(8,128)S(1)} %copy-done.1, s32[8,16,16]{2,1,0:T(8,128)S(1)} %copy-done.2, f32[8,16,16]{2,1,0:T(8,128)S(1)} %copy-done.3, ...), custom_call_target="tpu_custom_call" | custom-call | flops 10000000 | bytes 1000000 | tf_op jit(solution)/shard_map/gaussian_model/pallas_call | solution.py:408
  19.4 5.8 %collective-permute-done.3.p2 = f32[14,16,512]{2,1,0:T(8,128)S(1)} collective-permute-done((f32[14,16,512]{2,1,0:T(8,128)S(1)}, f32[14,16,512]{2,1,0:T(8,128)S(1)}, u32[]{:S(2)}, u32[]{:S(2)}) %collective-permute-start.3) | collective-permute-done | bytes 458784 | tf_op jit(solution)/shard_map/ppermute | solution.py:91
  25.2 8.4 %collective-permute-done.2.m2 = f32[14,16,512]{2,1,0:T(8,128)S(1)} collective-permute-done((f32[14,16,512]{2,1,0:T(8,128)S(1)}, f32[14,16,512]{2,1,0:T(8,128)S(1)}, u32[]{:S(2)}, u32[]{:S(2)}) %collective-permute-start.2) | collective-permute-done | bytes 458784 | tf_op jit(solution)/shard_map/ppermute | solution.py:91
  33.6 0.0 collective-permute-done.1.p1
  33.6 0.0 collective-permute-done.m1
  33.6 4.1 %wavelet_parts.1 = (f32[528,512]{1,0:T(8,128)S(1)}, f32[264,512]{1,0:T(8,128)S(1)}, f32[3,8,384]{2,1,0:T(8,128)S(1)}, bf16[16,160,512]{2,1,0:T(8,128)(2,1)S(1)}) custom-call(f32[5,1,512]{2,1,0:T(1,128)S(1)} %broadcast_in_dim.2.a_ref, f32[264,512]{1,0:T(8,128)S(1)} %collective-permute-done.m1, f32[264,512]{1,0:T(8,128)S(1)} %collective-permute-done.1.p1, ...), custom_call_target="tpu_custom_call" | custom-call | flops 4000000000 | bytes 9000000 | tf_op jit(solution)/shard_map/wavelet_parts/pallas_call | solution.py:332
  37.7 1.9 %collective-permute-start.4 = (f32[528,512]{1,0:T(8,128)S(1)}, f32[528,512]{1,0:T(8,128)S(1)}, u32[]{:S(2)}, u32[]{:S(2)}) collective-permute-start(f32[528,512]{1,0:T(8,128)S(1)} %get-tuple-element.14), channel_id=1, source_target_pairs={{0,1},{1,0},{2,3},{3,2},{4,5},{5,4},{6,7},{7,6},{8,9},{9,8},{10,11... | collective-permute-start | bytes 3244040 | tf_op jit(solution)/shard_map/ppermute | solution.py:538
  39.7 11.2 %collective-permute-start.5 = (f32[264,512]{1,0:T(8,128)S(1)}, f32[264,512]{1,0:T(8,128)S(1)}, u32[]{:S(2)}, u32[]{:S(2)}) collective-permute-start(f32[264,512]{1,0:T(8,128)S(1)} %get-tuple-element.15), channel_id=1, source_target_pairs={{1,3},{2,0},{3,5},{4,2},{5,7},{6,4},{7,9},{8,6},{9,11},{10,8},{11,... | collective-permute-start | bytes 1622024 | tf_op jit(solution)/shard_map/ppermute | solution.py:97
  50.9 0.8 %outward.1._ = f32[264,512]{1,0:T(8,128)S(1)} custom-call(bf16[6,80,160]{2,1,0:T(8,128)(2,1)S(1)} %copy-done, bf16[16,160,512]{2,1,0:T(8,128)(2,1)S(1)} %get-tuple-element.13.y_ref, f32[528,512]{1,0:T(8,128)S(1)} %collective-permute-done.4.swapped_ref), custom_call_target="tpu_custom_call" | custom-call | flops 100000 | bytes 1500000 | tf_op jit(solution)/shard_map/outward/pallas_call | solution.py:360
  51.7 1.9 %collective-permute-start.6 = (f32[264,512]{1,0:T(8,128)S(1)}, f32[264,512]{1,0:T(8,128)S(1)}, u32[]{:S(2)}, u32[]{:S(2)}) collective-permute-start(f32[264,512]{1,0:T(8,128)S(1)} %outward.1._), channel_id=1, source_target_pairs={{0,2},{2,4},{3,1},{4,6},{5,3},{6,8},{7,5},{8,10},{9,7},{10,12},{11... | collective-permute-start | bytes 1622024 | tf_op jit(solution)/shard_map/ppermute | solution.py:97
  53.6 0.8 %own_part.1.o_0 = f32[16,16,512]{2,1,0:T(8,128)S(1)} custom-call(f32[5,1,512]{2,1,0:T(1,128)S(1)} %broadcast_in_dim.2.a_ref, f32[264,512]{1,0:T(8,128)S(1)} %pack.1.x_ref, bf16[6,80,160]{2,1,0:T(8,128)(2,1)S(1)} %copy-done, bf16[16,160,512]{2,1,0:T(8,128)(2,1)S(1)} %get-tuple-element.13.y_ref, f32[264,512]{1,0:T(8,128)S(1)} %outward.1._), custom_call_target="tpu_custom_call" | custom-call | flops 100000000 | bytes 500000 | tf_op jit(solution)/shard_map/own_part/pallas_call | solution.py:217
  54.5 6.4 %collective-permute-done.5.far_ref = f32[264,512]{1,0:T(8,128)S(1)} collective-permute-done((f32[264,512]{1,0:T(8,128)S(1)}, f32[264,512]{1,0:T(8,128)S(1)}, u32[]{:S(2)}, u32[]{:S(2)}) %collective-permute-start.5) | collective-permute-done | bytes 540704 | tf_op jit(solution)/shard_map/ppermute | solution.py:97
  60.8 4.2 %collective-permute-done.6.near_ref = f32[264,512]{1,0:T(8,128)S(1)} collective-permute-done((f32[264,512]{1,0:T(8,128)S(1)}, f32[264,512]{1,0:T(8,128)S(1)}, u32[]{:S(2)}, u32[]{:S(2)}) %collective-permute-start.6) | collective-permute-done | bytes 540704 | tf_op jit(solution)/shard_map/ppermute | solution.py:97
  65.1 3.0 %gradient_step.1 = (f32[16,16,512]{2,1,0:T(8,128)}, f32[3,8,16,16]{3,2,1,0:T(8,128)}) custom-call(f32[16,16,512]{2,1,0:T(8,128)S(1)} %own_part.1.o_0, f32[528,512]{1,0:T(8,128)S(1)} %collective-permute-done.4.swapped_ref, f32[264,512]{1,0:T(8,128)S(1)} %collective-permute-done.5.far_ref, f32[264,512]{1,0:T(8,128)S(1)} %collective-permute-done.6.near_ref, ...), custom_call_target="tpu_custom_call" | custom-call | flops 15000000 | bytes 4000000 | tf_op jit(solution)/shard_map/gradient_step/pallas_call | solution.py:499
  (14 shorter events, 0.0 us)
Async XLA Ops:
  0.6 17.0 %copy-start.6 = (f32[5]{0:T(128)S(1)}, f32[5]{0:T(128)}, u32[]{:S(2)}) copy-start(f32[5]{0:T(128)} %constant.12.clone) | copy-start | bytes 64
  0.6 17.0 %copy-start.3 = (f32[8,16,16]{2,1,0:T(8,128)S(1)}, f32[8,16,16]{2,1,0:T(8,128)}, u32[]{:S(2)}) copy-start(f32[8,16,16]{2,1,0:T(8,128)} %spread_ref.1) | copy-start | bytes 24580
  0.7 17.0 %copy-start.2 = (s32[8,16,16]{2,1,0:T(8,128)S(1)}, s32[8,16,16]{2,1,0:T(8,128)}, u32[]{:S(2)}) copy-start(s32[8,16,16]{2,1,0:T(8,128)} %index_ref.1) | copy-start | bytes 24580
  0.7 17.0 %copy-start.1 = (f32[8,16,16]{2,1,0:T(8,128)S(1)}, f32[8,16,16]{2,1,0:T(8,128)}, u32[]{:S(2)}) copy-start(f32[8,16,16]{2,1,0:T(8,128)} %amp_ref.1) | copy-start | bytes 24580
  0.7 16.8 %copy-start.4 = (s32[4,512]{1,0:T(4,128)S(1)}, s32[4,512]{1,0:T(4,128)}, u32[]{:S(2)}) copy-start(s32[4,512]{1,0:T(4,128)} %param.11) | copy-start | bytes 24580
  0.7 16.8 %copy-start.5 = (f32[16]{0:T(128)S(1)}, f32[16]{0:T(128)}, u32[]{:S(2)}) copy-start(f32[16]{0:T(128)} %param.10) | copy-start | bytes 196
  2.0 31.6 %copy-start = (bf16[6,80,160]{2,1,0:T(8,128)(2,1)S(1)}, bf16[6,80,160]{2,1,0:T(8,128)(2,1)}, u32[]{:S(2)}) copy-start(bf16[6,80,160]{2,1,0:T(8,128)(2,1)} %constant.14.clone.k_ref) | copy-start | bytes 460804
  2.0 31.6 %collective-permute-start.1 = (f32[264,512]{1,0:T(8,128)S(1)}, f32[264,512]{1,0:T(8,128)S(1)}, u32[]{:S(2)}, u32[]{:S(2)}) collective-permute-start(f32[264,512]{1,0:T(8,128)S(1)} %pack.1.x_ref), channel_id=1, source_target_pairs={{32,0},{64,32},{96,64},{128,96},{160,128},{192,160},{224,192},{256... | collective-permute-start | bytes 1622024 | tf_op jit(solution)/shard_map/ppermute | solution.py:91
  5.4 28.2 %collective-permute-start = (f32[264,512]{1,0:T(8,128)S(1)}, f32[264,512]{1,0:T(8,128)S(1)}, u32[]{:S(2)}, u32[]{:S(2)}) collective-permute-start(f32[264,512]{1,0:T(8,128)S(1)} %pack.1.x_ref), channel_id=1, source_target_pairs={{0,32},{32,64},{64,96},{96,128},{128,160},{160,192},{192,224},{224... | collective-permute-start | bytes 1622024 | tf_op jit(solution)/shard_map/ppermute | solution.py:91
  11.6 13.6 %collective-permute-start.3 = (f32[14,16,512]{2,1,0:T(8,128)S(1)}, f32[14,16,512]{2,1,0:T(8,128)S(1)}, u32[]{:S(2)}, u32[]{:S(2)}) collective-permute-start(f32[14,16,512]{2,1,0:T(8,128)S(1)} %get-tuple-element.20), channel_id=1, source_target_pairs={{64,0},{96,32},{128,64},{160,96},{192,128},{224,160},{256,192},{28... | collective-permute-start | bytes 1376264 | tf_op jit(solution)/shard_map/ppermute | solution.py:91
  15.2 18.4 %collective-permute-start.2 = (f32[14,16,512]{2,1,0:T(8,128)S(1)}, f32[14,16,512]{2,1,0:T(8,128)S(1)}, u32[]{:S(2)}, u32[]{:S(2)}) collective-permute-start(f32[14,16,512]{2,1,0:T(8,128)S(1)} %get-tuple-element.21), channel_id=1, source_target_pairs={{0,64},{32,96},{64,128},{96,160},{128,192},{160,224},{192,256},{22... | collective-permute-start | bytes 1376264 | tf_op jit(solution)/shard_map/ppermute | solution.py:91
  37.7 13.2 %collective-permute-start.4 = (f32[528,512]{1,0:T(8,128)S(1)}, f32[528,512]{1,0:T(8,128)S(1)}, u32[]{:S(2)}, u32[]{:S(2)}) collective-permute-start(f32[528,512]{1,0:T(8,128)S(1)} %get-tuple-element.14), channel_id=1, source_target_pairs={{0,1},{1,0},{2,3},{3,2},{4,5},{5,4},{6,7},{7,6},{8,9},{9,8},{10,11... | collective-permute-start | bytes 3244040 | tf_op jit(solution)/shard_map/ppermute | solution.py:538
  39.7 21.2 %collective-permute-start.5 = (f32[264,512]{1,0:T(8,128)S(1)}, f32[264,512]{1,0:T(8,128)S(1)}, u32[]{:S(2)}, u32[]{:S(2)}) collective-permute-start(f32[264,512]{1,0:T(8,128)S(1)} %get-tuple-element.15), channel_id=1, source_target_pairs={{1,3},{2,0},{3,5},{4,2},{5,7},{6,4},{7,9},{8,6},{9,11},{10,8},{11,... | collective-permute-start | bytes 1622024 | tf_op jit(solution)/shard_map/ppermute | solution.py:97
  51.7 13.4 %collective-permute-start.6 = (f32[264,512]{1,0:T(8,128)S(1)}, f32[264,512]{1,0:T(8,128)S(1)}, u32[]{:S(2)}, u32[]{:S(2)}) collective-permute-start(f32[264,512]{1,0:T(8,128)S(1)} %outward.1._), channel_id=1, source_target_pairs={{0,2},{2,4},{3,1},{4,6},{5,3},{6,8},{7,5},{8,10},{9,7},{10,12},{11... | collective-permute-start | bytes 1622024 | tf_op jit(solution)/shard_map/ppermute | solution.py:97

commit v9 on v8

--- a/solution.py
+++ b/solution.py
@@ -106,7 +106,10 @@
 
 
 def pack_kernel(cube_hbm, amp_hbm, index_hbm, spread_hbm, out_ref, amp_ref, index_ref, spread_ref, sem):
-    pairs = ((amp_hbm, amp_ref), (index_hbm, index_ref), (spread_hbm, spread_ref), (cube_hbm, out_ref.at[0:PIXELS]))
+    pairs = [(amp_hbm, amp_ref), (index_hbm, index_ref), (spread_hbm, spread_ref)]
+    for i in range(4):
+        at = slice(i * PIXELS // 4, (i + 1) * PIXELS // 4)
+        pairs.append((cube_hbm.at[at], out_ref.at[at]))
     copies = [pltpu.make_async_copy(a, b, sem.at[i]) for i, (a, b) in enumerate(pairs)]
     for copy in copies:
         copy.start()
@@ -120,7 +123,8 @@
                 lane = start + (2 * t + r) * PITCH
                 got = own_row(t, first + r, amp_ref, index_ref, spread_ref, nch)
                 out_ref[PIXELS:, lane : lane + TILE] = got
-    copies[3].wait()
+    for copy in copies[3:]:
+        copy.wait()
 
 
 def packed(cube, amplitude, centre_index, spread):
@@ -130,7 +134,7 @@
         out_shape=pltpu.VMEM((PIXELS + COMPS, cube.shape[1]), jnp.float32),
         in_specs=[pl.BlockSpec(memory_space=pl.ANY)] * 4,
         out_specs=pl.BlockSpec(memory_space=pltpu.VMEM),
-        scratch_shapes=[pltpu.VMEM(v.shape, v.dtype) for v in hbm[1:]] + [pltpu.SemaphoreType.DMA((4,))],
+        scratch_shapes=[pltpu.VMEM(v.shape, v.dtype) for v in hbm[1:]] + [pltpu.SemaphoreType.DMA((7,))],
         compiler_params=pltpu.CompilerParams(vmem_limit_bytes=VMEM_LIMIT),
         cost_estimate=pl.CostEstimate(flops=1000, bytes_accessed=1_000_000, transcendentals=0),
         name="pack",
@@ -201,33 +205,9 @@
     return 2 * kind + lax.rem(ix, 2)
 
 
-def own_kernel(a_ref, x_ref, k_ref, y_ref, _, o_0):
-    columns = k_ref[column_kind(), 3 * TILE : 4 * TILE]
-
-    def column_pass(row, carry):
-        got = jnp.dot(columns, y_ref[row], preferred_element_type=jnp.float32)
-        o_0[row] = got + a_ref[0] * x_ref[pl.ds(pl.multiple_of(row * TILE, TILE), TILE)]
-        return carry
-
-    lax.fori_loop(0, TILE, column_pass, 0, unroll=4)
-
-
-def own_part(coeff, tile, k, y, after, nch):
-    vmem = pl.BlockSpec(memory_space=pltpu.VMEM)
-    return pl.pallas_call(
-        own_kernel,
-        out_shape=pltpu.VMEM((TILE, TILE, nch), jnp.float32),
-        in_specs=[vmem] * 4 + [pl.BlockSpec(memory_space=pl.ANY)],
-        out_specs=vmem,
-        compiler_params=pltpu.CompilerParams(vmem_limit_bytes=VMEM_LIMIT),
-        cost_estimate=pl.CostEstimate(flops=100_000_000, bytes_accessed=500_000, transcendentals=0),
-        name="own_part",
-    )(*[kept(x) for x in (coeff, tile, k, y, after)])
-
-
 def wavelet_kernel(
     a_ref, m1, p1, m2, p2, x_ref, k_ref, own_ref, w_ref,
-    swap_ref, far_ref, ext_ref, y_ref, rows_ref,
+    o_0, swap_ref, near_ref, far_ref, ext_ref, rows_ref, y_ref,
 ):
     nch = x_ref.shape[1]
     tiles = (m2, m1, x_ref, p1, p2)
@@ -300,7 +280,7 @@
                 y_ref[:, at : at + TILE, lane] = high
 
     odd = lax.rem(ix, 2)
-    columns = k_ref[column_kind(), : 3 * TILE]
+    columns = k_ref[column_kind()]
 
     def column_pass(row, carry):
         got = jnp.dot(columns, y_ref[row], preferred_element_type=jnp.float32)
@@ -308,7 +288,9 @@
         at_more = pl.ds(pl.multiple_of(row * TILE + PIXELS, TILE), TILE)
         swap_ref[at] = got[:TILE]
         swap_ref[at_more] = got[TILE : 2 * TILE]
-        far_ref[at] = got[2 * TILE :]
+        far_ref[at] = got[2 * TILE : 3 * TILE]
+        o_0[row] = got[3 * TILE : 4 * TILE] + a_ref[0] * x_ref[at]
+        near_ref[at] = got[4 * TILE :]
         return carry
 
     lax.fori_loop(0, TILE, column_pass, 0, unroll=4)
@@ -325,47 +307,48 @@
     return pltpu.with_memory_space_constraint(x, pltpu.VMEM)
 
 
-def wavelet_parts(coeff, tiles, k, own, w, nch):
+def wavelet_parts(coeff, tiles, own, w, nch, length):
+    k = jnp.asarray(scatter_matrices(length))
     vmem = pl.BlockSpec(memory_space=pltpu.VMEM)
-    shapes = [(2 * (PIXELS + COMPS), nch), (PIXELS + COMPS, nch), own.shape]
-    outs = [pltpu.VMEM(shape, jnp.float32) for shape in shapes]
+    heights = (2 * (PIXELS + COMPS), PIXELS, PIXELS + COMPS)
+    shapes = [(TILE, TILE, nch)] + [(n, nch) for n in heights] + [own.shape]
     return pl.pallas_call(
         wavelet_kernel,
-        out_shape=outs + [pltpu.VMEM((TILE, 10 * TILE, nch), jnp.bfloat16)],
+        out_shape=[pltpu.VMEM(shape, jnp.float32) for shape in shapes],
         in_specs=[vmem] * 9,
-        out_specs=[vmem] * 4,
-        scratch_shapes=[pltpu.VMEM((LEVELS, TILE, TILE, nch), jnp.float32)],
+        out_specs=[vmem] * 5,
+        scratch_shapes=[
+            pltpu.VMEM((LEVELS, TILE, TILE, nch), jnp.float32),
+            pltpu.VMEM((TILE, 10 * TILE, nch), jnp.bfloat16),
+        ],
         compiler_params=pltpu.CompilerParams(vmem_limit_bytes=VMEM_LIMIT),
         cost_estimate=pl.CostEstimate(flops=4_000_000_000, bytes_accessed=9_000_000, transcendentals=0),
         name="wavelet_parts",
     )(*[kept(x) for x in (coeff, *tiles, k, own, w)])
 
 
-def outward_kernel(k_ref, y_ref, swapped_ref, out_ref):
-    columns = k_ref[column_kind(), 4 * TILE :]
-
-    def column_pass(row, carry):
-        got = jnp.dot(columns, y_ref[row], preferred_element_type=jnp.float32)
+def add_kernel(near_ref, swapped_ref, out_ref):
+    def body(row, carry):
         at = pl.ds(pl.multiple_of(row * TILE, TILE), TILE)
         more = pl.ds(pl.multiple_of(row * TILE + PIXELS, TILE), TILE)
-        out_ref[at] = got + swapped_ref[more]
+        out_ref[at] = near_ref[at] + swapped_ref[more]
         return carry
 
-    lax.fori_loop(0, TILE, column_pass, 0, unroll=4)
+    lax.fori_loop(0, TILE, body, 0, unroll=4)
     out_ref[PIXELS:, :] = swapped_ref[2 * PIXELS + COMPS :]
 
 
-def outward(k, y, swapped):
+def outward(near, swapped):
     vmem = pl.BlockSpec(memory_space=pltpu.VMEM)
     return pl.pallas_call(
-        outward_kernel,
-        out_shape=pltpu.VMEM((PIXELS + COMPS, swapped.shape[1]), jnp.float32),
-        in_specs=[vmem] * 3,
+        add_kernel,
+        out_shape=pltpu.VMEM((PIXELS + COMPS, near.shape[1]), jnp.float32),
+        in_specs=[vmem] * 2,
         out_specs=vmem,
         compiler_params=pltpu.CompilerParams(vmem_limit_bytes=VMEM_LIMIT),
         cost_estimate=pl.CostEstimate(flops=100_000, bytes_accessed=1_500_000, transcendentals=0),
         name="outward",
-    )(*[kept(x) for x in (k, y, swapped)])
+    )(kept(near), kept(swapped))
 
 
 def model_kernel(amp_ref, index_ref, spread_ref, w_hbm, model_ref, flat_ref, own_ref, w_ref, bump_ref, scale_ref, sem):
@@ -532,14 +515,11 @@
     scale = jnp.array([16.0 ** (-3 * j) for j in range(LEVELS + 1)], jnp.float32)
     coeff = (coeff * scale[:, None])[:, None, :]
     model, flat, own, w, bump = model_of(amplitude, centre_index, spread, nch)
-    k = jnp.asarray(scatter_matrices(size * TILE))
-    swap, far, ext, y = wavelet_parts(coeff, (up1, down1, up2, down2, tile), k, own, w, nch)
+    o_0, swap, near, far, ext = wavelet_parts(coeff, (up1, down1, up2, down2, tile), own, w, nch, size * TILE)
 
     swapped = lax.ppermute(swap, "skyx", partner)
     far = away(far, "skyx", 2)
-    total = outward(k, y, swapped)
-    near = away(total, "skyx", -2)
-    o_0 = own_part(coeff, tile, k, y, total, nch)
+    near = away(outward(near, swapped), "skyx", -2)
     return gradient_step((o_0, swapped, far, near), model, bump, flat, ext)
 
 

time: 68.4 us -> 67.8 us (level)
  Pallas kernels: 11.7 us -> 10.3 us
  waiting for transfers between devices: 24.8 us -> 25.6 us
    pallas_call x3 -> x2, Pallas kernels: 5.76 us -> 4.26 us  [the longest x1 4.18 us: wavelet_parts(): pl.pallas_call(wavelet_kernel, out_shape=[pltpu.VMEM(shape, jnp.float32)...]
    ppermute x2, waiting for transfers between devices: 10.6 us -> 11.4 us  [away(): lax.ppermute(values, axis, [(i, j) for i, j in pairs if 0 <= j < size])]
  transfers between devices with their start and end apart: 7 -> 7, of which waited for: 4 -> 4; matrix products, arithmetic and copies ran while one was open for 2% -> 2% of each run, Pallas kernels for 5% -> 3%
where the time goes in v9:
time: 67.8 us; the launch traced here: 67.5 us
  starting transfers between devices  29.3 us (43%)
  waiting for transfers between devices  25.6 us (38%)
  Pallas kernels  10.3 us (15%)
  local copies, waits for them, and re-layouts  1.29 us (2%)
  between operations  0.84 us (1%)
    ppermute x4, starting transfers between devices, sent(): return lax.ppermute(values, axis, pairs)  14.2 us
    ppermute x4, waiting for transfers between devices, sent(): return lax.ppermute(values, axis, pairs)  14.1 us
    ppermute x2, starting transfers between devices, away(): lax.ppermute(values, axis, [(i, j) for i, j in pairs if 0 <= j < size])  13.1 us
    ppermute x2, waiting for transfers between devices, away(): lax.ppermute(values, axis, [(i, j) for i, j in pairs if 0 <= j < size])  11.4 us
    pallas_call x1, Pallas kernels, wavelet_parts(): pl.pallas_call(wavelet_kernel, out_shape=[pltpu.VMEM(shape, jnp.float32)...  4.18 us
    pallas_call x1, Pallas kernels, gradient_step(): pl.pallas_call(step_kernel, out_shape=[jax.ShapeDtypeStruct(shape, jnp.fl...  3.01 us
    ppermute x1, starting transfers between devices, on_device(): swapped = lax.ppermute(swap, 'skyx', partner)  1.92 us
    pallas_call x1, Pallas kernels, model_of(): pl.pallas_call(model_kernel, out_shape=[pltpu.VMEM((nch, pixels), jnp.flo...  1.72 us
  transfers between devices with their start and end apart: 7, of which 4 were waited for; matrix products, arithmetic and copies ran while one was open for 2% of the time, Pallas kernels for 3%

profile of v9, /device:TPU:38, one launch (start us, length us, event | category | flops | bytes accessed | tf_op | source)
XLA Modules:
  0.0 67.5 jit_solution(12368334519039706230)
XLA Ops:
  0.6 0.0 copy-start.6
  0.7 1.3 %pack.1.x_ref = f32[264,512]{1,0:T(8,128)S(1)} custom-call(f32[256,512]{1,0:T(8,128)} %bitcast.1, f32[8,16,16]{2,1,0:T(8,128)} %amp_ref.1, s32[8,16,16]{2,1,0:T(8,128)} %index_ref.1, f32[8,16,16]{2,1,0:T(8,128)} %spread_ref.1), custom_call_target="tpu_custom_call" | custom-call | flops 1000 | bytes 1000000 | tf_op jit(solution)/shard_map/pack/pallas_call | solution.py:132
  2.0 0.0 copy-start.3
  2.0 3.4 %collective-permute-start.1 = (f32[264,512]{1,0:T(8,128)S(1)}, f32[264,512]{1,0:T(8,128)S(1)}, u32[]{:S(2)}, u32[]{:S(2)}) collective-permute-start(f32[264,512]{1,0:T(8,128)S(1)} %pack.1.x_ref), channel_id=1, source_target_pairs={{32,0},{64,32},{96,64},{128,96},{160,128},{192,160},{224,192},{256... | collective-permute-start | bytes 1622024 | tf_op jit(solution)/shard_map/ppermute | solution.py:91
  5.5 4.9 %collective-permute-start = (f32[264,512]{1,0:T(8,128)S(1)}, f32[264,512]{1,0:T(8,128)S(1)}, u32[]{:S(2)}, u32[]{:S(2)}) collective-permute-start(f32[264,512]{1,0:T(8,128)S(1)} %pack.1.x_ref), channel_id=1, source_target_pairs={{0,32},{32,64},{64,96},{96,128},{128,160},{160,192},{192,224},{224... | collective-permute-start | bytes 1622024 | tf_op jit(solution)/shard_map/ppermute | solution.py:91
  10.4 1.2 %fusion = (f32[14,16,512]{2,1,0:T(8,128)S(1)}, f32[14,16,512]{2,1,0:T(8,128)S(1)}) fusion(f32[16,16,512]{2,1,0:T(8,128)} %param.9), kind=kLoop, calls=%fused_computation.3 | loop fusion | bytes 1835008 | tf_op jit(solution)/shard_map/slice | solution.py:508
  11.7 3.6 %collective-permute-start.3 = (f32[14,16,512]{2,1,0:T(8,128)S(1)}, f32[14,16,512]{2,1,0:T(8,128)S(1)}, u32[]{:S(2)}, u32[]{:S(2)}) collective-permute-start(f32[14,16,512]{2,1,0:T(8,128)S(1)} %get-tuple-element.22), channel_id=1, source_target_pairs={{64,0},{96,32},{128,64},{160,96},{192,128},{224,160},{256,192},{28... | collective-permute-start | bytes 1376264 | tf_op jit(solution)/shard_map/ppermute | solution.py:91
  15.3 2.3 %collective-permute-start.2 = (f32[14,16,512]{2,1,0:T(8,128)S(1)}, f32[14,16,512]{2,1,0:T(8,128)S(1)}, u32[]{:S(2)}, u32[]{:S(2)}) collective-permute-start(f32[14,16,512]{2,1,0:T(8,128)S(1)} %get-tuple-element.23), channel_id=1, source_target_pairs={{0,64},{32,96},{64,128},{96,160},{128,192},{160,224},{192,256},{22... | collective-permute-start | bytes 1376264 | tf_op jit(solution)/shard_map/ppermute | solution.py:91
  17.6 0.1 select_reduce_fusion
  17.7 0.1 subtract_multiply_fusion
  17.8 1.7 %gaussian_model.1 = (f32[512,256]{1,0:T(8,128)S(1)}, f32[3,8,256]{2,1,0:T(8,128)S(1)}, f32[3,8,384]{2,1,0:T(8,128)S(1)}, bf16[6,3,256,256]{3,2,1,0:T(8,128)(2,1)S(1)}, f32[8,512,256]{2,1,0:T(8,128)S(1)}) custom-call(f32[8,16,16]{2,1,0:T(8,128)S(1)} %copy-done, s32[8,16,16]{2,1,0:T(8,128)S(1)} %copy-done.1, f32[8,16,16]{2,1,0:T(8,128)S(1)} %copy-done.2, ...), custom_call_target="tpu_custom_call" | custom-call | flops 10000000 | bytes 1000000 | tf_op jit(solution)/shard_map/gaussian_model/pallas_call | solution.py:391
  19.5 5.8 %collective-permute-done.3.p2 = f32[14,16,512]{2,1,0:T(8,128)S(1)} collective-permute-done((f32[14,16,512]{2,1,0:T(8,128)S(1)}, f32[14,16,512]{2,1,0:T(8,128)S(1)}, u32[]{:S(2)}, u32[]{:S(2)}) %collective-permute-start.3) | collective-permute-done | bytes 458784 | tf_op jit(solution)/shard_map/ppermute | solution.py:91
  25.3 8.4 %collective-permute-done.2.m2 = f32[14,16,512]{2,1,0:T(8,128)S(1)} collective-permute-done((f32[14,16,512]{2,1,0:T(8,128)S(1)}, f32[14,16,512]{2,1,0:T(8,128)S(1)}, u32[]{:S(2)}, u32[]{:S(2)}) %collective-permute-start.2) | collective-permute-done | bytes 458784 | tf_op jit(solution)/shard_map/ppermute | solution.py:91
  33.7 0.0 collective-permute-done.1.p1
  33.7 0.0 collective-permute-done.m1
  33.7 4.2 %wavelet_parts.1 = (f32[16,16,512]{2,1,0:T(8,128)S(1)}, f32[528,512]{1,0:T(8,128)S(1)}, f32[256,512]{1,0:T(8,128)S(1)}, f32[264,512]{1,0:T(8,128)S(1)}, f32[3,8,384]{2,1,0:T(8,128)S(1)}) custom-call(f32[5,1,512]{2,1,0:T(1,128)S(1)} %broadcast_in_dim.2.a_ref, f32[264,512]{1,0:T(8,128)S(1)} %collective-permute-done.m1, ...), custom_call_target="tpu_custom_call" | custom-call | flops 4000000000 | bytes 9000000 | tf_op jit(solution)/shard_map/wavelet_parts/pallas_call | solution.py:315
  37.9 1.9 %collective-permute-start.4 = (f32[528,512]{1,0:T(8,128)S(1)}, f32[528,512]{1,0:T(8,128)S(1)}, u32[]{:S(2)}, u32[]{:S(2)}) collective-permute-start(f32[528,512]{1,0:T(8,128)S(1)} %get-tuple-element.15), channel_id=1, source_target_pairs={{0,1},{1,0},{2,3},{3,2},{4,5},{5,4},{6,7},{7,6},{8,9},{9,8},{10,11... | collective-permute-start | bytes 3244040 | tf_op jit(solution)/shard_map/ppermute | solution.py:520
  39.8 11.2 %collective-permute-start.5 = (f32[264,512]{1,0:T(8,128)S(1)}, f32[264,512]{1,0:T(8,128)S(1)}, u32[]{:S(2)}, u32[]{:S(2)}) collective-permute-start(f32[264,512]{1,0:T(8,128)S(1)} %get-tuple-element.16), channel_id=1, source_target_pairs={{1,3},{2,0},{3,5},{4,2},{5,7},{6,4},{7,9},{8,6},{9,11},{10,8},{11,... | collective-permute-start | bytes 1622024 | tf_op jit(solution)/shard_map/ppermute | solution.py:97
  51.0 0.0 collective-permute-done.4.swapped_ref
  51.0 0.1 outward.1
  51.1 1.9 %collective-permute-start.6 = (f32[264,512]{1,0:T(8,128)S(1)}, f32[264,512]{1,0:T(8,128)S(1)}, u32[]{:S(2)}, u32[]{:S(2)}) collective-permute-start(f32[264,512]{1,0:T(8,128)S(1)} %outward.1), channel_id=1, source_target_pairs={{0,2},{2,4},{3,1},{4,6},{5,3},{6,8},{7,5},{8,10},{9,7},{10,12},{11... | collective-permute-start | bytes 1622024 | tf_op jit(solution)/shard_map/ppermute | solution.py:97
  53.0 8.6 %collective-permute-done.5.far_ref = f32[264,512]{1,0:T(8,128)S(1)} collective-permute-done((f32[264,512]{1,0:T(8,128)S(1)}, f32[264,512]{1,0:T(8,128)S(1)}, u32[]{:S(2)}, u32[]{:S(2)}) %collective-permute-start.5) | collective-permute-done | bytes 540704 | tf_op jit(solution)/shard_map/ppermute | solution.py:97
  61.7 2.8 %collective-permute-done.6.near_ref = f32[264,512]{1,0:T(8,128)S(1)} collective-permute-done((f32[264,512]{1,0:T(8,128)S(1)}, f32[264,512]{1,0:T(8,128)S(1)}, u32[]{:S(2)}, u32[]{:S(2)}) %collective-permute-start.6) | collective-permute-done | bytes 540704 | tf_op jit(solution)/shard_map/ppermute | solution.py:97
  64.5 3.0 %gradient_step.1 = (f32[16,16,512]{2,1,0:T(8,128)}, f32[3,8,16,16]{3,2,1,0:T(8,128)}) custom-call(f32[16,16,512]{2,1,0:T(8,128)S(1)} %get-tuple-element.14.o_0, f32[528,512]{1,0:T(8,128)S(1)} %collective-permute-done.4.swapped_ref, f32[264,512]{1,0:T(8,128)S(1)} %collective-permute-done.5.far_ref, f32[264,512]{1,0:T(8,128)S(1)} %collective-permute-done.6.near_ref, ...), custom_call_target="tpu_custom_call" | custom-call | flops 15000000 | bytes 4000000 | tf_op jit(solution)/shard_map/gradient_step/pallas_call | solution.py:482
  (13 shorter events, 0.0 us)
Async XLA Ops:
  0.6 17.0 %copy-start.6 = (f32[5]{0:T(128)S(1)}, f32[5]{0:T(128)}, u32[]{:S(2)}) copy-start(f32[5]{0:T(128)} %constant.12.clone) | copy-start | bytes 64
  0.6 17.1 %copy-start.2 = (f32[8,16,16]{2,1,0:T(8,128)S(1)}, f32[8,16,16]{2,1,0:T(8,128)}, u32[]{:S(2)}) copy-start(f32[8,16,16]{2,1,0:T(8,128)} %spread_ref.1) | copy-start | bytes 24580
  0.7 17.1 %copy-start.1 = (s32[8,16,16]{2,1,0:T(8,128)S(1)}, s32[8,16,16]{2,1,0:T(8,128)}, u32[]{:S(2)}) copy-start(s32[8,16,16]{2,1,0:T(8,128)} %index_ref.1) | copy-start | bytes 24580
  0.7 17.1 %copy-start = (f32[8,16,16]{2,1,0:T(8,128)S(1)}, f32[8,16,16]{2,1,0:T(8,128)}, u32[]{:S(2)}) copy-start(f32[8,16,16]{2,1,0:T(8,128)} %amp_ref.1) | copy-start | bytes 24580
  0.7 16.9 %copy-start.4 = (s32[4,512]{1,0:T(4,128)S(1)}, s32[4,512]{1,0:T(4,128)}, u32[]{:S(2)}) copy-start(s32[4,512]{1,0:T(4,128)} %param.11) | copy-start | bytes 24580
  0.7 16.9 %copy-start.5 = (f32[16]{0:T(128)S(1)}, f32[16]{0:T(128)}, u32[]{:S(2)}) copy-start(f32[16]{0:T(128)} %param.10) | copy-start | bytes 196
  2.0 31.6 %copy-start.3 = (bf16[6,80,160]{2,1,0:T(8,128)(2,1)S(1)}, bf16[6,80,160]{2,1,0:T(8,128)(2,1)}, u32[]{:S(2)}) copy-start(bf16[6,80,160]{2,1,0:T(8,128)(2,1)} %constant.14.clone.k_ref) | copy-start | bytes 460804
  2.0 31.6 %collective-permute-start.1 = (f32[264,512]{1,0:T(8,128)S(1)}, f32[264,512]{1,0:T(8,128)S(1)}, u32[]{:S(2)}, u32[]{:S(2)}) collective-permute-start(f32[264,512]{1,0:T(8,128)S(1)} %pack.1.x_ref), channel_id=1, source_target_pairs={{32,0},{64,32},{96,64},{128,96},{160,128},{192,160},{224,192},{256... | collective-permute-start | bytes 1622024 | tf_op jit(solution)/shard_map/ppermute | solution.py:91
  5.5 28.2 %collective-permute-start = (f32[264,512]{1,0:T(8,128)S(1)}, f32[264,512]{1,0:T(8,128)S(1)}, u32[]{:S(2)}, u32[]{:S(2)}) collective-permute-start(f32[264,512]{1,0:T(8,128)S(1)} %pack.1.x_ref), channel_id=1, source_target_pairs={{0,32},{32,64},{64,96},{96,128},{128,160},{160,192},{192,224},{224... | collective-permute-start | bytes 1622024 | tf_op jit(solution)/shard_map/ppermute | solution.py:91
  11.7 13.6 %collective-permute-start.3 = (f32[14,16,512]{2,1,0:T(8,128)S(1)}, f32[14,16,512]{2,1,0:T(8,128)S(1)}, u32[]{:S(2)}, u32[]{:S(2)}) collective-permute-start(f32[14,16,512]{2,1,0:T(8,128)S(1)} %get-tuple-element.22), channel_id=1, source_target_pairs={{64,0},{96,32},{128,64},{160,96},{192,128},{224,160},{256,192},{28... | collective-permute-start | bytes 1376264 | tf_op jit(solution)/shard_map/ppermute | solution.py:91
  15.3 18.4 %collective-permute-start.2 = (f32[14,16,512]{2,1,0:T(8,128)S(1)}, f32[14,16,512]{2,1,0:T(8,128)S(1)}, u32[]{:S(2)}, u32[]{:S(2)}) collective-permute-start(f32[14,16,512]{2,1,0:T(8,128)S(1)} %get-tuple-element.23), channel_id=1, source_target_pairs={{0,64},{32,96},{64,128},{96,160},{128,192},{160,224},{192,256},{22... | collective-permute-start | bytes 1376264 | tf_op jit(solution)/shard_map/ppermute | solution.py:91
  37.9 13.2 %collective-permute-start.4 = (f32[528,512]{1,0:T(8,128)S(1)}, f32[528,512]{1,0:T(8,128)S(1)}, u32[]{:S(2)}, u32[]{:S(2)}) collective-permute-start(f32[528,512]{1,0:T(8,128)S(1)} %get-tuple-element.15), channel_id=1, source_target_pairs={{0,1},{1,0},{2,3},{3,2},{4,5},{5,4},{6,7},{7,6},{8,9},{9,8},{10,11... | collective-permute-start | bytes 3244040 | tf_op jit(solution)/shard_map/ppermute | solution.py:520
  39.8 21.9 %collective-permute-start.5 = (f32[264,512]{1,0:T(8,128)S(1)}, f32[264,512]{1,0:T(8,128)S(1)}, u32[]{:S(2)}, u32[]{:S(2)}) collective-permute-start(f32[264,512]{1,0:T(8,128)S(1)} %get-tuple-element.16), channel_id=1, source_target_pairs={{1,3},{2,0},{3,5},{4,2},{5,7},{6,4},{7,9},{8,6},{9,11},{10,8},{11,... | collective-permute-start | bytes 1622024 | tf_op jit(solution)/shard_map/ppermute | solution.py:97
  51.1 13.4 %collective-permute-start.6 = (f32[264,512]{1,0:T(8,128)S(1)}, f32[264,512]{1,0:T(8,128)S(1)}, u32[]{:S(2)}, u32[]{:S(2)}) collective-permute-start(f32[264,512]{1,0:T(8,128)S(1)} %outward.1), channel_id=1, source_target_pairs={{0,2},{2,4},{3,1},{4,6},{5,3},{6,8},{7,5},{8,10},{9,7},{10,12},{11... | collective-permute-start | bytes 1622024 | tf_op jit(solution)/shard_map/ppermute | solution.py:97

commit v10 on v9

--- a/solution.py
+++ b/solution.py
@@ -106,10 +106,7 @@
 
 
 def pack_kernel(cube_hbm, amp_hbm, index_hbm, spread_hbm, out_ref, amp_ref, index_ref, spread_ref, sem):
-    pairs = [(amp_hbm, amp_ref), (index_hbm, index_ref), (spread_hbm, spread_ref)]
-    for i in range(4):
-        at = slice(i * PIXELS // 4, (i + 1) * PIXELS // 4)
-        pairs.append((cube_hbm.at[at], out_ref.at[at]))
+    pairs = ((amp_hbm, amp_ref), (index_hbm, index_ref), (spread_hbm, spread_ref), (cube_hbm, out_ref.at[0:PIXELS]))
     copies = [pltpu.make_async_copy(a, b, sem.at[i]) for i, (a, b) in enumerate(pairs)]
     for copy in copies:
         copy.start()
@@ -123,8 +120,7 @@
                 lane = start + (2 * t + r) * PITCH
                 got = own_row(t, first + r, amp_ref, index_ref, spread_ref, nch)
                 out_ref[PIXELS:, lane : lane + TILE] = got
-    for copy in copies[3:]:
-        copy.wait()
+    copies[3].wait()
 
 
 def packed(cube, amplitude, centre_index, spread):
@@ -134,7 +130,7 @@
         out_shape=pltpu.VMEM((PIXELS + COMPS, cube.shape[1]), jnp.float32),
         in_specs=[pl.BlockSpec(memory_space=pl.ANY)] * 4,
         out_specs=pl.BlockSpec(memory_space=pltpu.VMEM),
-        scratch_shapes=[pltpu.VMEM(v.shape, v.dtype) for v in hbm[1:]] + [pltpu.SemaphoreType.DMA((7,))],
+        scratch_shapes=[pltpu.VMEM(v.shape, v.dtype) for v in hbm[1:]] + [pltpu.SemaphoreType.DMA((4,))],
         compiler_params=pltpu.CompilerParams(vmem_limit_bytes=VMEM_LIMIT),
         cost_estimate=pl.CostEstimate(flops=1000, bytes_accessed=1_000_000, transcendentals=0),
         name="pack",
@@ -249,19 +245,19 @@
 
     half, quarter = nch // 2, nch // 4
 
-    def product(v, index):
-        blocks = [
-            jnp.dot(v[:, at : at + half], w_ref[index, i], preferred_element_type=jnp.float32)
+    for level in range(LEVELS):
+        high, low = split(rows_ref[level].reshape(PIXELS, nch))
+        parts, index = [high, low], [level, level]
+        if level >= 2:
+            parts, index = parts + [high], index + [level + 2]
+        first, middle, last = [
+            jnp.dot(
+                jnp.concatenate([v[:, at : at + half] for v in parts], axis=1),
+                jnp.concatenate([w_ref[j, i] for j in index], axis=0),
+                preferred_element_type=jnp.float32,
+            )
             for i, at in enumerate((0, quarter, half))
         ]
-        return blocks
-
-    for level in range(LEVELS):
-        high, low = split(rows_ref[level].reshape(PIXELS, nch))
-        terms = [product(high, level), product(low, level)]
-        if level >= 2:
-            terms.append(product(high, level + 2))
-        first, middle, last = [functools.reduce(lambda a, b: a + b, v) for v in zip(*terms)]
         pieces = (
             first[:, :quarter],
             first[:, quarter:] + middle[:, :quarter],
@@ -293,7 +289,7 @@
         near_ref[at] = got[4 * TILE :]
         return carry
 
-    lax.fori_loop(0, TILE, column_pass, 0, unroll=4)
+    lax.fori_loop(0, TILE, column_pass, 0, unroll=16)
 
     params = with_rows(own_ref, m1[PIXELS:, :EXT], p1[PIXELS:, :EXT])
     for t in range(3):
@@ -453,7 +449,7 @@
                 return tuple(out)
 
             zero = jnp.zeros((8, LANES), jnp.float32)
-            done = lax.fori_loop(0, nch // 8, body, ((zero,) * 3,) * 4, unroll=8)
+            done = lax.fori_loop(0, nch // 8, body, ((zero,) * 3,) * 4, unroll=16)
             for four in done:
                 for t in range(3):
                     sums[t].append(jnp.sum(four[t], axis=0, keepdims=True))

time: 67.8 us -> 67 us (0.988)
  Pallas kernels: 10.3 us -> 9.45 us
    pallas_call x1, Pallas kernels: 4.18 us -> 3.47 us  [wavelet_parts(): pl.pallas_call(wavelet_kernel, out_shape=[pltpu.VMEM(shape, jnp.float32)...]
where the time goes in v10:
time: 67 us; the launch traced here: 66.6 us
  starting transfers between devices  29.3 us (44%)
  waiting for transfers between devices  25.6 us (38%)
  Pallas kernels  9.45 us (14%)
  local copies, waits for them, and re-layouts  1.29 us (2%)
  between operations  0.84 us (1%)
    ppermute x4, starting transfers between devices, sent(): return lax.ppermute(values, axis, pairs)  14.2 us
    ppermute x4, waiting for transfers between devices, sent(): return lax.ppermute(values, axis, pairs)  14.1 us
    ppermute x2, starting transfers between devices, away(): lax.ppermute(values, axis, [(i, j) for i, j in pairs if 0 <= j < size])  13.1 us
    ppermute x2, waiting for transfers between devices, away(): lax.ppermute(values, axis, [(i, j) for i, j in pairs if 0 <= j < size])  11.4 us
    pallas_call x1, Pallas kernels, wavelet_parts(): pl.pallas_call(wavelet_kernel, out_shape=[pltpu.VMEM(shape, jnp.float32)...  3.47 us
    pallas_call x1, Pallas kernels, gradient_step(): pl.pallas_call(step_kernel, out_shape=[jax.ShapeDtypeStruct(shape, jnp.fl...  2.92 us
    ppermute x1, starting transfers between devices, on_device(): swapped = lax.ppermute(swap, 'skyx', partner)  1.92 us
    pallas_call x1, Pallas kernels, model_of(): pl.pallas_call(model_kernel, out_shape=[pltpu.VMEM((nch, pixels), jnp.flo...  1.72 us
  transfers between devices with their start and end apart: 7, of which 4 were waited for; matrix products, arithmetic and copies ran while one was open for 2% of the time, Pallas kernels for 3%

profile of v10, /device:TPU:38, one launch (start us, length us, event | category | flops | bytes accessed | tf_op | source)
XLA Modules:
  0.0 66.6 jit_solution(2942629972897129390)
XLA Ops:
  0.6 0.0 copy-start.6
  0.7 1.3 %pack.1.x_ref = f32[264,512]{1,0:T(8,128)S(1)} custom-call(f32[256,512]{1,0:T(8,128)} %bitcast.1, f32[8,16,16]{2,1,0:T(8,128)} %amp_ref.1, s32[8,16,16]{2,1,0:T(8,128)} %index_ref.1, f32[8,16,16]{2,1,0:T(8,128)} %spread_ref.1), custom_call_target="tpu_custom_call" | custom-call | flops 1000 | bytes 1000000 | tf_op jit(solution)/shard_map/pack/pallas_call | solution.py:128
  2.0 0.0 copy-start.3
  2.0 3.4 %collective-permute-start.1 = (f32[264,512]{1,0:T(8,128)S(1)}, f32[264,512]{1,0:T(8,128)S(1)}, u32[]{:S(2)}, u32[]{:S(2)}) collective-permute-start(f32[264,512]{1,0:T(8,128)S(1)} %pack.1.x_ref), channel_id=1, source_target_pairs={{32,0},{64,32},{96,64},{128,96},{160,128},{192,160},{224,192},{256... | collective-permute-start | bytes 1622024 | tf_op jit(solution)/shard_map/ppermute | solution.py:91
  5.4 4.9 %collective-permute-start = (f32[264,512]{1,0:T(8,128)S(1)}, f32[264,512]{1,0:T(8,128)S(1)}, u32[]{:S(2)}, u32[]{:S(2)}) collective-permute-start(f32[264,512]{1,0:T(8,128)S(1)} %pack.1.x_ref), channel_id=1, source_target_pairs={{0,32},{32,64},{64,96},{96,128},{128,160},{160,192},{192,224},{224... | collective-permute-start | bytes 1622024 | tf_op jit(solution)/shard_map/ppermute | solution.py:91
  10.4 1.2 %fusion = (f32[14,16,512]{2,1,0:T(8,128)S(1)}, f32[14,16,512]{2,1,0:T(8,128)S(1)}) fusion(f32[16,16,512]{2,1,0:T(8,128)} %param.9), kind=kLoop, calls=%fused_computation.3 | loop fusion | bytes 1835008 | tf_op jit(solution)/shard_map/slice | solution.py:504
  11.6 3.6 %collective-permute-start.3 = (f32[14,16,512]{2,1,0:T(8,128)S(1)}, f32[14,16,512]{2,1,0:T(8,128)S(1)}, u32[]{:S(2)}, u32[]{:S(2)}) collective-permute-start(f32[14,16,512]{2,1,0:T(8,128)S(1)} %get-tuple-element.22), channel_id=1, source_target_pairs={{64,0},{96,32},{128,64},{160,96},{192,128},{224,160},{256,192},{28... | collective-permute-start | bytes 1376264 | tf_op jit(solution)/shard_map/ppermute | solution.py:91
  15.2 2.3 %collective-permute-start.2 = (f32[14,16,512]{2,1,0:T(8,128)S(1)}, f32[14,16,512]{2,1,0:T(8,128)S(1)}, u32[]{:S(2)}, u32[]{:S(2)}) collective-permute-start(f32[14,16,512]{2,1,0:T(8,128)S(1)} %get-tuple-element.23), channel_id=1, source_target_pairs={{0,64},{32,96},{64,128},{96,160},{128,192},{160,224},{192,256},{22... | collective-permute-start | bytes 1376264 | tf_op jit(solution)/shard_map/ppermute | solution.py:91
  17.5 0.1 select_reduce_fusion
  17.6 0.1 subtract_multiply_fusion
  17.7 1.7 %gaussian_model.1 = (f32[512,256]{1,0:T(8,128)S(1)}, f32[3,8,256]{2,1,0:T(8,128)S(1)}, f32[3,8,384]{2,1,0:T(8,128)S(1)}, bf16[6,3,256,256]{3,2,1,0:T(8,128)(2,1)S(1)}, f32[8,512,256]{2,1,0:T(8,128)S(1)}) custom-call(f32[8,16,16]{2,1,0:T(8,128)S(1)} %copy-done, s32[8,16,16]{2,1,0:T(8,128)S(1)} %copy-done.1, f32[8,16,16]{2,1,0:T(8,128)S(1)} %copy-done.2, ...), custom_call_target="tpu_custom_call" | custom-call | flops 10000000 | bytes 1000000 | tf_op jit(solution)/shard_map/gaussian_model/pallas_call | solution.py:387
  19.4 5.8 %collective-permute-done.3.p2 = f32[14,16,512]{2,1,0:T(8,128)S(1)} collective-permute-done((f32[14,16,512]{2,1,0:T(8,128)S(1)}, f32[14,16,512]{2,1,0:T(8,128)S(1)}, u32[]{:S(2)}, u32[]{:S(2)}) %collective-permute-start.3) | collective-permute-done | bytes 458784 | tf_op jit(solution)/shard_map/ppermute | solution.py:91
  25.2 8.4 %collective-permute-done.2.m2 = f32[14,16,512]{2,1,0:T(8,128)S(1)} collective-permute-done((f32[14,16,512]{2,1,0:T(8,128)S(1)}, f32[14,16,512]{2,1,0:T(8,128)S(1)}, u32[]{:S(2)}, u32[]{:S(2)}) %collective-permute-start.2) | collective-permute-done | bytes 458784 | tf_op jit(solution)/shard_map/ppermute | solution.py:91
  33.6 0.0 collective-permute-done.1.p1
  33.6 0.0 collective-permute-done.m1
  33.6 3.5 %wavelet_parts.1 = (f32[16,16,512]{2,1,0:T(8,128)S(1)}, f32[528,512]{1,0:T(8,128)S(1)}, f32[256,512]{1,0:T(8,128)S(1)}, f32[264,512]{1,0:T(8,128)S(1)}, f32[3,8,384]{2,1,0:T(8,128)S(1)}) custom-call(f32[5,1,512]{2,1,0:T(1,128)S(1)} %broadcast_in_dim.2.a_ref, f32[264,512]{1,0:T(8,128)S(1)} %collective-permute-done.m1, ...), custom_call_target="tpu_custom_call" | custom-call | flops 4000000000 | bytes 9000000 | tf_op jit(solution)/shard_map/wavelet_parts/pallas_call | solution.py:311
  37.1 1.9 %collective-permute-start.4 = (f32[528,512]{1,0:T(8,128)S(1)}, f32[528,512]{1,0:T(8,128)S(1)}, u32[]{:S(2)}, u32[]{:S(2)}) collective-permute-start(f32[528,512]{1,0:T(8,128)S(1)} %get-tuple-element.15), channel_id=1, source_target_pairs={{0,1},{1,0},{2,3},{3,2},{4,5},{5,4},{6,7},{7,6},{8,9},{9,8},{10,11... | collective-permute-start | bytes 3244040 | tf_op jit(solution)/shard_map/ppermute | solution.py:516
  39.0 11.2 %collective-permute-start.5 = (f32[264,512]{1,0:T(8,128)S(1)}, f32[264,512]{1,0:T(8,128)S(1)}, u32[]{:S(2)}, u32[]{:S(2)}) collective-permute-start(f32[264,512]{1,0:T(8,128)S(1)} %get-tuple-element.16), channel_id=1, source_target_pairs={{1,3},{2,0},{3,5},{4,2},{5,7},{6,4},{7,9},{8,6},{9,11},{10,8},{11,... | collective-permute-start | bytes 1622024 | tf_op jit(solution)/shard_map/ppermute | solution.py:97
  50.2 0.0 collective-permute-done.4.swapped_ref
  50.2 0.1 outward.1
  50.3 1.9 %collective-permute-start.6 = (f32[264,512]{1,0:T(8,128)S(1)}, f32[264,512]{1,0:T(8,128)S(1)}, u32[]{:S(2)}, u32[]{:S(2)}) collective-permute-start(f32[264,512]{1,0:T(8,128)S(1)} %outward.1), channel_id=1, source_target_pairs={{0,2},{2,4},{3,1},{4,6},{5,3},{6,8},{7,5},{8,10},{9,7},{10,12},{11... | collective-permute-start | bytes 1622024 | tf_op jit(solution)/shard_map/ppermute | solution.py:97
  52.3 8.6 %collective-permute-done.5.far_ref = f32[264,512]{1,0:T(8,128)S(1)} collective-permute-done((f32[264,512]{1,0:T(8,128)S(1)}, f32[264,512]{1,0:T(8,128)S(1)}, u32[]{:S(2)}, u32[]{:S(2)}) %collective-permute-start.5) | collective-permute-done | bytes 540704 | tf_op jit(solution)/shard_map/ppermute | solution.py:97
  60.9 2.8 %collective-permute-done.6.near_ref = f32[264,512]{1,0:T(8,128)S(1)} collective-permute-done((f32[264,512]{1,0:T(8,128)S(1)}, f32[264,512]{1,0:T(8,128)S(1)}, u32[]{:S(2)}, u32[]{:S(2)}) %collective-permute-start.6) | collective-permute-done | bytes 540704 | tf_op jit(solution)/shard_map/ppermute | solution.py:97
  63.7 2.9 %gradient_step.1 = (f32[16,16,512]{2,1,0:T(8,128)}, f32[3,8,16,16]{3,2,1,0:T(8,128)}) custom-call(f32[16,16,512]{2,1,0:T(8,128)S(1)} %get-tuple-element.14.o_0, f32[528,512]{1,0:T(8,128)S(1)} %collective-permute-done.4.swapped_ref, f32[264,512]{1,0:T(8,128)S(1)} %collective-permute-done.5.far_ref, f32[264,512]{1,0:T(8,128)S(1)} %collective-permute-done.6.near_ref, ...), custom_call_target="tpu_custom_call" | custom-call | flops 15000000 | bytes 4000000 | tf_op jit(solution)/shard_map/gradient_step/pallas_call | solution.py:478
  (13 shorter events, 0.0 us)
Async XLA Ops:
  0.6 17.0 %copy-start.6 = (f32[5]{0:T(128)S(1)}, f32[5]{0:T(128)}, u32[]{:S(2)}) copy-start(f32[5]{0:T(128)} %constant.12.clone) | copy-start | bytes 64
  0.6 17.0 %copy-start.2 = (f32[8,16,16]{2,1,0:T(8,128)S(1)}, f32[8,16,16]{2,1,0:T(8,128)}, u32[]{:S(2)}) copy-start(f32[8,16,16]{2,1,0:T(8,128)} %spread_ref.1) | copy-start | bytes 24580
  0.7 17.0 %copy-start.1 = (s32[8,16,16]{2,1,0:T(8,128)S(1)}, s32[8,16,16]{2,1,0:T(8,128)}, u32[]{:S(2)}) copy-start(s32[8,16,16]{2,1,0:T(8,128)} %index_ref.1) | copy-start | bytes 24580
  0.7 17.0 %copy-start = (f32[8,16,16]{2,1,0:T(8,128)S(1)}, f32[8,16,16]{2,1,0:T(8,128)}, u32[]{:S(2)}) copy-start(f32[8,16,16]{2,1,0:T(8,128)} %amp_ref.1) | copy-start | bytes 24580
  0.7 16.8 %copy-start.4 = (s32[4,512]{1,0:T(4,128)S(1)}, s32[4,512]{1,0:T(4,128)}, u32[]{:S(2)}) copy-start(s32[4,512]{1,0:T(4,128)} %param.11) | copy-start | bytes 24580
  0.7 16.8 %copy-start.5 = (f32[16]{0:T(128)S(1)}, f32[16]{0:T(128)}, u32[]{:S(2)}) copy-start(f32[16]{0:T(128)} %param.10) | copy-start | bytes 196
  2.0 31.6 %copy-start.3 = (bf16[6,80,160]{2,1,0:T(8,128)(2,1)S(1)}, bf16[6,80,160]{2,1,0:T(8,128)(2,1)}, u32[]{:S(2)}) copy-start(bf16[6,80,160]{2,1,0:T(8,128)(2,1)} %constant.14.clone.k_ref) | copy-start | bytes 460804
  2.0 31.6 %collective-permute-start.1 = (f32[264,512]{1,0:T(8,128)S(1)}, f32[264,512]{1,0:T(8,128)S(1)}, u32[]{:S(2)}, u32[]{:S(2)}) collective-permute-start(f32[264,512]{1,0:T(8,128)S(1)} %pack.1.x_ref), channel_id=1, source_target_pairs={{32,0},{64,32},{96,64},{128,96},{160,128},{192,160},{224,192},{256... | collective-permute-start | bytes 1622024 | tf_op jit(solution)/shard_map/ppermute | solution.py:91
  5.4 28.2 %collective-permute-start = (f32[264,512]{1,0:T(8,128)S(1)}, f32[264,512]{1,0:T(8,128)S(1)}, u32[]{:S(2)}, u32[]{:S(2)}) collective-permute-start(f32[264,512]{1,0:T(8,128)S(1)} %pack.1.x_ref), channel_id=1, source_target_pairs={{0,32},{32,64},{64,96},{96,128},{128,160},{160,192},{192,224},{224... | collective-permute-start | bytes 1622024 | tf_op jit(solution)/shard_map/ppermute | solution.py:91
  11.6 13.6 %collective-permute-start.3 = (f32[14,16,512]{2,1,0:T(8,128)S(1)}, f32[14,16,512]{2,1,0:T(8,128)S(1)}, u32[]{:S(2)}, u32[]{:S(2)}) collective-permute-start(f32[14,16,512]{2,1,0:T(8,128)S(1)} %get-tuple-element.22), channel_id=1, source_target_pairs={{64,0},{96,32},{128,64},{160,96},{192,128},{224,160},{256,192},{28... | collective-permute-start | bytes 1376264 | tf_op jit(solution)/shard_map/ppermute | solution.py:91
  15.2 18.4 %collective-permute-start.2 = (f32[14,16,512]{2,1,0:T(8,128)S(1)}, f32[14,16,512]{2,1,0:T(8,128)S(1)}, u32[]{:S(2)}, u32[]{:S(2)}) collective-permute-start(f32[14,16,512]{2,1,0:T(8,128)S(1)} %get-tuple-element.23), channel_id=1, source_target_pairs={{0,64},{32,96},{64,128},{96,160},{128,192},{160,224},{192,256},{22... | collective-permute-start | bytes 1376264 | tf_op jit(solution)/shard_map/ppermute | solution.py:91
  37.1 13.2 %collective-permute-start.4 = (f32[528,512]{1,0:T(8,128)S(1)}, f32[528,512]{1,0:T(8,128)S(1)}, u32[]{:S(2)}, u32[]{:S(2)}) collective-permute-start(f32[528,512]{1,0:T(8,128)S(1)} %get-tuple-element.15), channel_id=1, source_target_pairs={{0,1},{1,0},{2,3},{3,2},{4,5},{5,4},{6,7},{7,6},{8,9},{9,8},{10,11... | collective-permute-start | bytes 3244040 | tf_op jit(solution)/shard_map/ppermute | solution.py:516
  39.0 21.9 %collective-permute-start.5 = (f32[264,512]{1,0:T(8,128)S(1)}, f32[264,512]{1,0:T(8,128)S(1)}, u32[]{:S(2)}, u32[]{:S(2)}) collective-permute-start(f32[264,512]{1,0:T(8,128)S(1)} %get-tuple-element.16), channel_id=1, source_target_pairs={{1,3},{2,0},{3,5},{4,2},{5,7},{6,4},{7,9},{8,6},{9,11},{10,8},{11,... | collective-permute-start | bytes 1622024 | tf_op jit(solution)/shard_map/ppermute | solution.py:97
  50.3 13.4 %collective-permute-start.6 = (f32[264,512]{1,0:T(8,128)S(1)}, f32[264,512]{1,0:T(8,128)S(1)}, u32[]{:S(2)}, u32[]{:S(2)}) collective-permute-start(f32[264,512]{1,0:T(8,128)S(1)} %outward.1), channel_id=1, source_target_pairs={{0,2},{2,4},{3,1},{4,6},{5,3},{6,8},{7,5},{8,10},{9,7},{10,12},{11... | collective-permute-start | bytes 1622024 | tf_op jit(solution)/shard_map/ppermute | solution.py:97

commit v11 on v10

--- a/solution.py
+++ b/solution.py
@@ -15,6 +15,8 @@
 LANES = 128
 TAPS = (1, 4, 6, 4, 1)
 BEYOND = 2
+REACHED = TILE - BEYOND
+FAR_ROWS = TILE * REACHED + 8
 VMEM_LIMIT = 20 * 1024 * 1024
 ROLES = ((3, 1, 0, 2, 4), (1, 3, 4, 2, 0))
 PIXELS = TILE * TILE
@@ -78,7 +80,10 @@
         low = np.concatenate([p[1] for p in parts[2:]], axis=1)
         columns = np.concatenate([high, high, low], axis=1).reshape(5, TILE, -1)
         for order in ROLES:
-            kinds.append(np.concatenate([columns[i] for i in order]))
+            blocks = [columns[i] for i in order]
+            if order[2] == 0:
+                blocks[2] = np.roll(blocks[2], -BEYOND, axis=0)
+            kinds.append(np.concatenate(blocks))
     return np.stack(kinds)
 
 
@@ -278,18 +283,14 @@
     odd = lax.rem(ix, 2)
     columns = k_ref[column_kind()]
 
-    def column_pass(row, carry):
+    for row in range(TILE):
         got = jnp.dot(columns, y_ref[row], preferred_element_type=jnp.float32)
-        at = pl.ds(pl.multiple_of(row * TILE, TILE), TILE)
-        at_more = pl.ds(pl.multiple_of(row * TILE + PIXELS, TILE), TILE)
+        at = slice(row * TILE, (row + 1) * TILE)
         swap_ref[at] = got[:TILE]
-        swap_ref[at_more] = got[TILE : 2 * TILE]
-        far_ref[at] = got[2 * TILE : 3 * TILE]
+        swap_ref[row * TILE + PIXELS : (row + 1) * TILE + PIXELS] = got[TILE : 2 * TILE]
+        far_ref[row * REACHED : (row + 1) * REACHED] = got[2 * TILE : 2 * TILE + REACHED]
         o_0[row] = got[3 * TILE : 4 * TILE] + a_ref[0] * x_ref[at]
         near_ref[at] = got[4 * TILE :]
-        return carry
-
-    lax.fori_loop(0, TILE, column_pass, 0, unroll=16)
 
     params = with_rows(own_ref, m1[PIXELS:, :EXT], p1[PIXELS:, :EXT])
     for t in range(3):
@@ -306,7 +307,7 @@
 def wavelet_parts(coeff, tiles, own, w, nch, length):
     k = jnp.asarray(scatter_matrices(length))
     vmem = pl.BlockSpec(memory_space=pltpu.VMEM)
-    heights = (2 * (PIXELS + COMPS), PIXELS, PIXELS + COMPS)
+    heights = (2 * (PIXELS + COMPS), PIXELS, FAR_ROWS)
     shapes = [(TILE, TILE, nch)] + [(n, nch) for n in heights] + [own.shape]
     return pl.pallas_call(
         wavelet_kernel,
@@ -402,11 +403,40 @@
     )(amplitude, centre_index, spread, pltpu.with_memory_space_constraint(w, pltpu.HBM))
 
 
+def early_kernel(o_0, swapped_ref, far_ref, model_ref, part_ref, r_ref):
+    nch, pixels = model_ref.shape
+    even = lax.rem(lax.axis_index("skyx"), 2) == 0
+    place = lax.broadcasted_iota(jnp.int32, (TILE, nch), 0)
+    for row in range(TILE):
+        far = far_ref[row * REACHED : row * REACHED + TILE]
+        far = jnp.where(place < REACHED, far, 0.0)
+        far = jnp.where(even, pltpu.roll(far, BEYOND, 0), far)
+        part_ref[row] = (o_0[row] + swapped_ref[row * TILE : (row + 1) * TILE]) + far
+    rows = LANES // TILE
+    for part in range(pixels // LANES):
+        block = part_ref[part * rows : (part + 1) * rows].reshape(LANES, nch)
+        at = slice(part * LANES, (part + 1) * LANES)
+        r_ref[:, at] = model_ref[:, at] - block.T
+
+
+def early_part(o_0, swapped, far, model):
+    vmem = pl.BlockSpec(memory_space=pltpu.VMEM)
+    return pl.pallas_call(
+        early_kernel,
+        out_shape=[pltpu.VMEM(o_0.shape, jnp.float32), pltpu.VMEM(model.shape, jnp.float32)],
+        in_specs=[vmem] * 4,
+        out_specs=[vmem] * 2,
+        compiler_params=pltpu.CompilerParams(vmem_limit_bytes=VMEM_LIMIT),
+        cost_estimate=pl.CostEstimate(flops=2_000_000_000, bytes_accessed=9_000_000, transcendentals=0),
+        name="early_part",
+    )(*[kept(x) for x in (o_0, swapped, far, model)])
+
+
 def step_kernel(
-    o_0, swapped_ref, far_ref, near_ref, model_ref, bump_ref, flat_ref, ext_ref,
+    part_ref, early_ref, swapped_ref, near_ref, bump_ref, flat_ref, ext_ref,
     den_hbm, fit_ref, den_ref, r_ref, sem,
 ):
-    nch, pixels = model_ref.shape
+    nch, pixels = early_ref.shape
     rows = LANES // TILE
     parts = pixels // LANES
     copies = []
@@ -418,16 +448,15 @@
         at = slice(part * rows, (part + 1) * rows)
         for row in range(part * rows, (part + 1) * rows):
             flat = slice(row * TILE, (row + 1) * TILE)
-            den_ref[row] = (o_0[row] + swapped_ref[flat]) + (far_ref[flat] + near_ref[flat])
+            den_ref[row] = part_ref[row] + near_ref[flat]
         copies.append(pltpu.make_async_copy(den_ref.at[at], den_hbm.at[at], sem.at[part]))
         copies[-1].start()
 
     shape = (COMPS, rows, LANES)
     own_lanes = lax.broadcasted_iota(jnp.int32, shape, 2) // TILE == lax.broadcasted_iota(jnp.int32, shape, 1)
     for part in range(parts):
-        block = den_ref[part * rows : (part + 1) * rows].reshape(LANES, nch)
         at = slice(part * LANES, (part + 1) * LANES)
-        r_ref[:, at] = model_ref[:, at] - block.T
+        r_ref[:, at] = early_ref[:, at] - near_ref[at].T
 
     for part in range(parts):
         at = slice(part * LANES, (part + 1) * LANES)
@@ -472,26 +501,26 @@
         copy.wait()
 
 
-def gradient_step(parts, model, bump, flat, ext):
+def gradient_step(part, early, swapped, near, bump, flat, ext):
     vmem = pl.BlockSpec(memory_space=pltpu.VMEM)
-    shape = parts[0].shape
+    shape = part.shape
     return pl.pallas_call(
         step_kernel,
         out_shape=[
             jax.ShapeDtypeStruct(shape, jnp.float32),
             jax.ShapeDtypeStruct((3, COMPS, TILE, TILE), jnp.float32),
         ],
-        in_specs=[vmem] * 8,
+        in_specs=[vmem] * 7,
         out_specs=[pl.BlockSpec(memory_space=pl.ANY), vmem],
         scratch_shapes=[
             pltpu.VMEM(shape, jnp.float32),
-            pltpu.VMEM(model.shape, jnp.float32),
+            pltpu.VMEM(early.shape, jnp.float32),
             pltpu.SemaphoreType.DMA((2,)),
         ],
         compiler_params=pltpu.CompilerParams(vmem_limit_bytes=VMEM_LIMIT),
         cost_estimate=pl.CostEstimate(flops=15_000_000, bytes_accessed=4_000_000, transcendentals=1_100_000),
         name="gradient_step",
-    )(*[kept(x) for x in (*parts, model, bump, flat, ext)])
+    )(*[kept(x) for x in (part, early, swapped, near, bump, flat, ext)])
 
 
 def on_device(cube, level_table, level_index, amplitude, centre_index, spread):
@@ -516,7 +545,8 @@
     swapped = lax.ppermute(swap, "skyx", partner)
     far = away(far, "skyx", 2)
     near = away(outward(near, swapped), "skyx", -2)
-    return gradient_step((o_0, swapped, far, near), model, bump, flat, ext)
+    part, early = early_part(o_0, swapped, far, model)
+    return gradient_step(part, early, swapped, near, bump, flat, ext)
 
 
 def solution(mesh):

time: 67 us -> 66.9 us (level)
  no operation moved by 1% of the time
where the time goes in v11:
time: 66.9 us; the launch traced here: 66.6 us
  starting transfers between devices  29.3 us (44%)
  waiting for transfers between devices  25.3 us (38%)
  Pallas kernels  9.68 us (14%)
  local copies, waits for them, and re-layouts  1.28 us (2%)
  between operations  0.84 us (1%)
    ppermute x4, starting transfers between devices, sent(): return lax.ppermute(values, axis, pairs)  14.2 us
    ppermute x4, waiting for transfers between devices, sent(): return lax.ppermute(values, axis, pairs)  14.2 us
    ppermute x2, starting transfers between devices, away(): lax.ppermute(values, axis, [(i, j) for i, j in pairs if 0 <= j < size])  13.1 us
    ppermute x2, waiting for transfers between devices, away(): lax.ppermute(values, axis, [(i, j) for i, j in pairs if 0 <= j < size])  11.2 us
    pallas_call x1, Pallas kernels, wavelet_parts(): pl.pallas_call(wavelet_kernel, out_shape=[pltpu.VMEM(shape, jnp.float32)...  3.47 us
    pallas_call x1, Pallas kernels, gradient_step(): pl.pallas_call(step_kernel, out_shape=[jax.ShapeDtypeStruct(shape, jnp.fl...  2.9 us
    ppermute x1, starting transfers between devices, on_device(): swapped = lax.ppermute(swap, 'skyx', partner)  1.92 us
    pallas_call x1, Pallas kernels, model_of(): pl.pallas_call(model_kernel, out_shape=[pltpu.VMEM((nch, pixels), jnp.flo...  1.72 us
  transfers between devices with their start and end apart: 7, of which 4 were waited for; matrix products, arithmetic and copies ran while one was open for 2% of the time, Pallas kernels for 3%

profile of v11, /device:TPU:38, one launch (start us, length us, event | category | flops | bytes accessed | tf_op | source)
XLA Modules:
  0.0 66.6 jit_solution(9376287027126037309)
XLA Ops:
  0.6 0.0 copy-start.6
  0.7 1.3 %pack.1.x_ref = f32[264,512]{1,0:T(8,128)S(1)} custom-call(f32[256,512]{1,0:T(8,128)} %bitcast.1, f32[8,16,16]{2,1,0:T(8,128)} %amp_ref.1, s32[8,16,16]{2,1,0:T(8,128)} %index_ref.1, f32[8,16,16]{2,1,0:T(8,128)} %spread_ref.1), custom_call_target="tpu_custom_call" | custom-call | flops 1000 | bytes 1000000 | tf_op jit(solution)/shard_map/pack/pallas_call | solution.py:133
  2.0 0.0 copy-start.3
  2.0 3.4 %collective-permute-start.1 = (f32[264,512]{1,0:T(8,128)S(1)}, f32[264,512]{1,0:T(8,128)S(1)}, u32[]{:S(2)}, u32[]{:S(2)}) collective-permute-start(f32[264,512]{1,0:T(8,128)S(1)} %pack.1.x_ref), channel_id=1, source_target_pairs={{32,0},{64,32},{96,64},{128,96},{160,128},{192,160},{224,192},{256... | collective-permute-start | bytes 1622024 | tf_op jit(solution)/shard_map/ppermute | solution.py:96
  5.4 4.9 %collective-permute-start = (f32[264,512]{1,0:T(8,128)S(1)}, f32[264,512]{1,0:T(8,128)S(1)}, u32[]{:S(2)}, u32[]{:S(2)}) collective-permute-start(f32[264,512]{1,0:T(8,128)S(1)} %pack.1.x_ref), channel_id=1, source_target_pairs={{0,32},{32,64},{64,96},{96,128},{128,160},{160,192},{192,224},{224... | collective-permute-start | bytes 1622024 | tf_op jit(solution)/shard_map/ppermute | solution.py:96
  10.4 1.2 %fusion = (f32[14,16,512]{2,1,0:T(8,128)S(1)}, f32[14,16,512]{2,1,0:T(8,128)S(1)}) fusion(f32[16,16,512]{2,1,0:T(8,128)} %param.9), kind=kLoop, calls=%fused_computation.3 | loop fusion | bytes 1835008 | tf_op jit(solution)/shard_map/slice | solution.py:533
  11.6 3.6 %collective-permute-start.3 = (f32[14,16,512]{2,1,0:T(8,128)S(1)}, f32[14,16,512]{2,1,0:T(8,128)S(1)}, u32[]{:S(2)}, u32[]{:S(2)}) collective-permute-start(f32[14,16,512]{2,1,0:T(8,128)S(1)} %get-tuple-element.26), channel_id=1, source_target_pairs={{64,0},{96,32},{128,64},{160,96},{192,128},{224,160},{256,192},{28... | collective-permute-start | bytes 1376264 | tf_op jit(solution)/shard_map/ppermute | solution.py:96
  15.2 2.3 %collective-permute-start.2 = (f32[14,16,512]{2,1,0:T(8,128)S(1)}, f32[14,16,512]{2,1,0:T(8,128)S(1)}, u32[]{:S(2)}, u32[]{:S(2)}) collective-permute-start(f32[14,16,512]{2,1,0:T(8,128)S(1)} %get-tuple-element.27), channel_id=1, source_target_pairs={{0,64},{32,96},{64,128},{96,160},{128,192},{160,224},{192,256},{22... | collective-permute-start | bytes 1376264 | tf_op jit(solution)/shard_map/ppermute | solution.py:96
  17.5 0.1 select_reduce_fusion
  17.6 0.1 subtract_multiply_fusion
  17.7 1.7 %gaussian_model.1 = (f32[512,256]{1,0:T(8,128)S(1)}, f32[3,8,256]{2,1,0:T(8,128)S(1)}, f32[3,8,384]{2,1,0:T(8,128)S(1)}, bf16[6,3,256,256]{3,2,1,0:T(8,128)(2,1)S(1)}, f32[8,512,256]{2,1,0:T(8,128)S(1)}) custom-call(f32[8,16,16]{2,1,0:T(8,128)S(1)} %copy-done, s32[8,16,16]{2,1,0:T(8,128)S(1)} %copy-done.1, f32[8,16,16]{2,1,0:T(8,128)S(1)} %copy-done.2, ...), custom_call_target="tpu_custom_call" | custom-call | flops 10000000 | bytes 1000000 | tf_op jit(solution)/shard_map/gaussian_model/pallas_call | solution.py:388
  19.4 5.8 %collective-permute-done.3.p2 = f32[14,16,512]{2,1,0:T(8,128)S(1)} collective-permute-done((f32[14,16,512]{2,1,0:T(8,128)S(1)}, f32[14,16,512]{2,1,0:T(8,128)S(1)}, u32[]{:S(2)}, u32[]{:S(2)}) %collective-permute-start.3) | collective-permute-done | bytes 458784 | tf_op jit(solution)/shard_map/ppermute | solution.py:96
  25.2 8.4 %collective-permute-done.2.m2 = f32[14,16,512]{2,1,0:T(8,128)S(1)} collective-permute-done((f32[14,16,512]{2,1,0:T(8,128)S(1)}, f32[14,16,512]{2,1,0:T(8,128)S(1)}, u32[]{:S(2)}, u32[]{:S(2)}) %collective-permute-start.2) | collective-permute-done | bytes 458784 | tf_op jit(solution)/shard_map/ppermute | solution.py:96
  33.6 0.0 collective-permute-done.1.p1
  33.6 0.0 collective-permute-done.m1
  33.6 3.5 %wavelet_parts.1 = (f32[16,16,512]{2,1,0:T(8,128)S(1)}, f32[528,512]{1,0:T(8,128)S(1)}, f32[256,512]{1,0:T(8,128)S(1)}, f32[232,512]{1,0:T(8,128)S(1)}, f32[3,8,384]{2,1,0:T(8,128)S(1)}) custom-call(f32[5,1,512]{2,1,0:T(1,128)S(1)} %broadcast_in_dim.2.a_ref, f32[264,512]{1,0:T(8,128)S(1)} %collective-permute-done.m1, ...), custom_call_target="tpu_custom_call" | custom-call | flops 4000000000 | bytes 9000000 | tf_op jit(solution)/shard_map/wavelet_parts/pallas_call | solution.py:312
  37.1 1.9 %collective-permute-start.4 = (f32[528,512]{1,0:T(8,128)S(1)}, f32[528,512]{1,0:T(8,128)S(1)}, u32[]{:S(2)}, u32[]{:S(2)}) collective-permute-start(f32[528,512]{1,0:T(8,128)S(1)} %get-tuple-element.17), channel_id=1, source_target_pairs={{0,1},{1,0},{2,3},{3,2},{4,5},{5,4},{6,7},{7,6},{8,9},{9,8},{10,11... | collective-permute-start | bytes 3244040 | tf_op jit(solution)/shard_map/ppermute | solution.py:545
  39.0 11.2 %collective-permute-start.5 = (f32[232,512]{1,0:T(8,128)S(1)}, f32[232,512]{1,0:T(8,128)S(1)}, u32[]{:S(2)}, u32[]{:S(2)}) collective-permute-start(f32[232,512]{1,0:T(8,128)S(1)} %get-tuple-element.18), channel_id=1, source_target_pairs={{1,3},{2,0},{3,5},{4,2},{5,7},{6,4},{7,9},{8,6},{9,11},{10,8},{11,... | collective-permute-start | bytes 1425416 | tf_op jit(solution)/shard_map/ppermute | solution.py:102
  50.2 0.1 outward.1
  50.3 1.9 %collective-permute-start.6 = (f32[264,512]{1,0:T(8,128)S(1)}, f32[264,512]{1,0:T(8,128)S(1)}, u32[]{:S(2)}, u32[]{:S(2)}) collective-permute-start(f32[264,512]{1,0:T(8,128)S(1)} %outward.1), channel_id=1, source_target_pairs={{0,2},{2,4},{3,1},{4,6},{5,3},{6,8},{7,5},{8,10},{9,7},{10,12},{11... | collective-permute-start | bytes 1622024 | tf_op jit(solution)/shard_map/ppermute | solution.py:102
  52.3 7.2 %collective-permute-done.5.far_ref = f32[232,512]{1,0:T(8,128)S(1)} collective-permute-done((f32[232,512]{1,0:T(8,128)S(1)}, f32[232,512]{1,0:T(8,128)S(1)}, u32[]{:S(2)}, u32[]{:S(2)}) %collective-permute-start.5) | collective-permute-done | bytes 475168 | tf_op jit(solution)/shard_map/ppermute | solution.py:102
  59.5 0.2 early_part.1
  59.7 4.0 %collective-permute-done.6.near_ref = f32[264,512]{1,0:T(8,128)S(1)} collective-permute-done((f32[264,512]{1,0:T(8,128)S(1)}, f32[264,512]{1,0:T(8,128)S(1)}, u32[]{:S(2)}, u32[]{:S(2)}) %collective-permute-start.6) | collective-permute-done | bytes 540704 | tf_op jit(solution)/shard_map/ppermute | solution.py:102
  63.7 2.9 %gradient_step.1 = (f32[16,16,512]{2,1,0:T(8,128)}, f32[3,8,16,16]{3,2,1,0:T(8,128)}) custom-call(f32[16,16,512]{2,1,0:T(8,128)S(1)} %get-tuple-element.20.part_ref, f32[512,256]{1,0:T(8,128)S(1)} %get-tuple-element.21.early_ref, f32[528,512]{1,0:T(8,128)S(1)} %collective-permute-done.4.swapped_ref, f32[264,512]{1,0:T(8,128)S(1)} %collective-permute-done.6.near_ref, ...), custom_call_target="tpu_custom_call" | custom-call | flops 15000000 | bytes 4000000 | tf_op jit(solution)/shard_map/gradient_step/pallas_call | solution.py:507
  (14 shorter events, 0.0 us)
Async XLA Ops:
  0.6 17.0 %copy-start.6 = (f32[5]{0:T(128)S(1)}, f32[5]{0:T(128)}, u32[]{:S(2)}) copy-start(f32[5]{0:T(128)} %constant.12.clone) | copy-start | bytes 64
  0.6 17.0 %copy-start.2 = (f32[8,16,16]{2,1,0:T(8,128)S(1)}, f32[8,16,16]{2,1,0:T(8,128)}, u32[]{:S(2)}) copy-start(f32[8,16,16]{2,1,0:T(8,128)} %spread_ref.1) | copy-start | bytes 24580
  0.7 17.0 %copy-start.1 = (s32[8,16,16]{2,1,0:T(8,128)S(1)}, s32[8,16,16]{2,1,0:T(8,128)}, u32[]{:S(2)}) copy-start(s32[8,16,16]{2,1,0:T(8,128)} %index_ref.1) | copy-start | bytes 24580
  0.7 17.0 %copy-start = (f32[8,16,16]{2,1,0:T(8,128)S(1)}, f32[8,16,16]{2,1,0:T(8,128)}, u32[]{:S(2)}) copy-start(f32[8,16,16]{2,1,0:T(8,128)} %amp_ref.1) | copy-start | bytes 24580
  0.7 16.8 %copy-start.4 = (s32[4,512]{1,0:T(4,128)S(1)}, s32[4,512]{1,0:T(4,128)}, u32[]{:S(2)}) copy-start(s32[4,512]{1,0:T(4,128)} %param.11) | copy-start | bytes 24580
  0.7 16.8 %copy-start.5 = (f32[16]{0:T(128)S(1)}, f32[16]{0:T(128)}, u32[]{:S(2)}) copy-start(f32[16]{0:T(128)} %param.10) | copy-start | bytes 196
  2.0 31.6 %copy-start.3 = (bf16[6,80,160]{2,1,0:T(8,128)(2,1)S(1)}, bf16[6,80,160]{2,1,0:T(8,128)(2,1)}, u32[]{:S(2)}) copy-start(bf16[6,80,160]{2,1,0:T(8,128)(2,1)} %constant.14.clone.k_ref) | copy-start | bytes 460804
  2.0 31.6 %collective-permute-start.1 = (f32[264,512]{1,0:T(8,128)S(1)}, f32[264,512]{1,0:T(8,128)S(1)}, u32[]{:S(2)}, u32[]{:S(2)}) collective-permute-start(f32[264,512]{1,0:T(8,128)S(1)} %pack.1.x_ref), channel_id=1, source_target_pairs={{32,0},{64,32},{96,64},{128,96},{160,128},{192,160},{224,192},{256... | collective-permute-start | bytes 1622024 | tf_op jit(solution)/shard_map/ppermute | solution.py:96
  5.4 28.2 %collective-permute-start = (f32[264,512]{1,0:T(8,128)S(1)}, f32[264,512]{1,0:T(8,128)S(1)}, u32[]{:S(2)}, u32[]{:S(2)}) collective-permute-start(f32[264,512]{1,0:T(8,128)S(1)} %pack.1.x_ref), channel_id=1, source_target_pairs={{0,32},{32,64},{64,96},{96,128},{128,160},{160,192},{192,224},{224... | collective-permute-start | bytes 1622024 | tf_op jit(solution)/shard_map/ppermute | solution.py:96
  11.6 13.6 %collective-permute-start.3 = (f32[14,16,512]{2,1,0:T(8,128)S(1)}, f32[14,16,512]{2,1,0:T(8,128)S(1)}, u32[]{:S(2)}, u32[]{:S(2)}) collective-permute-start(f32[14,16,512]{2,1,0:T(8,128)S(1)} %get-tuple-element.26), channel_id=1, source_target_pairs={{64,0},{96,32},{128,64},{160,96},{192,128},{224,160},{256,192},{28... | collective-permute-start | bytes 1376264 | tf_op jit(solution)/shard_map/ppermute | solution.py:96
  15.2 18.4 %collective-permute-start.2 = (f32[14,16,512]{2,1,0:T(8,128)S(1)}, f32[14,16,512]{2,1,0:T(8,128)S(1)}, u32[]{:S(2)}, u32[]{:S(2)}) collective-permute-start(f32[14,16,512]{2,1,0:T(8,128)S(1)} %get-tuple-element.27), channel_id=1, source_target_pairs={{0,64},{32,96},{64,128},{96,160},{128,192},{160,224},{192,256},{22... | collective-permute-start | bytes 1376264 | tf_op jit(solution)/shard_map/ppermute | solution.py:96
  37.1 13.2 %collective-permute-start.4 = (f32[528,512]{1,0:T(8,128)S(1)}, f32[528,512]{1,0:T(8,128)S(1)}, u32[]{:S(2)}, u32[]{:S(2)}) collective-permute-start(f32[528,512]{1,0:T(8,128)S(1)} %get-tuple-element.17), channel_id=1, source_target_pairs={{0,1},{1,0},{2,3},{3,2},{4,5},{5,4},{6,7},{7,6},{8,9},{9,8},{10,11... | collective-permute-start | bytes 3244040 | tf_op jit(solution)/shard_map/ppermute | solution.py:545
  39.0 20.5 %collective-permute-start.5 = (f32[232,512]{1,0:T(8,128)S(1)}, f32[232,512]{1,0:T(8,128)S(1)}, u32[]{:S(2)}, u32[]{:S(2)}) collective-permute-start(f32[232,512]{1,0:T(8,128)S(1)} %get-tuple-element.18), channel_id=1, source_target_pairs={{1,3},{2,0},{3,5},{4,2},{5,7},{6,4},{7,9},{8,6},{9,11},{10,8},{11,... | collective-permute-start | bytes 1425416 | tf_op jit(solution)/shard_map/ppermute | solution.py:102
  50.3 13.4 %collective-permute-start.6 = (f32[264,512]{1,0:T(8,128)S(1)}, f32[264,512]{1,0:T(8,128)S(1)}, u32[]{:S(2)}, u32[]{:S(2)}) collective-permute-start(f32[264,512]{1,0:T(8,128)S(1)} %outward.1), channel_id=1, source_target_pairs={{0,2},{2,4},{3,1},{4,6},{5,3},{6,8},{7,5},{8,10},{9,7},{10,12},{11... | collective-permute-start | bytes 1622024 | tf_op jit(solution)/shard_map/ppermute | solution.py:102

commit v12 on v11

--- a/solution.py
+++ b/solution.py
@@ -207,18 +207,17 @@
 
 
 def wavelet_kernel(
-    a_ref, m1, p1, m2, p2, x_ref, k_ref, own_ref, w_ref,
+    a_ref, inside_ref, outside_ref, m2, p2, x_ref, k_ref, own_ref, w_ref,
     o_0, swap_ref, near_ref, far_ref, ext_ref, rows_ref, y_ref,
 ):
     nch = x_ref.shape[1]
-    tiles = (m2, m1, x_ref, p1, p2)
     iy, ix = lax.axis_index("skyy"), lax.axis_index("skyx")
     near = [iy + i for i in (-2, -1, 0, 1, 2)]
     flags = [jnp.where((i >= 0) & (i < lax.axis_size("skyy")), 1.0, 0.0) for i in near]
 
     lane_tiles = nch // LANES
 
-    def row_pass(step, carry):
+    def row_pass(tiles, step, carry):
         sub = pl.ds(pl.multiple_of((step // lane_tiles) * 8, 8), 8)
         lane = pl.ds(pl.multiple_of((step % lane_tiles) * LANES, LANES), LANES)
 
@@ -246,7 +245,18 @@
                         rows_ref[level - 1, row, sub, lane] = got
         return carry
 
-    lax.fori_loop(0, 2 * lane_tiles, row_pass, 0)
+    even_row = lax.rem(iy, 2) == 0
+
+    @pl.when(even_row)
+    def _():
+        tiles = (m2, outside_ref, x_ref, inside_ref, p2)
+        lax.fori_loop(0, 2 * lane_tiles, functools.partial(row_pass, tiles), 0)
+
+    @pl.when(jnp.logical_not(even_row))
+    def _():
+        tiles = (m2, inside_ref, x_ref, outside_ref, p2)
+        lax.fori_loop(0, 2 * lane_tiles, functools.partial(row_pass, tiles), 0)
+
 
     half, quarter = nch // 2, nch // 4
 
@@ -292,7 +302,9 @@
         o_0[row] = got[3 * TILE : 4 * TILE] + a_ref[0] * x_ref[at]
         near_ref[at] = got[4 * TILE :]
 
-    params = with_rows(own_ref, m1[PIXELS:, :EXT], p1[PIXELS:, :EXT])
+    inside, outside = inside_ref[PIXELS:, :EXT], outside_ref[PIXELS:, :EXT]
+    above, below = jnp.where(even_row, outside, inside), jnp.where(even_row, inside, outside)
+    params = with_rows(own_ref, above, below)
     for t in range(3):
         ext_ref[t] = params[t]
     to_right, to_left = border_columns(ext_ref, TILE - 2), border_columns(ext_ref, 0)
@@ -461,8 +473,8 @@
     for part in range(parts):
         at = slice(part * LANES, (part + 1) * LANES)
         sums = [[] for _ in range(3)]
-        for first in range(0, COMPS, 4):
-            chosen = range(first, first + 4)
+        for first in range(0, COMPS, 8):
+            chosen = range(first, first + 8)
             mus = [jnp.broadcast_to(flat_ref[1, k : k + 1, at], (8, LANES)) for k in chosen]
 
             def body(step, carry):
@@ -478,10 +490,10 @@
                 return tuple(out)
 
             zero = jnp.zeros((8, LANES), jnp.float32)
-            done = lax.fori_loop(0, nch // 8, body, ((zero,) * 3,) * 4, unroll=16)
-            for four in done:
+            done = lax.fori_loop(0, nch // 8, body, ((zero,) * 3,) * 8, unroll=16)
+            for sums_of_one in done:
                 for t in range(3):
-                    sums[t].append(jnp.sum(four[t], axis=0, keepdims=True))
+                    sums[t].append(jnp.sum(sums_of_one[t], axis=0, keepdims=True))
         amp = flat_ref[0, :, at]
         inv = flat_ref[2, :, at]
         slope = amp * inv * inv
@@ -529,7 +541,8 @@
     partner = [(i, i ^ 1) for i in range(size)]
 
     tile = packed(cube.reshape(PIXELS, nch), amplitude, centre_index, spread)
-    up1, down1 = sent(tile, "skyy", 1), sent(tile, "skyy", -1)
+    inside = lax.ppermute(tile, "skyy", [(i, i ^ 1) for i in range(lax.axis_size("skyy"))])
+    outside = away(tile, "skyy", 1)
     up2, down2 = sent(cube[BEYOND:], "skyy", 2), sent(cube[:-BEYOND], "skyy", -2)
 
     entries = jnp.arange(level_table.shape[0], dtype=jnp.int32)
@@ -540,7 +553,7 @@
     scale = jnp.array([16.0 ** (-3 * j) for j in range(LEVELS + 1)], jnp.float32)
     coeff = (coeff * scale[:, None])[:, None, :]
     model, flat, own, w, bump = model_of(amplitude, centre_index, spread, nch)
-    o_0, swap, near, far, ext = wavelet_parts(coeff, (up1, down1, up2, down2, tile), own, w, nch, size * TILE)
+    o_0, swap, near, far, ext = wavelet_parts(coeff, (inside, outside, up2, down2, tile), own, w, nch, size * TILE)
 
     swapped = lax.ppermute(swap, "skyx", partner)
     far = away(far, "skyx", 2)

time: 66.9 us -> 66.4 us (level)
  the two profiles are of different devices: /device:TPU:38 before, /device:TPU:30 now
where the time goes in v12:
time: 66.4 us; the launch traced here: 66.1 us
  starting transfers between devices  29.7 us (45%)
  waiting for transfers between devices  24.5 us (37%)
  Pallas kernels  9.55 us (14%)
  local copies, waits for them, and re-layouts  1.28 us (2%)
  between operations  0.84 us (1%)
    ppermute x3, starting transfers between devices, away(): lax.ppermute(values, axis, [(i, j) for i, j in pairs if 0 <= j < size])  18.8 us
    ppermute x3, waiting for transfers between devices, away(): lax.ppermute(values, axis, [(i, j) for i, j in pairs if 0 <= j < size])  11.2 us
    ppermute x2, waiting for transfers between devices, sent(): return lax.ppermute(values, axis, pairs)  9.17 us
    ppermute x2, starting transfers between devices, sent(): return lax.ppermute(values, axis, pairs)  7.05 us
    ppermute x1, waiting for transfers between devices, on_device(): lax.ppermute(tile, 'skyy', [(i, i ^ 1) for i in range(lax.axis_size('skyy...  4.18 us
    pallas_call x1, Pallas kernels, wavelet_parts(): pl.pallas_call(wavelet_kernel, out_shape=[pltpu.VMEM(shape, jnp.float32)...  3.41 us
    pallas_call x1, Pallas kernels, gradient_step(): pl.pallas_call(step_kernel, out_shape=[jax.ShapeDtypeStruct(shape, jnp.fl...  2.84 us
    ppermute x1, starting transfers between devices, on_device(): swapped = lax.ppermute(swap, 'skyx', partner)  1.93 us
  transfers between devices with their start and end apart: 7, of which 5 were waited for; matrix products, arithmetic and copies ran while one was open for 2% of the time, Pallas kernels for 3%

profile of v12, /device:TPU:30, one launch (start us, length us, event | category | flops | bytes accessed | tf_op | source)
XLA Modules:
  0.0 66.1 jit_solution(7624654409211676445)
XLA Ops:
  0.6 0.0 copy-start.6
  0.7 1.3 %pack.1.x_ref = f32[264,512]{1,0:T(8,128)S(1)} custom-call(f32[256,512]{1,0:T(8,128)} %bitcast.1, f32[8,16,16]{2,1,0:T(8,128)} %amp_ref.1, s32[8,16,16]{2,1,0:T(8,128)} %index_ref.1, f32[8,16,16]{2,1,0:T(8,128)} %spread_ref.1), custom_call_target="tpu_custom_call" | custom-call | flops 1000 | bytes 1000000 | tf_op jit(solution)/shard_map/pack/pallas_call | solution.py:133
  2.0 0.0 copy-start.3
  2.0 5.7 %collective-permute-start.1 = (f32[264,512]{1,0:T(8,128)S(1)}, f32[264,512]{1,0:T(8,128)S(1)}, u32[]{:S(2)}, u32[]{:S(2)}) collective-permute-start(f32[264,512]{1,0:T(8,128)S(1)} %pack.1.x_ref), channel_id=1, source_target_pairs={{32,64},{64,32},{96,128},{128,96},{160,192},{192,160},{224,256},{2... | collective-permute-start | bytes 1622024 | tf_op jit(solution)/shard_map/ppermute | solution.py:102
  7.6 1.9 %collective-permute-start = (f32[264,512]{1,0:T(8,128)S(1)}, f32[264,512]{1,0:T(8,128)S(1)}, u32[]{:S(2)}, u32[]{:S(2)}) collective-permute-start(f32[264,512]{1,0:T(8,128)S(1)} %pack.1.x_ref), channel_id=1, source_target_pairs={{0,32},{32,0},{64,96},{96,64},{128,160},{160,128},{192,224},{224,1... | collective-permute-start | bytes 1622024 | tf_op jit(solution)/shard_map/ppermute | solution.py:544
  9.6 1.2 %fusion = (f32[14,16,512]{2,1,0:T(8,128)S(1)}, f32[14,16,512]{2,1,0:T(8,128)S(1)}) fusion(f32[16,16,512]{2,1,0:T(8,128)} %param.9), kind=kLoop, calls=%fused_computation.3 | loop fusion | bytes 1835008 | tf_op jit(solution)/shard_map/slice | solution.py:546
  10.8 2.1 %collective-permute-start.3 = (f32[14,16,512]{2,1,0:T(8,128)S(1)}, f32[14,16,512]{2,1,0:T(8,128)S(1)}, u32[]{:S(2)}, u32[]{:S(2)}) collective-permute-start(f32[14,16,512]{2,1,0:T(8,128)S(1)} %get-tuple-element.26), channel_id=1, source_target_pairs={{64,0},{96,32},{128,64},{160,96},{192,128},{224,160},{256,192},{28... | collective-permute-start | bytes 1376264 | tf_op jit(solution)/shard_map/ppermute | solution.py:96
  13.0 4.9 %collective-permute-start.2 = (f32[14,16,512]{2,1,0:T(8,128)S(1)}, f32[14,16,512]{2,1,0:T(8,128)S(1)}, u32[]{:S(2)}, u32[]{:S(2)}) collective-permute-start(f32[14,16,512]{2,1,0:T(8,128)S(1)} %get-tuple-element.27), channel_id=1, source_target_pairs={{0,64},{32,96},{64,128},{96,160},{128,192},{160,224},{192,256},{22... | collective-permute-start | bytes 1376264 | tf_op jit(solution)/shard_map/ppermute | solution.py:96
  17.9 0.1 select_reduce_fusion
  18.0 0.1 subtract_multiply_fusion
  18.1 1.7 %gaussian_model.1 = (f32[512,256]{1,0:T(8,128)S(1)}, f32[3,8,256]{2,1,0:T(8,128)S(1)}, f32[3,8,384]{2,1,0:T(8,128)S(1)}, bf16[6,3,256,256]{3,2,1,0:T(8,128)(2,1)S(1)}, f32[8,512,256]{2,1,0:T(8,128)S(1)}) custom-call(f32[8,16,16]{2,1,0:T(8,128)S(1)} %copy-done, s32[8,16,16]{2,1,0:T(8,128)S(1)} %copy-done.1, f32[8,16,16]{2,1,0:T(8,128)S(1)} %copy-done.2, ...), custom_call_target="tpu_custom_call" | custom-call | flops 10000000 | bytes 1000000 | tf_op jit(solution)/shard_map/gaussian_model/pallas_call | solution.py:400
  19.9 6.0 %collective-permute-done.3.p2 = f32[14,16,512]{2,1,0:T(8,128)S(1)} collective-permute-done((f32[14,16,512]{2,1,0:T(8,128)S(1)}, f32[14,16,512]{2,1,0:T(8,128)S(1)}, u32[]{:S(2)}, u32[]{:S(2)}) %collective-permute-start.3) | collective-permute-done | bytes 458784 | tf_op jit(solution)/shard_map/ppermute | solution.py:96
  25.9 3.1 %collective-permute-done.2.m2 = f32[14,16,512]{2,1,0:T(8,128)S(1)} collective-permute-done((f32[14,16,512]{2,1,0:T(8,128)S(1)}, f32[14,16,512]{2,1,0:T(8,128)S(1)}, u32[]{:S(2)}, u32[]{:S(2)}) %collective-permute-start.2) | collective-permute-done | bytes 458784 | tf_op jit(solution)/shard_map/ppermute | solution.py:96
  29.0 0.0 collective-permute-done.1.outside_ref
  29.0 4.2 %collective-permute-done.inside_ref = f32[264,512]{1,0:T(8,128)S(1)} collective-permute-done((f32[264,512]{1,0:T(8,128)S(1)}, f32[264,512]{1,0:T(8,128)S(1)}, u32[]{:S(2)}, u32[]{:S(2)}) %collective-permute-start) | collective-permute-done | bytes 540704 | tf_op jit(solution)/shard_map/ppermute | solution.py:544
  33.2 3.4 %wavelet_parts.1 = (f32[16,16,512]{2,1,0:T(8,128)S(1)}, f32[528,512]{1,0:T(8,128)S(1)}, f32[256,512]{1,0:T(8,128)S(1)}, f32[232,512]{1,0:T(8,128)S(1)}, f32[3,8,384]{2,1,0:T(8,128)S(1)}) custom-call(f32[5,1,512]{2,1,0:T(1,128)S(1)} %broadcast_in_dim.2.a_ref, f32[264,512]{1,0:T(8,128)S(1)} %collective-permute-done.inside_ref, ...), custom_call_target="tpu_custom_call" | custom-call | flops 4000000000 | bytes 9000000 | tf_op jit(solution)/shard_map/wavelet_parts/pallas_call | solution.py:324
  36.6 1.9 %collective-permute-start.4 = (f32[528,512]{1,0:T(8,128)S(1)}, f32[528,512]{1,0:T(8,128)S(1)}, u32[]{:S(2)}, u32[]{:S(2)}) collective-permute-start(f32[528,512]{1,0:T(8,128)S(1)} %get-tuple-element.17), channel_id=1, source_target_pairs={{0,1},{1,0},{2,3},{3,2},{4,5},{5,4},{6,7},{7,6},{8,9},{9,8},{10,11... | collective-permute-start | bytes 3244040 | tf_op jit(solution)/shard_map/ppermute | solution.py:558
  38.6 11.2 %collective-permute-start.5 = (f32[232,512]{1,0:T(8,128)S(1)}, f32[232,512]{1,0:T(8,128)S(1)}, u32[]{:S(2)}, u32[]{:S(2)}) collective-permute-start(f32[232,512]{1,0:T(8,128)S(1)} %get-tuple-element.18), channel_id=1, source_target_pairs={{1,3},{2,0},{3,5},{4,2},{5,7},{6,4},{7,9},{8,6},{9,11},{10,8},{11,... | collective-permute-start | bytes 1425416 | tf_op jit(solution)/shard_map/ppermute | solution.py:102
  49.8 0.1 outward.1
  49.9 1.9 %collective-permute-start.6 = (f32[264,512]{1,0:T(8,128)S(1)}, f32[264,512]{1,0:T(8,128)S(1)}, u32[]{:S(2)}, u32[]{:S(2)}) collective-permute-start(f32[264,512]{1,0:T(8,128)S(1)} %outward.1), channel_id=1, source_target_pairs={{0,2},{2,4},{3,1},{4,6},{5,3},{6,8},{7,5},{8,10},{9,7},{10,12},{11... | collective-permute-start | bytes 1622024 | tf_op jit(solution)/shard_map/ppermute | solution.py:102
  51.8 7.2 %collective-permute-done.5.far_ref = f32[232,512]{1,0:T(8,128)S(1)} collective-permute-done((f32[232,512]{1,0:T(8,128)S(1)}, f32[232,512]{1,0:T(8,128)S(1)}, u32[]{:S(2)}, u32[]{:S(2)}) %collective-permute-start.5) | collective-permute-done | bytes 475168 | tf_op jit(solution)/shard_map/ppermute | solution.py:102
  59.0 0.2 early_part.1
  59.3 4.0 %collective-permute-done.6.near_ref = f32[264,512]{1,0:T(8,128)S(1)} collective-permute-done((f32[264,512]{1,0:T(8,128)S(1)}, f32[264,512]{1,0:T(8,128)S(1)}, u32[]{:S(2)}, u32[]{:S(2)}) %collective-permute-start.6) | collective-permute-done | bytes 540704 | tf_op jit(solution)/shard_map/ppermute | solution.py:102
  63.2 2.8 %gradient_step.1 = (f32[16,16,512]{2,1,0:T(8,128)}, f32[3,8,16,16]{3,2,1,0:T(8,128)}) custom-call(f32[16,16,512]{2,1,0:T(8,128)S(1)} %get-tuple-element.20.part_ref, f32[512,256]{1,0:T(8,128)S(1)} %get-tuple-element.21.early_ref, f32[528,512]{1,0:T(8,128)S(1)} %collective-permute-done.4.swapped_ref, f32[264,512]{1,0:T(8,128)S(1)} %collective-permute-done.6.near_ref, ...), custom_call_target="tpu_custom_call" | custom-call | flops 15000000 | bytes 4000000 | tf_op jit(solution)/shard_map/gradient_step/pallas_call | solution.py:519
  (14 shorter events, 0.0 us)
Async XLA Ops:
  0.6 17.4 %copy-start.6 = (f32[5]{0:T(128)S(1)}, f32[5]{0:T(128)}, u32[]{:S(2)}) copy-start(f32[5]{0:T(128)} %constant.12.clone) | copy-start | bytes 64
  0.6 17.5 %copy-start.2 = (f32[8,16,16]{2,1,0:T(8,128)S(1)}, f32[8,16,16]{2,1,0:T(8,128)}, u32[]{:S(2)}) copy-start(f32[8,16,16]{2,1,0:T(8,128)} %spread_ref.1) | copy-start | bytes 24580
  0.7 17.5 %copy-start.1 = (s32[8,16,16]{2,1,0:T(8,128)S(1)}, s32[8,16,16]{2,1,0:T(8,128)}, u32[]{:S(2)}) copy-start(s32[8,16,16]{2,1,0:T(8,128)} %index_ref.1) | copy-start | bytes 24580
  0.7 17.5 %copy-start = (f32[8,16,16]{2,1,0:T(8,128)S(1)}, f32[8,16,16]{2,1,0:T(8,128)}, u32[]{:S(2)}) copy-start(f32[8,16,16]{2,1,0:T(8,128)} %amp_ref.1) | copy-start | bytes 24580
  0.7 17.2 %copy-start.4 = (s32[4,512]{1,0:T(4,128)S(1)}, s32[4,512]{1,0:T(4,128)}, u32[]{:S(2)}) copy-start(s32[4,512]{1,0:T(4,128)} %param.11) | copy-start | bytes 24580
  0.7 17.2 %copy-start.5 = (f32[16]{0:T(128)S(1)}, f32[16]{0:T(128)}, u32[]{:S(2)}) copy-start(f32[16]{0:T(128)} %param.10) | copy-start | bytes 196
  2.0 31.3 %copy-start.3 = (bf16[6,80,160]{2,1,0:T(8,128)(2,1)S(1)}, bf16[6,80,160]{2,1,0:T(8,128)(2,1)}, u32[]{:S(2)}) copy-start(bf16[6,80,160]{2,1,0:T(8,128)(2,1)} %constant.14.clone.k_ref) | copy-start | bytes 460804
  2.0 27.1 %collective-permute-start.1 = (f32[264,512]{1,0:T(8,128)S(1)}, f32[264,512]{1,0:T(8,128)S(1)}, u32[]{:S(2)}, u32[]{:S(2)}) collective-permute-start(f32[264,512]{1,0:T(8,128)S(1)} %pack.1.x_ref), channel_id=1, source_target_pairs={{32,64},{64,32},{96,128},{128,96},{160,192},{192,160},{224,256},{2... | collective-permute-start | bytes 1622024 | tf_op jit(solution)/shard_map/ppermute | solution.py:102
  7.6 25.6 %collective-permute-start = (f32[264,512]{1,0:T(8,128)S(1)}, f32[264,512]{1,0:T(8,128)S(1)}, u32[]{:S(2)}, u32[]{:S(2)}) collective-permute-start(f32[264,512]{1,0:T(8,128)S(1)} %pack.1.x_ref), channel_id=1, source_target_pairs={{0,32},{32,0},{64,96},{96,64},{128,160},{160,128},{192,224},{224,1... | collective-permute-start | bytes 1622024 | tf_op jit(solution)/shard_map/ppermute | solution.py:544
  10.8 15.1 %collective-permute-start.3 = (f32[14,16,512]{2,1,0:T(8,128)S(1)}, f32[14,16,512]{2,1,0:T(8,128)S(1)}, u32[]{:S(2)}, u32[]{:S(2)}) collective-permute-start(f32[14,16,512]{2,1,0:T(8,128)S(1)} %get-tuple-element.26), channel_id=1, source_target_pairs={{64,0},{96,32},{128,64},{160,96},{192,128},{224,160},{256,192},{28... | collective-permute-start | bytes 1376264 | tf_op jit(solution)/shard_map/ppermute | solution.py:96
  13.0 16.1 %collective-permute-start.2 = (f32[14,16,512]{2,1,0:T(8,128)S(1)}, f32[14,16,512]{2,1,0:T(8,128)S(1)}, u32[]{:S(2)}, u32[]{:S(2)}) collective-permute-start(f32[14,16,512]{2,1,0:T(8,128)S(1)} %get-tuple-element.27), channel_id=1, source_target_pairs={{0,64},{32,96},{64,128},{96,160},{128,192},{160,224},{192,256},{22... | collective-permute-start | bytes 1376264 | tf_op jit(solution)/shard_map/ppermute | solution.py:96
  36.6 13.2 %collective-permute-start.4 = (f32[528,512]{1,0:T(8,128)S(1)}, f32[528,512]{1,0:T(8,128)S(1)}, u32[]{:S(2)}, u32[]{:S(2)}) collective-permute-start(f32[528,512]{1,0:T(8,128)S(1)} %get-tuple-element.17), channel_id=1, source_target_pairs={{0,1},{1,0},{2,3},{3,2},{4,5},{5,4},{6,7},{7,6},{8,9},{9,8},{10,11... | collective-permute-start | bytes 3244040 | tf_op jit(solution)/shard_map/ppermute | solution.py:558
  38.6 20.5 %collective-permute-start.5 = (f32[232,512]{1,0:T(8,128)S(1)}, f32[232,512]{1,0:T(8,128)S(1)}, u32[]{:S(2)}, u32[]{:S(2)}) collective-permute-start(f32[232,512]{1,0:T(8,128)S(1)} %get-tuple-element.18), channel_id=1, source_target_pairs={{1,3},{2,0},{3,5},{4,2},{5,7},{6,4},{7,9},{8,6},{9,11},{10,8},{11,... | collective-permute-start | bytes 1425416 | tf_op jit(solution)/shard_map/ppermute | solution.py:102
  49.9 13.4 %collective-permute-start.6 = (f32[264,512]{1,0:T(8,128)S(1)}, f32[264,512]{1,0:T(8,128)S(1)}, u32[]{:S(2)}, u32[]{:S(2)}) collective-permute-start(f32[264,512]{1,0:T(8,128)S(1)} %outward.1), channel_id=1, source_target_pairs={{0,2},{2,4},{3,1},{4,6},{5,3},{6,8},{7,5},{8,10},{9,7},{10,12},{11... | collective-permute-start | bytes 1622024 | tf_op jit(solution)/shard_map/ppermute | solution.py:102

commit v13 on v11

--- a/solution.py
+++ b/solution.py
@@ -443,7 +443,6 @@
     inner, outer = swapped_ref[2 * PIXELS : 2 * PIXELS + COMPS, :EXT], near_ref[PIXELS:, :EXT]
     even = lax.rem(lax.axis_index("skyx"), 2) == 0
     left, right = jnp.where(even, outer, inner), jnp.where(even, inner, outer)
-    bases = smoothed([ext_ref[t] for t in range(3)], left, right)
     for part in range(parts):
         at = slice(part * rows, (part + 1) * rows)
         for row in range(part * rows, (part + 1) * rows):
@@ -452,6 +451,7 @@
         copies.append(pltpu.make_async_copy(den_ref.at[at], den_hbm.at[at], sem.at[part]))
         copies[-1].start()
 
+    bases = smoothed([ext_ref[t] for t in range(3)], left, right)
     shape = (COMPS, rows, LANES)
     own_lanes = lax.broadcasted_iota(jnp.int32, shape, 2) // TILE == lax.broadcasted_iota(jnp.int32, shape, 1)
     for part in range(parts):
@@ -461,8 +461,8 @@
     for part in range(parts):
         at = slice(part * LANES, (part + 1) * LANES)
         sums = [[] for _ in range(3)]
-        for first in range(0, COMPS, 4):
-            chosen = range(first, first + 4)
+        for first in range(0, COMPS, 8):
+            chosen = range(first, first + 8)
             mus = [jnp.broadcast_to(flat_ref[1, k : k + 1, at], (8, LANES)) for k in chosen]
 
             def body(step, carry):
@@ -478,10 +478,10 @@
                 return tuple(out)
 
             zero = jnp.zeros((8, LANES), jnp.float32)
-            done = lax.fori_loop(0, nch // 8, body, ((zero,) * 3,) * 4, unroll=16)
-            for four in done:
+            done = lax.fori_loop(0, nch // 8, body, ((zero,) * 3,) * 8, unroll=16)
+            for sums_of_one in done:
                 for t in range(3):
-                    sums[t].append(jnp.sum(four[t], axis=0, keepdims=True))
+                    sums[t].append(jnp.sum(sums_of_one[t], axis=0, keepdims=True))
         amp = flat_ref[0, :, at]
         inv = flat_ref[2, :, at]
         slope = amp * inv * inv

time: 66.9 us -> 66.9 us (level)
  no operation moved by 1% of the time
where the time goes in v13:
time: 66.9 us; the launch traced here: 66.5 us
  starting transfers between devices  29.3 us (44%)
  waiting for transfers between devices  25.3 us (38%)
  Pallas kernels  9.61 us (14%)
  local copies, waits for them, and re-layouts  1.28 us (2%)
  between operations  0.84 us (1%)
    ppermute x4, starting transfers between devices, sent(): return lax.ppermute(values, axis, pairs)  14.2 us
    ppermute x4, waiting for transfers between devices, sent(): return lax.ppermute(values, axis, pairs)  14.2 us
    ppermute x2, starting transfers between devices, away(): lax.ppermute(values, axis, [(i, j) for i, j in pairs if 0 <= j < size])  13.1 us
    ppermute x2, waiting for transfers between devices, away(): lax.ppermute(values, axis, [(i, j) for i, j in pairs if 0 <= j < size])  11.2 us
    pallas_call x1, Pallas kernels, wavelet_parts(): pl.pallas_call(wavelet_kernel, out_shape=[pltpu.VMEM(shape, jnp.float32)...  3.47 us
    pallas_call x1, Pallas kernels, gradient_step(): pl.pallas_call(step_kernel, out_shape=[jax.ShapeDtypeStruct(shape, jnp.fl...  2.84 us
    ppermute x1, starting transfers between devices, on_device(): swapped = lax.ppermute(swap, 'skyx', partner)  1.92 us
    pallas_call x1, Pallas kernels, model_of(): pl.pallas_call(model_kernel, out_shape=[pltpu.VMEM((nch, pixels), jnp.flo...  1.72 us
  transfers between devices with their start and end apart: 7, of which 4 were waited for; matrix products, arithmetic and copies ran while one was open for 2% of the time, Pallas kernels for 3%

profile of v13, /device:TPU:38, one launch (start us, length us, event | category | flops | bytes accessed | tf_op | source)
XLA Modules:
  0.0 66.5 jit_solution(17089610446229129839)
XLA Ops:
  0.6 0.0 copy-start.6
  0.7 1.3 %pack.1.x_ref = f32[264,512]{1,0:T(8,128)S(1)} custom-call(f32[256,512]{1,0:T(8,128)} %bitcast.1, f32[8,16,16]{2,1,0:T(8,128)} %amp_ref.1, s32[8,16,16]{2,1,0:T(8,128)} %index_ref.1, f32[8,16,16]{2,1,0:T(8,128)} %spread_ref.1), custom_call_target="tpu_custom_call" | custom-call | flops 1000 | bytes 1000000 | tf_op jit(solution)/shard_map/pack/pallas_call | solution.py:133
  2.0 0.0 copy-start.3
  2.0 3.4 %collective-permute-start.1 = (f32[264,512]{1,0:T(8,128)S(1)}, f32[264,512]{1,0:T(8,128)S(1)}, u32[]{:S(2)}, u32[]{:S(2)}) collective-permute-start(f32[264,512]{1,0:T(8,128)S(1)} %pack.1.x_ref), channel_id=1, source_target_pairs={{32,0},{64,32},{96,64},{128,96},{160,128},{192,160},{224,192},{256... | collective-permute-start | bytes 1622024 | tf_op jit(solution)/shard_map/ppermute | solution.py:96
  5.4 4.9 %collective-permute-start = (f32[264,512]{1,0:T(8,128)S(1)}, f32[264,512]{1,0:T(8,128)S(1)}, u32[]{:S(2)}, u32[]{:S(2)}) collective-permute-start(f32[264,512]{1,0:T(8,128)S(1)} %pack.1.x_ref), channel_id=1, source_target_pairs={{0,32},{32,64},{64,96},{96,128},{128,160},{160,192},{192,224},{224... | collective-permute-start | bytes 1622024 | tf_op jit(solution)/shard_map/ppermute | solution.py:96
  10.4 1.2 %fusion = (f32[14,16,512]{2,1,0:T(8,128)S(1)}, f32[14,16,512]{2,1,0:T(8,128)S(1)}) fusion(f32[16,16,512]{2,1,0:T(8,128)} %param.9), kind=kLoop, calls=%fused_computation.3 | loop fusion | bytes 1835008 | tf_op jit(solution)/shard_map/slice | solution.py:533
  11.6 3.6 %collective-permute-start.3 = (f32[14,16,512]{2,1,0:T(8,128)S(1)}, f32[14,16,512]{2,1,0:T(8,128)S(1)}, u32[]{:S(2)}, u32[]{:S(2)}) collective-permute-start(f32[14,16,512]{2,1,0:T(8,128)S(1)} %get-tuple-element.26), channel_id=1, source_target_pairs={{64,0},{96,32},{128,64},{160,96},{192,128},{224,160},{256,192},{28... | collective-permute-start | bytes 1376264 | tf_op jit(solution)/shard_map/ppermute | solution.py:96
  15.2 2.3 %collective-permute-start.2 = (f32[14,16,512]{2,1,0:T(8,128)S(1)}, f32[14,16,512]{2,1,0:T(8,128)S(1)}, u32[]{:S(2)}, u32[]{:S(2)}) collective-permute-start(f32[14,16,512]{2,1,0:T(8,128)S(1)} %get-tuple-element.27), channel_id=1, source_target_pairs={{0,64},{32,96},{64,128},{96,160},{128,192},{160,224},{192,256},{22... | collective-permute-start | bytes 1376264 | tf_op jit(solution)/shard_map/ppermute | solution.py:96
  17.5 0.1 select_reduce_fusion
  17.6 0.1 subtract_multiply_fusion
  17.7 1.7 %gaussian_model.1 = (f32[512,256]{1,0:T(8,128)S(1)}, f32[3,8,256]{2,1,0:T(8,128)S(1)}, f32[3,8,384]{2,1,0:T(8,128)S(1)}, bf16[6,3,256,256]{3,2,1,0:T(8,128)(2,1)S(1)}, f32[8,512,256]{2,1,0:T(8,128)S(1)}) custom-call(f32[8,16,16]{2,1,0:T(8,128)S(1)} %copy-done, s32[8,16,16]{2,1,0:T(8,128)S(1)} %copy-done.1, f32[8,16,16]{2,1,0:T(8,128)S(1)} %copy-done.2, ...), custom_call_target="tpu_custom_call" | custom-call | flops 10000000 | bytes 1000000 | tf_op jit(solution)/shard_map/gaussian_model/pallas_call | solution.py:388
  19.4 5.8 %collective-permute-done.3.p2 = f32[14,16,512]{2,1,0:T(8,128)S(1)} collective-permute-done((f32[14,16,512]{2,1,0:T(8,128)S(1)}, f32[14,16,512]{2,1,0:T(8,128)S(1)}, u32[]{:S(2)}, u32[]{:S(2)}) %collective-permute-start.3) | collective-permute-done | bytes 458784 | tf_op jit(solution)/shard_map/ppermute | solution.py:96
  25.2 8.4 %collective-permute-done.2.m2 = f32[14,16,512]{2,1,0:T(8,128)S(1)} collective-permute-done((f32[14,16,512]{2,1,0:T(8,128)S(1)}, f32[14,16,512]{2,1,0:T(8,128)S(1)}, u32[]{:S(2)}, u32[]{:S(2)}) %collective-permute-start.2) | collective-permute-done | bytes 458784 | tf_op jit(solution)/shard_map/ppermute | solution.py:96
  33.6 0.0 collective-permute-done.1.p1
  33.6 0.0 collective-permute-done.m1
  33.6 3.5 %wavelet_parts.1 = (f32[16,16,512]{2,1,0:T(8,128)S(1)}, f32[528,512]{1,0:T(8,128)S(1)}, f32[256,512]{1,0:T(8,128)S(1)}, f32[232,512]{1,0:T(8,128)S(1)}, f32[3,8,384]{2,1,0:T(8,128)S(1)}) custom-call(f32[5,1,512]{2,1,0:T(1,128)S(1)} %broadcast_in_dim.2.a_ref, f32[264,512]{1,0:T(8,128)S(1)} %collective-permute-done.m1, ...), custom_call_target="tpu_custom_call" | custom-call | flops 4000000000 | bytes 9000000 | tf_op jit(solution)/shard_map/wavelet_parts/pallas_call | solution.py:312
  37.1 1.9 %collective-permute-start.4 = (f32[528,512]{1,0:T(8,128)S(1)}, f32[528,512]{1,0:T(8,128)S(1)}, u32[]{:S(2)}, u32[]{:S(2)}) collective-permute-start(f32[528,512]{1,0:T(8,128)S(1)} %get-tuple-element.17), channel_id=1, source_target_pairs={{0,1},{1,0},{2,3},{3,2},{4,5},{5,4},{6,7},{7,6},{8,9},{9,8},{10,11... | collective-permute-start | bytes 3244040 | tf_op jit(solution)/shard_map/ppermute | solution.py:545
  39.0 11.2 %collective-permute-start.5 = (f32[232,512]{1,0:T(8,128)S(1)}, f32[232,512]{1,0:T(8,128)S(1)}, u32[]{:S(2)}, u32[]{:S(2)}) collective-permute-start(f32[232,512]{1,0:T(8,128)S(1)} %get-tuple-element.18), channel_id=1, source_target_pairs={{1,3},{2,0},{3,5},{4,2},{5,7},{6,4},{7,9},{8,6},{9,11},{10,8},{11,... | collective-permute-start | bytes 1425416 | tf_op jit(solution)/shard_map/ppermute | solution.py:102
  50.2 0.1 outward.1
  50.3 1.9 %collective-permute-start.6 = (f32[264,512]{1,0:T(8,128)S(1)}, f32[264,512]{1,0:T(8,128)S(1)}, u32[]{:S(2)}, u32[]{:S(2)}) collective-permute-start(f32[264,512]{1,0:T(8,128)S(1)} %outward.1), channel_id=1, source_target_pairs={{0,2},{2,4},{3,1},{4,6},{5,3},{6,8},{7,5},{8,10},{9,7},{10,12},{11... | collective-permute-start | bytes 1622024 | tf_op jit(solution)/shard_map/ppermute | solution.py:102
  52.3 7.2 %collective-permute-done.5.far_ref = f32[232,512]{1,0:T(8,128)S(1)} collective-permute-done((f32[232,512]{1,0:T(8,128)S(1)}, f32[232,512]{1,0:T(8,128)S(1)}, u32[]{:S(2)}, u32[]{:S(2)}) %collective-permute-start.5) | collective-permute-done | bytes 475168 | tf_op jit(solution)/shard_map/ppermute | solution.py:102
  59.5 0.2 early_part.1
  59.7 4.0 %collective-permute-done.6.near_ref = f32[264,512]{1,0:T(8,128)S(1)} collective-permute-done((f32[264,512]{1,0:T(8,128)S(1)}, f32[264,512]{1,0:T(8,128)S(1)}, u32[]{:S(2)}, u32[]{:S(2)}) %collective-permute-start.6) | collective-permute-done | bytes 540704 | tf_op jit(solution)/shard_map/ppermute | solution.py:102
  63.7 2.8 %gradient_step.1 = (f32[16,16,512]{2,1,0:T(8,128)}, f32[3,8,16,16]{3,2,1,0:T(8,128)}) custom-call(f32[16,16,512]{2,1,0:T(8,128)S(1)} %get-tuple-element.20.part_ref, f32[512,256]{1,0:T(8,128)S(1)} %get-tuple-element.21.early_ref, f32[528,512]{1,0:T(8,128)S(1)} %collective-permute-done.4.swapped_ref, f32[264,512]{1,0:T(8,128)S(1)} %collective-permute-done.6.near_ref, ...), custom_call_target="tpu_custom_call" | custom-call | flops 15000000 | bytes 4000000 | tf_op jit(solution)/shard_map/gradient_step/pallas_call | solution.py:507
  (14 shorter events, 0.0 us)
Async XLA Ops:
  0.6 17.0 %copy-start.6 = (f32[5]{0:T(128)S(1)}, f32[5]{0:T(128)}, u32[]{:S(2)}) copy-start(f32[5]{0:T(128)} %constant.12.clone) | copy-start | bytes 64
  0.6 17.0 %copy-start.2 = (f32[8,16,16]{2,1,0:T(8,128)S(1)}, f32[8,16,16]{2,1,0:T(8,128)}, u32[]{:S(2)}) copy-start(f32[8,16,16]{2,1,0:T(8,128)} %spread_ref.1) | copy-start | bytes 24580
  0.7 17.0 %copy-start.1 = (s32[8,16,16]{2,1,0:T(8,128)S(1)}, s32[8,16,16]{2,1,0:T(8,128)}, u32[]{:S(2)}) copy-start(s32[8,16,16]{2,1,0:T(8,128)} %index_ref.1) | copy-start | bytes 24580
  0.7 17.0 %copy-start = (f32[8,16,16]{2,1,0:T(8,128)S(1)}, f32[8,16,16]{2,1,0:T(8,128)}, u32[]{:S(2)}) copy-start(f32[8,16,16]{2,1,0:T(8,128)} %amp_ref.1) | copy-start | bytes 24580
  0.7 16.8 %copy-start.4 = (s32[4,512]{1,0:T(4,128)S(1)}, s32[4,512]{1,0:T(4,128)}, u32[]{:S(2)}) copy-start(s32[4,512]{1,0:T(4,128)} %param.11) | copy-start | bytes 24580
  0.7 16.8 %copy-start.5 = (f32[16]{0:T(128)S(1)}, f32[16]{0:T(128)}, u32[]{:S(2)}) copy-start(f32[16]{0:T(128)} %param.10) | copy-start | bytes 196
  2.0 31.6 %copy-start.3 = (bf16[6,80,160]{2,1,0:T(8,128)(2,1)S(1)}, bf16[6,80,160]{2,1,0:T(8,128)(2,1)}, u32[]{:S(2)}) copy-start(bf16[6,80,160]{2,1,0:T(8,128)(2,1)} %constant.14.clone.k_ref) | copy-start | bytes 460804
  2.0 31.6 %collective-permute-start.1 = (f32[264,512]{1,0:T(8,128)S(1)}, f32[264,512]{1,0:T(8,128)S(1)}, u32[]{:S(2)}, u32[]{:S(2)}) collective-permute-start(f32[264,512]{1,0:T(8,128)S(1)} %pack.1.x_ref), channel_id=1, source_target_pairs={{32,0},{64,32},{96,64},{128,96},{160,128},{192,160},{224,192},{256... | collective-permute-start | bytes 1622024 | tf_op jit(solution)/shard_map/ppermute | solution.py:96
  5.4 28.2 %collective-permute-start = (f32[264,512]{1,0:T(8,128)S(1)}, f32[264,512]{1,0:T(8,128)S(1)}, u32[]{:S(2)}, u32[]{:S(2)}) collective-permute-start(f32[264,512]{1,0:T(8,128)S(1)} %pack.1.x_ref), channel_id=1, source_target_pairs={{0,32},{32,64},{64,96},{96,128},{128,160},{160,192},{192,224},{224... | collective-permute-start | bytes 1622024 | tf_op jit(solution)/shard_map/ppermute | solution.py:96
  11.6 13.6 %collective-permute-start.3 = (f32[14,16,512]{2,1,0:T(8,128)S(1)}, f32[14,16,512]{2,1,0:T(8,128)S(1)}, u32[]{:S(2)}, u32[]{:S(2)}) collective-permute-start(f32[14,16,512]{2,1,0:T(8,128)S(1)} %get-tuple-element.26), channel_id=1, source_target_pairs={{64,0},{96,32},{128,64},{160,96},{192,128},{224,160},{256,192},{28... | collective-permute-start | bytes 1376264 | tf_op jit(solution)/shard_map/ppermute | solution.py:96
  15.2 18.4 %collective-permute-start.2 = (f32[14,16,512]{2,1,0:T(8,128)S(1)}, f32[14,16,512]{2,1,0:T(8,128)S(1)}, u32[]{:S(2)}, u32[]{:S(2)}) collective-permute-start(f32[14,16,512]{2,1,0:T(8,128)S(1)} %get-tuple-element.27), channel_id=1, source_target_pairs={{0,64},{32,96},{64,128},{96,160},{128,192},{160,224},{192,256},{22... | collective-permute-start | bytes 1376264 | tf_op jit(solution)/shard_map/ppermute | solution.py:96
  37.1 13.2 %collective-permute-start.4 = (f32[528,512]{1,0:T(8,128)S(1)}, f32[528,512]{1,0:T(8,128)S(1)}, u32[]{:S(2)}, u32[]{:S(2)}) collective-permute-start(f32[528,512]{1,0:T(8,128)S(1)} %get-tuple-element.17), channel_id=1, source_target_pairs={{0,1},{1,0},{2,3},{3,2},{4,5},{5,4},{6,7},{7,6},{8,9},{9,8},{10,11... | collective-permute-start | bytes 3244040 | tf_op jit(solution)/shard_map/ppermute | solution.py:545
  39.0 20.5 %collective-permute-start.5 = (f32[232,512]{1,0:T(8,128)S(1)}, f32[232,512]{1,0:T(8,128)S(1)}, u32[]{:S(2)}, u32[]{:S(2)}) collective-permute-start(f32[232,512]{1,0:T(8,128)S(1)} %get-tuple-element.18), channel_id=1, source_target_pairs={{1,3},{2,0},{3,5},{4,2},{5,7},{6,4},{7,9},{8,6},{9,11},{10,8},{11,... | collective-permute-start | bytes 1425416 | tf_op jit(solution)/shard_map/ppermute | solution.py:102
  50.3 13.4 %collective-permute-start.6 = (f32[264,512]{1,0:T(8,128)S(1)}, f32[264,512]{1,0:T(8,128)S(1)}, u32[]{:S(2)}, u32[]{:S(2)}) collective-permute-start(f32[264,512]{1,0:T(8,128)S(1)} %outward.1), channel_id=1, source_target_pairs={{0,2},{2,4},{3,1},{4,6},{5,3},{6,8},{7,5},{8,10},{9,7},{10,12},{11... | collective-permute-start | bytes 1622024 | tf_op jit(solution)/shard_map/ppermute | solution.py:102

commit v14 on v13

--- a/solution.py
+++ b/solution.py
@@ -478,7 +478,7 @@
                 return tuple(out)
 
             zero = jnp.zeros((8, LANES), jnp.float32)
-            done = lax.fori_loop(0, nch // 8, body, ((zero,) * 3,) * 8, unroll=16)
+            done = lax.fori_loop(0, nch // 8, body, ((zero,) * 3,) * 8, unroll=32)
             for sums_of_one in done:
                 for t in range(3):
                     sums[t].append(jnp.sum(sums_of_one[t], axis=0, keepdims=True))

time: 66.9 us -> 66.8 us (level)
  no operation moved by 1% of the time
where the time goes in v14:
time: 66.8 us; the launch traced here: 66.5 us
  starting transfers between devices  29.3 us (44%)
  waiting for transfers between devices  25.3 us (38%)
  Pallas kernels  9.58 us (14%)
  local copies, waits for them, and re-layouts  1.28 us (2%)
  between operations  0.84 us (1%)
    ppermute x4, starting transfers between devices, sent(): return lax.ppermute(values, axis, pairs)  14.2 us
    ppermute x4, waiting for transfers between devices, sent(): return lax.ppermute(values, axis, pairs)  14.2 us
    ppermute x2, starting transfers between devices, away(): lax.ppermute(values, axis, [(i, j) for i, j in pairs if 0 <= j < size])  13.1 us
    ppermute x2, waiting for transfers between devices, away(): lax.ppermute(values, axis, [(i, j) for i, j in pairs if 0 <= j < size])  11.2 us
    pallas_call x1, Pallas kernels, wavelet_parts(): pl.pallas_call(wavelet_kernel, out_shape=[pltpu.VMEM(shape, jnp.float32)...  3.47 us
    pallas_call x1, Pallas kernels, gradient_step(): pl.pallas_call(step_kernel, out_shape=[jax.ShapeDtypeStruct(shape, jnp.fl...  2.8 us
    ppermute x1, starting transfers between devices, on_device(): swapped = lax.ppermute(swap, 'skyx', partner)  1.92 us
    pallas_call x1, Pallas kernels, model_of(): pl.pallas_call(model_kernel, out_shape=[pltpu.VMEM((nch, pixels), jnp.flo...  1.72 us
  transfers between devices with their start and end apart: 7, of which 4 were waited for; matrix products, arithmetic and copies ran while one was open for 2% of the time, Pallas kernels for 3%

profile of v14, /device:TPU:38, one launch (start us, length us, event | category | flops | bytes accessed | tf_op | source)
XLA Modules:
  0.0 66.5 jit_solution(116068369713328378)
XLA Ops:
  0.6 0.0 copy-start.6
  0.7 1.3 %pack.1.x_ref = f32[264,512]{1,0:T(8,128)S(1)} custom-call(f32[256,512]{1,0:T(8,128)} %bitcast.1, f32[8,16,16]{2,1,0:T(8,128)} %amp_ref.1, s32[8,16,16]{2,1,0:T(8,128)} %index_ref.1, f32[8,16,16]{2,1,0:T(8,128)} %spread_ref.1), custom_call_target="tpu_custom_call" | custom-call | flops 1000 | bytes 1000000 | tf_op jit(solution)/shard_map/pack/pallas_call | solution.py:133
  2.0 0.0 copy-start.3
  2.0 3.4 %collective-permute-start.1 = (f32[264,512]{1,0:T(8,128)S(1)}, f32[264,512]{1,0:T(8,128)S(1)}, u32[]{:S(2)}, u32[]{:S(2)}) collective-permute-start(f32[264,512]{1,0:T(8,128)S(1)} %pack.1.x_ref), channel_id=1, source_target_pairs={{32,0},{64,32},{96,64},{128,96},{160,128},{192,160},{224,192},{256... | collective-permute-start | bytes 1622024 | tf_op jit(solution)/shard_map/ppermute | solution.py:96
  5.4 4.9 %collective-permute-start = (f32[264,512]{1,0:T(8,128)S(1)}, f32[264,512]{1,0:T(8,128)S(1)}, u32[]{:S(2)}, u32[]{:S(2)}) collective-permute-start(f32[264,512]{1,0:T(8,128)S(1)} %pack.1.x_ref), channel_id=1, source_target_pairs={{0,32},{32,64},{64,96},{96,128},{128,160},{160,192},{192,224},{224... | collective-permute-start | bytes 1622024 | tf_op jit(solution)/shard_map/ppermute | solution.py:96
  10.4 1.2 %fusion = (f32[14,16,512]{2,1,0:T(8,128)S(1)}, f32[14,16,512]{2,1,0:T(8,128)S(1)}) fusion(f32[16,16,512]{2,1,0:T(8,128)} %param.9), kind=kLoop, calls=%fused_computation.3 | loop fusion | bytes 1835008 | tf_op jit(solution)/shard_map/slice | solution.py:533
  11.6 3.6 %collective-permute-start.3 = (f32[14,16,512]{2,1,0:T(8,128)S(1)}, f32[14,16,512]{2,1,0:T(8,128)S(1)}, u32[]{:S(2)}, u32[]{:S(2)}) collective-permute-start(f32[14,16,512]{2,1,0:T(8,128)S(1)} %get-tuple-element.26), channel_id=1, source_target_pairs={{64,0},{96,32},{128,64},{160,96},{192,128},{224,160},{256,192},{28... | collective-permute-start | bytes 1376264 | tf_op jit(solution)/shard_map/ppermute | solution.py:96
  15.2 2.3 %collective-permute-start.2 = (f32[14,16,512]{2,1,0:T(8,128)S(1)}, f32[14,16,512]{2,1,0:T(8,128)S(1)}, u32[]{:S(2)}, u32[]{:S(2)}) collective-permute-start(f32[14,16,512]{2,1,0:T(8,128)S(1)} %get-tuple-element.27), channel_id=1, source_target_pairs={{0,64},{32,96},{64,128},{96,160},{128,192},{160,224},{192,256},{22... | collective-permute-start | bytes 1376264 | tf_op jit(solution)/shard_map/ppermute | solution.py:96
  17.5 0.1 select_reduce_fusion
  17.6 0.1 subtract_multiply_fusion
  17.7 1.7 %gaussian_model.1 = (f32[512,256]{1,0:T(8,128)S(1)}, f32[3,8,256]{2,1,0:T(8,128)S(1)}, f32[3,8,384]{2,1,0:T(8,128)S(1)}, bf16[6,3,256,256]{3,2,1,0:T(8,128)(2,1)S(1)}, f32[8,512,256]{2,1,0:T(8,128)S(1)}) custom-call(f32[8,16,16]{2,1,0:T(8,128)S(1)} %copy-done, s32[8,16,16]{2,1,0:T(8,128)S(1)} %copy-done.1, f32[8,16,16]{2,1,0:T(8,128)S(1)} %copy-done.2, ...), custom_call_target="tpu_custom_call" | custom-call | flops 10000000 | bytes 1000000 | tf_op jit(solution)/shard_map/gaussian_model/pallas_call | solution.py:388
  19.4 5.8 %collective-permute-done.3.p2 = f32[14,16,512]{2,1,0:T(8,128)S(1)} collective-permute-done((f32[14,16,512]{2,1,0:T(8,128)S(1)}, f32[14,16,512]{2,1,0:T(8,128)S(1)}, u32[]{:S(2)}, u32[]{:S(2)}) %collective-permute-start.3) | collective-permute-done | bytes 458784 | tf_op jit(solution)/shard_map/ppermute | solution.py:96
  25.2 8.4 %collective-permute-done.2.m2 = f32[14,16,512]{2,1,0:T(8,128)S(1)} collective-permute-done((f32[14,16,512]{2,1,0:T(8,128)S(1)}, f32[14,16,512]{2,1,0:T(8,128)S(1)}, u32[]{:S(2)}, u32[]{:S(2)}) %collective-permute-start.2) | collective-permute-done | bytes 458784 | tf_op jit(solution)/shard_map/ppermute | solution.py:96
  33.6 0.0 collective-permute-done.1.p1
  33.6 0.0 collective-permute-done.m1
  33.6 3.5 %wavelet_parts.1 = (f32[16,16,512]{2,1,0:T(8,128)S(1)}, f32[528,512]{1,0:T(8,128)S(1)}, f32[256,512]{1,0:T(8,128)S(1)}, f32[232,512]{1,0:T(8,128)S(1)}, f32[3,8,384]{2,1,0:T(8,128)S(1)}) custom-call(f32[5,1,512]{2,1,0:T(1,128)S(1)} %broadcast_in_dim.2.a_ref, f32[264,512]{1,0:T(8,128)S(1)} %collective-permute-done.m1, ...), custom_call_target="tpu_custom_call" | custom-call | flops 4000000000 | bytes 9000000 | tf_op jit(solution)/shard_map/wavelet_parts/pallas_call | solution.py:312
  37.1 1.9 %collective-permute-start.4 = (f32[528,512]{1,0:T(8,128)S(1)}, f32[528,512]{1,0:T(8,128)S(1)}, u32[]{:S(2)}, u32[]{:S(2)}) collective-permute-start(f32[528,512]{1,0:T(8,128)S(1)} %get-tuple-element.17), channel_id=1, source_target_pairs={{0,1},{1,0},{2,3},{3,2},{4,5},{5,4},{6,7},{7,6},{8,9},{9,8},{10,11... | collective-permute-start | bytes 3244040 | tf_op jit(solution)/shard_map/ppermute | solution.py:545
  39.0 11.2 %collective-permute-start.5 = (f32[232,512]{1,0:T(8,128)S(1)}, f32[232,512]{1,0:T(8,128)S(1)}, u32[]{:S(2)}, u32[]{:S(2)}) collective-permute-start(f32[232,512]{1,0:T(8,128)S(1)} %get-tuple-element.18), channel_id=1, source_target_pairs={{1,3},{2,0},{3,5},{4,2},{5,7},{6,4},{7,9},{8,6},{9,11},{10,8},{11,... | collective-permute-start | bytes 1425416 | tf_op jit(solution)/shard_map/ppermute | solution.py:102
  50.2 0.1 outward.1
  50.3 1.9 %collective-permute-start.6 = (f32[264,512]{1,0:T(8,128)S(1)}, f32[264,512]{1,0:T(8,128)S(1)}, u32[]{:S(2)}, u32[]{:S(2)}) collective-permute-start(f32[264,512]{1,0:T(8,128)S(1)} %outward.1), channel_id=1, source_target_pairs={{0,2},{2,4},{3,1},{4,6},{5,3},{6,8},{7,5},{8,10},{9,7},{10,12},{11... | collective-permute-start | bytes 1622024 | tf_op jit(solution)/shard_map/ppermute | solution.py:102
  52.3 7.2 %collective-permute-done.5.far_ref = f32[232,512]{1,0:T(8,128)S(1)} collective-permute-done((f32[232,512]{1,0:T(8,128)S(1)}, f32[232,512]{1,0:T(8,128)S(1)}, u32[]{:S(2)}, u32[]{:S(2)}) %collective-permute-start.5) | collective-permute-done | bytes 475168 | tf_op jit(solution)/shard_map/ppermute | solution.py:102
  59.5 0.2 early_part.1
  59.7 4.0 %collective-permute-done.6.near_ref = f32[264,512]{1,0:T(8,128)S(1)} collective-permute-done((f32[264,512]{1,0:T(8,128)S(1)}, f32[264,512]{1,0:T(8,128)S(1)}, u32[]{:S(2)}, u32[]{:S(2)}) %collective-permute-start.6) | collective-permute-done | bytes 540704 | tf_op jit(solution)/shard_map/ppermute | solution.py:102
  63.7 2.8 %gradient_step.1 = (f32[16,16,512]{2,1,0:T(8,128)}, f32[3,8,16,16]{3,2,1,0:T(8,128)}) custom-call(f32[16,16,512]{2,1,0:T(8,128)S(1)} %get-tuple-element.20.part_ref, f32[512,256]{1,0:T(8,128)S(1)} %get-tuple-element.21.early_ref, f32[528,512]{1,0:T(8,128)S(1)} %collective-permute-done.4.swapped_ref, f32[264,512]{1,0:T(8,128)S(1)} %collective-permute-done.6.near_ref, ...), custom_call_target="tpu_custom_call" | custom-call | flops 15000000 | bytes 4000000 | tf_op jit(solution)/shard_map/gradient_step/pallas_call | solution.py:507
  (14 shorter events, 0.0 us)
Async XLA Ops:
  0.6 17.0 %copy-start.6 = (f32[5]{0:T(128)S(1)}, f32[5]{0:T(128)}, u32[]{:S(2)}) copy-start(f32[5]{0:T(128)} %constant.12.clone) | copy-start | bytes 64
  0.6 17.0 %copy-start.2 = (f32[8,16,16]{2,1,0:T(8,128)S(1)}, f32[8,16,16]{2,1,0:T(8,128)}, u32[]{:S(2)}) copy-start(f32[8,16,16]{2,1,0:T(8,128)} %spread_ref.1) | copy-start | bytes 24580
  0.7 17.0 %copy-start.1 = (s32[8,16,16]{2,1,0:T(8,128)S(1)}, s32[8,16,16]{2,1,0:T(8,128)}, u32[]{:S(2)}) copy-start(s32[8,16,16]{2,1,0:T(8,128)} %index_ref.1) | copy-start | bytes 24580
  0.7 17.0 %copy-start = (f32[8,16,16]{2,1,0:T(8,128)S(1)}, f32[8,16,16]{2,1,0:T(8,128)}, u32[]{:S(2)}) copy-start(f32[8,16,16]{2,1,0:T(8,128)} %amp_ref.1) | copy-start | bytes 24580
  0.7 16.8 %copy-start.4 = (s32[4,512]{1,0:T(4,128)S(1)}, s32[4,512]{1,0:T(4,128)}, u32[]{:S(2)}) copy-start(s32[4,512]{1,0:T(4,128)} %param.11) | copy-start | bytes 24580
  0.7 16.8 %copy-start.5 = (f32[16]{0:T(128)S(1)}, f32[16]{0:T(128)}, u32[]{:S(2)}) copy-start(f32[16]{0:T(128)} %param.10) | copy-start | bytes 196
  2.0 31.6 %copy-start.3 = (bf16[6,80,160]{2,1,0:T(8,128)(2,1)S(1)}, bf16[6,80,160]{2,1,0:T(8,128)(2,1)}, u32[]{:S(2)}) copy-start(bf16[6,80,160]{2,1,0:T(8,128)(2,1)} %constant.14.clone.k_ref) | copy-start | bytes 460804
  2.0 31.6 %collective-permute-start.1 = (f32[264,512]{1,0:T(8,128)S(1)}, f32[264,512]{1,0:T(8,128)S(1)}, u32[]{:S(2)}, u32[]{:S(2)}) collective-permute-start(f32[264,512]{1,0:T(8,128)S(1)} %pack.1.x_ref), channel_id=1, source_target_pairs={{32,0},{64,32},{96,64},{128,96},{160,128},{192,160},{224,192},{256... | collective-permute-start | bytes 1622024 | tf_op jit(solution)/shard_map/ppermute | solution.py:96
  5.4 28.2 %collective-permute-start = (f32[264,512]{1,0:T(8,128)S(1)}, f32[264,512]{1,0:T(8,128)S(1)}, u32[]{:S(2)}, u32[]{:S(2)}) collective-permute-start(f32[264,512]{1,0:T(8,128)S(1)} %pack.1.x_ref), channel_id=1, source_target_pairs={{0,32},{32,64},{64,96},{96,128},{128,160},{160,192},{192,224},{224... | collective-permute-start | bytes 1622024 | tf_op jit(solution)/shard_map/ppermute | solution.py:96
  11.6 13.6 %collective-permute-start.3 = (f32[14,16,512]{2,1,0:T(8,128)S(1)}, f32[14,16,512]{2,1,0:T(8,128)S(1)}, u32[]{:S(2)}, u32[]{:S(2)}) collective-permute-start(f32[14,16,512]{2,1,0:T(8,128)S(1)} %get-tuple-element.26), channel_id=1, source_target_pairs={{64,0},{96,32},{128,64},{160,96},{192,128},{224,160},{256,192},{28... | collective-permute-start | bytes 1376264 | tf_op jit(solution)/shard_map/ppermute | solution.py:96
  15.2 18.4 %collective-permute-start.2 = (f32[14,16,512]{2,1,0:T(8,128)S(1)}, f32[14,16,512]{2,1,0:T(8,128)S(1)}, u32[]{:S(2)}, u32[]{:S(2)}) collective-permute-start(f32[14,16,512]{2,1,0:T(8,128)S(1)} %get-tuple-element.27), channel_id=1, source_target_pairs={{0,64},{32,96},{64,128},{96,160},{128,192},{160,224},{192,256},{22... | collective-permute-start | bytes 1376264 | tf_op jit(solution)/shard_map/ppermute | solution.py:96
  37.1 13.2 %collective-permute-start.4 = (f32[528,512]{1,0:T(8,128)S(1)}, f32[528,512]{1,0:T(8,128)S(1)}, u32[]{:S(2)}, u32[]{:S(2)}) collective-permute-start(f32[528,512]{1,0:T(8,128)S(1)} %get-tuple-element.17), channel_id=1, source_target_pairs={{0,1},{1,0},{2,3},{3,2},{4,5},{5,4},{6,7},{7,6},{8,9},{9,8},{10,11... | collective-permute-start | bytes 3244040 | tf_op jit(solution)/shard_map/ppermute | solution.py:545
  39.0 20.5 %collective-permute-start.5 = (f32[232,512]{1,0:T(8,128)S(1)}, f32[232,512]{1,0:T(8,128)S(1)}, u32[]{:S(2)}, u32[]{:S(2)}) collective-permute-start(f32[232,512]{1,0:T(8,128)S(1)} %get-tuple-element.18), channel_id=1, source_target_pairs={{1,3},{2,0},{3,5},{4,2},{5,7},{6,4},{7,9},{8,6},{9,11},{10,8},{11,... | collective-permute-start | bytes 1425416 | tf_op jit(solution)/shard_map/ppermute | solution.py:102
  50.3 13.4 %collective-permute-start.6 = (f32[264,512]{1,0:T(8,128)S(1)}, f32[264,512]{1,0:T(8,128)S(1)}, u32[]{:S(2)}, u32[]{:S(2)}) collective-permute-start(f32[264,512]{1,0:T(8,128)S(1)} %outward.1), channel_id=1, source_target_pairs={{0,2},{2,4},{3,1},{4,6},{5,3},{6,8},{7,5},{8,10},{9,7},{10,12},{11... | collective-permute-start | bytes 1622024 | tf_op jit(solution)/shard_map/ppermute | solution.py:102
